TPU v7x, 32 devices: a whole 2x2x4 slice. The times are simulated.
32 devices in a mesh: sec: 4 (over y, x), seq: 4 (over z), tp: 2 (over core).
Axes of the slice: x: 2, y: 2, z: 4, core: 2. Of those that a mesh axis runs over, the one named last changes fastest.
Arguments:
- hidden: bfloat16 [1024, 5120], P('seq', ('sec', 'tp')), may hold values from -6 to 6
- projection: bfloat16 [5120, 5120], P('seq', ('sec', 'tp')), may hold values from -0.078125 to 0.078125
- norm_gain: float32 [5120], replicated, may hold values from 0.1 to 1.9
- old_logp: float32 [1024], P('seq'), may hold values from -2.5 to 0
- ref_logp: float32 [1024], P('seq'), may hold values from -2.5 to 0
- lengths: int32 [16], P('seq'), may hold values from 1 to 64, 512 in all
- group_of: int32 [16], P('seq'), may hold values from 0 to 1, as said below
- rewards: int32 [16], P('seq'), may hold values from 0 to 4
Outputs:
- ref_states: bfloat16 [512, 5120], P('seq', ('sec', 'tp'))
- token_terms: bfloat16 [512, 2], P('seq')
Inputs may be any that keep to these rules, and one draw needn't show every extreme that they name: `group_of`: each group number names exactly 8 responses. The lengths sum to 512; the longest is exactly 64.
All inputs are finite; a program needn't handle non-finite values. No bound on the sum of `lengths` on one device may be relied on, other than what follows from the above.
Results may differ from a plain program's by a relative error of at most 0.0039.
Values may be sent and summed in bfloat16 or wider, within the bound.
No kernel may reach another device: no remote copies, remote signals or barrier semaphores. Data moves between devices by JAX's collectives and lax.ppermute only.
A program may use at most 64 MiB of HBM per device.

v0:
```python
import jax
import jax.numpy as jnp
from jax import lax
from jax.sharding import PartitionSpec as P

D = 5120
TOK_DEV = 128
RESP_DEV = 4
GROUP = 8
LMAX = 64
SLOTS = 256


def refine(input_rows, projection, norm_gain):
    widened = input_rows.astype(jnp.float32)
    full_rows = lax.all_gather(input_rows, ("sec", "tp"), axis=1, tiled=True).astype(jnp.float32)
    squares = jnp.sum(full_rows * full_rows, axis=1, keepdims=True)
    normed = (full_rows * lax.rsqrt(squares / D + 1e-06) * norm_gain).astype(jnp.bfloat16)
    mixing = jnp.dot(
        normed,
        lax.all_gather(projection, "seq", axis=0, tiled=True),
        preferred_element_type=jnp.float32,
    )
    return (widened + mixing).astype(jnp.bfloat16)


def deliver(
    input_rows, token_terms, lengths, first_index, own_total, starts, seq_index, tile_rows, n_seq
):
    slot_count = input_rows.shape[0]
    slot_index = jnp.arange(slot_count, dtype=jnp.int32)
    offset = jnp.mod(slot_index - first_index, slot_count)
    filled = offset < own_total
    finish = jnp.cumsum(lengths)
    response = jnp.sum((finish[None, :] <= offset[:, None]).astype(jnp.int32), axis=1)
    response = jnp.minimum(response, lengths.shape[0] - 1)
    opening = jnp.take(finish - lengths, response)
    source = jnp.where(filled, response * LMAX + offset - opening, 0)
    send_rows = jnp.where(
        filled[:, None], jnp.take(input_rows, source, axis=0), jnp.zeros((), input_rows.dtype)
    )
    send_terms = jnp.where(
        filled[:, None], jnp.take(token_terms, source, axis=0), jnp.zeros((), token_terms.dtype)
    )
    arrived, arrived_terms = (
        lax.all_to_all(
            send_rows.reshape(n_seq, tile_rows, -1), "seq", split_axis=0, concat_axis=0, tiled=True
        ),
        lax.all_to_all(
            send_terms.reshape(n_seq, tile_rows, 2), "seq", split_axis=0, concat_axis=0, tiled=True
        ),
    )
    learner_row = jnp.arange(TOK_DEV, dtype=jnp.int32)
    packed = learner_row // tile_rows * slot_count + seq_index * tile_rows + learner_row % tile_rows
    sender = jnp.sum((starts[None, :] <= packed[:, None]).astype(jnp.int32), axis=1) - 1
    pick_index = sender * tile_rows + learner_row % tile_rows
    states = jnp.take(arrived.reshape(slot_count, -1), pick_index, axis=0)
    moved_terms = jnp.take(arrived_terms.reshape(slot_count, 2), pick_index, axis=0)
    return (states, moved_terms)


def shards(hidden, projection, norm_gain, old_logp, ref_logp, lengths, group_of, rewards):
    n_seq = lax.axis_size("seq")
    seq_index = lax.axis_index("seq")
    tile_rows = SLOTS // n_seq
    group_count = RESP_DEV * n_seq // GROUP
    member_table = (group_of[:, None] == jnp.arange(group_count, dtype=jnp.int32)[None, :]).astype(
        jnp.float32
    )
    reward_value = rewards.astype(jnp.float32)
    partial_value = jnp.stack(
        [
            jnp.dot(reward_value, member_table, precision=lax.Precision.HIGHEST),
            jnp.dot(reward_value * reward_value, member_table, precision=lax.Precision.HIGHEST),
        ]
    )
    own_total = jnp.sum(lengths)
    group_sums = lax.psum(partial_value, "seq")
    counts = lax.all_gather(jnp.reshape(own_total, (1,)), "seq", axis=0, tiled=True)
    group_mean = group_sums[0] / GROUP
    spread = jnp.maximum(jnp.sqrt(group_sums[1] / GROUP - group_mean * group_mean), 1.0)
    advantage = (
        reward_value - jnp.dot(member_table, group_mean, precision=lax.Precision.HIGHEST)
    ) / jnp.dot(member_table, spread, precision=lax.Precision.HIGHEST)
    log_ratio = ref_logp - old_logp
    penalty = jnp.exp(log_ratio) - log_ratio - 1.0
    token_terms = jnp.stack([jnp.repeat(advantage, LMAX), penalty], axis=1).astype(jnp.bfloat16)
    starts = jnp.cumsum(counts) - counts
    first_index = jnp.take(starts, seq_index)
    refined = refine(hidden, projection, norm_gain)
    return deliver(
        refined, token_terms, lengths, first_index, own_total, starts, seq_index, tile_rows, n_seq
    )


def solution(mesh):
    in_specs = (
        P("seq", ("sec", "tp")),
        P("seq", ("sec", "tp")),
        P(),
        P("seq"),
        P("seq"),
        P("seq"),
        P("seq"),
        P("seq"),
    )
    out_specs = (P("seq", ("sec", "tp")), P("seq", None))
    return jax.shard_map(shards, mesh=mesh, in_specs=in_specs, out_specs=out_specs, check_vma=False)
```

profile of v0, /device:TPU:0, one launch (start us, length us, event | category | flops | bytes accessed | tf_op | source)
XLA Modules:
  0.0 194.8 jit_solution(8165057458369865206)
XLA Ops:
  7.2 0.0 all-gather.3.cloned.1.call-start
  7.2 0.7 all-gather.3.cloned.1.call-update
  7.9 0.0 all-gather.5.cloned.1.call-start
  8.0 0.7 all-gather.5.cloned.1.call-update
  8.7 0.8 reduce-window.18
  9.5 1.2 dynamic-slice.3
  10.7 1.3 fusion.45
  12.0 1.4 dynamic-update-slice.1
  13.4 0.9 fusion.17
  14.3 0.9 fusion.18
  15.2 9.9 %all-reduce = s32[4]{0:T(128)S(1)} all-reduce(s32[4]{0:T(128)S(1)} %dynamic-update-slice.1), channel_id=1, replica_groups=mesh['sec'=4,'seq'=4,'tp'=2] {'seq'}, use_global_device_ids=true, to_apply=%add | all-reduce | flops 4 | bytes 32
  25.1 9.9 %psum.7 = f32[2,2]{1,0:T(2,128)S(1)} all-reduce(f32[2,2]{1,0:T(2,128)S(1)} %pad_maximum_fusion), channel_id=1, replica_groups=mesh['sec'=4,'seq'=4,'tp'=2] {'seq'}, use_global_device_ids=true, to_apply=%region_6.7 | all-reduce | flops 4 | bytes 32 | tf_op jit(solution)/shard_map/psum | solution.py:78
  35.0 0.2 reduce-window.17
  35.2 0.6 dynamic-slice.2
  36.4 0.1 convert_reduce_fusion
  36.5 0.1 min.37
  36.5 0.7 fusion.46
  37.2 0.5 broadcast.537
  37.7 3.1 %fusion.44 = (s32[256]{0:T(256)S(1)}, s32[256,1]{0,1:T(1,128)S(1)}) fusion(s32[]{:T(128)} %broadcast.537, s32[]{:T(128)} %bitcast.12, s32[]{:T(128)} %bitcast.11, s32[]{:T(128)} %bitcast.10, s32[]{:T(128)} %bitcast.9, s32[256,1]{0,1:T(1,128)S(1)} %bitcast.72), kind=kLoop, calls=%fused_computation.98 | loop fusion | flops 2304 | bytes 3092 | tf_op jit(solution)/shard_map/jit(_take)/gather | solution.py:37
  40.8 0.1 gather.34
  40.9 0.7 fusion.20
  41.6 0.8 convolution_bitcast_fusion
  42.5 0.9 fusion.15
  43.3 0.1 broadcast_in_dim.103
  43.4 0.1 stack_reshape.4
  43.5 0.1 copy.18
  43.7 0.7 compare_select_fusion
  44.3 0.9 gather_fusion.2
  45.2 0.1 copy.19
  45.3 0.7 compare_and_fusion
  46.0 0.6 broadcast_select_fusion.3
  46.6 3.2 %all-to-all-start.1 = ((bf16[4,64,2]{1,2,0:T(2,128)(2,1)}), bf16[4,64,2]{1,2,0:T(2,128)(2,1)S(1)}, u32[]{:S(2)}, u32[]{:S(2)}) async-start(bf16[4,64,2]{1,2,0:T(2,128)(2,1)} %broadcast_select_fusion.3), calls=%async_computation.1 | async-start | bytes 4096 | tf_op jit(solution)/shard_map/all_to_all | solution.py:49
  49.8 0.1 convert_reduce_fusion.1
  49.9 0.0 all-gather.3.cloned.1.call-done
  49.9 2.6 %fusion = f32[256]{0:T(256)S(1)} fusion(bf16[256,5120]{1,0:T(8,128)(2,1)} %all-gather.3.cloned.1.call-done), kind=kLoop, calls=%fused_computation.6 | loop fusion | flops 3931904 | bytes 2622464 | tf_op jit(solution)/shard_map/reduce_sum | solution.py:17
  52.6 111.5 %all-gather.5.cloned.1.call-done = bf16[5120,640]{1,0:T(8,128)(2,1)} async-done(((bf16[1280,640]{1,0:T(8,128)(2,1)}), bf16[5120,640]{1,0:T(8,128)(2,1)}) %all-gather.5.cloned.1.call-update) | async-done | bytes 6553616 | tf_op jit(solution)/shard_map/all_gather | solution.py:21
  164.1 5.9 %fusion.10 = bf16[256,640]{1,0:T(8,128)(2,1)S(1)} fusion(bf16[5120,640]{1,0:T(8,128)(2,1)} %all-gather.5.cloned.1.call-done, bf16[256,5120]{1,0:T(8,128)(2,1)} %all-gather.3.cloned.1.call-done, f32[5120]{0:T(1024)S(1)} %copy-done.1, f32[256]{0:T(256)S(1)} %add_rsqrt_fusion, bf16[256,640]{1,0:T(8,128)(2,1)S(1)} %copy-done), kind=kOutput, calls=%fused_computation.13 | convolution fusion | flops 1683456000 | bytes 9851904 | tf_op jit(solution)/shard_map/dot_general | solution.py:19
  170.0 1.2 gather_fusion
  171.2 0.9 select_select_fusion
  172.1 0.0 all-to-all-done.1
  172.1 3.5 %all-to-all-start = ((bf16[4,64,640]{2,1,0:T(8,128)(2,1)}), bf16[4,64,640]{2,1,0:T(8,128)(2,1)S(1)}, u32[]{:S(2)}, u32[]{:S(2)}) async-start(bf16[4,64,640]{2,1,0:T(8,128)(2,1)} %select_select_fusion), calls=%async_computation | async-start | bytes 655360 | tf_op jit(solution)/shard_map/all_to_all | solution.py:46
  175.6 0.1 copy.20
  175.7 0.7 gather_fusion.3
  176.4 0.1 broadcast_select_fusion.1
  176.5 0.6 copy.21
  177.1 9.2 %all-to-all-done = bf16[4,64,640]{2,1,0:T(8,128)(2,1)S(1)} async-done(((bf16[4,64,640]{2,1,0:T(8,128)(2,1)}), bf16[4,64,640]{2,1,0:T(8,128)(2,1)S(1)}, u32[]{:S(2)}, u32[]{:S(2)}) %all-to-all-start) | async-done | bytes 327712 | tf_op jit(solution)/shard_map/all_to_all | solution.py:46
  186.3 0.9 gather_fusion.1
  187.2 0.8 broadcast_select_fusion
  (17 shorter events, 0.1 us)
Async XLA Ops:
  7.2 156.9 %copy-start = (bf16[256,640]{1,0:T(8,128)(2,1)S(1)}, bf16[256,640]{1,0:T(8,128)(2,1)}, u32[]{:S(2)}) copy-start(bf16[256,640]{1,0:T(8,128)(2,1)} %param.8) | copy-start | bytes 983044
  7.2 156.9 %copy-start.1 = (f32[5120]{0:T(1024)S(1)}, f32[5120]{0:T(1024)}, u32[]{:S(2)}) copy-start(f32[5120]{0:T(1024)} %param.10) | copy-start | bytes 61444
  7.2 42.7 %all-gather.3.cloned.1.call-start = ((), (), s32[]{:S(2)}) async-start(), calls=%async_computation.2 | async-start | bytes 2949120 | tf_op jit(solution)/shard_map/all_gather | solution.py:16
  7.9 156.1 %all-gather.5.cloned.1.call-start = ((), (), s32[]{:S(2)}) async-start(), calls=%async_computation.3 | async-start | bytes 8192000 | tf_op jit(solution)/shard_map/all_gather | solution.py:21
  46.6 125.5 %all-to-all-start.1 = ((bf16[4,64,2]{1,2,0:T(2,128)(2,1)}), bf16[4,64,2]{1,2,0:T(2,128)(2,1)S(1)}, u32[]{:S(2)}, u32[]{:S(2)}) async-start(bf16[4,64,2]{1,2,0:T(2,128)(2,1)} %broadcast_select_fusion.3), calls=%async_computation.1 | async-start | bytes 4096 | tf_op jit(solution)/shard_map/all_to_all | solution.py:49
  172.1 14.2 %all-to-all-start = ((bf16[4,64,640]{2,1,0:T(8,128)(2,1)}), bf16[4,64,640]{2,1,0:T(8,128)(2,1)S(1)}, u32[]{:S(2)}, u32[]{:S(2)}) async-start(bf16[4,64,640]{2,1,0:T(8,128)(2,1)} %select_select_fusion), calls=%async_computation | async-start | bytes 655360 | tf_op jit(solution)/shard_map/all_to_all | solution.py:46
Sparse Core Ops, SparseCore 0:
  9.9 32.7 all-gather.2
  44.3 119.7 all-gather.4
where the time goes:
time: 195 us
  waiting for transfers between devices  122 us (63%)
  blocking collectives  19.8 us (10%)
  between operations  14.7 us (8%)
  other arithmetic  12.7 us (7%)
  local copies, waits for them, and re-layouts  9.39 us (5%)
  matrix products  9.35 us (5%)
  starting transfers between devices  6.75 us (3%)
    all_gather x1, waiting for transfers between devices, refine(): lax.all_gather(projection, 'seq', axis=0, tiled=True)  111 us
    unnamed x1, blocking collectives  9.92 us
    psum x1, blocking collectives, shards(): group_sums = lax.psum(partial_value, 'seq')  9.92 us
    all_to_all x1, waiting for transfers between devices, deliver(): lax.all_to_all(send_rows.reshape(n_seq, tile_rows, -1), 'seq', split_axis...  9.16 us
    dot_general x1, matrix products, refine(): jnp.dot(normed, lax.all_gather(projection, 'seq', axis=0, tiled=True), pr...  5.92 us
  transfers between devices with their start and end apart: 4, of which 2 were waited for; matrix products, arithmetic and copies ran while one was open for 15% of the time, Pallas kernels for 0%

commit v1 on v0

--- a/solution.py
+++ b/solution.py
@@ -1,6 +1,10 @@
+import functools
+
 import jax
 import jax.numpy as jnp
 from jax import lax
+from jax.experimental import pallas as pl
+from jax.experimental.pallas import tpu as pltpu
 from jax.sharding import PartitionSpec as P
 
 D = 5120
@@ -8,7 +12,274 @@
 RESP_DEV = 4
 GROUP = 8
 LMAX = 64
+TILE = 64
 SLOTS = 256
+EPS = 1e-06
+BF16 = jnp.bfloat16
+F32 = jnp.float32
+I32 = jnp.int32
+
+VMEM = pl.BlockSpec(memory_space=pltpu.VMEM)
+SMEM = pl.BlockSpec(memory_space=pltpu.SMEM)
+
+
+def iota(shape, dim):
+    return lax.broadcasted_iota(I32, shape, dim)
+
+
+def swap(x, axis, k):
+    n = lax.axis_size(axis)
+    return lax.ppermute(x, axis, [(i, i ^ k) for i in range(n)])
+
+
+def info_kernel(lengths, group_of, rewards, old_logp, ref_logp, out):
+    n = lengths.shape[0]
+    rows = old_logp.shape[0]
+    log_ratio = ref_logp[...] - old_logp[...]
+    penalty = jnp.exp(log_ratio) - log_ratio - 1.0
+    lane = iota((1, 128), 1)
+    last = jnp.zeros((1, 128), F32)
+    for r in range(n):
+        for place, ref in enumerate((lengths, group_of, rewards)):
+            last = jnp.where(lane == place * n + r, ref[r].astype(F32), last)
+    out[...] = jnp.zeros_like(out)
+    out[0:rows, :] = penalty.astype(BF16).astype(F32)
+    out[rows : rows + 1, :] = last
+
+
+def spread_kernel(n_sec, n_tp, lengths, own, sibling, *outs):
+    a = lax.axis_index("sec")
+    t = lax.axis_index("tp")
+    n_class = n_sec * n_tp
+    slots, width = outs[0].shape[0], own.shape[1]
+    rows = own.shape[0]
+    place = iota((n_sec * slots, 1), 0)
+    index = (place % slots) * n_class + ((place // slots) ^ a) * n_tp + t
+    source, finish = index, 0
+    for r in range(lengths.shape[0]):
+        finish = finish + lengths[r]
+        source = source + jnp.where(index >= finish, LMAX - lengths[r], 0)
+    source = jnp.where(index < finish, source, -1)
+    pick = (iota((n_sec * slots, rows), 1) == source).astype(BF16)
+    mine = jnp.dot(pick, own[...], preferred_element_type=F32)
+    other = jnp.dot(pick, sibling[...], preferred_element_type=F32)
+    first = jnp.where(t == 0, mine, other).astype(BF16)
+    second = jnp.where(t == 0, other, mine).astype(BF16)
+    for k, out in enumerate(outs):
+        out[:, 0:width] = first[k * slots : (k + 1) * slots]
+        out[:, width : 2 * width] = second[k * slots : (k + 1) * slots]
+
+
+def norm_kernel(n, gain, *refs):
+    inputs, outs, held = refs[:n], refs[n : 2 * n], refs[2 * n]
+    a = lax.axis_index("sec")
+    s = lax.axis_index("seq")
+    width = inputs[0].shape[1]
+    squares = 0.0
+    for ref in inputs:
+        x = ref[...].astype(F32)
+        squares = squares + jnp.sum(x * x, axis=1, keepdims=True)
+    scale = lax.rsqrt(squares / D + EPS)
+    for k, ref in enumerate(inputs):
+        start = pl.multiple_of((a ^ k) * width, 128)
+        held[k] = (ref[...].astype(F32) * scale * gain[:, pl.ds(start, width)]).astype(BF16)
+    for m, out in enumerate(outs):
+        out[...] = held[a ^ s ^ m]
+
+
+def put_counts(infos, row, n, counts):
+    s = lax.axis_index("seq")
+    for m, info in enumerate(infos):
+        total = 0.0
+        for r in range(n):
+            total = total + info[row, r]
+        counts[s ^ m] = total.astype(I32)
+
+
+def pack_kernel(n, n_class, n_resp, row, *refs):
+    infos, inputs, out, held, counts = refs[:n], refs[n : 2 * n], refs[2 * n], refs[2 * n + 1], refs[2 * n + 2]
+    s = lax.axis_index("seq")
+    c = lax.axis_index("sec") * lax.axis_size("tp") + lax.axis_index("tp")
+    slots = inputs[0].shape[0]
+    put_counts(infos, row, n_resp, counts)
+    lane = iota((1, n * slots), 1)
+    place = jnp.zeros((1, n * slots), I32)
+    first = 0
+    for b in range(n):
+        live = (counts[b] - c + n_class - 1) // n_class
+        block = lane // slots == (s ^ b)
+        q = lane % slots
+        place = jnp.where(block, jnp.where(q < live, first + q, -1), place)
+        first = first + live
+    for m, ref in enumerate(inputs):
+        held[m * slots : (m + 1) * slots, :] = ref[...]
+    pick = (iota((out.shape[0], n * slots), 0) == place).astype(BF16)
+    out[...] = jnp.dot(pick, held[...], preferred_element_type=F32).astype(BF16)
+
+
+def mix_kernel(n, n_class, n_resp, row, *refs):
+    infos = refs[:n]
+    lengths, hidden, projection, mine, other = refs[n : n + 5]
+    outs = refs[n + 5 : 2 * n + 5]
+    counts = refs[2 * n + 5]
+    s = lax.axis_index("seq")
+    t = lax.axis_index("tp")
+    n_tp = lax.axis_size("tp")
+    put_counts(infos, row, n_resp, counts)
+    tok = outs[0].shape[0]
+    tokens = n * tok
+    per_sec = mine.shape[0] * n_tp // n_class
+    place = iota((tokens, 1), 0)
+    w = place % tok
+    packed = w // TILE * (TILE * n) + ((place // tok) ^ s) * TILE + w % TILE
+    seq_of = jnp.zeros((tokens, 1), I32)
+    start = jnp.zeros((tokens, 1), I32)
+    finish = 0
+    for b in range(n):
+        finish = finish + counts[b]
+        passed = packed >= finish
+        seq_of = seq_of + passed.astype(I32)
+        start = jnp.where(passed, finish, start)
+    index = packed - start
+    cls = index % n_class
+    position = index // n_class
+    for b in range(n - 1):
+        live = (counts[b] - cls + n_class - 1) // n_class
+        position = position + jnp.where(seq_of > b, live, 0)
+    column = ((cls % n_tp) ^ t) * mine.shape[0] + (cls // n_tp) * per_sec + position
+    half = mine.shape[0]
+    pick_mine = (iota((tokens, half), 1) == column).astype(BF16)
+    pick_other = (iota((tokens, half), 1) + half == column).astype(BF16)
+    normed = jnp.dot(pick_mine, mine[...], preferred_element_type=F32) + jnp.dot(
+        pick_other, other[...], preferred_element_type=F32
+    )
+    mixing = jnp.dot(normed.astype(BF16), projection[...], preferred_element_type=F32)
+    source, ends = index, 0
+    for r in range(n_resp):
+        ends = ends + lengths[r]
+        source = source + jnp.where(index >= ends, LMAX - lengths[r], 0)
+    source = jnp.where(seq_of == s, source, -1)
+    pick = (iota((tokens, hidden.shape[0]), 1) == source).astype(BF16)
+    total = mixing + jnp.dot(pick, hidden[...], preferred_element_type=F32)
+    for m, out in enumerate(outs):
+        out[...] = total[m * tok : (m + 1) * tok].astype(out.dtype)
+
+
+def terms_kernel(n, n_resp, row, *refs):
+    infos, out, words, table = refs[:n], refs[n], refs[n + 1], refs[n + 2]
+    s = lax.axis_index("seq")
+    tok = out.shape[1]
+    group_count = n * n_resp // GROUP
+    for m, info in enumerate(infos):
+        table[pl.ds((s ^ m) * row, row), :] = info[0:row, :]
+        for r in range(3 * n_resp):
+            words[s ^ m, r] = jnp.sum(jnp.where(iota((1, 128), 1) == r, info[row : row + 1, :], 0.0)).astype(I32)
+    w = iota((1, tok), 1)
+    packed = w // TILE * (TILE * n) + s * TILE + w % TILE
+    source, finish = packed, 0
+    reward = jnp.zeros((1, tok), F32)
+    group = jnp.zeros((1, tok), I32)
+    total = [0] * group_count
+    square = [0] * group_count
+    for b in range(n):
+        for r in range(n_resp):
+            length, number, gain = words[b, r], words[b, n_resp + r], words[b, 2 * n_resp + r]
+            within = packed >= finish
+            reward = jnp.where(within, gain.astype(F32), reward)
+            group = jnp.where(within, number, group)
+            finish = finish + length
+            source = source + jnp.where(packed >= finish, LMAX - length, 0)
+            for g in range(group_count):
+                total[g] = total[g] + jnp.where(number == g, gain, 0)
+                square[g] = square[g] + jnp.where(number == g, gain * gain, 0)
+    total_of = jnp.zeros((1, tok), F32)
+    square_of = jnp.zeros((1, tok), F32)
+    for g in range(group_count):
+        total_of = jnp.where(group == g, total[g].astype(F32), total_of)
+        square_of = jnp.where(group == g, square[g].astype(F32), square_of)
+    mean = total_of / GROUP
+    spread = jnp.maximum(jnp.sqrt(square_of / GROUP - mean * mean), 1.0)
+    advantage = (reward - mean) / spread
+    pick = (iota((128, tok), 0) == source % 128).astype(BF16)
+    found = jnp.dot(table[...].astype(BF16), pick, preferred_element_type=F32)
+    chosen = iota(found.shape, 0) == source // 128
+    penalty = jnp.sum(jnp.where(chosen, found, 0.0), axis=0, keepdims=True)
+    out[0:1, :] = advantage
+    out[1:2, :] = penalty
+
+
+def call(kernel, out_shape, in_specs, out_specs, scratch=()):
+    return pl.pallas_call(
+        kernel,
+        out_shape=out_shape,
+        in_specs=in_specs,
+        out_specs=out_specs,
+        scratch_shapes=list(scratch),
+        compiler_params=pltpu.CompilerParams(vmem_limit_bytes=48 * 1024 * 1024),
+    )
+
+
+def shards_in_place(hidden, projection, norm_gain, old_logp, ref_logp, lengths, group_of, rewards):
+    n = lax.axis_size("seq")
+    n_tp = lax.axis_size("tp")
+    n_class = n * n_tp
+    rows, cols = hidden.shape
+    n_resp = lengths.shape[0]
+    width = cols * n_tp
+    slots = rows // n_class
+    row = rows // 128
+    tokens = TOK_DEV * n
+    packed_rows = -(-((tokens + (n_class - 1) * n) // n_class) // 16) * 16
+    shape = jax.ShapeDtypeStruct
+
+    sibling = swap(hidden, "tp", 1)
+    info = call(info_kernel, shape((8, 128), F32), [SMEM] * 3 + [VMEM] * 2, VMEM)(
+        lengths, group_of, rewards, old_logp.reshape(row, 128), ref_logp.reshape(row, 128)
+    )
+    dealt = call(
+        functools.partial(spread_kernel, n, n_tp),
+        [shape((slots, width), BF16)] * n,
+        [SMEM, VMEM, VMEM],
+        [VMEM] * n,
+    )(lengths, hidden, sibling)
+    whole = [dealt[0]] + [swap(dealt[k], "sec", k) for k in range(1, n)]
+    infos = [info] + [swap(info, "seq", m) for m in range(1, n)]
+    normed = call(
+        functools.partial(norm_kernel, n),
+        [shape((slots, width), BF16)] * n,
+        [VMEM] * (n + 1),
+        [VMEM] * n,
+        [pltpu.VMEM((n, slots, width), BF16)],
+    )(norm_gain.reshape(1, D), *whole)
+    moved = [normed[0]] + [swap(normed[m], "seq", m) for m in range(1, n)]
+    packed = call(
+        functools.partial(pack_kernel, n, n_class, n_resp, row),
+        shape((packed_rows, width), BF16),
+        [SMEM] * n + [VMEM] * n,
+        VMEM,
+        [pltpu.VMEM((n * slots, width), BF16), pltpu.SMEM((n,), I32)],
+    )(*infos, *moved)
+    mine = lax.all_gather(packed, "sec", axis=0, tiled=True)
+    other = swap(mine, "tp", 1)
+    partial = call(
+        functools.partial(mix_kernel, n, n_class, n_resp, row),
+        [shape((TOK_DEV, cols), F32)] + [shape((TOK_DEV, cols), BF16)] * (n - 1),
+        [SMEM] * (n + 1) + [VMEM] * 4,
+        [VMEM] * n,
+        [pltpu.SMEM((n,), I32)],
+    )(*infos, lengths, hidden, projection, mine, other)
+    arrived = [swap(partial[m], "seq", m) for m in range(n - 1, 0, -1)]
+    terms = call(
+        functools.partial(terms_kernel, n, n_resp, row),
+        shape((2, TOK_DEV), F32),
+        [VMEM] * n,
+        VMEM,
+        [pltpu.SMEM((n, 3 * n_resp), I32), pltpu.VMEM((n * row, 128), F32)],
+    )(*infos)
+    states = partial[0]
+    for part in arrived:
+        states = states + part.astype(F32)
+    return states.astype(BF16), terms.astype(BF16).T
 
 
 def refine(input_rows, projection, norm_gain):
@@ -105,4 +376,5 @@
         P("seq"),
     )
     out_specs = (P("seq", ("sec", "tp")), P("seq", None))
-    return jax.shard_map(shards, mesh=mesh, in_specs=in_specs, out_specs=out_specs, check_vma=False)
+    body = shards_in_place if mesh.shape["sec"] == mesh.shape["seq"] else shards
+    return jax.shard_map(body, mesh=mesh, in_specs=in_specs, out_specs=out_specs, check_vma=False)

time: 195 us -> 70.3 us (0.36)
  waiting for transfers between devices: 122 us -> 21.3 us
  starting transfers between devices: 6.75 us -> 21.2 us
  between operations: 14.7 us -> 0.71 us
  other arithmetic: 12.7 us -> 1.26 us
  matrix products: 9.35 us -> 0 us
  Pallas kernels: 0 us -> 9.28 us
  blocking collectives: 19.8 us -> 10.6 us
  local copies, waits for them, and re-layouts: 9.39 us -> 5.68 us
    all_gather x2 -> x0, waiting for transfers between devices: 111 us -> none  [the longest x1 111 us: refine(): lax.all_gather(projection, 'seq', axis=0, tiled=True)]
    ppermute x0 -> x14, waiting for transfers between devices: none -> 21.3 us  [swap(): return lax.ppermute(x, axis, [(i, i ^ k) for i in range(n)])]
    ppermute x0 -> x14, starting transfers between devices: none -> 21.2 us  [swap(): return lax.ppermute(x, axis, [(i, i ^ k) for i in range(n)])]
    all_gather x0 -> x1, blocking collectives: none -> 10.6 us  [shards_in_place(): mine = lax.all_gather(packed, 'sec', axis=0, tiled=True)]
    unnamed x1 -> x0, blocking collectives: 9.92 us -> none
    psum x1 -> x0, blocking collectives: 9.92 us -> none  [shards(): group_sums = lax.psum(partial_value, 'seq')]
    dot_general x5 -> x0, matrix products: 9.35 us -> none  [the longest x1 5.92 us: refine(): jnp.dot(normed, lax.all_gather(projection, 'seq', axis=0, tiled=True), pr...]
    pallas_call x0 -> x6, Pallas kernels: none -> 9.28 us  [the longest x1 6.26 us: shards_in_place(): call(functools.partial(mix_kernel, n, n_class, n_resp, row), [shape((TOK_...]
  transfers between devices with their start and end apart: 4 -> 14, of which waited for: 2 -> 8; matrix products, arithmetic and copies ran while one was open for 15% -> 1% of each run, Pallas kernels for 0% -> 1%
where the time goes in v1:
time: 70.3 us; the launch traced here: 70 us
  waiting for transfers between devices  21.3 us (30%)
  starting transfers between devices  21.2 us (30%)
  blocking collectives  10.6 us (15%)
  Pallas kernels  9.28 us (13%)
  local copies, waits for them, and re-layouts  5.68 us (8%)
  other arithmetic  1.26 us (2%)
  between operations  0.71 us (1%)
    ppermute x14, waiting for transfers between devices, swap(): return lax.ppermute(x, axis, [(i, i ^ k) for i in range(n)])  21.3 us
    ppermute x14, starting transfers between devices, swap(): return lax.ppermute(x, axis, [(i, i ^ k) for i in range(n)])  21.2 us
    all_gather x1, blocking collectives, shards_in_place(): mine = lax.all_gather(packed, 'sec', axis=0, tiled=True)  10.6 us
    pallas_call x1, Pallas kernels, shards_in_place(): call(functools.partial(mix_kernel, n, n_class, n_resp, row), [shape((TOK_...  6.26 us
    unnamed x20, local copies, waits for them, and re-layouts  5.68 us
  transfers between devices with their start and end apart: 14, of which 8 were waited for; matrix products, arithmetic and copies ran while one was open for 1% of the time, Pallas kernels for 1%

profile of v1, /device:TPU:0, one launch (start us, length us, event | category | flops | bytes accessed | tf_op | source)
XLA Modules:
  0.0 70.0 jit_solution(4430296236463692103)
XLA Ops:
  0.6 0.0 copy-start
  0.6 0.5 collective-permute-start.3
  1.2 1.5 %collective-permute-done.3.sibling = bf16[256,640]{1,0:T(8,128)(2,1)S(1)} collective-permute-done((bf16[256,640]{1,0:T(8,128)(2,1)}, bf16[256,640]{1,0:T(8,128)(2,1)S(1)}, u32[]{:S(2)}, u32[]{:S(2)}) %collective-permute-start.3) | collective-permute-done | bytes 327712 | tf_op jit(solution)/shard_map/ppermute | solution.py:32
  2.6 1.0 %copy-done.1 = bf16[256,640]{1,0:T(8,128)(2,1)S(1)} copy-done((bf16[256,640]{1,0:T(8,128)(2,1)S(1)}, bf16[256,640]{1,0:T(8,128)(2,1)}, u32[]{:S(2)}) %copy-start.1) | copy-done | bytes 327704
  3.6 0.7 copy-done.4
  4.3 0.8 %shard_map.96 = (bf16[32,1280]{1,0:T(8,128)(2,1)S(1)}, bf16[32,1280]{1,0:T(8,128)(2,1)S(1)}, bf16[32,1280]{1,0:T(8,128)(2,1)S(1)}, bf16[32,1280]{1,0:T(8,128)(2,1)S(1)}) custom-call(s32[4]{0:T(128)S(1)} %copy-done.4, bf16[256,640]{1,0:T(8,128)(2,1)S(1)} %copy-done.1, bf16[256,640]{1,0:T(8,128)(2,1)S(1)} %collective-permute-done.3.sibling), custom_call_target="tpu_custom_call" | custom-call | tf_op jit(solution)/shard_map/pallas_call | solution.py:239
  5.1 2.9 %collective-permute-start.4 = (bf16[32,1280]{1,0:T(8,128)(2,1)S(1)}, bf16[32,1280]{1,0:T(8,128)(2,1)S(1)}, u32[]{:S(2)}, u32[]{:S(2)}) collective-permute-start(bf16[32,1280]{1,0:T(8,128)(2,1)S(1)} %get-tuple-element.15), channel_id=1, source_target_pairs={{0,8},{8,0},{16,24},{24,16},{1,9},{9,1},{17,25},{25,17},{2,10},{10... | collective-permute-start | bytes 245768 | tf_op jit(solution)/shard_map/ppermute | solution.py:32
  8.0 1.5 %collective-permute-start.5 = (bf16[32,1280]{1,0:T(8,128)(2,1)S(1)}, bf16[32,1280]{1,0:T(8,128)(2,1)S(1)}, u32[]{:S(2)}, u32[]{:S(2)}) collective-permute-start(bf16[32,1280]{1,0:T(8,128)(2,1)S(1)} %get-tuple-element.16), channel_id=1, source_target_pairs={{0,16},{8,24},{16,0},{24,8},{1,17},{9,25},{17,1},{25,9},{2,18},{10... | collective-permute-start | bytes 245768 | tf_op jit(solution)/shard_map/ppermute | solution.py:32
  9.5 0.0 collective-permute-start.6
  9.6 1.2 %collective-permute-done.4.refs_1_ = bf16[32,1280]{1,0:T(8,128)(2,1)S(1)} collective-permute-done((bf16[32,1280]{1,0:T(8,128)(2,1)S(1)}, bf16[32,1280]{1,0:T(8,128)(2,1)S(1)}, u32[]{:S(2)}, u32[]{:S(2)}) %collective-permute-start.4) | collective-permute-done | bytes 81952 | tf_op jit(solution)/shard_map/ppermute | solution.py:32
  10.8 2.5 %collective-permute-done.5.refs_2_ = bf16[32,1280]{1,0:T(8,128)(2,1)S(1)} collective-permute-done((bf16[32,1280]{1,0:T(8,128)(2,1)S(1)}, bf16[32,1280]{1,0:T(8,128)(2,1)S(1)}, u32[]{:S(2)}, u32[]{:S(2)}) %collective-permute-start.5) | collective-permute-done | bytes 81952 | tf_op jit(solution)/shard_map/ppermute | solution.py:32
  13.3 1.6 %collective-permute-done.6.refs_3_ = bf16[32,1280]{1,0:T(8,128)(2,1)S(1)} collective-permute-done((bf16[32,1280]{1,0:T(8,128)(2,1)S(1)}, bf16[32,1280]{1,0:T(8,128)(2,1)S(1)}, u32[]{:S(2)}, u32[]{:S(2)}) %collective-permute-start.6) | collective-permute-done | bytes 81952 | tf_op jit(solution)/shard_map/ppermute | solution.py:32
  14.9 0.7 %copy-done.3 = f32[5120]{0:T(1024)S(1)} copy-done((f32[5120]{0:T(1024)S(1)}, f32[5120]{0:T(1024)}, u32[]{:S(2)}) %copy-start.3) | copy-done | bytes 20504
  15.6 0.2 shard_map.97
  15.8 1.6 %collective-permute-start.7 = (bf16[32,1280]{1,0:T(8,128)(2,1)S(1)}, bf16[32,1280]{1,0:T(8,128)(2,1)S(1)}, u32[]{:S(2)}, u32[]{:S(2)}) collective-permute-start(bf16[32,1280]{1,0:T(8,128)(2,1)S(1)} %get-tuple-element.19), channel_id=1, source_target_pairs={{0,2},{2,0},{4,6},{6,4},{1,3},{3,1},{5,7},{7,5},{8,10},{10,8},{12,... | collective-permute-start | bytes 245768 | tf_op jit(solution)/shard_map/ppermute | solution.py:32
  17.5 2.6 %collective-permute-start.8 = (bf16[32,1280]{1,0:T(8,128)(2,1)S(1)}, bf16[32,1280]{1,0:T(8,128)(2,1)S(1)}, u32[]{:S(2)}, u32[]{:S(2)}) collective-permute-start(bf16[32,1280]{1,0:T(8,128)(2,1)S(1)} %get-tuple-element.20), channel_id=1, source_target_pairs={{0,4},{2,6},{4,0},{6,2},{1,5},{3,7},{5,1},{7,3},{8,12},{10,14},{12... | collective-permute-start | bytes 245768 | tf_op jit(solution)/shard_map/ppermute | solution.py:32
  20.1 0.2 collective-permute-start.9
  20.3 0.7 copy-done.5
  20.9 0.7 copy-done.6
  21.6 0.7 copy-done.7
  22.3 0.7 copy-done.8
  23.0 0.7 copy-done.9
  23.6 0.6 shard_map.95.refs_0_
  24.2 0.7 %collective-permute-start = (f32[8,128]{1,0:T(8,128)S(1)}, f32[8,128]{1,0:T(8,128)S(1)}, u32[]{:S(2)}, u32[]{:S(2)}) collective-permute-start(f32[8,128]{1,0:T(8,128)S(1)} %shard_map.95.refs_0_), channel_id=1, source_target_pairs={{0,2},{2,0},{4,6},{6,4},{1,3},{3,1},{5,7},{7,5},{8,10},{10,8},{12,... | collective-permute-start | bytes 12296 | tf_op jit(solution)/shard_map/ppermute | solution.py:32
  24.9 3.5 %collective-permute-start.1 = (f32[8,128]{1,0:T(8,128)S(1)}, f32[8,128]{1,0:T(8,128)S(1)}, u32[]{:S(2)}, u32[]{:S(2)}) collective-permute-start(f32[8,128]{1,0:T(8,128)S(1)} %shard_map.95.refs_0_), channel_id=1, source_target_pairs={{0,4},{2,6},{4,0},{6,2},{1,5},{3,7},{5,1},{7,3},{8,12},{10,14},{12... | collective-permute-start | bytes 12296 | tf_op jit(solution)/shard_map/ppermute | solution.py:32
  28.4 0.0 collective-permute-done.refs_1_
  28.4 3.0 %collective-permute-start.2 = (f32[8,128]{1,0:T(8,128)S(1)}, f32[8,128]{1,0:T(8,128)S(1)}, u32[]{:S(2)}, u32[]{:S(2)}) collective-permute-start(f32[8,128]{1,0:T(8,128)S(1)} %shard_map.95.refs_0_), channel_id=1, source_target_pairs={{0,6},{2,4},{4,2},{6,0},{1,7},{3,5},{5,3},{7,1},{8,14},{10,12},{12... | collective-permute-start | bytes 12296 | tf_op jit(solution)/shard_map/ppermute | solution.py:32
  31.5 0.0 collective-permute-done.1.refs_2_
  31.5 2.4 %collective-permute-done.2.refs_3_ = f32[8,128]{1,0:T(8,128)S(1)} collective-permute-done((f32[8,128]{1,0:T(8,128)S(1)}, f32[8,128]{1,0:T(8,128)S(1)}, u32[]{:S(2)}, u32[]{:S(2)}) %collective-permute-start.2) | collective-permute-done | bytes 4128 | tf_op jit(solution)/shard_map/ppermute | solution.py:32
  33.8 0.0 collective-permute-done.7.refs_5_
  33.8 0.0 collective-permute-done.8.refs_6_
  33.8 0.0 collective-permute-done.9.refs_7_
  33.8 1.0 %shard_map.98 = bf16[80,1280]{1,0:T(8,128)(2,1)S(1)} custom-call(f32[8,128]{1,0:T(8,128)S(1)} %shard_map.95.refs_0_, f32[8,128]{1,0:T(8,128)S(1)} %collective-permute-done.refs_1_, f32[8,128]{1,0:T(8,128)S(1)} %collective-permute-done.1.refs_2_, f32[8,128]{1,0:T(8,128)S(1)} %collective-permute-done.2.refs_3_, ...), custom_call_target="tpu_custom_call" | custom-call | tf_op jit(solution)/shard_map/pallas_call | solution.py:255
  34.9 10.6 %all_gather.3.refs_7_ = bf16[320,1280]{1,0:T(8,128)(2,1)S(1)} all-gather(bf16[80,1280]{1,0:T(8,128)(2,1)S(1)} %shard_map.98), channel_id=1, replica_groups=mesh['sec'=4,'seq'=4,'tp'=2] {'sec'}, dimensions={0}, use_global_device_ids=true | all-gather | bytes 1024000 | tf_op jit(solution)/shard_map/all_gather | solution.py:262
  45.5 0.0 collective-permute-start.10
  45.5 0.4 shard_map.100
  45.9 2.0 %collective-permute-done.10.refs_8_ = bf16[320,1280]{1,0:T(8,128)(2,1)S(1)} collective-permute-done((bf16[320,1280]{1,0:T(8,128)(2,1)S(1)}, bf16[320,1280]{1,0:T(8,128)(2,1)S(1)}, u32[]{:S(2)}, u32[]{:S(2)}) %collective-permute-start.10) | collective-permute-done | bytes 819232 | tf_op jit(solution)/shard_map/ppermute | solution.py:32
  47.8 0.0 copy-done
  47.8 0.0 copy-done.2
  47.8 6.3 %shard_map.99 = (f32[128,640]{1,0:T(8,128)S(1)}, bf16[128,640]{1,0:T(8,128)(2,1)S(1)}, bf16[128,640]{1,0:T(8,128)(2,1)S(1)}, bf16[128,640]{1,0:T(8,128)(2,1)S(1)}) custom-call(f32[8,128]{1,0:T(8,128)S(1)} %shard_map.95.refs_0_, f32[8,128]{1,0:T(8,128)S(1)} %collective-permute-done.refs_1_, f32[8,128]{1,0:T(8,128)S(1)} %collective-permute-done.1.refs_2_, ...), custom_call_target="tpu_custom_call" | custom-call | tf_op jit(solution)/shard_map/pallas_call | solution.py:264
  54.1 3.1 %collective-permute-start.11 = (bf16[128,640]{1,0:T(8,128)(2,1)S(1)}, bf16[128,640]{1,0:T(8,128)(2,1)S(1)}, u32[]{:S(2)}, u32[]{:S(2)}) collective-permute-start(bf16[128,640]{1,0:T(8,128)(2,1)S(1)} %get-tuple-element.23), channel_id=1, source_target_pairs={{0,6},{2,4},{4,2},{6,0},{1,7},{3,5},{5,3},{7,1},{8,14},{10,12},{12... | collective-permute-start | bytes 491528 | tf_op jit(solution)/shard_map/ppermute | solution.py:32
  57.2 0.0 collective-permute-start.12
  57.2 1.4 %collective-permute-start.13 = (bf16[128,640]{1,0:T(8,128)(2,1)S(1)}, bf16[128,640]{1,0:T(8,128)(2,1)S(1)}, u32[]{:S(2)}, u32[]{:S(2)}) collective-permute-start(bf16[128,640]{1,0:T(8,128)(2,1)S(1)} %get-tuple-element.25), channel_id=1, source_target_pairs={{0,2},{2,0},{4,6},{6,4},{1,3},{3,1},{5,7},{7,5},{8,10},{10,8},{12,... | collective-permute-start | bytes 491528 | tf_op jit(solution)/shard_map/ppermute | solution.py:32
  58.6 0.5 convert_bitcast_fusion
  59.1 4.1 %collective-permute-done.11 = bf16[128,640]{1,0:T(8,128)(2,1)S(1)} collective-permute-done((bf16[128,640]{1,0:T(8,128)(2,1)S(1)}, bf16[128,640]{1,0:T(8,128)(2,1)S(1)}, u32[]{:S(2)}, u32[]{:S(2)}) %collective-permute-start.11) | collective-permute-done | bytes 163872 | tf_op jit(solution)/shard_map/ppermute | solution.py:32
  63.2 6.1 %collective-permute-done.12 = bf16[128,640]{1,0:T(8,128)(2,1)S(1)} collective-permute-done((bf16[128,640]{1,0:T(8,128)(2,1)S(1)}, bf16[128,640]{1,0:T(8,128)(2,1)S(1)}, u32[]{:S(2)}, u32[]{:S(2)}) %collective-permute-start.12) | collective-permute-done | bytes 163872 | tf_op jit(solution)/shard_map/ppermute | solution.py:32
  69.3 0.0 collective-permute-done.13
  69.3 0.8 %add_convert_fusion = bf16[128,640]{1,0:T(8,128)(2,1)} fusion(bf16[128,640]{1,0:T(8,128)(2,1)S(1)} %collective-permute-done.13, bf16[128,640]{1,0:T(8,128)(2,1)S(1)} %collective-permute-done.12, f32[128,640]{1,0:T(8,128)S(1)} %get-tuple-element.22, bf16[128,640]{1,0:T(8,128)(2,1)S(1)} %collective-permute-done.11), kind=kLoop, calls=%fused_computation | loop fusion | flops 573440 | bytes 983040 | tf_op jit(solution)/shard_map/convert_element_type | solution.py:282
  (9 shorter events, 0.0 us)
Async XLA Ops:
  0.6 47.2 %copy-start = (bf16[1280,640]{1,0:T(8,128)(2,1)S(1)}, bf16[1280,640]{1,0:T(8,128)(2,1)}, u32[]{:S(2)}) copy-start(bf16[1280,640]{1,0:T(8,128)(2,1)} %refs_6_.1) | copy-start | bytes 4915204
  0.6 2.0 %collective-permute-start.3 = (bf16[256,640]{1,0:T(8,128)(2,1)}, bf16[256,640]{1,0:T(8,128)(2,1)S(1)}, u32[]{:S(2)}, u32[]{:S(2)}) collective-permute-start(bf16[256,640]{1,0:T(8,128)(2,1)} %refs_5_.1), channel_id=1, source_target_pairs={{0,1},{1,0},{2,3},{3,2},{4,5},{5,4},{6,7},{7,6},{8,9},{9,8},{10,11... | collective-permute-start | bytes 983048 | tf_op jit(solution)/shard_map/ppermute | solution.py:32
  2.6 1.0 %copy-start.1 = (bf16[256,640]{1,0:T(8,128)(2,1)S(1)}, bf16[256,640]{1,0:T(8,128)(2,1)}, u32[]{:S(2)}) copy-start(bf16[256,640]{1,0:T(8,128)(2,1)} %refs_5_.1) | copy-start | bytes 983044
  3.6 0.7 copy-start.4
  4.3 43.6 %copy-start.2 = (bf16[256,640]{1,0:T(8,128)(2,1)S(1)}, bf16[256,640]{1,0:T(8,128)(2,1)}, u32[]{:S(2)}) copy-start(bf16[256,640]{1,0:T(8,128)(2,1)} %refs_5_.1) | copy-start | bytes 983044
  5.1 5.7 %collective-permute-start.4 = (bf16[32,1280]{1,0:T(8,128)(2,1)S(1)}, bf16[32,1280]{1,0:T(8,128)(2,1)S(1)}, u32[]{:S(2)}, u32[]{:S(2)}) collective-permute-start(bf16[32,1280]{1,0:T(8,128)(2,1)S(1)} %get-tuple-element.15), channel_id=1, source_target_pairs={{0,8},{8,0},{16,24},{24,16},{1,9},{9,1},{17,25},{25,17},{2,10},{10... | collective-permute-start | bytes 245768 | tf_op jit(solution)/shard_map/ppermute | solution.py:32
  8.0 5.3 %collective-permute-start.5 = (bf16[32,1280]{1,0:T(8,128)(2,1)S(1)}, bf16[32,1280]{1,0:T(8,128)(2,1)S(1)}, u32[]{:S(2)}, u32[]{:S(2)}) collective-permute-start(bf16[32,1280]{1,0:T(8,128)(2,1)S(1)} %get-tuple-element.16), channel_id=1, source_target_pairs={{0,16},{8,24},{16,0},{24,8},{1,17},{9,25},{17,1},{25,9},{2,18},{10... | collective-permute-start | bytes 245768 | tf_op jit(solution)/shard_map/ppermute | solution.py:32
  9.5 5.3 %collective-permute-start.6 = (bf16[32,1280]{1,0:T(8,128)(2,1)S(1)}, bf16[32,1280]{1,0:T(8,128)(2,1)S(1)}, u32[]{:S(2)}, u32[]{:S(2)}) collective-permute-start(bf16[32,1280]{1,0:T(8,128)(2,1)S(1)} %get-tuple-element.17), channel_id=1, source_target_pairs={{0,24},{8,16},{16,8},{24,0},{1,25},{9,17},{17,9},{25,1},{2,26},{10... | collective-permute-start | bytes 245768 | tf_op jit(solution)/shard_map/ppermute | solution.py:32
  14.9 0.7 %copy-start.3 = (f32[5120]{0:T(1024)S(1)}, f32[5120]{0:T(1024)}, u32[]{:S(2)}) copy-start(f32[5120]{0:T(1024)} %param.10) | copy-start | bytes 61444
  15.8 18.0 %collective-permute-start.7 = (bf16[32,1280]{1,0:T(8,128)(2,1)S(1)}, bf16[32,1280]{1,0:T(8,128)(2,1)S(1)}, u32[]{:S(2)}, u32[]{:S(2)}) collective-permute-start(bf16[32,1280]{1,0:T(8,128)(2,1)S(1)} %get-tuple-element.19), channel_id=1, source_target_pairs={{0,2},{2,0},{4,6},{6,4},{1,3},{3,1},{5,7},{7,5},{8,10},{10,8},{12,... | collective-permute-start | bytes 245768 | tf_op jit(solution)/shard_map/ppermute | solution.py:32
  17.5 16.4 %collective-permute-start.8 = (bf16[32,1280]{1,0:T(8,128)(2,1)S(1)}, bf16[32,1280]{1,0:T(8,128)(2,1)S(1)}, u32[]{:S(2)}, u32[]{:S(2)}) collective-permute-start(bf16[32,1280]{1,0:T(8,128)(2,1)S(1)} %get-tuple-element.20), channel_id=1, source_target_pairs={{0,4},{2,6},{4,0},{6,2},{1,5},{3,7},{5,1},{7,3},{8,12},{10,14},{12... | collective-permute-start | bytes 245768 | tf_op jit(solution)/shard_map/ppermute | solution.py:32
  20.1 13.8 %collective-permute-start.9 = (bf16[32,1280]{1,0:T(8,128)(2,1)S(1)}, bf16[32,1280]{1,0:T(8,128)(2,1)S(1)}, u32[]{:S(2)}, u32[]{:S(2)}) collective-permute-start(bf16[32,1280]{1,0:T(8,128)(2,1)S(1)} %get-tuple-element.21), channel_id=1, source_target_pairs={{0,6},{2,4},{4,2},{6,0},{1,7},{3,5},{5,3},{7,1},{8,14},{10,12},{12... | collective-permute-start | bytes 245768 | tf_op jit(solution)/shard_map/ppermute | solution.py:32
  20.3 0.7 copy-start.5
  20.9 0.7 copy-start.6
  21.6 0.7 copy-start.7
  22.3 0.7 copy-start.8
  23.0 0.7 copy-start.9
  24.2 4.2 %collective-permute-start = (f32[8,128]{1,0:T(8,128)S(1)}, f32[8,128]{1,0:T(8,128)S(1)}, u32[]{:S(2)}, u32[]{:S(2)}) collective-permute-start(f32[8,128]{1,0:T(8,128)S(1)} %shard_map.95.refs_0_), channel_id=1, source_target_pairs={{0,2},{2,0},{4,6},{6,4},{1,3},{3,1},{5,7},{7,5},{8,10},{10,8},{12,... | collective-permute-start | bytes 12296 | tf_op jit(solution)/shard_map/ppermute | solution.py:32
  24.9 6.5 %collective-permute-start.1 = (f32[8,128]{1,0:T(8,128)S(1)}, f32[8,128]{1,0:T(8,128)S(1)}, u32[]{:S(2)}, u32[]{:S(2)}) collective-permute-start(f32[8,128]{1,0:T(8,128)S(1)} %shard_map.95.refs_0_), channel_id=1, source_target_pairs={{0,4},{2,6},{4,0},{6,2},{1,5},{3,7},{5,1},{7,3},{8,12},{10,14},{12... | collective-permute-start | bytes 12296 | tf_op jit(solution)/shard_map/ppermute | solution.py:32
  28.4 5.4 %collective-permute-start.2 = (f32[8,128]{1,0:T(8,128)S(1)}, f32[8,128]{1,0:T(8,128)S(1)}, u32[]{:S(2)}, u32[]{:S(2)}) collective-permute-start(f32[8,128]{1,0:T(8,128)S(1)} %shard_map.95.refs_0_), channel_id=1, source_target_pairs={{0,6},{2,4},{4,2},{6,0},{1,7},{3,5},{5,3},{7,1},{8,14},{10,12},{12... | collective-permute-start | bytes 12296 | tf_op jit(solution)/shard_map/ppermute | solution.py:32
  45.5 2.3 %collective-permute-start.10 = (bf16[320,1280]{1,0:T(8,128)(2,1)S(1)}, bf16[320,1280]{1,0:T(8,128)(2,1)S(1)}, u32[]{:S(2)}, u32[]{:S(2)}) collective-permute-start(bf16[320,1280]{1,0:T(8,128)(2,1)S(1)} %all_gather.3.refs_7_), channel_id=1, source_target_pairs={{0,1},{1,0},{2,3},{3,2},{4,5},{5,4},{6,7},{7,6},{8,9},{9,8},{10,11... | collective-permute-start | bytes 2457608 | tf_op jit(solution)/shard_map/ppermute | solution.py:32
  54.1 9.1 %collective-permute-start.11 = (bf16[128,640]{1,0:T(8,128)(2,1)S(1)}, bf16[128,640]{1,0:T(8,128)(2,1)S(1)}, u32[]{:S(2)}, u32[]{:S(2)}) collective-permute-start(bf16[128,640]{1,0:T(8,128)(2,1)S(1)} %get-tuple-element.23), channel_id=1, source_target_pairs={{0,6},{2,4},{4,2},{6,0},{1,7},{3,5},{5,3},{7,1},{8,14},{10,12},{12... | collective-permute-start | bytes 491528 | tf_op jit(solution)/shard_map/ppermute | solution.py:32
  57.2 12.1 %collective-permute-start.12 = (bf16[128,640]{1,0:T(8,128)(2,1)S(1)}, bf16[128,640]{1,0:T(8,128)(2,1)S(1)}, u32[]{:S(2)}, u32[]{:S(2)}) collective-permute-start(bf16[128,640]{1,0:T(8,128)(2,1)S(1)} %get-tuple-element.24), channel_id=1, source_target_pairs={{0,4},{2,6},{4,0},{6,2},{1,5},{3,7},{5,1},{7,3},{8,12},{10,14},{12... | collective-permute-start | bytes 491528 | tf_op jit(solution)/shard_map/ppermute | solution.py:32
  57.2 12.1 %collective-permute-start.13 = (bf16[128,640]{1,0:T(8,128)(2,1)S(1)}, bf16[128,640]{1,0:T(8,128)(2,1)S(1)}, u32[]{:S(2)}, u32[]{:S(2)}) collective-permute-start(bf16[128,640]{1,0:T(8,128)(2,1)S(1)} %get-tuple-element.25), channel_id=1, source_target_pairs={{0,2},{2,0},{4,6},{6,4},{1,3},{3,1},{5,7},{7,5},{8,10},{10,8},{12,... | collective-permute-start | bytes 491528 | tf_op jit(solution)/shard_map/ppermute | solution.py:32

commit v2 on v0

--- a/solution.py
+++ b/solution.py
@@ -1,6 +1,10 @@
+import functools
+
 import jax
 import jax.numpy as jnp
 from jax import lax
+from jax.experimental import pallas as pl
+from jax.experimental.pallas import tpu as pltpu
 from jax.sharding import PartitionSpec as P
 
 D = 5120
@@ -8,7 +12,430 @@
 RESP_DEV = 4
 GROUP = 8
 LMAX = 64
+TILE = 64
 SLOTS = 256
+EPS = 1e-06
+BF16 = jnp.bfloat16
+F32 = jnp.float32
+I32 = jnp.int32
+LANES = 128
+INFO = 16
+
+VMEM = pl.BlockSpec(memory_space=pltpu.VMEM)
+SMEM = pl.BlockSpec(memory_space=pltpu.SMEM)
+ANY = pl.BlockSpec(memory_space=pl.ANY)
+
+
+def iota(shape, dim):
+    return lax.broadcasted_iota(I32, shape, dim)
+
+
+def bits(n):
+    return n.bit_length() - 1
+
+
+def div(x, n):
+    return lax.shift_right_arithmetic(x, jnp.full(jnp.shape(x), bits(n), I32))
+
+
+def mod(x, n):
+    return x & (n - 1)
+
+
+def swap(x, axis, k):
+    n = lax.axis_size(axis)
+    return lax.ppermute(x, axis, [(i, i ^ k) for i in range(n)])
+
+
+def early_kernel(n_sec, n_tp, hidden, lengths, group_of, rewards, old_logp, ref_logp, gain, *refs):
+    pick, mine, info, gain_out = refs[:4]
+    rows_in, length, group, reward, old, ref, sems = refs[4:]
+    copies = []
+    for i, (src, dst) in enumerate(
+        (
+            (lengths, length),
+            (hidden, rows_in),
+            (old_logp, old),
+            (ref_logp, ref),
+            (group_of, group),
+            (rewards, reward),
+            (gain, gain_out),
+        )
+    ):
+        copies.append(pltpu.make_async_copy(src, dst, sems.at[i]))
+        copies[-1].start()
+    a = lax.axis_index("sec")
+    t = lax.axis_index("tp")
+    n_class = n_sec * n_tp
+    rows = rows_in.shape[0]
+    n_resp = length.shape[0]
+    total = pick.shape[0]
+    slots = total // n_sec
+    place = iota((total, rows), 0)
+    index = mod(place, slots) * n_class + (div(place, slots) ^ a) * n_tp + t
+    copies[0].wait()
+    source, finish = index, 0
+    for r in range(n_resp):
+        finish = finish + length[r]
+        source = source + jnp.where(index >= finish, LMAX - length[r], 0)
+    source = jnp.where(index < finish, source, -1)
+    chosen = (iota((total, rows), 1) == source).astype(BF16)
+    pick[...] = chosen
+    for copy in copies[1:]:
+        copy.wait()
+    mine[...] = jnp.dot(chosen, rows_in[...], preferred_element_type=F32).astype(BF16)
+    log_ratio = ref[...] - old[...]
+    penalty = jnp.exp(log_ratio) - log_ratio - 1.0
+    lane = iota((1, LANES), 1)
+    words = jnp.zeros((1, LANES), F32)
+    for r in range(n_resp):
+        for i, held in enumerate((length, group, reward)):
+            words = jnp.where(lane == i * n_resp + r, held[r].astype(F32), words)
+    n_pen = penalty.shape[0]
+    filler = jnp.zeros((info.shape[0] - n_pen - 1, LANES), F32)
+    info[...] = jnp.concatenate([penalty, words, filler], axis=0).astype(BF16)
+
+
+def spread_kernel(n_tp, pick, mine, sibling, *outs):
+    t = lax.axis_index("tp")
+    slots, width = outs[0].shape[0], mine.shape[1]
+    own = mine[...].astype(F32)
+    other = jnp.dot(pick[...], sibling[...], preferred_element_type=F32)
+    first = jnp.where(t == 0, own, other).astype(BF16)
+    second = jnp.where(t == 0, other, own).astype(BF16)
+    for k, out in enumerate(outs):
+        out[:, 0:width] = first[k * slots : (k + 1) * slots]
+        out[:, width : 2 * width] = second[k * slots : (k + 1) * slots]
+
+
+def norm_kernel(n, gain, info, *refs):
+    inputs, outs, held = refs[:n], refs[n : 2 * n], refs[2 * n]
+    a = lax.axis_index("sec")
+    s = lax.axis_index("seq")
+    slots, width = inputs[0].shape
+    squares = 0.0
+    for ref in inputs:
+        x = ref[...].astype(F32)
+        squares = squares + jnp.sum(x * x, axis=1, keepdims=True)
+    scale = lax.rsqrt(squares / D + EPS)
+    for k, ref in enumerate(inputs):
+        start = pl.multiple_of((a ^ k) * width, LANES)
+        held[k] = (ref[...].astype(F32) * scale * gain[:, pl.ds(start, width)]).astype(BF16)
+    beside = jnp.concatenate([info[...]] * (slots // info.shape[0]), axis=0)
+    for m, out in enumerate(outs):
+        out[:, 0:width] = held[a ^ s ^ m]
+        out[:, width : width + LANES] = beside
+
+
+def info_of(ref, width):
+    return ref[0:INFO, width : width + LANES].astype(F32)
+
+
+def word_sum(block, row, first, last):
+    lane = iota(block.shape, 1)
+    inside = (iota(block.shape, 0) == row) & (lane >= first) & (lane < last)
+    return jnp.sum(jnp.where(inside, block, 0.0)).astype(I32)
+
+
+def put_counts(moved, width, row, n_resp, counts):
+    s = lax.axis_index("seq")
+    for m, ref in enumerate(moved):
+        counts[s ^ m] = word_sum(info_of(ref, width), row, 0, n_resp)
+
+
+def class_rows(x, c, n_class):
+    return div(x - c + n_class - 1, n_class)
+
+
+def list_place(counts, n, n_class, tok, s, c, seq_of, position, packed):
+    span = tok * n // 4
+    edges = []
+    for j in range(5):
+        edge, start = 0, 0
+        for b in range(n):
+            edge = edge + class_rows(jnp.clip(j * span - start, 0, counts[b]), c, n_class)
+            start = start + counts[b]
+        edges.append(edge)
+    size = [edges[j + 1] - edges[j] for j in range(4)]
+    high = div(s, n // 2)
+    far_first = jnp.where(high == 0, size[1], size[0])
+    far_rows = jnp.where(high == 0, size[1] + size[3], size[0] + size[2])
+    near_first = jnp.where(high == 0, size[0], size[1])
+    prefix = 0
+    before = jnp.zeros_like(position)
+    for b in range(n):
+        before = jnp.where(seq_of == b, prefix, before)
+        prefix = prefix + class_rows(counts[b], c, n_class)
+    group = div(packed, span)
+    opening = jnp.where(group == 0, edges[0], jnp.where(group == 1, edges[1], jnp.where(group == 2, edges[2], edges[3])))
+    within = before + position - opening
+    later = group >= 2
+    far = mod(group, 2) != high
+    far_place = within + jnp.where(later, far_first, 0)
+    near_place = far_rows + within + jnp.where(later, near_first, 0)
+    return jnp.where(far, far_place, near_place)
+
+
+def pack_kernel(n, n_class, n_resp, tok, row, *refs):
+    moved, first, second, held, counts = refs[:n], refs[n], refs[n + 1], refs[n + 2], refs[n + 3]
+    s = lax.axis_index("seq")
+    c = lax.axis_index("sec") * lax.axis_size("tp") + lax.axis_index("tp")
+    slots, width = moved[0].shape[0], first.shape[1]
+    put_counts(moved, width, row, n_resp, counts)
+    lane = iota((1, n * slots), 1)
+    seq_of = div(lane, slots) ^ s
+    q = mod(lane, slots)
+    live = jnp.zeros(lane.shape, jnp.bool_)
+    start = jnp.zeros(lane.shape, I32)
+    total = 0
+    for b in range(n):
+        live = live | ((seq_of == b) & (q < class_rows(counts[b], c, n_class)))
+        start = jnp.where(seq_of == b, total, start)
+        total = total + counts[b]
+    packed = start + q * n_class + c
+    place = list_place(counts, n, n_class, tok, s, c, seq_of, q, packed)
+    place = jnp.where(live, place, -1)
+    for m, ref in enumerate(moved):
+        held[m * slots : (m + 1) * slots, :] = ref[:, 0:width]
+    r1, r2 = first.shape[0], second.shape[0]
+    pick = (iota((r1 + r2, n * slots), 0) == place).astype(BF16)
+    out = jnp.dot(pick, held[...], preferred_element_type=F32).astype(BF16)
+    first[...] = out[0:r1]
+    second[...] = out[r1 : r1 + r2]
+
+
+def upright(x):
+    return jnp.transpose(jnp.broadcast_to(x.astype(F32), (LANES, x.shape[1]))).astype(I32)
+
+
+def one_hot(column, out):
+    for j in range(out.shape[1] // LANES):
+        out[:, j * LANES : (j + 1) * LANES] = (iota(column.shape, 1) + j * LANES == column).astype(BF16)
+
+
+def index_kernel(n, n_class, n_resp, tok, row, r1, r2, *refs):
+    moved, hidden = refs[:n], refs[n]
+    pick_far, pick_near, rest_far, rest_near, counts, lens, own = refs[n + 1 :]
+    a = lax.axis_index("sec")
+    s = lax.axis_index("seq")
+    t = lax.axis_index("tp")
+    n_tp = lax.axis_size("tp")
+    width = moved[0].shape[1] - LANES
+    put_counts(moved, width, row, n_resp, counts)
+    block = info_of(moved[0], width)
+    for r in range(n_resp):
+        lens[r] = word_sum(block, row, r, r + 1)
+    half = n // 2 * tok
+    for far, pick, rest in ((True, pick_far, rest_far), (False, pick_near, rest_near)):
+        lane = iota((1, half), 1)
+        w = mod(lane, tok)
+        shard = (div(lane, tok) + (n // 2 if far else 0)) ^ s
+        packed = div(w, TILE) * (TILE * n) + shard * TILE + mod(w, TILE)
+        seq_of = jnp.zeros(lane.shape, I32)
+        start = jnp.zeros(lane.shape, I32)
+        finish = 0
+        for b in range(n):
+            finish = finish + counts[b]
+            passed = packed >= finish
+            seq_of = seq_of + passed.astype(I32)
+            start = jnp.where(passed, finish, start)
+        index = packed - start
+        c = mod(index, n_class)
+        place = list_place(counts, n, n_class, tok, s, c, seq_of, div(index, n_class), packed)
+        side = (mod(c, n_tp) ^ t) * n + (div(c, n_tp) ^ a)
+        column = side * r1 + place
+        if not far:
+            column = jnp.where(place < r1, column, n_class * r1 + side * r2 + place - r1)
+        one_hot(upright(column), pick)
+        source, ends = index, 0
+        for r in range(n_resp):
+            ends = ends + lens[r]
+            source = source + jnp.where(index >= ends, LMAX - lens[r], 0)
+        one_hot(upright(jnp.where(seq_of == s, source, -1)), own)
+        rest[...] = jnp.dot(own[...], hidden[...], preferred_element_type=F32)
+
+
+def mix_kernel(n_lists, sizes, pick, rest, projection, *refs):
+    pieces, outs, held = refs[:n_lists], refs[n_lists:-1], refs[-1]
+    offset = 0
+    for piece in pieces:
+        size = piece.shape[0]
+        held[offset : offset + size, :] = piece[...]
+        offset += size
+    tokens = jnp.dot(pick[...], held[...], preferred_element_type=F32).astype(BF16)
+    total = jnp.dot(tokens, projection[...], preferred_element_type=F32) + rest[...]
+    tok = outs[0].shape[0]
+    for m, out in enumerate(outs):
+        out[...] = total[m * tok : (m + 1) * tok].astype(out.dtype)
+
+
+def terms_kernel(n, n_resp, row, *refs):
+    moved, out, words, table = refs[:n], refs[n], refs[n + 1], refs[n + 2]
+    s = lax.axis_index("seq")
+    width = moved[0].shape[1] - LANES
+    tok = out.shape[1]
+    group_count = n * n_resp // GROUP
+    for m, ref in enumerate(moved):
+        block = info_of(ref, width)
+        table[pl.ds((s ^ m) * INFO, INFO), :] = block
+        for r in range(3 * n_resp):
+            words[s ^ m, r] = word_sum(block, row, r, r + 1)
+    w = iota((1, tok), 1)
+    packed = div(w, TILE) * (TILE * n) + s * TILE + mod(w, TILE)
+    source, finish = packed, 0
+    reward = jnp.zeros((1, tok), F32)
+    group = jnp.zeros((1, tok), I32)
+    total = [0] * group_count
+    square = [0] * group_count
+    for b in range(n):
+        for r in range(n_resp):
+            length, number, gain = words[b, r], words[b, n_resp + r], words[b, 2 * n_resp + r]
+            within = packed >= finish
+            reward = jnp.where(within, gain.astype(F32), reward)
+            group = jnp.where(within, number, group)
+            finish = finish + length
+            source = source + jnp.where(packed >= finish, LMAX - length, 0)
+            for g in range(group_count):
+                total[g] = total[g] + jnp.where(number == g, gain, 0)
+                square[g] = square[g] + jnp.where(number == g, gain * gain, 0)
+    total_of = jnp.zeros((1, tok), F32)
+    square_of = jnp.zeros((1, tok), F32)
+    for g in range(group_count):
+        total_of = jnp.where(group == g, total[g].astype(F32), total_of)
+        square_of = jnp.where(group == g, square[g].astype(F32), square_of)
+    mean = total_of / GROUP
+    spread = jnp.maximum(jnp.sqrt(square_of / GROUP - mean * mean), 1.0)
+    advantage = (reward - mean) / spread
+    pick = (iota((LANES, tok), 0) == mod(source, LANES)).astype(BF16)
+    found = jnp.dot(table[...].astype(BF16), pick, preferred_element_type=F32)
+    line = div(source, LANES)
+    chosen = iota(found.shape, 0) == div(line, row) * INFO + mod(line, row)
+    penalty = jnp.sum(jnp.where(chosen, found, 0.0), axis=0, keepdims=True)
+    out[0:1, :] = advantage
+    out[1:2, :] = penalty
+
+
+def call(kernel, out_shape, in_specs, out_specs, scratch=()):
+    return pl.pallas_call(
+        kernel,
+        out_shape=out_shape,
+        in_specs=in_specs,
+        out_specs=out_specs,
+        scratch_shapes=list(scratch),
+        compiler_params=pltpu.CompilerParams(vmem_limit_bytes=48 * 1024 * 1024),
+    )
+
+
+def shards_in_place(hidden, projection, norm_gain, old_logp, ref_logp, lengths, group_of, rewards):
+    n = lax.axis_size("seq")
+    n_tp = lax.axis_size("tp")
+    n_class = n * n_tp
+    rows, cols = hidden.shape
+    n_resp = lengths.shape[0]
+    width = cols * n_tp
+    slots = rows // n_class
+    row = rows // LANES
+    tok = TOK_DEV
+    tokens = tok * n
+    up16 = lambda x: -(-x // 16) * 16
+    far_rows = up16((tokens // 2 + (n_class - 1) * (n + 1)) // n_class)
+    all_rows = up16((tokens + (n_class - 1) * n) // n_class)
+    r1, r2 = far_rows, max(16, all_rows - far_rows)
+    shape = jax.ShapeDtypeStruct
+    info_like = shape((slots, width + LANES), BF16)
+
+    sibling = swap(hidden, "tp", 1)
+    pick, mine, info, gain = call(
+        functools.partial(early_kernel, n, n_tp),
+        [
+            shape((rows // n_tp, rows), BF16),
+            shape((rows // n_tp, cols), BF16),
+            shape((INFO, LANES), BF16),
+            shape((1, D), F32),
+        ],
+        [ANY] * 7,
+        [VMEM] * 4,
+        [
+            pltpu.VMEM((rows, cols), BF16),
+            pltpu.SMEM((n_resp,), I32),
+            pltpu.SMEM((n_resp,), I32),
+            pltpu.SMEM((n_resp,), I32),
+            pltpu.VMEM((row, LANES), F32),
+            pltpu.VMEM((row, LANES), F32),
+            pltpu.SemaphoreType.DMA((7,)),
+        ],
+    )(
+        hidden,
+        lengths,
+        group_of,
+        rewards,
+        old_logp.reshape(row, LANES),
+        ref_logp.reshape(row, LANES),
+        norm_gain.reshape(1, D),
+    )
+    dealt = call(
+        functools.partial(spread_kernel, n_tp), [shape((slots, width), BF16)] * n, [VMEM] * 3, [VMEM] * n
+    )(pick, mine, sibling)
+    whole = [dealt[0]] + [swap(dealt[k], "sec", k) for k in range(1, n)]
+    normed = call(
+        functools.partial(norm_kernel, n),
+        [info_like] * n,
+        [VMEM] * (n + 2),
+        [VMEM] * n,
+        [pltpu.VMEM((n, slots, width), BF16)],
+    )(gain, info, *whole)
+    moved = [normed[0]] + [swap(normed[m], "seq", m) for m in range(n - 1, 0, -1)][::-1]
+    lists = call(
+        functools.partial(pack_kernel, n, n_class, n_resp, tok, row),
+        [shape((r1, width), BF16), shape((r2, width), BF16)],
+        [VMEM] * n,
+        [VMEM] * 2,
+        [pltpu.VMEM((n * slots, width), BF16), pltpu.SMEM((n,), I32)],
+    )(*moved)
+    half = n // 2 * tok
+    pick_far, pick_near, rest_far, rest_near = call(
+        functools.partial(index_kernel, n, n_class, n_resp, tok, row, r1, r2),
+        [
+            shape((half, n_class * r1), BF16),
+            shape((half, n_class * (r1 + r2)), BF16),
+            shape((half, cols), F32),
+            shape((half, cols), F32),
+        ],
+        [VMEM] * (n + 1),
+        [VMEM] * 4,
+        [pltpu.SMEM((n,), I32), pltpu.SMEM((n_resp,), I32), pltpu.VMEM((half, rows), BF16)],
+    )(*moved, hidden)
+    terms = call(
+        functools.partial(terms_kernel, n, n_resp, row),
+        shape((2, tok), F32),
+        [VMEM] * n,
+        VMEM,
+        [pltpu.SMEM((n, 3 * n_resp), I32), pltpu.VMEM((n * INFO, LANES), F32)],
+    )(*moved)
+    pieces = []
+    for part in lists:
+        same = [part] + [swap(part, "sec", k) for k in range(1, n)]
+        pieces.append(same + [swap(x, "tp", 1) for x in same])
+    far = call(
+        functools.partial(mix_kernel, n_class, None),
+        [shape((tok, cols), BF16)] * (n // 2),
+        [VMEM] * (n_class + 3),
+        [VMEM] * (n // 2),
+        [pltpu.VMEM((n_class * r1, width), BF16)],
+    )(pick_far, rest_far, projection, *pieces[0])
+    near = call(
+        functools.partial(mix_kernel, 2 * n_class, None),
+        [shape((tok, cols), F32)] + [shape((tok, cols), BF16)] * (n // 2 - 1),
+        [VMEM] * (2 * n_class + 3),
+        [VMEM] * (n // 2),
+        [pltpu.VMEM((n_class * (r1 + r2), width), BF16)],
+    )(pick_near, rest_near, projection, *pieces[0], *pieces[1])
+    partial = [*near, *far]
+    arrived = [swap(partial[m], "seq", m) for m in range(n - 1, 0, -1)]
+    states = partial[0]
+    for part in arrived:
+        states = states + part.astype(F32)
+    return states.astype(BF16), terms.astype(BF16).T
 
 
 def refine(input_rows, projection, norm_gain):
@@ -105,4 +532,7 @@
         P("seq"),
     )
     out_specs = (P("seq", ("sec", "tp")), P("seq", None))
-    return jax.shard_map(shards, mesh=mesh, in_specs=in_specs, out_specs=out_specs, check_vma=False)
+    n = mesh.shape["seq"]
+    in_place = mesh.shape["sec"] == n and n >= 4 and n & (n - 1) == 0
+    body = shards_in_place if in_place else shards
+    return jax.shard_map(body, mesh=mesh, in_specs=in_specs, out_specs=out_specs, check_vma=False)

time: 195 us -> 65.4 us (0.34)
  waiting for transfers between devices: 122 us -> 30.6 us
  blocking collectives: 19.8 us -> 0 us
  starting transfers between devices: 6.75 us -> 21.4 us
  between operations: 14.7 us -> 0.75 us
  other arithmetic: 12.7 us -> 1.27 us
  matrix products: 9.35 us -> 0 us
  Pallas kernels: 0 us -> 5 us
  local copies, waits for them, and re-layouts: 9.39 us -> 6 us
    all_gather x2 -> x0, waiting for transfers between devices: 111 us -> none  [the longest x1 111 us: refine(): lax.all_gather(projection, 'seq', axis=0, tiled=True)]
    ppermute x0 -> x24, waiting for transfers between devices: none -> 30.6 us  [swap(): return lax.ppermute(x, axis, [(i, i ^ k) for i in range(n)])]
    ppermute x0 -> x24, starting transfers between devices: none -> 21.4 us  [swap(): return lax.ppermute(x, axis, [(i, i ^ k) for i in range(n)])]
    unnamed x1 -> x0, blocking collectives: 9.92 us -> none
    psum x1 -> x0, blocking collectives: 9.92 us -> none  [shards(): group_sums = lax.psum(partial_value, 'seq')]
    dot_general x5 -> x0, matrix products: 9.35 us -> none  [the longest x1 5.92 us: refine(): jnp.dot(normed, lax.all_gather(projection, 'seq', axis=0, tiled=True), pr...]
    all_to_all x2 -> x0, waiting for transfers between devices: 9.17 us -> none  [the longest x1 9.16 us: deliver(): lax.all_to_all(send_rows.reshape(n_seq, tile_rows, -1), 'seq', split_axis...]
    all_to_all x2 -> x0, starting transfers between devices: 6.68 us -> none  [the longest x1 3.45 us: deliver(): lax.all_to_all(send_rows.reshape(n_seq, tile_rows, -1), 'seq', split_axis...]
  transfers between devices with their start and end apart: 4 -> 24, of which waited for: 2 -> 11; matrix products, arithmetic and copies ran while one was open for 15% -> 1% of each run, Pallas kernels for 0% -> 6%
where the time goes in v2:
time: 65.4 us; the launch traced here: 65.1 us
  waiting for transfers between devices  30.6 us (47%)
  starting transfers between devices  21.4 us (33%)
  local copies, waits for them, and re-layouts  6 us (9%)
  Pallas kernels  5 us (8%)
  other arithmetic  1.27 us (2%)
  between operations  0.75 us (1%)
    ppermute x24, waiting for transfers between devices, swap(): return lax.ppermute(x, axis, [(i, i ^ k) for i in range(n)])  30.6 us
    ppermute x24, starting transfers between devices, swap(): return lax.ppermute(x, axis, [(i, i ^ k) for i in range(n)])  21.4 us
    unnamed x18, local copies, waits for them, and re-layouts  6 us
  transfers between devices with their start and end apart: 24, of which 11 were waited for; matrix products, arithmetic and copies ran while one was open for 1% of the time, Pallas kernels for 6%

profile of v2, /device:TPU:0, one launch (start us, length us, event | category | flops | bytes accessed | tf_op | source)
XLA Modules:
  0.0 65.1 jit_solution(8302027976047205357)
XLA Ops:
  0.6 0.5 collective-permute-start
  1.2 1.0 %copy-done.1 = bf16[256,640]{1,0:T(8,128)(2,1)S(1)} copy-done((bf16[256,640]{1,0:T(8,128)(2,1)S(1)}, bf16[256,640]{1,0:T(8,128)(2,1)}, u32[]{:S(2)}) %copy-start.1) | copy-done | bytes 327704
  2.1 0.7 %copy-done.3 = f32[5120]{0:T(1024)S(1)} copy-done((f32[5120]{0:T(1024)S(1)}, f32[5120]{0:T(1024)}, u32[]{:S(2)}) %copy-start.3) | copy-done | bytes 20504
  2.9 0.7 %copy-done.4 = f32[256]{0:T(256)S(1)} copy-done((f32[256]{0:T(256)S(1)}, f32[256]{0:T(256)}, u32[]{:S(2)}) %copy-start.4) | copy-done | bytes 1048
  3.5 0.7 %copy-done.5 = f32[256]{0:T(256)S(1)} copy-done((f32[256]{0:T(256)S(1)}, f32[256]{0:T(256)}, u32[]{:S(2)}) %copy-start.5) | copy-done | bytes 1048
  4.2 0.7 %copy-done.6 = s32[4]{0:T(128)S(1)} copy-done((s32[4]{0:T(128)S(1)}, s32[4]{0:T(128)}, u32[]{:S(2)}) %copy-start.6) | copy-done | bytes 40
  4.9 0.7 %copy-done.7 = s32[4]{0:T(128)S(1)} copy-done((s32[4]{0:T(128)S(1)}, s32[4]{0:T(128)}, u32[]{:S(2)}) %copy-start.7) | copy-done | bytes 40
  5.5 0.7 %copy-done.8 = s32[4]{0:T(128)S(1)} copy-done((s32[4]{0:T(128)S(1)}, s32[4]{0:T(128)}, u32[]{:S(2)}) %copy-start.8) | copy-done | bytes 40
  6.2 0.9 %shard_map.95 = (bf16[128,256]{1,0:T(8,128)(2,1)S(1)}, bf16[128,640]{1,0:T(8,128)(2,1)S(1)}, bf16[16,128]{1,0:T(8,128)(2,1)S(1)}, f32[1,5120]{1,0:T(1,128)S(1)}) custom-call(bf16[256,640]{1,0:T(8,128)(2,1)S(1)} %copy-done.1, s32[4]{0:T(128)S(1)} %copy-done.6, s32[4]{0:T(128)S(1)} %copy-done.7, s32[4]{0:T(128)S(1)} %copy-done.8, f32[2,128]{1,0:T(2,128)S(1)} %bitcast.6, ...), custom_call_target="tpu_custom_call" | custom-call | tf_op jit(solution)/shard_map/pallas_call | solution.py:348
  7.1 0.2 shard_map.96
  7.4 2.7 %collective-permute-start.1 = (bf16[32,1280]{1,0:T(8,128)(2,1)S(1)}, bf16[32,1280]{1,0:T(8,128)(2,1)S(1)}, u32[]{:S(2)}, u32[]{:S(2)}) collective-permute-start(bf16[32,1280]{1,0:T(8,128)(2,1)S(1)} %get-tuple-element.29), channel_id=1, source_target_pairs={{0,8},{8,0},{16,24},{24,16},{1,9},{9,1},{17,25},{25,17},{2,10},{10... | collective-permute-start | bytes 245768 | tf_op jit(solution)/shard_map/ppermute | solution.py:47
  10.1 1.5 %collective-permute-start.2 = (bf16[32,1280]{1,0:T(8,128)(2,1)S(1)}, bf16[32,1280]{1,0:T(8,128)(2,1)S(1)}, u32[]{:S(2)}, u32[]{:S(2)}) collective-permute-start(bf16[32,1280]{1,0:T(8,128)(2,1)S(1)} %get-tuple-element.30), channel_id=1, source_target_pairs={{0,16},{8,24},{16,0},{24,8},{1,17},{9,25},{17,1},{25,9},{2,18},{10... | collective-permute-start | bytes 245768 | tf_op jit(solution)/shard_map/ppermute | solution.py:47
  11.6 1.4 %collective-permute-done.1.refs_1_ = bf16[32,1280]{1,0:T(8,128)(2,1)S(1)} collective-permute-done((bf16[32,1280]{1,0:T(8,128)(2,1)S(1)}, bf16[32,1280]{1,0:T(8,128)(2,1)S(1)}, u32[]{:S(2)}, u32[]{:S(2)}) %collective-permute-start.1) | collective-permute-done | bytes 81952 | tf_op jit(solution)/shard_map/ppermute | solution.py:47
  13.0 2.3 %collective-permute-done.2.refs_2_ = bf16[32,1280]{1,0:T(8,128)(2,1)S(1)} collective-permute-done((bf16[32,1280]{1,0:T(8,128)(2,1)S(1)}, bf16[32,1280]{1,0:T(8,128)(2,1)S(1)}, u32[]{:S(2)}, u32[]{:S(2)}) %collective-permute-start.2) | collective-permute-done | bytes 81952 | tf_op jit(solution)/shard_map/ppermute | solution.py:47
  15.3 1.6 %collective-permute-done.3.refs_3_ = bf16[32,1280]{1,0:T(8,128)(2,1)S(1)} collective-permute-done((bf16[32,1280]{1,0:T(8,128)(2,1)S(1)}, bf16[32,1280]{1,0:T(8,128)(2,1)S(1)}, u32[]{:S(2)}, u32[]{:S(2)}) %collective-permute-start.3) | collective-permute-done | bytes 81952 | tf_op jit(solution)/shard_map/ppermute | solution.py:47
  16.9 0.2 shard_map.97
  17.2 1.6 %collective-permute-start.4 = (bf16[32,1408]{1,0:T(8,128)(2,1)S(1)}, bf16[32,1408]{1,0:T(8,128)(2,1)S(1)}, u32[]{:S(2)}, u32[]{:S(2)}) collective-permute-start(bf16[32,1408]{1,0:T(8,128)(2,1)S(1)} %get-tuple-element.33), channel_id=1, source_target_pairs={{0,2},{2,0},{4,6},{6,4},{1,3},{3,1},{5,7},{7,5},{8,10},{10,8},{12,... | collective-permute-start | bytes 270344 | tf_op jit(solution)/shard_map/ppermute | solution.py:47
  18.8 2.6 %collective-permute-start.5 = (bf16[32,1408]{1,0:T(8,128)(2,1)S(1)}, bf16[32,1408]{1,0:T(8,128)(2,1)S(1)}, u32[]{:S(2)}, u32[]{:S(2)}) collective-permute-start(bf16[32,1408]{1,0:T(8,128)(2,1)S(1)} %get-tuple-element.34), channel_id=1, source_target_pairs={{0,4},{2,6},{4,0},{6,2},{1,5},{3,7},{5,1},{7,3},{8,12},{10,14},{12... | collective-permute-start | bytes 270344 | tf_op jit(solution)/shard_map/ppermute | solution.py:47
  21.4 0.2 collective-permute-start.6
  21.6 0.9 %collective-permute-done.4.refs_1_ = bf16[32,1408]{1,0:T(8,128)(2,1)S(1)} collective-permute-done((bf16[32,1408]{1,0:T(8,128)(2,1)S(1)}, bf16[32,1408]{1,0:T(8,128)(2,1)S(1)}, u32[]{:S(2)}, u32[]{:S(2)}) %collective-permute-start.4) | collective-permute-done | bytes 90144 | tf_op jit(solution)/shard_map/ppermute | solution.py:47
  22.5 3.9 %collective-permute-done.5.refs_2_ = bf16[32,1408]{1,0:T(8,128)(2,1)S(1)} collective-permute-done((bf16[32,1408]{1,0:T(8,128)(2,1)S(1)}, bf16[32,1408]{1,0:T(8,128)(2,1)S(1)}, u32[]{:S(2)}, u32[]{:S(2)}) %collective-permute-start.5) | collective-permute-done | bytes 90144 | tf_op jit(solution)/shard_map/ppermute | solution.py:47
  26.5 1.4 %collective-permute-done.6.refs_3_ = bf16[32,1408]{1,0:T(8,128)(2,1)S(1)} collective-permute-done((bf16[32,1408]{1,0:T(8,128)(2,1)S(1)}, bf16[32,1408]{1,0:T(8,128)(2,1)S(1)}, u32[]{:S(2)}, u32[]{:S(2)}) %collective-permute-start.6) | collective-permute-done | bytes 90144 | tf_op jit(solution)/shard_map/ppermute | solution.py:47
  27.8 0.4 shard_map.99
  28.2 0.6 collective-permute-start.7
  28.8 0.8 %collective-permute-start.8 = (bf16[48,1280]{1,0:T(8,128)(2,1)S(1)}, bf16[48,1280]{1,0:T(8,128)(2,1)S(1)}, u32[]{:S(2)}, u32[]{:S(2)}) collective-permute-start(bf16[48,1280]{1,0:T(8,128)(2,1)S(1)} %get-tuple-element.38.refs_0_), channel_id=1, source_target_pairs={{0,16},{8,24},{16,0},{24,8},{1,17},{9,25},{17,1},{25,9},{2,18},{10... | collective-permute-start | bytes 368648 | tf_op jit(solution)/shard_map/ppermute | solution.py:47
  29.7 1.5 %collective-permute-start.14 = (bf16[32,1280]{1,0:T(8,128)(2,1)S(1)}, bf16[32,1280]{1,0:T(8,128)(2,1)S(1)}, u32[]{:S(2)}, u32[]{:S(2)}) collective-permute-start(bf16[32,1280]{1,0:T(8,128)(2,1)S(1)} %get-tuple-element.39.refs_8_), channel_id=1, source_target_pairs={{0,8},{8,0},{16,24},{24,16},{1,9},{9,1},{17,25},{25,17},{2,10},{10... | collective-permute-start | bytes 245768 | tf_op jit(solution)/shard_map/ppermute | solution.py:47
  31.2 1.2 %collective-permute-start.9 = (bf16[48,1280]{1,0:T(8,128)(2,1)S(1)}, bf16[48,1280]{1,0:T(8,128)(2,1)S(1)}, u32[]{:S(2)}, u32[]{:S(2)}) collective-permute-start(bf16[48,1280]{1,0:T(8,128)(2,1)S(1)} %get-tuple-element.38.refs_0_), channel_id=1, source_target_pairs={{0,24},{8,16},{16,8},{24,0},{1,25},{9,17},{17,9},{25,1},{2,26},{10... | collective-permute-start | bytes 368648 | tf_op jit(solution)/shard_map/ppermute | solution.py:47
  32.3 0.8 %collective-permute-start.15 = (bf16[32,1280]{1,0:T(8,128)(2,1)S(1)}, bf16[32,1280]{1,0:T(8,128)(2,1)S(1)}, u32[]{:S(2)}, u32[]{:S(2)}) collective-permute-start(bf16[32,1280]{1,0:T(8,128)(2,1)S(1)} %get-tuple-element.39.refs_8_), channel_id=1, source_target_pairs={{0,16},{8,24},{16,0},{24,8},{1,17},{9,25},{17,1},{25,9},{2,18},{10... | collective-permute-start | bytes 245768 | tf_op jit(solution)/shard_map/ppermute | solution.py:47
  33.2 1.7 %collective-permute-done.14.refs_9_ = bf16[32,1280]{1,0:T(8,128)(2,1)S(1)} collective-permute-done((bf16[32,1280]{1,0:T(8,128)(2,1)S(1)}, bf16[32,1280]{1,0:T(8,128)(2,1)S(1)}, u32[]{:S(2)}, u32[]{:S(2)}) %collective-permute-start.14) | collective-permute-done | bytes 81952 | tf_op jit(solution)/shard_map/ppermute | solution.py:47
  34.8 0.5 collective-permute-start.11
  35.3 0.1 collective-permute-start.12
  35.4 2.4 %collective-permute-done.15.refs_10_ = bf16[32,1280]{1,0:T(8,128)(2,1)S(1)} collective-permute-done((bf16[32,1280]{1,0:T(8,128)(2,1)S(1)}, bf16[32,1280]{1,0:T(8,128)(2,1)S(1)}, u32[]{:S(2)}, u32[]{:S(2)}) %collective-permute-start.15) | collective-permute-done | bytes 81952 | tf_op jit(solution)/shard_map/ppermute | solution.py:47
  37.8 1.2 %collective-permute-start.16 = (bf16[32,1280]{1,0:T(8,128)(2,1)S(1)}, bf16[32,1280]{1,0:T(8,128)(2,1)S(1)}, u32[]{:S(2)}, u32[]{:S(2)}) collective-permute-start(bf16[32,1280]{1,0:T(8,128)(2,1)S(1)} %get-tuple-element.39.refs_8_), channel_id=1, source_target_pairs={{0,24},{8,16},{16,8},{24,0},{1,25},{9,17},{17,9},{25,1},{2,26},{10... | collective-permute-start | bytes 245768 | tf_op jit(solution)/shard_map/ppermute | solution.py:47
  39.0 4.2 %collective-permute-done.16.refs_11_ = bf16[32,1280]{1,0:T(8,128)(2,1)S(1)} collective-permute-done((bf16[32,1280]{1,0:T(8,128)(2,1)S(1)}, bf16[32,1280]{1,0:T(8,128)(2,1)S(1)}, u32[]{:S(2)}, u32[]{:S(2)}) %collective-permute-start.16) | collective-permute-done | bytes 81952 | tf_op jit(solution)/shard_map/ppermute | solution.py:47
  43.2 0.5 collective-permute-start.18
  43.7 0.4 collective-permute-start.20
  44.2 1.0 %copy-done.2 = bf16[256,640]{1,0:T(8,128)(2,1)S(1)} copy-done((bf16[256,640]{1,0:T(8,128)(2,1)S(1)}, bf16[256,640]{1,0:T(8,128)(2,1)}, u32[]{:S(2)}) %copy-start.2) | copy-done | bytes 327704
  45.2 0.6 shard_map.98
  45.8 0.4 shard_map.102
  46.2 1.0 %shard_map.101 = (bf16[128,640]{1,0:T(8,128)(2,1)S(1)}, bf16[128,640]{1,0:T(8,128)(2,1)S(1)}) custom-call(bf16[256,384]{1,0:T(8,128)(2,1)S(1)} %get-tuple-element.41.pick, f32[256,640]{1,0:T(8,128)S(1)} %get-tuple-element.42.rest, bf16[1280,640]{1,0:T(8,128)(2,1)S(1)} %copy-done, bf16[48,1280]{1,0:T(8,128)(2,1)S(1)} %get-tuple-element.38.refs_0_, ...), custom_call_target="tpu_custom_call" | custom-call | tf_op jit(solution)/shard_map/pallas_call | solution.py:419
  47.2 1.9 %collective-permute-start.21 = (bf16[128,640]{1,0:T(8,128)(2,1)S(1)}, bf16[128,640]{1,0:T(8,128)(2,1)S(1)}, u32[]{:S(2)}, u32[]{:S(2)}) collective-permute-start(bf16[128,640]{1,0:T(8,128)(2,1)S(1)} %get-tuple-element.43), channel_id=1, source_target_pairs={{0,6},{2,4},{4,2},{6,0},{1,7},{3,5},{5,3},{7,1},{8,14},{10,12},{12... | collective-permute-start | bytes 491528 | tf_op jit(solution)/shard_map/ppermute | solution.py:47
  49.1 0.5 collective-permute-start.22
  49.7 1.2 %shard_map.100 = (f32[128,640]{1,0:T(8,128)S(1)}, bf16[128,640]{1,0:T(8,128)(2,1)S(1)}) custom-call(bf16[256,640]{1,0:T(8,128)(2,1)S(1)} %get-tuple-element.36.pick, f32[256,640]{1,0:T(8,128)S(1)} %get-tuple-element.37.rest, bf16[1280,640]{1,0:T(8,128)(2,1)S(1)} %copy-done, bf16[48,1280]{1,0:T(8,128)(2,1)S(1)} %get-tuple-element.38.refs_0_, ...), custom_call_target="tpu_custom_call" | custom-call | tf_op jit(solution)/shard_map/pallas_call | solution.py:426
  50.9 2.1 %collective-permute-start.23 = (bf16[128,640]{1,0:T(8,128)(2,1)S(1)}, bf16[128,640]{1,0:T(8,128)(2,1)S(1)}, u32[]{:S(2)}, u32[]{:S(2)}) collective-permute-start(bf16[128,640]{1,0:T(8,128)(2,1)S(1)} %get-tuple-element.45), channel_id=1, source_target_pairs={{0,2},{2,0},{4,6},{6,4},{1,3},{3,1},{5,7},{7,5},{8,10},{10,8},{12,... | collective-permute-start | bytes 491528 | tf_op jit(solution)/shard_map/ppermute | solution.py:47
  53.0 0.5 convert_bitcast_fusion
  53.5 2.8 %collective-permute-done.21 = bf16[128,640]{1,0:T(8,128)(2,1)S(1)} collective-permute-done((bf16[128,640]{1,0:T(8,128)(2,1)S(1)}, bf16[128,640]{1,0:T(8,128)(2,1)S(1)}, u32[]{:S(2)}, u32[]{:S(2)}) %collective-permute-start.21) | collective-permute-done | bytes 163872 | tf_op jit(solution)/shard_map/ppermute | solution.py:47
  56.3 8.1 %collective-permute-done.22 = bf16[128,640]{1,0:T(8,128)(2,1)S(1)} collective-permute-done((bf16[128,640]{1,0:T(8,128)(2,1)S(1)}, bf16[128,640]{1,0:T(8,128)(2,1)S(1)}, u32[]{:S(2)}, u32[]{:S(2)}) %collective-permute-start.22) | collective-permute-done | bytes 163872 | tf_op jit(solution)/shard_map/ppermute | solution.py:47
  64.3 0.8 %add_convert_fusion = bf16[128,640]{1,0:T(8,128)(2,1)} fusion(bf16[128,640]{1,0:T(8,128)(2,1)S(1)} %collective-permute-done.23, bf16[128,640]{1,0:T(8,128)(2,1)S(1)} %collective-permute-done.22, f32[128,640]{1,0:T(8,128)S(1)} %get-tuple-element.40, bf16[128,640]{1,0:T(8,128)(2,1)S(1)} %collective-permute-done.21), kind=kLoop, calls=%fused_computation | loop fusion | flops 573440 | bytes 983040 | tf_op jit(solution)/shard_map/convert_element_type | solution.py:438
  (28 shorter events, 0.2 us)
Async XLA Ops:
  0.6 45.6 %copy-start = (bf16[1280,640]{1,0:T(8,128)(2,1)S(1)}, bf16[1280,640]{1,0:T(8,128)(2,1)}, u32[]{:S(2)}) copy-start(bf16[1280,640]{1,0:T(8,128)(2,1)} %projection.3) | copy-start | bytes 4915204
  0.6 6.5 %collective-permute-start = (bf16[256,640]{1,0:T(8,128)(2,1)}, bf16[256,640]{1,0:T(8,128)(2,1)S(1)}, u32[]{:S(2)}, u32[]{:S(2)}) collective-permute-start(bf16[256,640]{1,0:T(8,128)(2,1)} %refs_4_.1), channel_id=1, source_target_pairs={{0,1},{1,0},{2,3},{3,2},{4,5},{5,4},{6,7},{7,6},{8,9},{9,8},{10,11... | collective-permute-start | bytes 983048 | tf_op jit(solution)/shard_map/ppermute | solution.py:47
  1.2 1.0 %copy-start.1 = (bf16[256,640]{1,0:T(8,128)(2,1)S(1)}, bf16[256,640]{1,0:T(8,128)(2,1)}, u32[]{:S(2)}) copy-start(bf16[256,640]{1,0:T(8,128)(2,1)} %refs_4_.1) | copy-start | bytes 983044
  2.1 0.7 %copy-start.3 = (f32[5120]{0:T(1024)S(1)}, f32[5120]{0:T(1024)}, u32[]{:S(2)}) copy-start(f32[5120]{0:T(1024)} %param.10) | copy-start | bytes 61444
  2.9 0.7 %copy-start.4 = (f32[256]{0:T(256)S(1)}, f32[256]{0:T(256)}, u32[]{:S(2)}) copy-start(f32[256]{0:T(256)} %param.11) | copy-start | bytes 3076
  3.5 0.7 %copy-start.5 = (f32[256]{0:T(256)S(1)}, f32[256]{0:T(256)}, u32[]{:S(2)}) copy-start(f32[256]{0:T(256)} %param.12) | copy-start | bytes 3076
  4.2 0.7 %copy-start.6 = (s32[4]{0:T(128)S(1)}, s32[4]{0:T(128)}, u32[]{:S(2)}) copy-start(s32[4]{0:T(128)} %lengths.1) | copy-start | bytes 52
  4.9 0.7 %copy-start.7 = (s32[4]{0:T(128)S(1)}, s32[4]{0:T(128)}, u32[]{:S(2)}) copy-start(s32[4]{0:T(128)} %group_of.1) | copy-start | bytes 52
  5.5 0.7 %copy-start.8 = (s32[4]{0:T(128)S(1)}, s32[4]{0:T(128)}, u32[]{:S(2)}) copy-start(s32[4]{0:T(128)} %rewards.1) | copy-start | bytes 52
  7.4 5.7 %collective-permute-start.1 = (bf16[32,1280]{1,0:T(8,128)(2,1)S(1)}, bf16[32,1280]{1,0:T(8,128)(2,1)S(1)}, u32[]{:S(2)}, u32[]{:S(2)}) collective-permute-start(bf16[32,1280]{1,0:T(8,128)(2,1)S(1)} %get-tuple-element.29), channel_id=1, source_target_pairs={{0,8},{8,0},{16,24},{24,16},{1,9},{9,1},{17,25},{25,17},{2,10},{10... | collective-permute-start | bytes 245768 | tf_op jit(solution)/shard_map/ppermute | solution.py:47
  10.1 5.3 %collective-permute-start.2 = (bf16[32,1280]{1,0:T(8,128)(2,1)S(1)}, bf16[32,1280]{1,0:T(8,128)(2,1)S(1)}, u32[]{:S(2)}, u32[]{:S(2)}) collective-permute-start(bf16[32,1280]{1,0:T(8,128)(2,1)S(1)} %get-tuple-element.30), channel_id=1, source_target_pairs={{0,16},{8,24},{16,0},{24,8},{1,17},{9,25},{17,1},{25,9},{2,18},{10... | collective-permute-start | bytes 245768 | tf_op jit(solution)/shard_map/ppermute | solution.py:47
  11.6 5.3 %collective-permute-start.3 = (bf16[32,1280]{1,0:T(8,128)(2,1)S(1)}, bf16[32,1280]{1,0:T(8,128)(2,1)S(1)}, u32[]{:S(2)}, u32[]{:S(2)}) collective-permute-start(bf16[32,1280]{1,0:T(8,128)(2,1)S(1)} %get-tuple-element.31), channel_id=1, source_target_pairs={{0,24},{8,16},{16,8},{24,0},{1,25},{9,17},{17,9},{25,1},{2,26},{10... | collective-permute-start | bytes 245768 | tf_op jit(solution)/shard_map/ppermute | solution.py:47
  17.2 5.4 %collective-permute-start.4 = (bf16[32,1408]{1,0:T(8,128)(2,1)S(1)}, bf16[32,1408]{1,0:T(8,128)(2,1)S(1)}, u32[]{:S(2)}, u32[]{:S(2)}) collective-permute-start(bf16[32,1408]{1,0:T(8,128)(2,1)S(1)} %get-tuple-element.33), channel_id=1, source_target_pairs={{0,2},{2,0},{4,6},{6,4},{1,3},{3,1},{5,7},{7,5},{8,10},{10,8},{12,... | collective-permute-start | bytes 270344 | tf_op jit(solution)/shard_map/ppermute | solution.py:47
  18.8 7.7 %collective-permute-start.5 = (bf16[32,1408]{1,0:T(8,128)(2,1)S(1)}, bf16[32,1408]{1,0:T(8,128)(2,1)S(1)}, u32[]{:S(2)}, u32[]{:S(2)}) collective-permute-start(bf16[32,1408]{1,0:T(8,128)(2,1)S(1)} %get-tuple-element.34), channel_id=1, source_target_pairs={{0,4},{2,6},{4,0},{6,2},{1,5},{3,7},{5,1},{7,3},{8,12},{10,14},{12... | collective-permute-start | bytes 270344 | tf_op jit(solution)/shard_map/ppermute | solution.py:47
  21.4 6.4 %collective-permute-start.6 = (bf16[32,1408]{1,0:T(8,128)(2,1)S(1)}, bf16[32,1408]{1,0:T(8,128)(2,1)S(1)}, u32[]{:S(2)}, u32[]{:S(2)}) collective-permute-start(bf16[32,1408]{1,0:T(8,128)(2,1)S(1)} %get-tuple-element.35), channel_id=1, source_target_pairs={{0,6},{2,4},{4,2},{6,0},{1,7},{3,5},{5,3},{7,1},{8,14},{10,12},{12... | collective-permute-start | bytes 270344 | tf_op jit(solution)/shard_map/ppermute | solution.py:47
  28.2 6.6 %collective-permute-start.7 = (bf16[48,1280]{1,0:T(8,128)(2,1)S(1)}, bf16[48,1280]{1,0:T(8,128)(2,1)S(1)}, u32[]{:S(2)}, u32[]{:S(2)}) collective-permute-start(bf16[48,1280]{1,0:T(8,128)(2,1)S(1)} %get-tuple-element.38.refs_0_), channel_id=1, source_target_pairs={{0,8},{8,0},{16,24},{24,16},{1,9},{9,1},{17,25},{25,17},{2,10},{10... | collective-permute-start | bytes 368648 | tf_op jit(solution)/shard_map/ppermute | solution.py:47
  28.8 6.5 %collective-permute-start.8 = (bf16[48,1280]{1,0:T(8,128)(2,1)S(1)}, bf16[48,1280]{1,0:T(8,128)(2,1)S(1)}, u32[]{:S(2)}, u32[]{:S(2)}) collective-permute-start(bf16[48,1280]{1,0:T(8,128)(2,1)S(1)} %get-tuple-element.38.refs_0_), channel_id=1, source_target_pairs={{0,16},{8,24},{16,0},{24,8},{1,17},{9,25},{17,1},{25,9},{2,18},{10... | collective-permute-start | bytes 368648 | tf_op jit(solution)/shard_map/ppermute | solution.py:47
  29.7 5.2 %collective-permute-start.14 = (bf16[32,1280]{1,0:T(8,128)(2,1)S(1)}, bf16[32,1280]{1,0:T(8,128)(2,1)S(1)}, u32[]{:S(2)}, u32[]{:S(2)}) collective-permute-start(bf16[32,1280]{1,0:T(8,128)(2,1)S(1)} %get-tuple-element.39.refs_8_), channel_id=1, source_target_pairs={{0,8},{8,0},{16,24},{24,16},{1,9},{9,1},{17,25},{25,17},{2,10},{10... | collective-permute-start | bytes 245768 | tf_op jit(solution)/shard_map/ppermute | solution.py:47
  31.2 7.8 %collective-permute-start.9 = (bf16[48,1280]{1,0:T(8,128)(2,1)S(1)}, bf16[48,1280]{1,0:T(8,128)(2,1)S(1)}, u32[]{:S(2)}, u32[]{:S(2)}) collective-permute-start(bf16[48,1280]{1,0:T(8,128)(2,1)S(1)} %get-tuple-element.38.refs_0_), channel_id=1, source_target_pairs={{0,24},{8,16},{16,8},{24,0},{1,25},{9,17},{17,9},{25,1},{2,26},{10... | collective-permute-start | bytes 368648 | tf_op jit(solution)/shard_map/ppermute | solution.py:47
  32.3 5.5 %collective-permute-start.15 = (bf16[32,1280]{1,0:T(8,128)(2,1)S(1)}, bf16[32,1280]{1,0:T(8,128)(2,1)S(1)}, u32[]{:S(2)}, u32[]{:S(2)}) collective-permute-start(bf16[32,1280]{1,0:T(8,128)(2,1)S(1)} %get-tuple-element.39.refs_8_), channel_id=1, source_target_pairs={{0,16},{8,24},{16,0},{24,8},{1,17},{9,25},{17,1},{25,9},{2,18},{10... | collective-permute-start | bytes 245768 | tf_op jit(solution)/shard_map/ppermute | solution.py:47
  34.8 8.3 %collective-permute-start.10 = (bf16[48,1280]{1,0:T(8,128)(2,1)S(1)}, bf16[48,1280]{1,0:T(8,128)(2,1)S(1)}, u32[]{:S(2)}, u32[]{:S(2)}) collective-permute-start(bf16[48,1280]{1,0:T(8,128)(2,1)S(1)} %get-tuple-element.38.refs_0_), channel_id=1, source_target_pairs={{0,1},{1,0},{2,3},{3,2},{4,5},{5,4},{6,7},{7,6},{8,9},{9,8},{10,11... | collective-permute-start | bytes 368648 | tf_op jit(solution)/shard_map/ppermute | solution.py:47
  34.8 8.8 %collective-permute-start.11 = (bf16[48,1280]{1,0:T(8,128)(2,1)S(1)}, bf16[48,1280]{1,0:T(8,128)(2,1)S(1)}, u32[]{:S(2)}, u32[]{:S(2)}) collective-permute-start(bf16[48,1280]{1,0:T(8,128)(2,1)S(1)} %collective-permute-done.7.refs_1_), channel_id=1, source_target_pairs={{0,1},{1,0},{2,3},{3,2},{4,5},{5,4},{6,7},{7,6},{8,9},{9,8},{10,11... | collective-permute-start | bytes 368648 | tf_op jit(solution)/shard_map/ppermute | solution.py:47
  35.3 8.4 %collective-permute-start.12 = (bf16[48,1280]{1,0:T(8,128)(2,1)S(1)}, bf16[48,1280]{1,0:T(8,128)(2,1)S(1)}, u32[]{:S(2)}, u32[]{:S(2)}) collective-permute-start(bf16[48,1280]{1,0:T(8,128)(2,1)S(1)} %collective-permute-done.8.refs_2_), channel_id=1, source_target_pairs={{0,1},{1,0},{2,3},{3,2},{4,5},{5,4},{6,7},{7,6},{8,9},{9,8},{10,11... | collective-permute-start | bytes 368648 | tf_op jit(solution)/shard_map/ppermute | solution.py:47
  37.8 5.3 %collective-permute-start.16 = (bf16[32,1280]{1,0:T(8,128)(2,1)S(1)}, bf16[32,1280]{1,0:T(8,128)(2,1)S(1)}, u32[]{:S(2)}, u32[]{:S(2)}) collective-permute-start(bf16[32,1280]{1,0:T(8,128)(2,1)S(1)} %get-tuple-element.39.refs_8_), channel_id=1, source_target_pairs={{0,24},{8,16},{16,8},{24,0},{1,25},{9,17},{17,9},{25,1},{2,26},{10... | collective-permute-start | bytes 245768 | tf_op jit(solution)/shard_map/ppermute | solution.py:47
  39.0 7.2 %collective-permute-start.13 = (bf16[48,1280]{1,0:T(8,128)(2,1)S(1)}, bf16[48,1280]{1,0:T(8,128)(2,1)S(1)}, u32[]{:S(2)}, u32[]{:S(2)}) collective-permute-start(bf16[48,1280]{1,0:T(8,128)(2,1)S(1)} %collective-permute-done.9.refs_3_), channel_id=1, source_target_pairs={{0,1},{1,0},{2,3},{3,2},{4,5},{5,4},{6,7},{7,6},{8,9},{9,8},{10,11... | collective-permute-start | bytes 368648 | tf_op jit(solution)/shard_map/ppermute | solution.py:47
  43.2 6.0 %collective-permute-start.17 = (bf16[32,1280]{1,0:T(8,128)(2,1)S(1)}, bf16[32,1280]{1,0:T(8,128)(2,1)S(1)}, u32[]{:S(2)}, u32[]{:S(2)}) collective-permute-start(bf16[32,1280]{1,0:T(8,128)(2,1)S(1)} %get-tuple-element.39.refs_8_), channel_id=1, source_target_pairs={{0,1},{1,0},{2,3},{3,2},{4,5},{5,4},{6,7},{7,6},{8,9},{9,8},{10,11... | collective-permute-start | bytes 245768 | tf_op jit(solution)/shard_map/ppermute | solution.py:47
  43.2 6.5 %collective-permute-start.18 = (bf16[32,1280]{1,0:T(8,128)(2,1)S(1)}, bf16[32,1280]{1,0:T(8,128)(2,1)S(1)}, u32[]{:S(2)}, u32[]{:S(2)}) collective-permute-start(bf16[32,1280]{1,0:T(8,128)(2,1)S(1)} %collective-permute-done.14.refs_9_), channel_id=1, source_target_pairs={{0,1},{1,0},{2,3},{3,2},{4,5},{5,4},{6,7},{7,6},{8,9},{9,8},{10,11... | collective-permute-start | bytes 245768 | tf_op jit(solution)/shard_map/ppermute | solution.py:47
  43.7 6.0 %collective-permute-start.19 = (bf16[32,1280]{1,0:T(8,128)(2,1)S(1)}, bf16[32,1280]{1,0:T(8,128)(2,1)S(1)}, u32[]{:S(2)}, u32[]{:S(2)}) collective-permute-start(bf16[32,1280]{1,0:T(8,128)(2,1)S(1)} %collective-permute-done.15.refs_10_), channel_id=1, source_target_pairs={{0,1},{1,0},{2,3},{3,2},{4,5},{5,4},{6,7},{7,6},{8,9},{9,8},{10,11... | collective-permute-start | bytes 245768 | tf_op jit(solution)/shard_map/ppermute | solution.py:47
  43.7 5.9 %collective-permute-start.20 = (bf16[32,1280]{1,0:T(8,128)(2,1)S(1)}, bf16[32,1280]{1,0:T(8,128)(2,1)S(1)}, u32[]{:S(2)}, u32[]{:S(2)}) collective-permute-start(bf16[32,1280]{1,0:T(8,128)(2,1)S(1)} %collective-permute-done.16.refs_11_), channel_id=1, source_target_pairs={{0,1},{1,0},{2,3},{3,2},{4,5},{5,4},{6,7},{7,6},{8,9},{9,8},{10,11... | collective-permute-start | bytes 245768 | tf_op jit(solution)/shard_map/ppermute | solution.py:47
  44.2 1.0 %copy-start.2 = (bf16[256,640]{1,0:T(8,128)(2,1)S(1)}, bf16[256,640]{1,0:T(8,128)(2,1)}, u32[]{:S(2)}) copy-start(bf16[256,640]{1,0:T(8,128)(2,1)} %refs_4_.1) | copy-start | bytes 983044
  47.2 9.0 %collective-permute-start.21 = (bf16[128,640]{1,0:T(8,128)(2,1)S(1)}, bf16[128,640]{1,0:T(8,128)(2,1)S(1)}, u32[]{:S(2)}, u32[]{:S(2)}) collective-permute-start(bf16[128,640]{1,0:T(8,128)(2,1)S(1)} %get-tuple-element.43), channel_id=1, source_target_pairs={{0,6},{2,4},{4,2},{6,0},{1,7},{3,5},{5,3},{7,1},{8,14},{10,12},{12... | collective-permute-start | bytes 491528 | tf_op jit(solution)/shard_map/ppermute | solution.py:47
  49.1 15.2 %collective-permute-start.22 = (bf16[128,640]{1,0:T(8,128)(2,1)S(1)}, bf16[128,640]{1,0:T(8,128)(2,1)S(1)}, u32[]{:S(2)}, u32[]{:S(2)}) collective-permute-start(bf16[128,640]{1,0:T(8,128)(2,1)S(1)} %get-tuple-element.44), channel_id=1, source_target_pairs={{0,4},{2,6},{4,0},{6,2},{1,5},{3,7},{5,1},{7,3},{8,12},{10,14},{12... | collective-permute-start | bytes 491528 | tf_op jit(solution)/shard_map/ppermute | solution.py:47
  50.9 13.5 %collective-permute-start.23 = (bf16[128,640]{1,0:T(8,128)(2,1)S(1)}, bf16[128,640]{1,0:T(8,128)(2,1)S(1)}, u32[]{:S(2)}, u32[]{:S(2)}) collective-permute-start(bf16[128,640]{1,0:T(8,128)(2,1)S(1)} %get-tuple-element.45), channel_id=1, source_target_pairs={{0,2},{2,0},{4,6},{6,4},{1,3},{3,1},{5,7},{7,5},{8,10},{10,8},{12,... | collective-permute-start | bytes 491528 | tf_op jit(solution)/shard_map/ppermute | solution.py:47

commit v3 on v2

--- a/solution.py
+++ b/solution.py
@@ -23,7 +23,7 @@
 
 VMEM = pl.BlockSpec(memory_space=pltpu.VMEM)
 SMEM = pl.BlockSpec(memory_space=pltpu.SMEM)
-ANY = pl.BlockSpec(memory_space=pl.ANY)
+HBM = pl.BlockSpec(memory_space=pltpu.HBM)
 
 
 def iota(shape, dim):
@@ -109,7 +109,7 @@
 
 
 def norm_kernel(n, gain, info, *refs):
-    inputs, outs, held = refs[:n], refs[n : 2 * n], refs[2 * n]
+    inputs, outs, held = refs[n - 1 :: -1], refs[n : 2 * n], refs[2 * n]
     a = lax.axis_index("sec")
     s = lax.axis_index("seq")
     slots, width = inputs[0].shape
@@ -177,7 +177,7 @@
 
 
 def pack_kernel(n, n_class, n_resp, tok, row, *refs):
-    moved, first, second, held, counts = refs[:n], refs[n], refs[n + 1], refs[n + 2], refs[n + 3]
+    moved, (first, second, both, held, counts) = refs[n - 1 :: -1], refs[n:]
     s = lax.axis_index("seq")
     c = lax.axis_index("sec") * lax.axis_size("tp") + lax.axis_index("tp")
     slots, width = moved[0].shape[0], first.shape[1]
@@ -200,6 +200,7 @@
     r1, r2 = first.shape[0], second.shape[0]
     pick = (iota((r1 + r2, n * slots), 0) == place).astype(BF16)
     out = jnp.dot(pick, held[...], preferred_element_type=F32).astype(BF16)
+    both[...] = out
     first[...] = out[0:r1]
     second[...] = out[r1 : r1 + r2]
 
@@ -242,10 +243,13 @@
         index = packed - start
         c = mod(index, n_class)
         place = list_place(counts, n, n_class, tok, s, c, seq_of, div(index, n_class), packed)
-        side = (mod(c, n_tp) ^ t) * n + (div(c, n_tp) ^ a)
-        column = side * r1 + place
-        if not far:
-            column = jnp.where(place < r1, column, n_class * r1 + side * r2 + place - r1)
+        core, k = mod(c, n_tp) ^ t, div(c, n_tp) ^ a
+        if far:
+            column = (core * n + k) * r1 + place
+        else:
+            column = core * (n * r1 + r2) + k * r1 + jnp.where(k > 0, r2, 0) + place
+            rest_of = n_class * r1 + n_tp * r2 + (core * (n - 1) + k - 1) * r2 + place - r1
+            column = jnp.where((k > 0) & (place >= r1), rest_of, column)
         one_hot(upright(column), pick)
         source, ends = index, 0
         for r in range(n_resp):
@@ -255,12 +259,11 @@
         rest[...] = jnp.dot(own[...], hidden[...], preferred_element_type=F32)
 
 
-def mix_kernel(n_lists, sizes, pick, rest, projection, *refs):
-    pieces, outs, held = refs[:n_lists], refs[n_lists:-1], refs[-1]
+def mix_kernel(sizes, pick, rest, projection, *refs):
+    pieces, outs, held = refs[: len(sizes)], refs[len(sizes) : -1], refs[-1]
     offset = 0
-    for piece in pieces:
-        size = piece.shape[0]
-        held[offset : offset + size, :] = piece[...]
+    for size, piece in zip(sizes, pieces, strict=True):
+        held[offset : offset + size, :] = piece[0:size, :]
         offset += size
     tokens = jnp.dot(pick[...], held[...], preferred_element_type=F32).astype(BF16)
     total = jnp.dot(tokens, projection[...], preferred_element_type=F32) + rest[...]
@@ -353,7 +356,7 @@
             shape((INFO, LANES), BF16),
             shape((1, D), F32),
         ],
-        [ANY] * 7,
+        [HBM] * 7,
         [VMEM] * 4,
         [
             pltpu.VMEM((rows, cols), BF16),
@@ -365,13 +368,18 @@
             pltpu.SemaphoreType.DMA((7,)),
         ],
     )(
-        hidden,
-        lengths,
-        group_of,
-        rewards,
-        old_logp.reshape(row, LANES),
-        ref_logp.reshape(row, LANES),
-        norm_gain.reshape(1, D),
+        *(
+            pltpu.with_memory_space_constraint(x, pltpu.HBM)
+            for x in (
+                hidden,
+                lengths,
+                group_of,
+                rewards,
+                old_logp.reshape(row, LANES),
+                ref_logp.reshape(row, LANES),
+                norm_gain.reshape(1, D),
+            )
+        )
     )
     dealt = call(
         functools.partial(spread_kernel, n_tp), [shape((slots, width), BF16)] * n, [VMEM] * 3, [VMEM] * n
@@ -383,15 +391,15 @@
         [VMEM] * (n + 2),
         [VMEM] * n,
         [pltpu.VMEM((n, slots, width), BF16)],
-    )(gain, info, *whole)
+    )(gain, info, *whole[::-1])
     moved = [normed[0]] + [swap(normed[m], "seq", m) for m in range(n - 1, 0, -1)][::-1]
-    lists = call(
+    first, second, both = call(
         functools.partial(pack_kernel, n, n_class, n_resp, tok, row),
-        [shape((r1, width), BF16), shape((r2, width), BF16)],
+        [shape((r, width), BF16) for r in (r1, r2, r1 + r2)],
         [VMEM] * n,
-        [VMEM] * 2,
+        [VMEM] * 3,
         [pltpu.VMEM((n * slots, width), BF16), pltpu.SMEM((n,), I32)],
-    )(*moved)
+    )(*moved[::-1])
     half = n // 2 * tok
     pick_far, pick_near, rest_far, rest_near = call(
         functools.partial(index_kernel, n, n_class, n_resp, tok, row, r1, r2),
@@ -412,24 +420,27 @@
         VMEM,
         [pltpu.SMEM((n, 3 * n_resp), I32), pltpu.VMEM((n * INFO, LANES), F32)],
     )(*moved)
-    pieces = []
-    for part in lists:
-        same = [part] + [swap(part, "sec", k) for k in range(1, n)]
-        pieces.append(same + [swap(x, "tp", 1) for x in same])
+    after = lambda x, *ys: lax.optimization_barrier((x, *ys))[0]
+    other = swap(both, "tp", 1)
+    far_in = [swap(first, "sec", k) for k in range(1, n)]
+    far_other = [swap(x, "tp", 1) for x in far_in]
+    second = after(second, *far_in)
+    near_in = [swap(second, "sec", k) for k in range(1, n)]
     far = call(
-        functools.partial(mix_kernel, n_class, None),
+        functools.partial(mix_kernel, (r1,) * n_class),
         [shape((tok, cols), BF16)] * (n // 2),
         [VMEM] * (n_class + 3),
         [VMEM] * (n // 2),
         [pltpu.VMEM((n_class * r1, width), BF16)],
-    )(pick_far, rest_far, projection, *pieces[0])
+    )(pick_far, rest_far, projection, both, *far_in, other, *far_other)
+    near_other = [swap(after(x, *far), "tp", 1) for x in near_in]
     near = call(
-        functools.partial(mix_kernel, 2 * n_class, None),
+        functools.partial(mix_kernel, (r1 + r2, *(r1,) * (n - 1)) * 2 + (r2,) * (2 * n - 2)),
         [shape((tok, cols), F32)] + [shape((tok, cols), BF16)] * (n // 2 - 1),
-        [VMEM] * (2 * n_class + 3),
+        [VMEM] * (2 * n_class + 1),
         [VMEM] * (n // 2),
         [pltpu.VMEM((n_class * (r1 + r2), width), BF16)],
-    )(pick_near, rest_near, projection, *pieces[0], *pieces[1])
+    )(pick_near, rest_near, projection, both, *far_in, other, *far_other, *near_in, *near_other)
     partial = [*near, *far]
     arrived = [swap(partial[m], "seq", m) for m in range(n - 1, 0, -1)]
     states = partial[0]

time: 65.4 us -> 59.2 us (0.905)
  local copies, waits for them, and re-layouts: 6 us -> 0.01 us
    unnamed x18 -> x4, local copies, waits for them, and re-layouts: 6 us -> 0.01 us
    ppermute x24 -> x23, waiting for transfers between devices: 30.6 us -> 30.4 us  [swap(): return lax.ppermute(x, axis, [(i, i ^ k) for i in range(n)])]
    ppermute x24 -> x23, starting transfers between devices: 21.4 us -> 21.3 us  [swap(): return lax.ppermute(x, axis, [(i, i ^ k) for i in range(n)])]
  transfers between devices with their start and end apart: 24 -> 23, of which waited for: 11 -> 14; matrix products, arithmetic and copies ran while one was open for 1% -> 1% of each run, Pallas kernels for 6% -> 8%
where the time goes in v3:
time: 59.2 us; the launch traced here: 59 us
  waiting for transfers between devices  30.4 us (51%)
  starting transfers between devices  21.3 us (36%)
  Pallas kernels  5.39 us (9%)
  other arithmetic  1.26 us (2%)
  between operations  0.75 us (1%)
    ppermute x23, waiting for transfers between devices, swap(): return lax.ppermute(x, axis, [(i, i ^ k) for i in range(n)])  30.4 us
    ppermute x23, starting transfers between devices, swap(): return lax.ppermute(x, axis, [(i, i ^ k) for i in range(n)])  21.3 us
    pallas_call x1, Pallas kernels, shards_in_place(): call(functools.partial(early_kernel, n, n_tp), [shape((rows // n_tp, rows...  1.32 us
    pallas_call x1, Pallas kernels, shards_in_place(): call(functools.partial(mix_kernel, (r1 + r2, *(r1,) * (n - 1)) * 2 + (r2,...  1.2 us
  transfers between devices with their start and end apart: 23, of which 14 were waited for; matrix products, arithmetic and copies ran while one was open for 1% of the time, Pallas kernels for 8%

profile of v3, /device:TPU:0, one launch (start us, length us, event | category | flops | bytes accessed | tf_op | source)
XLA Modules:
  0.0 59.0 jit_solution(4971529916692362137)
XLA Ops:
  0.7 0.5 collective-permute-start
  1.2 1.3 %shard_map.95 = (bf16[128,256]{1,0:T(8,128)(2,1)S(1)}, bf16[128,640]{1,0:T(8,128)(2,1)S(1)}, bf16[16,128]{1,0:T(8,128)(2,1)S(1)}, f32[1,5120]{1,0:T(1,128)S(1)}) custom-call(bf16[256,640]{1,0:T(8,128)(2,1)} %refs_4_.1, s32[4]{0:T(128)} %lengths.1, s32[4]{0:T(128)} %group_of.1, s32[4]{0:T(128)} %rewards.1, f32[2,128]{1,0:T(2,128)} %bitcast.6, ...), custom_call_target="tpu_custom_call" | custom-call | tf_op jit(solution)/shard_map/pallas_call | solution.py:351
  2.5 0.1 collective-permute-done.sibling
  2.6 0.2 shard_map.96
  2.9 3.9 %collective-permute-start.1 = (bf16[32,1280]{1,0:T(8,128)(2,1)S(1)}, bf16[32,1280]{1,0:T(8,128)(2,1)S(1)}, u32[]{:S(2)}, u32[]{:S(2)}) collective-permute-start(bf16[32,1280]{1,0:T(8,128)(2,1)S(1)} %get-tuple-element.33), channel_id=1, source_target_pairs={{0,24},{8,16},{16,8},{24,0},{1,25},{9,17},{17,9},{25,1},{2,26},{10... | collective-permute-start | bytes 245768 | tf_op jit(solution)/shard_map/ppermute | solution.py:47
  6.7 0.5 collective-permute-start.2
  7.2 0.1 collective-permute-start.3
  7.4 2.2 %collective-permute-done.1.refs_0_ = bf16[32,1280]{1,0:T(8,128)(2,1)S(1)} collective-permute-done((bf16[32,1280]{1,0:T(8,128)(2,1)S(1)}, bf16[32,1280]{1,0:T(8,128)(2,1)S(1)}, u32[]{:S(2)}, u32[]{:S(2)}) %collective-permute-start.1) | collective-permute-done | bytes 81952 | tf_op jit(solution)/shard_map/ppermute | solution.py:47
  9.6 1.7 %collective-permute-done.2.refs_1_ = bf16[32,1280]{1,0:T(8,128)(2,1)S(1)} collective-permute-done((bf16[32,1280]{1,0:T(8,128)(2,1)S(1)}, bf16[32,1280]{1,0:T(8,128)(2,1)S(1)}, u32[]{:S(2)}, u32[]{:S(2)}) %collective-permute-start.2) | collective-permute-done | bytes 81952 | tf_op jit(solution)/shard_map/ppermute | solution.py:47
  11.2 0.5 collective-permute-done.3.refs_2_
  11.7 0.2 shard_map.97
  11.9 1.6 %collective-permute-start.4 = (bf16[32,1408]{1,0:T(8,128)(2,1)S(1)}, bf16[32,1408]{1,0:T(8,128)(2,1)S(1)}, u32[]{:S(2)}, u32[]{:S(2)}) collective-permute-start(bf16[32,1408]{1,0:T(8,128)(2,1)S(1)} %get-tuple-element.38), channel_id=1, source_target_pairs={{0,2},{2,0},{4,6},{6,4},{1,3},{3,1},{5,7},{7,5},{8,10},{10,8},{12,... | collective-permute-start | bytes 270344 | tf_op jit(solution)/shard_map/ppermute | solution.py:47
  13.6 2.6 %collective-permute-start.5 = (bf16[32,1408]{1,0:T(8,128)(2,1)S(1)}, bf16[32,1408]{1,0:T(8,128)(2,1)S(1)}, u32[]{:S(2)}, u32[]{:S(2)}) collective-permute-start(bf16[32,1408]{1,0:T(8,128)(2,1)S(1)} %get-tuple-element.39), channel_id=1, source_target_pairs={{0,4},{2,6},{4,0},{6,2},{1,5},{3,7},{5,1},{7,3},{8,12},{10,14},{12... | collective-permute-start | bytes 270344 | tf_op jit(solution)/shard_map/ppermute | solution.py:47
  16.1 0.2 collective-permute-start.6
  16.4 1.0 %collective-permute-done.4.refs_1_.refs_2_ = bf16[32,1408]{1,0:T(8,128)(2,1)S(1)} collective-permute-done((bf16[32,1408]{1,0:T(8,128)(2,1)S(1)}, bf16[32,1408]{1,0:T(8,128)(2,1)S(1)}, u32[]{:S(2)}, u32[]{:S(2)}) %collective-permute-start.4) | collective-permute-done | bytes 90144 | tf_op jit(solution)/shard_map/ppermute | solution.py:47
  17.4 5.3 %collective-permute-done.5.refs_2_.refs_1_ = bf16[32,1408]{1,0:T(8,128)(2,1)S(1)} collective-permute-done((bf16[32,1408]{1,0:T(8,128)(2,1)S(1)}, bf16[32,1408]{1,0:T(8,128)(2,1)S(1)}, u32[]{:S(2)}, u32[]{:S(2)}) %collective-permute-start.5) | collective-permute-done | bytes 90144 | tf_op jit(solution)/shard_map/ppermute | solution.py:47
  22.7 0.0 collective-permute-done.6.refs_3_.refs_0_
  22.8 0.4 shard_map.99
  23.1 1.4 %collective-permute-start.9 = (bf16[48,1280]{1,0:T(8,128)(2,1)S(1)}, bf16[48,1280]{1,0:T(8,128)(2,1)S(1)}, u32[]{:S(2)}, u32[]{:S(2)}) collective-permute-start(bf16[48,1280]{1,0:T(8,128)(2,1)S(1)} %get-tuple-element.44), channel_id=1, source_target_pairs={{0,24},{8,16},{16,8},{24,0},{1,25},{9,17},{17,9},{25,1},{2,26},{10... | collective-permute-start | bytes 368648 | tf_op jit(solution)/shard_map/ppermute | solution.py:47
  24.5 2.2 %collective-permute-start.8 = (bf16[48,1280]{1,0:T(8,128)(2,1)S(1)}, bf16[48,1280]{1,0:T(8,128)(2,1)S(1)}, u32[]{:S(2)}, u32[]{:S(2)}) collective-permute-start(bf16[48,1280]{1,0:T(8,128)(2,1)S(1)} %get-tuple-element.44), channel_id=1, source_target_pairs={{0,16},{8,24},{16,0},{24,8},{1,17},{9,25},{17,1},{25,9},{2,18},{10... | collective-permute-start | bytes 368648 | tf_op jit(solution)/shard_map/ppermute | solution.py:47
  26.8 0.0 collective-permute-start.7
  26.8 2.3 %collective-permute-done.9.refs_3_ = bf16[48,1280]{1,0:T(8,128)(2,1)S(1)} collective-permute-done((bf16[48,1280]{1,0:T(8,128)(2,1)S(1)}, bf16[48,1280]{1,0:T(8,128)(2,1)S(1)}, u32[]{:S(2)}, u32[]{:S(2)}) %collective-permute-start.9) | collective-permute-done | bytes 122912 | tf_op jit(solution)/shard_map/ppermute | solution.py:47
  29.1 0.0 collective-permute-start.13
  29.1 2.5 %collective-permute-done.8.refs_2_ = bf16[48,1280]{1,0:T(8,128)(2,1)S(1)} collective-permute-done((bf16[48,1280]{1,0:T(8,128)(2,1)S(1)}, bf16[48,1280]{1,0:T(8,128)(2,1)S(1)}, u32[]{:S(2)}, u32[]{:S(2)}) %collective-permute-start.8) | collective-permute-done | bytes 122912 | tf_op jit(solution)/shard_map/ppermute | solution.py:47
  31.6 0.1 collective-permute-start.12
  31.7 0.5 collective-permute-done.7.refs_1_
  32.2 0.0 collective-permute-start.11
  32.2 1.5 %collective-permute-start.16 = (bf16[32,1280]{1,0:T(8,128)(2,1)S(1)}, bf16[32,1280]{1,0:T(8,128)(2,1)S(1)}, u32[]{:S(2)}, u32[]{:S(2)}) collective-permute-start(bf16[32,1280]{1,0:T(8,128)(2,1)S(1)} %get-tuple-element.46), channel_id=1, source_target_pairs={{0,24},{8,16},{16,8},{24,0},{1,25},{9,17},{17,9},{25,1},{2,26},{10... | collective-permute-start | bytes 245768 | tf_op jit(solution)/shard_map/ppermute | solution.py:47
  33.7 0.0 collective-permute-done.10.refs_4_
  33.7 2.0 %collective-permute-start.15 = (bf16[32,1280]{1,0:T(8,128)(2,1)S(1)}, bf16[32,1280]{1,0:T(8,128)(2,1)S(1)}, u32[]{:S(2)}, u32[]{:S(2)}) collective-permute-start(bf16[32,1280]{1,0:T(8,128)(2,1)S(1)} %get-tuple-element.46), channel_id=1, source_target_pairs={{0,16},{8,24},{16,0},{24,8},{1,17},{9,25},{17,1},{25,9},{2,18},{10... | collective-permute-start | bytes 245768 | tf_op jit(solution)/shard_map/ppermute | solution.py:47
  35.7 0.0 collective-permute-done.13.refs_7_
  35.7 0.1 collective-permute-start.14
  35.7 0.6 %shard_map.98 = (bf16[256,384]{1,0:T(8,128)(2,1)S(1)}, bf16[256,640]{1,0:T(8,128)(2,1)S(1)}, f32[256,640]{1,0:T(8,128)S(1)}, f32[256,640]{1,0:T(8,128)S(1)}) custom-call(bf16[32,1408]{1,0:T(8,128)(2,1)S(1)} %get-tuple-element.37.refs_0_.refs_3_, bf16[32,1408]{1,0:T(8,128)(2,1)S(1)} %collective-permute-done.4.refs_1_.refs_2_, ...), custom_call_target="tpu_custom_call" | custom-call | tf_op jit(solution)/shard_map/pallas_call | solution.py:404
  36.4 1.0 %shard_map.100 = (bf16[128,640]{1,0:T(8,128)(2,1)S(1)}, bf16[128,640]{1,0:T(8,128)(2,1)S(1)}) custom-call(bf16[256,384]{1,0:T(8,128)(2,1)S(1)} %get-tuple-element.47.pick, f32[256,640]{1,0:T(8,128)S(1)} %get-tuple-element.48.rest, bf16[1280,640]{1,0:T(8,128)(2,1)S(1)} %copy-done, bf16[80,1280]{1,0:T(8,128)(2,1)S(1)} %get-tuple-element.43.refs_0_, ...), custom_call_target="tpu_custom_call" | custom-call | tf_op jit(solution)/shard_map/pallas_call | solution.py:429
  37.5 0.8 %collective-permute-done.16.refs_10_ = bf16[32,1280]{1,0:T(8,128)(2,1)S(1)} collective-permute-done((bf16[32,1280]{1,0:T(8,128)(2,1)S(1)}, bf16[32,1280]{1,0:T(8,128)(2,1)S(1)}, u32[]{:S(2)}, u32[]{:S(2)}) %collective-permute-start.16) | collective-permute-done | bytes 81952 | tf_op jit(solution)/shard_map/ppermute | solution.py:47
  38.2 1.5 %collective-permute-done.15.refs_9_ = bf16[32,1280]{1,0:T(8,128)(2,1)S(1)} collective-permute-done((bf16[32,1280]{1,0:T(8,128)(2,1)S(1)}, bf16[32,1280]{1,0:T(8,128)(2,1)S(1)}, u32[]{:S(2)}, u32[]{:S(2)}) %collective-permute-start.15) | collective-permute-done | bytes 81952 | tf_op jit(solution)/shard_map/ppermute | solution.py:47
  39.7 0.4 collective-permute-done.14.refs_8_
  40.1 0.5 collective-permute-start.18
  40.6 0.0 collective-permute-start.19
  40.7 0.4 shard_map.102
  41.0 2.6 %collective-permute-start.21 = (bf16[128,640]{1,0:T(8,128)(2,1)S(1)}, bf16[128,640]{1,0:T(8,128)(2,1)S(1)}, u32[]{:S(2)}, u32[]{:S(2)}) collective-permute-start(bf16[128,640]{1,0:T(8,128)(2,1)S(1)} %get-tuple-element.49), channel_id=1, source_target_pairs={{0,4},{2,6},{4,0},{6,2},{1,5},{3,7},{5,1},{7,3},{8,12},{10,14},{12... | collective-permute-start | bytes 491528 | tf_op jit(solution)/shard_map/ppermute | solution.py:47
  43.6 1.4 %collective-permute-start.20 = (bf16[128,640]{1,0:T(8,128)(2,1)S(1)}, bf16[128,640]{1,0:T(8,128)(2,1)S(1)}, u32[]{:S(2)}, u32[]{:S(2)}) collective-permute-start(bf16[128,640]{1,0:T(8,128)(2,1)S(1)} %get-tuple-element.50), channel_id=1, source_target_pairs={{0,6},{2,4},{4,2},{6,0},{1,7},{3,5},{5,3},{7,1},{8,14},{10,12},{12... | collective-permute-start | bytes 491528 | tf_op jit(solution)/shard_map/ppermute | solution.py:47
  45.0 1.2 %shard_map.101 = (f32[128,640]{1,0:T(8,128)S(1)}, bf16[128,640]{1,0:T(8,128)(2,1)S(1)}) custom-call(bf16[256,640]{1,0:T(8,128)(2,1)S(1)} %get-tuple-element.41.pick, f32[256,640]{1,0:T(8,128)S(1)} %get-tuple-element.42.rest, bf16[1280,640]{1,0:T(8,128)(2,1)S(1)} %copy-done, bf16[80,1280]{1,0:T(8,128)(2,1)S(1)} %get-tuple-element.43.refs_0_, ...), custom_call_target="tpu_custom_call" | custom-call | tf_op jit(solution)/shard_map/pallas_call | solution.py:437
  46.2 0.1 collective-permute-start.22
  46.3 0.5 convert_bitcast_fusion
  46.8 9.3 %collective-permute-done.21 = bf16[128,640]{1,0:T(8,128)(2,1)S(1)} collective-permute-done((bf16[128,640]{1,0:T(8,128)(2,1)S(1)}, bf16[128,640]{1,0:T(8,128)(2,1)S(1)}, u32[]{:S(2)}, u32[]{:S(2)}) %collective-permute-start.21) | collective-permute-done | bytes 163872 | tf_op jit(solution)/shard_map/ppermute | solution.py:47
  56.1 2.2 %collective-permute-done.22 = bf16[128,640]{1,0:T(8,128)(2,1)S(1)} collective-permute-done((bf16[128,640]{1,0:T(8,128)(2,1)S(1)}, bf16[128,640]{1,0:T(8,128)(2,1)S(1)}, u32[]{:S(2)}, u32[]{:S(2)}) %collective-permute-start.22) | collective-permute-done | bytes 163872 | tf_op jit(solution)/shard_map/ppermute | solution.py:47
  58.3 0.8 %add_convert_fusion = bf16[128,640]{1,0:T(8,128)(2,1)} fusion(bf16[128,640]{1,0:T(8,128)(2,1)S(1)} %collective-permute-done.22, bf16[128,640]{1,0:T(8,128)(2,1)S(1)} %collective-permute-done.21, f32[128,640]{1,0:T(8,128)S(1)} %get-tuple-element.54, bf16[128,640]{1,0:T(8,128)(2,1)S(1)} %collective-permute-done.20), kind=kLoop, calls=%fused_computation | loop fusion | flops 573440 | bytes 983040 | tf_op jit(solution)/shard_map/convert_element_type | solution.py:449
  (12 shorter events, 0.0 us)
Async XLA Ops:
  0.6 35.1 %copy-start.1 = (bf16[256,640]{1,0:T(8,128)(2,1)S(1)}, bf16[256,640]{1,0:T(8,128)(2,1)}, u32[]{:S(2)}) copy-start(bf16[256,640]{1,0:T(8,128)(2,1)} %refs_4_.1) | copy-start | bytes 983044
  0.6 35.8 %copy-start = (bf16[1280,640]{1,0:T(8,128)(2,1)S(1)}, bf16[1280,640]{1,0:T(8,128)(2,1)}, u32[]{:S(2)}) copy-start(bf16[1280,640]{1,0:T(8,128)(2,1)} %projection.3) | copy-start | bytes 4915204
  0.7 2.0 %collective-permute-start = (bf16[256,640]{1,0:T(8,128)(2,1)}, bf16[256,640]{1,0:T(8,128)(2,1)S(1)}, u32[]{:S(2)}, u32[]{:S(2)}) collective-permute-start(bf16[256,640]{1,0:T(8,128)(2,1)} %refs_4_.1), channel_id=1, source_target_pairs={{0,1},{1,0},{2,3},{3,2},{4,5},{5,4},{6,7},{7,6},{8,9},{9,8},{10,11... | collective-permute-start | bytes 983048 | tf_op jit(solution)/shard_map/ppermute | solution.py:47
  2.9 6.7 %collective-permute-start.1 = (bf16[32,1280]{1,0:T(8,128)(2,1)S(1)}, bf16[32,1280]{1,0:T(8,128)(2,1)S(1)}, u32[]{:S(2)}, u32[]{:S(2)}) collective-permute-start(bf16[32,1280]{1,0:T(8,128)(2,1)S(1)} %get-tuple-element.33), channel_id=1, source_target_pairs={{0,24},{8,16},{16,8},{24,0},{1,25},{9,17},{17,9},{25,1},{2,26},{10... | collective-permute-start | bytes 245768 | tf_op jit(solution)/shard_map/ppermute | solution.py:47
  6.7 4.5 %collective-permute-start.2 = (bf16[32,1280]{1,0:T(8,128)(2,1)S(1)}, bf16[32,1280]{1,0:T(8,128)(2,1)S(1)}, u32[]{:S(2)}, u32[]{:S(2)}) collective-permute-start(bf16[32,1280]{1,0:T(8,128)(2,1)S(1)} %get-tuple-element.34), channel_id=1, source_target_pairs={{0,16},{8,24},{16,0},{24,8},{1,17},{9,25},{17,1},{25,9},{2,18},{10... | collective-permute-start | bytes 245768 | tf_op jit(solution)/shard_map/ppermute | solution.py:47
  7.2 4.4 %collective-permute-start.3 = (bf16[32,1280]{1,0:T(8,128)(2,1)S(1)}, bf16[32,1280]{1,0:T(8,128)(2,1)S(1)}, u32[]{:S(2)}, u32[]{:S(2)}) collective-permute-start(bf16[32,1280]{1,0:T(8,128)(2,1)S(1)} %get-tuple-element.35), channel_id=1, source_target_pairs={{0,8},{8,0},{16,24},{24,16},{1,9},{9,1},{17,25},{25,17},{2,10},{10... | collective-permute-start | bytes 245768 | tf_op jit(solution)/shard_map/ppermute | solution.py:47
  11.9 5.5 %collective-permute-start.4 = (bf16[32,1408]{1,0:T(8,128)(2,1)S(1)}, bf16[32,1408]{1,0:T(8,128)(2,1)S(1)}, u32[]{:S(2)}, u32[]{:S(2)}) collective-permute-start(bf16[32,1408]{1,0:T(8,128)(2,1)S(1)} %get-tuple-element.38), channel_id=1, source_target_pairs={{0,2},{2,0},{4,6},{6,4},{1,3},{3,1},{5,7},{7,5},{8,10},{10,8},{12,... | collective-permute-start | bytes 270344 | tf_op jit(solution)/shard_map/ppermute | solution.py:47
  13.6 9.2 %collective-permute-start.5 = (bf16[32,1408]{1,0:T(8,128)(2,1)S(1)}, bf16[32,1408]{1,0:T(8,128)(2,1)S(1)}, u32[]{:S(2)}, u32[]{:S(2)}) collective-permute-start(bf16[32,1408]{1,0:T(8,128)(2,1)S(1)} %get-tuple-element.39), channel_id=1, source_target_pairs={{0,4},{2,6},{4,0},{6,2},{1,5},{3,7},{5,1},{7,3},{8,12},{10,14},{12... | collective-permute-start | bytes 270344 | tf_op jit(solution)/shard_map/ppermute | solution.py:47
  16.1 6.6 %collective-permute-start.6 = (bf16[32,1408]{1,0:T(8,128)(2,1)S(1)}, bf16[32,1408]{1,0:T(8,128)(2,1)S(1)}, u32[]{:S(2)}, u32[]{:S(2)}) collective-permute-start(bf16[32,1408]{1,0:T(8,128)(2,1)S(1)} %get-tuple-element.40), channel_id=1, source_target_pairs={{0,6},{2,4},{4,2},{6,0},{1,7},{3,5},{5,3},{7,1},{8,14},{10,12},{12... | collective-permute-start | bytes 270344 | tf_op jit(solution)/shard_map/ppermute | solution.py:47
  23.1 5.9 %collective-permute-start.9 = (bf16[48,1280]{1,0:T(8,128)(2,1)S(1)}, bf16[48,1280]{1,0:T(8,128)(2,1)S(1)}, u32[]{:S(2)}, u32[]{:S(2)}) collective-permute-start(bf16[48,1280]{1,0:T(8,128)(2,1)S(1)} %get-tuple-element.44), channel_id=1, source_target_pairs={{0,24},{8,16},{16,8},{24,0},{1,25},{9,17},{17,9},{25,1},{2,26},{10... | collective-permute-start | bytes 368648 | tf_op jit(solution)/shard_map/ppermute | solution.py:47
  24.5 9.2 %collective-permute-start.10 = (bf16[80,1280]{1,0:T(8,128)(2,1)S(1)}, bf16[80,1280]{1,0:T(8,128)(2,1)S(1)}, u32[]{:S(2)}, u32[]{:S(2)}) collective-permute-start(bf16[80,1280]{1,0:T(8,128)(2,1)S(1)} %get-tuple-element.43.refs_0_), channel_id=1, source_target_pairs={{0,1},{1,0},{2,3},{3,2},{4,5},{5,4},{6,7},{7,6},{8,9},{9,8},{10,11... | collective-permute-start | bytes 614408 | tf_op jit(solution)/shard_map/ppermute | solution.py:47
  24.5 7.1 %collective-permute-start.8 = (bf16[48,1280]{1,0:T(8,128)(2,1)S(1)}, bf16[48,1280]{1,0:T(8,128)(2,1)S(1)}, u32[]{:S(2)}, u32[]{:S(2)}) collective-permute-start(bf16[48,1280]{1,0:T(8,128)(2,1)S(1)} %get-tuple-element.44), channel_id=1, source_target_pairs={{0,16},{8,24},{16,0},{24,8},{1,17},{9,25},{17,1},{25,9},{2,18},{10... | collective-permute-start | bytes 368648 | tf_op jit(solution)/shard_map/ppermute | solution.py:47
  26.8 5.5 %collective-permute-start.7 = (bf16[48,1280]{1,0:T(8,128)(2,1)S(1)}, bf16[48,1280]{1,0:T(8,128)(2,1)S(1)}, u32[]{:S(2)}, u32[]{:S(2)}) collective-permute-start(bf16[48,1280]{1,0:T(8,128)(2,1)S(1)} %get-tuple-element.44), channel_id=1, source_target_pairs={{0,8},{8,0},{16,24},{24,16},{1,9},{9,1},{17,25},{25,17},{2,10},{10... | collective-permute-start | bytes 368648 | tf_op jit(solution)/shard_map/ppermute | solution.py:47
  29.1 6.6 %collective-permute-start.13 = (bf16[48,1280]{1,0:T(8,128)(2,1)S(1)}, bf16[48,1280]{1,0:T(8,128)(2,1)S(1)}, u32[]{:S(2)}, u32[]{:S(2)}) collective-permute-start(bf16[48,1280]{1,0:T(8,128)(2,1)S(1)} %collective-permute-done.9.refs_3_), channel_id=1, source_target_pairs={{0,1},{1,0},{2,3},{3,2},{4,5},{5,4},{6,7},{7,6},{8,9},{9,8},{10,11... | collective-permute-start | bytes 368648 | tf_op jit(solution)/shard_map/ppermute | solution.py:47
  31.6 4.8 %collective-permute-start.12 = (bf16[48,1280]{1,0:T(8,128)(2,1)S(1)}, bf16[48,1280]{1,0:T(8,128)(2,1)S(1)}, u32[]{:S(2)}, u32[]{:S(2)}) collective-permute-start(bf16[48,1280]{1,0:T(8,128)(2,1)S(1)} %collective-permute-done.8.refs_2_), channel_id=1, source_target_pairs={{0,1},{1,0},{2,3},{3,2},{4,5},{5,4},{6,7},{7,6},{8,9},{9,8},{10,11... | collective-permute-start | bytes 368648 | tf_op jit(solution)/shard_map/ppermute | solution.py:47
  32.2 4.2 %collective-permute-start.11 = (bf16[48,1280]{1,0:T(8,128)(2,1)S(1)}, bf16[48,1280]{1,0:T(8,128)(2,1)S(1)}, u32[]{:S(2)}, u32[]{:S(2)}) collective-permute-start(bf16[48,1280]{1,0:T(8,128)(2,1)S(1)} %collective-permute-done.7.refs_1_), channel_id=1, source_target_pairs={{0,1},{1,0},{2,3},{3,2},{4,5},{5,4},{6,7},{7,6},{8,9},{9,8},{10,11... | collective-permute-start | bytes 368648 | tf_op jit(solution)/shard_map/ppermute | solution.py:47
  32.2 6.0 %collective-permute-start.16 = (bf16[32,1280]{1,0:T(8,128)(2,1)S(1)}, bf16[32,1280]{1,0:T(8,128)(2,1)S(1)}, u32[]{:S(2)}, u32[]{:S(2)}) collective-permute-start(bf16[32,1280]{1,0:T(8,128)(2,1)S(1)} %get-tuple-element.46), channel_id=1, source_target_pairs={{0,24},{8,16},{16,8},{24,0},{1,25},{9,17},{17,9},{25,1},{2,26},{10... | collective-permute-start | bytes 245768 | tf_op jit(solution)/shard_map/ppermute | solution.py:47
  33.7 6.0 %collective-permute-start.15 = (bf16[32,1280]{1,0:T(8,128)(2,1)S(1)}, bf16[32,1280]{1,0:T(8,128)(2,1)S(1)}, u32[]{:S(2)}, u32[]{:S(2)}) collective-permute-start(bf16[32,1280]{1,0:T(8,128)(2,1)S(1)} %get-tuple-element.46), channel_id=1, source_target_pairs={{0,16},{8,24},{16,0},{24,8},{1,17},{9,25},{17,1},{25,9},{2,18},{10... | collective-permute-start | bytes 245768 | tf_op jit(solution)/shard_map/ppermute | solution.py:47
  35.7 4.4 %collective-permute-start.14 = (bf16[32,1280]{1,0:T(8,128)(2,1)S(1)}, bf16[32,1280]{1,0:T(8,128)(2,1)S(1)}, u32[]{:S(2)}, u32[]{:S(2)}) collective-permute-start(bf16[32,1280]{1,0:T(8,128)(2,1)S(1)} %get-tuple-element.46), channel_id=1, source_target_pairs={{0,8},{8,0},{16,24},{24,16},{1,9},{9,1},{17,25},{25,17},{2,10},{10... | collective-permute-start | bytes 245768 | tf_op jit(solution)/shard_map/ppermute | solution.py:47
  40.1 4.9 %collective-permute-start.17 = (bf16[32,1280]{1,0:T(8,128)(2,1)S(1)}, bf16[32,1280]{1,0:T(8,128)(2,1)S(1)}, u32[]{:S(2)}, u32[]{:S(2)}) collective-permute-start(bf16[32,1280]{1,0:T(8,128)(2,1)S(1)} %collective-permute-done.14.refs_8_), channel_id=1, source_target_pairs={{0,1},{1,0},{2,3},{3,2},{4,5},{5,4},{6,7},{7,6},{8,9},{9,8},{10,11... | collective-permute-start | bytes 245768 | tf_op jit(solution)/shard_map/ppermute | solution.py:47
  40.1 4.9 %collective-permute-start.18 = (bf16[32,1280]{1,0:T(8,128)(2,1)S(1)}, bf16[32,1280]{1,0:T(8,128)(2,1)S(1)}, u32[]{:S(2)}, u32[]{:S(2)}) collective-permute-start(bf16[32,1280]{1,0:T(8,128)(2,1)S(1)} %collective-permute-done.15.refs_9_), channel_id=1, source_target_pairs={{0,1},{1,0},{2,3},{3,2},{4,5},{5,4},{6,7},{7,6},{8,9},{9,8},{10,11... | collective-permute-start | bytes 245768 | tf_op jit(solution)/shard_map/ppermute | solution.py:47
  40.6 4.3 %collective-permute-start.19 = (bf16[32,1280]{1,0:T(8,128)(2,1)S(1)}, bf16[32,1280]{1,0:T(8,128)(2,1)S(1)}, u32[]{:S(2)}, u32[]{:S(2)}) collective-permute-start(bf16[32,1280]{1,0:T(8,128)(2,1)S(1)} %collective-permute-done.16.refs_10_), channel_id=1, source_target_pairs={{0,1},{1,0},{2,3},{3,2},{4,5},{5,4},{6,7},{7,6},{8,9},{9,8},{10,11... | collective-permute-start | bytes 245768 | tf_op jit(solution)/shard_map/ppermute | solution.py:47
  41.0 15.0 %collective-permute-start.21 = (bf16[128,640]{1,0:T(8,128)(2,1)S(1)}, bf16[128,640]{1,0:T(8,128)(2,1)S(1)}, u32[]{:S(2)}, u32[]{:S(2)}) collective-permute-start(bf16[128,640]{1,0:T(8,128)(2,1)S(1)} %get-tuple-element.49), channel_id=1, source_target_pairs={{0,4},{2,6},{4,0},{6,2},{1,5},{3,7},{5,1},{7,3},{8,12},{10,14},{12... | collective-permute-start | bytes 491528 | tf_op jit(solution)/shard_map/ppermute | solution.py:47
  43.6 12.5 %collective-permute-start.20 = (bf16[128,640]{1,0:T(8,128)(2,1)S(1)}, bf16[128,640]{1,0:T(8,128)(2,1)S(1)}, u32[]{:S(2)}, u32[]{:S(2)}) collective-permute-start(bf16[128,640]{1,0:T(8,128)(2,1)S(1)} %get-tuple-element.50), channel_id=1, source_target_pairs={{0,6},{2,4},{4,2},{6,0},{1,7},{3,5},{5,3},{7,1},{8,14},{10,12},{12... | collective-permute-start | bytes 491528 | tf_op jit(solution)/shard_map/ppermute | solution.py:47
  46.2 12.1 %collective-permute-start.22 = (bf16[128,640]{1,0:T(8,128)(2,1)S(1)}, bf16[128,640]{1,0:T(8,128)(2,1)S(1)}, u32[]{:S(2)}, u32[]{:S(2)}) collective-permute-start(bf16[128,640]{1,0:T(8,128)(2,1)S(1)} %get-tuple-element.55), channel_id=1, source_target_pairs={{0,2},{2,0},{4,6},{6,4},{1,3},{3,1},{5,7},{7,5},{8,10},{10,8},{12,... | collective-permute-start | bytes 491528 | tf_op jit(solution)/shard_map/ppermute | solution.py:47

commit v4 on v3

--- a/solution.py
+++ b/solution.py
@@ -109,7 +109,7 @@
 
 
 def norm_kernel(n, gain, info, *refs):
-    inputs, outs, held = refs[n - 1 :: -1], refs[n : 2 * n], refs[2 * n]
+    inputs, outs, held = refs[:n], refs[2 * n - 1 : n - 1 : -1], refs[2 * n]
     a = lax.axis_index("sec")
     s = lax.axis_index("seq")
     slots, width = inputs[0].shape
@@ -177,10 +177,10 @@
 
 
 def pack_kernel(n, n_class, n_resp, tok, row, *refs):
-    moved, (first, second, both, held, counts) = refs[n - 1 :: -1], refs[n:]
+    moved, (out, held, counts) = refs[n - 1 :: -1], refs[n:]
     s = lax.axis_index("seq")
     c = lax.axis_index("sec") * lax.axis_size("tp") + lax.axis_index("tp")
-    slots, width = moved[0].shape[0], first.shape[1]
+    slots, width = moved[0].shape[0], out.shape[1]
     put_counts(moved, width, row, n_resp, counts)
     lane = iota((1, n * slots), 1)
     seq_of = div(lane, slots) ^ s
@@ -197,12 +197,8 @@
     place = jnp.where(live, place, -1)
     for m, ref in enumerate(moved):
         held[m * slots : (m + 1) * slots, :] = ref[:, 0:width]
-    r1, r2 = first.shape[0], second.shape[0]
-    pick = (iota((r1 + r2, n * slots), 0) == place).astype(BF16)
-    out = jnp.dot(pick, held[...], preferred_element_type=F32).astype(BF16)
-    both[...] = out
-    first[...] = out[0:r1]
-    second[...] = out[r1 : r1 + r2]
+    pick = (iota((out.shape[0], n * slots), 0) == place).astype(BF16)
+    out[...] = jnp.dot(pick, held[...], preferred_element_type=F32).astype(BF16)
 
 
 def upright(x):
@@ -214,8 +210,8 @@
         out[:, j * LANES : (j + 1) * LANES] = (iota(column.shape, 1) + j * LANES == column).astype(BF16)
 
 
-def index_kernel(n, n_class, n_resp, tok, row, r1, r2, *refs):
-    moved, hidden = refs[:n], refs[n]
+def index_kernel(n, n_class, n_resp, tok, row, listed, *refs):
+    moved, hidden = refs[n - 1 :: -1], refs[n]
     pick_far, pick_near, rest_far, rest_near, counts, lens, own = refs[n + 1 :]
     a = lax.axis_index("sec")
     s = lax.axis_index("seq")
@@ -243,13 +239,7 @@
         index = packed - start
         c = mod(index, n_class)
         place = list_place(counts, n, n_class, tok, s, c, seq_of, div(index, n_class), packed)
-        core, k = mod(c, n_tp) ^ t, div(c, n_tp) ^ a
-        if far:
-            column = (core * n + k) * r1 + place
-        else:
-            column = core * (n * r1 + r2) + k * r1 + jnp.where(k > 0, r2, 0) + place
-            rest_of = n_class * r1 + n_tp * r2 + (core * (n - 1) + k - 1) * r2 + place - r1
-            column = jnp.where((k > 0) & (place >= r1), rest_of, column)
+        column = ((mod(c, n_tp) ^ t) * n + (div(c, n_tp) ^ a)) * listed + place
         one_hot(upright(column), pick)
         source, ends = index, 0
         for r in range(n_resp):
@@ -259,12 +249,11 @@
         rest[...] = jnp.dot(own[...], hidden[...], preferred_element_type=F32)
 
 
-def mix_kernel(sizes, pick, rest, projection, *refs):
-    pieces, outs, held = refs[: len(sizes)], refs[len(sizes) : -1], refs[-1]
-    offset = 0
-    for size, piece in zip(sizes, pieces, strict=True):
-        held[offset : offset + size, :] = piece[0:size, :]
-        offset += size
+def mix_kernel(n_lists, pick, rest, projection, *refs):
+    pieces, outs, held = refs[:n_lists], refs[n_lists:-1], refs[-1]
+    listed = pieces[0].shape[0]
+    for k, piece in enumerate(pieces):
+        held[k * listed : (k + 1) * listed, :] = piece[...]
     tokens = jnp.dot(pick[...], held[...], preferred_element_type=F32).astype(BF16)
     total = jnp.dot(tokens, projection[...], preferred_element_type=F32) + rest[...]
     tok = outs[0].shape[0]
@@ -273,7 +262,7 @@
 
 
 def terms_kernel(n, n_resp, row, *refs):
-    moved, out, words, table = refs[:n], refs[n], refs[n + 1], refs[n + 2]
+    moved, out, words, table = refs[n - 1 :: -1], refs[n], refs[n + 1], refs[n + 2]
     s = lax.axis_index("seq")
     width = moved[0].shape[1] - LANES
     tok = out.shape[1]
@@ -340,10 +329,7 @@
     row = rows // LANES
     tok = TOK_DEV
     tokens = tok * n
-    up16 = lambda x: -(-x // 16) * 16
-    far_rows = up16((tokens // 2 + (n_class - 1) * (n + 1)) // n_class)
-    all_rows = up16((tokens + (n_class - 1) * n) // n_class)
-    r1, r2 = far_rows, max(16, all_rows - far_rows)
+    listed = -(-((tokens + (n_class - 1) * n) // n_class) // 16) * 16
     shape = jax.ShapeDtypeStruct
     info_like = shape((slots, width + LANES), BF16)
 
@@ -391,56 +377,47 @@
         [VMEM] * (n + 2),
         [VMEM] * n,
         [pltpu.VMEM((n, slots, width), BF16)],
-    )(gain, info, *whole[::-1])
+    )(gain, info, *whole)[::-1]
     moved = [normed[0]] + [swap(normed[m], "seq", m) for m in range(n - 1, 0, -1)][::-1]
-    first, second, both = call(
+    mine = call(
         functools.partial(pack_kernel, n, n_class, n_resp, tok, row),
-        [shape((r, width), BF16) for r in (r1, r2, r1 + r2)],
+        shape((listed, width), BF16),
         [VMEM] * n,
-        [VMEM] * 3,
+        VMEM,
         [pltpu.VMEM((n * slots, width), BF16), pltpu.SMEM((n,), I32)],
     )(*moved[::-1])
     half = n // 2 * tok
     pick_far, pick_near, rest_far, rest_near = call(
-        functools.partial(index_kernel, n, n_class, n_resp, tok, row, r1, r2),
+        functools.partial(index_kernel, n, n_class, n_resp, tok, row, listed),
         [
-            shape((half, n_class * r1), BF16),
-            shape((half, n_class * (r1 + r2)), BF16),
+            shape((half, n_class * listed), BF16),
+            shape((half, n_class * listed), BF16),
             shape((half, cols), F32),
             shape((half, cols), F32),
         ],
         [VMEM] * (n + 1),
         [VMEM] * 4,
         [pltpu.SMEM((n,), I32), pltpu.SMEM((n_resp,), I32), pltpu.VMEM((half, rows), BF16)],
-    )(*moved, hidden)
+    )(*moved[::-1], hidden)
     terms = call(
         functools.partial(terms_kernel, n, n_resp, row),
         shape((2, tok), F32),
         [VMEM] * n,
         VMEM,
         [pltpu.SMEM((n, 3 * n_resp), I32), pltpu.VMEM((n * INFO, LANES), F32)],
-    )(*moved)
+    )(*moved[::-1])
     after = lambda x, *ys: lax.optimization_barrier((x, *ys))[0]
-    other = swap(both, "tp", 1)
-    far_in = [swap(first, "sec", k) for k in range(1, n)]
-    far_other = [swap(x, "tp", 1) for x in far_in]
-    second = after(second, *far_in)
-    near_in = [swap(second, "sec", k) for k in range(1, n)]
-    far = call(
-        functools.partial(mix_kernel, (r1,) * n_class),
-        [shape((tok, cols), BF16)] * (n // 2),
+    same = [mine] + [swap(mine, "sec", k) for k in range(1, n)]
+    lists = same + [swap(after(x, pick_far, terms), "tp", 1) for x in same]
+    mix = lambda pick, rest, kind: call(
+        functools.partial(mix_kernel, n_class),
+        [shape((tok, cols), kind)] + [shape((tok, cols), BF16)] * (n // 2 - 1),
         [VMEM] * (n_class + 3),
         [VMEM] * (n // 2),
-        [pltpu.VMEM((n_class * r1, width), BF16)],
-    )(pick_far, rest_far, projection, both, *far_in, other, *far_other)
-    near_other = [swap(after(x, *far), "tp", 1) for x in near_in]
-    near = call(
-        functools.partial(mix_kernel, (r1 + r2, *(r1,) * (n - 1)) * 2 + (r2,) * (2 * n - 2)),
-        [shape((tok, cols), F32)] + [shape((tok, cols), BF16)] * (n // 2 - 1),
-        [VMEM] * (2 * n_class + 1),
-        [VMEM] * (n // 2),
-        [pltpu.VMEM((n_class * (r1 + r2), width), BF16)],
-    )(pick_near, rest_near, projection, both, *far_in, other, *far_other, *near_in, *near_other)
+        [pltpu.VMEM((n_class * listed, width), BF16)],
+    )(pick, rest, projection, *lists)
+    far = mix(pick_far, rest_far, BF16)
+    near = mix(after(pick_near, *far), rest_near, F32)
     partial = [*near, *far]
     arrived = [swap(partial[m], "seq", m) for m in range(n - 1, 0, -1)]
     states = partial[0]

time: 59.2 us -> 54.3 us (0.917)
  starting transfers between devices: 21.3 us -> 17.2 us
  waiting for transfers between devices: 30.4 us -> 29.4 us
    ppermute x23 -> x17, starting transfers between devices: 21.3 us -> 17.2 us  [swap(): return lax.ppermute(x, axis, [(i, i ^ k) for i in range(n)])]
    ppermute x23 -> x17, waiting for transfers between devices: 30.4 us -> 29.4 us  [swap(): return lax.ppermute(x, axis, [(i, i ^ k) for i in range(n)])]
  transfers between devices with their start and end apart: 23 -> 17, of which waited for: 14 -> 12; matrix products, arithmetic and copies ran while one was open for 1% -> 1% of each run, Pallas kernels for 8% -> 7%
where the time goes in v4:
time: 54.3 us; the launch traced here: 54.1 us
  waiting for transfers between devices  29.4 us (54%)
  starting transfers between devices  17.2 us (32%)
  Pallas kernels  5.56 us (10%)
  other arithmetic  1.25 us (2%)
  between operations  0.74 us (1%)
    ppermute x17, waiting for transfers between devices, swap(): return lax.ppermute(x, axis, [(i, i ^ k) for i in range(n)])  29.4 us
    ppermute x17, starting transfers between devices, swap(): return lax.ppermute(x, axis, [(i, i ^ k) for i in range(n)])  17.2 us
    pallas_call x2, Pallas kernels, shards_in_place(): call(functools.partial(mix_kernel, n_class), [shape((tok, cols), kind)] +...  2.39 us
    pallas_call x1, Pallas kernels, shards_in_place(): call(functools.partial(early_kernel, n, n_tp), [shape((rows // n_tp, rows...  1.32 us
  transfers between devices with their start and end apart: 17, of which 12 were waited for; matrix products, arithmetic and copies ran while one was open for 1% of the time, Pallas kernels for 7%

profile of v4, /device:TPU:0, one launch (start us, length us, event | category | flops | bytes accessed | tf_op | source)
XLA Modules:
  0.0 54.1 jit_solution(17823134614540369432)
XLA Ops:
  0.6 0.0 copy-start.1
  0.6 0.0 copy-start
  0.7 0.5 collective-permute-start
  1.2 1.3 %shard_map.95 = (bf16[128,256]{1,0:T(8,128)(2,1)S(1)}, bf16[128,640]{1,0:T(8,128)(2,1)S(1)}, bf16[16,128]{1,0:T(8,128)(2,1)S(1)}, f32[1,5120]{1,0:T(1,128)S(1)}) custom-call(bf16[256,640]{1,0:T(8,128)(2,1)} %refs_4_.1, s32[4]{0:T(128)} %lengths.1, s32[4]{0:T(128)} %group_of.1, s32[4]{0:T(128)} %rewards.1, f32[2,128]{1,0:T(2,128)} %bitcast.6, ...), custom_call_target="tpu_custom_call" | custom-call | tf_op jit(solution)/shard_map/pallas_call | solution.py:337
  2.5 0.1 collective-permute-done.sibling
  2.6 0.2 shard_map.96
  2.9 2.9 %collective-permute-start.1 = (bf16[32,1280]{1,0:T(8,128)(2,1)S(1)}, bf16[32,1280]{1,0:T(8,128)(2,1)S(1)}, u32[]{:S(2)}, u32[]{:S(2)}) collective-permute-start(bf16[32,1280]{1,0:T(8,128)(2,1)S(1)} %get-tuple-element.32), channel_id=1, source_target_pairs={{0,8},{8,0},{16,24},{24,16},{1,9},{9,1},{17,25},{25,17},{2,10},{10... | collective-permute-start | bytes 245768 | tf_op jit(solution)/shard_map/ppermute | solution.py:47
  5.8 1.5 %collective-permute-start.2 = (bf16[32,1280]{1,0:T(8,128)(2,1)S(1)}, bf16[32,1280]{1,0:T(8,128)(2,1)S(1)}, u32[]{:S(2)}, u32[]{:S(2)}) collective-permute-start(bf16[32,1280]{1,0:T(8,128)(2,1)S(1)} %get-tuple-element.33), channel_id=1, source_target_pairs={{0,16},{8,24},{16,0},{24,8},{1,17},{9,25},{17,1},{25,9},{2,18},{10... | collective-permute-start | bytes 245768 | tf_op jit(solution)/shard_map/ppermute | solution.py:47
  7.3 0.0 collective-permute-start.3
  7.3 1.2 %collective-permute-done.1.refs_1_ = bf16[32,1280]{1,0:T(8,128)(2,1)S(1)} collective-permute-done((bf16[32,1280]{1,0:T(8,128)(2,1)S(1)}, bf16[32,1280]{1,0:T(8,128)(2,1)S(1)}, u32[]{:S(2)}, u32[]{:S(2)}) %collective-permute-start.1) | collective-permute-done | bytes 81952 | tf_op jit(solution)/shard_map/ppermute | solution.py:47
  8.5 2.5 %collective-permute-done.2.refs_2_ = bf16[32,1280]{1,0:T(8,128)(2,1)S(1)} collective-permute-done((bf16[32,1280]{1,0:T(8,128)(2,1)S(1)}, bf16[32,1280]{1,0:T(8,128)(2,1)S(1)}, u32[]{:S(2)}, u32[]{:S(2)}) %collective-permute-start.2) | collective-permute-done | bytes 81952 | tf_op jit(solution)/shard_map/ppermute | solution.py:47
  11.1 1.6 %collective-permute-done.3.refs_3_ = bf16[32,1280]{1,0:T(8,128)(2,1)S(1)} collective-permute-done((bf16[32,1280]{1,0:T(8,128)(2,1)S(1)}, bf16[32,1280]{1,0:T(8,128)(2,1)S(1)}, u32[]{:S(2)}, u32[]{:S(2)}) %collective-permute-start.3) | collective-permute-done | bytes 81952 | tf_op jit(solution)/shard_map/ppermute | solution.py:47
  12.6 0.2 shard_map.97
  12.9 3.7 %collective-permute-start.4 = (bf16[32,1408]{1,0:T(8,128)(2,1)S(1)}, bf16[32,1408]{1,0:T(8,128)(2,1)S(1)}, u32[]{:S(2)}, u32[]{:S(2)}) collective-permute-start(bf16[32,1408]{1,0:T(8,128)(2,1)S(1)} %get-tuple-element.35), channel_id=1, source_target_pairs={{0,6},{2,4},{4,2},{6,0},{1,7},{3,5},{5,3},{7,1},{8,14},{10,12},{12... | collective-permute-start | bytes 270344 | tf_op jit(solution)/shard_map/ppermute | solution.py:47
  16.5 0.0 collective-permute-start.5
  16.5 0.8 %collective-permute-start.6 = (bf16[32,1408]{1,0:T(8,128)(2,1)S(1)}, bf16[32,1408]{1,0:T(8,128)(2,1)S(1)}, u32[]{:S(2)}, u32[]{:S(2)}) collective-permute-start(bf16[32,1408]{1,0:T(8,128)(2,1)S(1)} %get-tuple-element.37), channel_id=1, source_target_pairs={{0,2},{2,0},{4,6},{6,4},{1,3},{3,1},{5,7},{7,5},{8,10},{10,8},{12,... | collective-permute-start | bytes 270344 | tf_op jit(solution)/shard_map/ppermute | solution.py:47
  17.3 1.9 %collective-permute-done.4.refs_0_ = bf16[32,1408]{1,0:T(8,128)(2,1)S(1)} collective-permute-done((bf16[32,1408]{1,0:T(8,128)(2,1)S(1)}, bf16[32,1408]{1,0:T(8,128)(2,1)S(1)}, u32[]{:S(2)}, u32[]{:S(2)}) %collective-permute-start.4) | collective-permute-done | bytes 90144 | tf_op jit(solution)/shard_map/ppermute | solution.py:47
  19.3 3.7 %collective-permute-done.5.refs_1_ = bf16[32,1408]{1,0:T(8,128)(2,1)S(1)} collective-permute-done((bf16[32,1408]{1,0:T(8,128)(2,1)S(1)}, bf16[32,1408]{1,0:T(8,128)(2,1)S(1)}, u32[]{:S(2)}, u32[]{:S(2)}) %collective-permute-start.5) | collective-permute-done | bytes 90144 | tf_op jit(solution)/shard_map/ppermute | solution.py:47
  23.0 0.0 collective-permute-done.6.refs_2_
  23.0 0.4 shard_map.99.refs_0_
  23.3 0.9 %collective-permute-start.9 = (bf16[80,1280]{1,0:T(8,128)(2,1)S(1)}, bf16[80,1280]{1,0:T(8,128)(2,1)S(1)}, u32[]{:S(2)}, u32[]{:S(2)}) collective-permute-start(bf16[80,1280]{1,0:T(8,128)(2,1)S(1)} %shard_map.99.refs_0_), channel_id=1, source_target_pairs={{0,24},{8,16},{16,8},{24,0},{1,25},{9,17},{17,9},{25,1},{2,26},{10... | collective-permute-start | bytes 614408 | tf_op jit(solution)/shard_map/ppermute | solution.py:47
  24.3 1.4 %collective-permute-start.8 = (bf16[80,1280]{1,0:T(8,128)(2,1)S(1)}, bf16[80,1280]{1,0:T(8,128)(2,1)S(1)}, u32[]{:S(2)}, u32[]{:S(2)}) collective-permute-start(bf16[80,1280]{1,0:T(8,128)(2,1)S(1)} %shard_map.99.refs_0_), channel_id=1, source_target_pairs={{0,16},{8,24},{16,0},{24,8},{1,17},{9,25},{17,1},{25,9},{2,18},{10... | collective-permute-start | bytes 614408 | tf_op jit(solution)/shard_map/ppermute | solution.py:47
  25.7 1.2 %collective-permute-start.7 = (bf16[80,1280]{1,0:T(8,128)(2,1)S(1)}, bf16[80,1280]{1,0:T(8,128)(2,1)S(1)}, u32[]{:S(2)}, u32[]{:S(2)}) collective-permute-start(bf16[80,1280]{1,0:T(8,128)(2,1)S(1)} %shard_map.99.refs_0_), channel_id=1, source_target_pairs={{0,8},{8,0},{16,24},{24,16},{1,9},{9,1},{17,25},{25,17},{2,10},{10... | collective-permute-start | bytes 614408 | tf_op jit(solution)/shard_map/ppermute | solution.py:47
  26.9 0.4 shard_map.100
  27.3 0.0 copy-done.1
  27.3 0.7 %shard_map.98 = (bf16[256,640]{1,0:T(8,128)(2,1)S(1)}, bf16[256,640]{1,0:T(8,128)(2,1)S(1)}, f32[256,640]{1,0:T(8,128)S(1)}, f32[256,640]{1,0:T(8,128)S(1)}) custom-call(bf16[32,1408]{1,0:T(8,128)(2,1)S(1)} %collective-permute-done.4.refs_0_, bf16[32,1408]{1,0:T(8,128)(2,1)S(1)} %collective-permute-done.5.refs_1_, ...), custom_call_target="tpu_custom_call" | custom-call | tf_op jit(solution)/shard_map/pallas_call | solution.py:390
  28.0 0.1 collective-permute-start.10
  28.0 4.3 %collective-permute-done.9.refs_3_ = bf16[80,1280]{1,0:T(8,128)(2,1)S(1)} collective-permute-done((bf16[80,1280]{1,0:T(8,128)(2,1)S(1)}, bf16[80,1280]{1,0:T(8,128)(2,1)S(1)}, u32[]{:S(2)}, u32[]{:S(2)}) %collective-permute-start.9) | collective-permute-done | bytes 204832 | tf_op jit(solution)/shard_map/ppermute | solution.py:47
  32.3 2.3 %collective-permute-done.8.refs_2_ = bf16[80,1280]{1,0:T(8,128)(2,1)S(1)} collective-permute-done((bf16[80,1280]{1,0:T(8,128)(2,1)S(1)}, bf16[80,1280]{1,0:T(8,128)(2,1)S(1)}, u32[]{:S(2)}, u32[]{:S(2)}) %collective-permute-start.8) | collective-permute-done | bytes 204832 | tf_op jit(solution)/shard_map/ppermute | solution.py:47
  34.6 0.0 collective-permute-done.7.refs_1_
  34.6 0.0 collective-permute-start.11
  34.6 0.5 collective-permute-start.12
  35.1 0.0 collective-permute-start.13
  35.1 0.0 collective-permute-done.10.refs_4_
  35.1 0.9 %collective-permute-done.11.refs_5_ = bf16[80,1280]{1,0:T(8,128)(2,1)S(1)} collective-permute-done((bf16[80,1280]{1,0:T(8,128)(2,1)S(1)}, bf16[80,1280]{1,0:T(8,128)(2,1)S(1)}, u32[]{:S(2)}, u32[]{:S(2)}) %collective-permute-start.11) | collective-permute-done | bytes 204832 | tf_op jit(solution)/shard_map/ppermute | solution.py:47
  36.1 0.3 collective-permute-done.12.refs_6_
  36.3 0.3 collective-permute-done.13.refs_7_
  36.6 0.0 copy-done
  36.6 1.2 %shard_map.101 = (bf16[128,640]{1,0:T(8,128)(2,1)S(1)}, bf16[128,640]{1,0:T(8,128)(2,1)S(1)}) custom-call(bf16[256,640]{1,0:T(8,128)(2,1)S(1)} %get-tuple-element.40.pick, f32[256,640]{1,0:T(8,128)S(1)} %get-tuple-element.41.rest, bf16[1280,640]{1,0:T(8,128)(2,1)S(1)} %copy-done, bf16[80,1280]{1,0:T(8,128)(2,1)S(1)} %shard_map.99.refs_0_, ...), custom_call_target="tpu_custom_call" | custom-call | tf_op jit(solution)/shard_map/pallas_call | solution.py:412
  37.8 0.1 collective-permute-start.15
  37.9 1.1 %collective-permute-start.14 = (bf16[128,640]{1,0:T(8,128)(2,1)S(1)}, bf16[128,640]{1,0:T(8,128)(2,1)S(1)}, u32[]{:S(2)}, u32[]{:S(2)}) collective-permute-start(bf16[128,640]{1,0:T(8,128)(2,1)S(1)} %get-tuple-element.47), channel_id=1, source_target_pairs={{0,6},{2,4},{4,2},{6,0},{1,7},{3,5},{5,3},{7,1},{8,14},{10,12},{12... | collective-permute-start | bytes 491528 | tf_op jit(solution)/shard_map/ppermute | solution.py:47
  39.1 1.2 %shard_map.102 = (f32[128,640]{1,0:T(8,128)S(1)}, bf16[128,640]{1,0:T(8,128)(2,1)S(1)}) custom-call(bf16[256,640]{1,0:T(8,128)(2,1)S(1)} %get-tuple-element.48.pick, f32[256,640]{1,0:T(8,128)S(1)} %get-tuple-element.49.rest, bf16[1280,640]{1,0:T(8,128)(2,1)S(1)} %copy-done, bf16[80,1280]{1,0:T(8,128)(2,1)S(1)} %shard_map.99.refs_0_, ...), custom_call_target="tpu_custom_call" | custom-call | tf_op jit(solution)/shard_map/pallas_call | solution.py:412
  40.3 2.4 %collective-permute-start.16 = (bf16[128,640]{1,0:T(8,128)(2,1)S(1)}, bf16[128,640]{1,0:T(8,128)(2,1)S(1)}, u32[]{:S(2)}, u32[]{:S(2)}) collective-permute-start(bf16[128,640]{1,0:T(8,128)(2,1)S(1)} %get-tuple-element.51), channel_id=1, source_target_pairs={{0,2},{2,0},{4,6},{6,4},{1,3},{3,1},{5,7},{7,5},{8,10},{10,8},{12,... | collective-permute-start | bytes 491528 | tf_op jit(solution)/shard_map/ppermute | solution.py:47
  42.7 0.5 convert_bitcast_fusion
  43.2 10.2 %collective-permute-done.16 = bf16[128,640]{1,0:T(8,128)(2,1)S(1)} collective-permute-done((bf16[128,640]{1,0:T(8,128)(2,1)S(1)}, bf16[128,640]{1,0:T(8,128)(2,1)S(1)}, u32[]{:S(2)}, u32[]{:S(2)}) %collective-permute-start.16) | collective-permute-done | bytes 163872 | tf_op jit(solution)/shard_map/ppermute | solution.py:47
  53.4 0.0 collective-permute-done.15
  53.4 0.0 collective-permute-done.14
  53.4 0.7 %add_convert_fusion = bf16[128,640]{1,0:T(8,128)(2,1)} fusion(bf16[128,640]{1,0:T(8,128)(2,1)S(1)} %collective-permute-done.16, bf16[128,640]{1,0:T(8,128)(2,1)S(1)} %collective-permute-done.15, f32[128,640]{1,0:T(8,128)S(1)} %get-tuple-element.50, bf16[128,640]{1,0:T(8,128)(2,1)S(1)} %collective-permute-done.14), kind=kLoop, calls=%fused_computation | loop fusion | flops 573440 | bytes 983040 | tf_op jit(solution)/shard_map/convert_element_type | solution.py:426
Async XLA Ops:
  0.6 26.7 %copy-start.1 = (bf16[256,640]{1,0:T(8,128)(2,1)S(1)}, bf16[256,640]{1,0:T(8,128)(2,1)}, u32[]{:S(2)}) copy-start(bf16[256,640]{1,0:T(8,128)(2,1)} %refs_4_.1) | copy-start | bytes 983044
  0.6 36.0 %copy-start = (bf16[1280,640]{1,0:T(8,128)(2,1)S(1)}, bf16[1280,640]{1,0:T(8,128)(2,1)}, u32[]{:S(2)}) copy-start(bf16[1280,640]{1,0:T(8,128)(2,1)} %projection.3) | copy-start | bytes 4915204
  0.7 2.0 %collective-permute-start = (bf16[256,640]{1,0:T(8,128)(2,1)}, bf16[256,640]{1,0:T(8,128)(2,1)S(1)}, u32[]{:S(2)}, u32[]{:S(2)}) collective-permute-start(bf16[256,640]{1,0:T(8,128)(2,1)} %refs_4_.1), channel_id=1, source_target_pairs={{0,1},{1,0},{2,3},{3,2},{4,5},{5,4},{6,7},{7,6},{8,9},{9,8},{10,11... | collective-permute-start | bytes 983048 | tf_op jit(solution)/shard_map/ppermute | solution.py:47
  2.9 5.7 %collective-permute-start.1 = (bf16[32,1280]{1,0:T(8,128)(2,1)S(1)}, bf16[32,1280]{1,0:T(8,128)(2,1)S(1)}, u32[]{:S(2)}, u32[]{:S(2)}) collective-permute-start(bf16[32,1280]{1,0:T(8,128)(2,1)S(1)} %get-tuple-element.32), channel_id=1, source_target_pairs={{0,8},{8,0},{16,24},{24,16},{1,9},{9,1},{17,25},{25,17},{2,10},{10... | collective-permute-start | bytes 245768 | tf_op jit(solution)/shard_map/ppermute | solution.py:47
  5.8 5.3 %collective-permute-start.2 = (bf16[32,1280]{1,0:T(8,128)(2,1)S(1)}, bf16[32,1280]{1,0:T(8,128)(2,1)S(1)}, u32[]{:S(2)}, u32[]{:S(2)}) collective-permute-start(bf16[32,1280]{1,0:T(8,128)(2,1)S(1)} %get-tuple-element.33), channel_id=1, source_target_pairs={{0,16},{8,24},{16,0},{24,8},{1,17},{9,25},{17,1},{25,9},{2,18},{10... | collective-permute-start | bytes 245768 | tf_op jit(solution)/shard_map/ppermute | solution.py:47
  7.3 5.3 %collective-permute-start.3 = (bf16[32,1280]{1,0:T(8,128)(2,1)S(1)}, bf16[32,1280]{1,0:T(8,128)(2,1)S(1)}, u32[]{:S(2)}, u32[]{:S(2)}) collective-permute-start(bf16[32,1280]{1,0:T(8,128)(2,1)S(1)} %get-tuple-element.34), channel_id=1, source_target_pairs={{0,24},{8,16},{16,8},{24,0},{1,25},{9,17},{17,9},{25,1},{2,26},{10... | collective-permute-start | bytes 245768 | tf_op jit(solution)/shard_map/ppermute | solution.py:47
  12.9 6.4 %collective-permute-start.4 = (bf16[32,1408]{1,0:T(8,128)(2,1)S(1)}, bf16[32,1408]{1,0:T(8,128)(2,1)S(1)}, u32[]{:S(2)}, u32[]{:S(2)}) collective-permute-start(bf16[32,1408]{1,0:T(8,128)(2,1)S(1)} %get-tuple-element.35), channel_id=1, source_target_pairs={{0,6},{2,4},{4,2},{6,0},{1,7},{3,5},{5,3},{7,1},{8,14},{10,12},{12... | collective-permute-start | bytes 270344 | tf_op jit(solution)/shard_map/ppermute | solution.py:47
  16.5 6.4 %collective-permute-start.5 = (bf16[32,1408]{1,0:T(8,128)(2,1)S(1)}, bf16[32,1408]{1,0:T(8,128)(2,1)S(1)}, u32[]{:S(2)}, u32[]{:S(2)}) collective-permute-start(bf16[32,1408]{1,0:T(8,128)(2,1)S(1)} %get-tuple-element.36), channel_id=1, source_target_pairs={{0,4},{2,6},{4,0},{6,2},{1,5},{3,7},{5,1},{7,3},{8,12},{10,14},{12... | collective-permute-start | bytes 270344 | tf_op jit(solution)/shard_map/ppermute | solution.py:47
  16.5 6.4 %collective-permute-start.6 = (bf16[32,1408]{1,0:T(8,128)(2,1)S(1)}, bf16[32,1408]{1,0:T(8,128)(2,1)S(1)}, u32[]{:S(2)}, u32[]{:S(2)}) collective-permute-start(bf16[32,1408]{1,0:T(8,128)(2,1)S(1)} %get-tuple-element.37), channel_id=1, source_target_pairs={{0,2},{2,0},{4,6},{6,4},{1,3},{3,1},{5,7},{7,5},{8,10},{10,8},{12,... | collective-permute-start | bytes 270344 | tf_op jit(solution)/shard_map/ppermute | solution.py:47
  23.3 9.0 %collective-permute-start.9 = (bf16[80,1280]{1,0:T(8,128)(2,1)S(1)}, bf16[80,1280]{1,0:T(8,128)(2,1)S(1)}, u32[]{:S(2)}, u32[]{:S(2)}) collective-permute-start(bf16[80,1280]{1,0:T(8,128)(2,1)S(1)} %shard_map.99.refs_0_), channel_id=1, source_target_pairs={{0,24},{8,16},{16,8},{24,0},{1,25},{9,17},{17,9},{25,1},{2,26},{10... | collective-permute-start | bytes 614408 | tf_op jit(solution)/shard_map/ppermute | solution.py:47
  24.3 10.3 %collective-permute-start.8 = (bf16[80,1280]{1,0:T(8,128)(2,1)S(1)}, bf16[80,1280]{1,0:T(8,128)(2,1)S(1)}, u32[]{:S(2)}, u32[]{:S(2)}) collective-permute-start(bf16[80,1280]{1,0:T(8,128)(2,1)S(1)} %shard_map.99.refs_0_), channel_id=1, source_target_pairs={{0,16},{8,24},{16,0},{24,8},{1,17},{9,25},{17,1},{25,9},{2,18},{10... | collective-permute-start | bytes 614408 | tf_op jit(solution)/shard_map/ppermute | solution.py:47
  25.7 8.9 %collective-permute-start.7 = (bf16[80,1280]{1,0:T(8,128)(2,1)S(1)}, bf16[80,1280]{1,0:T(8,128)(2,1)S(1)}, u32[]{:S(2)}, u32[]{:S(2)}) collective-permute-start(bf16[80,1280]{1,0:T(8,128)(2,1)S(1)} %shard_map.99.refs_0_), channel_id=1, source_target_pairs={{0,8},{8,0},{16,24},{24,16},{1,9},{9,1},{17,25},{25,17},{2,10},{10... | collective-permute-start | bytes 614408 | tf_op jit(solution)/shard_map/ppermute | solution.py:47
  28.0 7.2 %collective-permute-start.10 = (bf16[80,1280]{1,0:T(8,128)(2,1)S(1)}, bf16[80,1280]{1,0:T(8,128)(2,1)S(1)}, u32[]{:S(2)}, u32[]{:S(2)}) collective-permute-start(bf16[80,1280]{1,0:T(8,128)(2,1)S(1)} %shard_map.99.refs_0_), channel_id=1, source_target_pairs={{0,1},{1,0},{2,3},{3,2},{4,5},{5,4},{6,7},{7,6},{8,9},{9,8},{10,11... | collective-permute-start | bytes 614408 | tf_op jit(solution)/shard_map/ppermute | solution.py:47
  34.6 1.5 %collective-permute-start.11 = (bf16[80,1280]{1,0:T(8,128)(2,1)S(1)}, bf16[80,1280]{1,0:T(8,128)(2,1)S(1)}, u32[]{:S(2)}, u32[]{:S(2)}) collective-permute-start(bf16[80,1280]{1,0:T(8,128)(2,1)S(1)} %collective-permute-done.7.refs_1_), channel_id=1, source_target_pairs={{0,1},{1,0},{2,3},{3,2},{4,5},{5,4},{6,7},{7,6},{8,9},{9,8},{10,11... | collective-permute-start | bytes 614408 | tf_op jit(solution)/shard_map/ppermute | solution.py:47
  34.6 1.7 %collective-permute-start.12 = (bf16[80,1280]{1,0:T(8,128)(2,1)S(1)}, bf16[80,1280]{1,0:T(8,128)(2,1)S(1)}, u32[]{:S(2)}, u32[]{:S(2)}) collective-permute-start(bf16[80,1280]{1,0:T(8,128)(2,1)S(1)} %collective-permute-done.8.refs_2_), channel_id=1, source_target_pairs={{0,1},{1,0},{2,3},{3,2},{4,5},{5,4},{6,7},{7,6},{8,9},{9,8},{10,11... | collective-permute-start | bytes 614408 | tf_op jit(solution)/shard_map/ppermute | solution.py:47
  35.1 1.5 %collective-permute-start.13 = (bf16[80,1280]{1,0:T(8,128)(2,1)S(1)}, bf16[80,1280]{1,0:T(8,128)(2,1)S(1)}, u32[]{:S(2)}, u32[]{:S(2)}) collective-permute-start(bf16[80,1280]{1,0:T(8,128)(2,1)S(1)} %collective-permute-done.9.refs_3_), channel_id=1, source_target_pairs={{0,1},{1,0},{2,3},{3,2},{4,5},{5,4},{6,7},{7,6},{8,9},{9,8},{10,11... | collective-permute-start | bytes 614408 | tf_op jit(solution)/shard_map/ppermute | solution.py:47
  37.8 15.5 %collective-permute-start.15 = (bf16[128,640]{1,0:T(8,128)(2,1)S(1)}, bf16[128,640]{1,0:T(8,128)(2,1)S(1)}, u32[]{:S(2)}, u32[]{:S(2)}) collective-permute-start(bf16[128,640]{1,0:T(8,128)(2,1)S(1)} %get-tuple-element.46), channel_id=1, source_target_pairs={{0,4},{2,6},{4,0},{6,2},{1,5},{3,7},{5,1},{7,3},{8,12},{10,14},{12... | collective-permute-start | bytes 491528 | tf_op jit(solution)/shard_map/ppermute | solution.py:47
  37.9 15.5 %collective-permute-start.14 = (bf16[128,640]{1,0:T(8,128)(2,1)S(1)}, bf16[128,640]{1,0:T(8,128)(2,1)S(1)}, u32[]{:S(2)}, u32[]{:S(2)}) collective-permute-start(bf16[128,640]{1,0:T(8,128)(2,1)S(1)} %get-tuple-element.47), channel_id=1, source_target_pairs={{0,6},{2,4},{4,2},{6,0},{1,7},{3,5},{5,3},{7,1},{8,14},{10,12},{12... | collective-permute-start | bytes 491528 | tf_op jit(solution)/shard_map/ppermute | solution.py:47
  40.3 13.1 %collective-permute-start.16 = (bf16[128,640]{1,0:T(8,128)(2,1)S(1)}, bf16[128,640]{1,0:T(8,128)(2,1)S(1)}, u32[]{:S(2)}, u32[]{:S(2)}) collective-permute-start(bf16[128,640]{1,0:T(8,128)(2,1)S(1)} %get-tuple-element.51), channel_id=1, source_target_pairs={{0,2},{2,0},{4,6},{6,4},{1,3},{3,1},{5,7},{7,5},{8,10},{10,8},{12,... | collective-permute-start | bytes 491528 | tf_op jit(solution)/shard_map/ppermute | solution.py:47

commit v5 on v4

--- a/solution.py
+++ b/solution.py
@@ -210,7 +210,7 @@
         out[:, j * LANES : (j + 1) * LANES] = (iota(column.shape, 1) + j * LANES == column).astype(BF16)
 
 
-def index_kernel(n, n_class, n_resp, tok, row, listed, *refs):
+def index_kernel(n, n_class, n_resp, tok, row, step, *refs):
     moved, hidden = refs[n - 1 :: -1], refs[n]
     pick_far, pick_near, rest_far, rest_near, counts, lens, own = refs[n + 1 :]
     a = lax.axis_index("sec")
@@ -239,7 +239,7 @@
         index = packed - start
         c = mod(index, n_class)
         place = list_place(counts, n, n_class, tok, s, c, seq_of, div(index, n_class), packed)
-        column = ((mod(c, n_tp) ^ t) * n + (div(c, n_tp) ^ a)) * listed + place
+        column = ((mod(c, n_tp) ^ t) * n + (div(c, n_tp) ^ a)) * step + place
         one_hot(upright(column), pick)
         source, ends = index, 0
         for r in range(n_resp):
@@ -251,14 +251,37 @@
 
 def mix_kernel(n_lists, pick, rest, projection, *refs):
     pieces, outs, held = refs[:n_lists], refs[n_lists:-1], refs[-1]
-    listed = pieces[0].shape[0]
+    listed, step = pieces[0].shape[0], held.shape[0] // n_lists
     for k, piece in enumerate(pieces):
-        held[k * listed : (k + 1) * listed, :] = piece[...]
+        rows = piece[...].astype(F32)
+        if step > listed:
+            rows = jnp.concatenate([rows, jnp.zeros((step - listed, rows.shape[1]), F32)], axis=0)
+        held[k * step : (k + 1) * step, :] = rows.astype(BF16)
     tokens = jnp.dot(pick[...], held[...], preferred_element_type=F32).astype(BF16)
     total = jnp.dot(tokens, projection[...], preferred_element_type=F32) + rest[...]
-    tok = outs[0].shape[0]
-    for m, out in enumerate(outs):
-        out[...] = total[m * tok : (m + 1) * tok].astype(out.dtype)
+    first = 0
+    for out in outs:
+        out[...] = total[first : first + out.shape[0]].astype(out.dtype)
+        first += out.shape[0]
+
+
+def join_kernel(own, other, out):
+    out[...] = (own[...] + other[...].astype(F32)).astype(out.dtype)
+
+
+def final_kernel(n_whole, n_first, *refs):
+    own, parts, out = refs[0], refs[1:-1], refs[-1]
+    half = out.shape[0] // 2
+    total = own[...]
+    for part in parts[:n_whole]:
+        total = total + part[...].astype(F32)
+    first, second = total[0:half], total[half:]
+    for part in parts[n_whole : n_whole + n_first]:
+        first = first + part[...].astype(F32)
+    for part in parts[n_whole + n_first :]:
+        second = second + part[...].astype(F32)
+    out[0:half] = first.astype(out.dtype)
+    out[half:] = second.astype(out.dtype)
 
 
 def terms_kernel(n, n_resp, row, *refs):
@@ -329,7 +352,9 @@
     row = rows // LANES
     tok = TOK_DEV
     tokens = tok * n
-    listed = -(-((tokens + (n_class - 1) * n) // n_class) // 16) * 16
+    up = lambda x, m: -(-x // m) * m
+    listed = up((tokens + (n_class - 1) * n) // n_class, 8)
+    step = up(listed, 16)
     shape = jax.ShapeDtypeStruct
     info_like = shape((slots, width + LANES), BF16)
 
@@ -388,10 +413,10 @@
     )(*moved[::-1])
     half = n // 2 * tok
     pick_far, pick_near, rest_far, rest_near = call(
-        functools.partial(index_kernel, n, n_class, n_resp, tok, row, listed),
+        functools.partial(index_kernel, n, n_class, n_resp, tok, row, step),
         [
-            shape((half, n_class * listed), BF16),
-            shape((half, n_class * listed), BF16),
+            shape((half, n_class * step), BF16),
+            shape((half, n_class * step), BF16),
             shape((half, cols), F32),
             shape((half, cols), F32),
         ],
@@ -409,21 +434,38 @@
     after = lambda x, *ys: lax.optimization_barrier((x, *ys))[0]
     same = [mine] + [swap(mine, "sec", k) for k in range(1, n)]
     lists = same + [swap(after(x, pick_far, terms), "tp", 1) for x in same]
-    mix = lambda pick, rest, kind: call(
+    mix = lambda pick, rest, outs: call(
         functools.partial(mix_kernel, n_class),
-        [shape((tok, cols), kind)] + [shape((tok, cols), BF16)] * (n // 2 - 1),
+        outs,
         [VMEM] * (n_class + 3),
-        [VMEM] * (n // 2),
-        [pltpu.VMEM((n_class * listed, width), BF16)],
+        [VMEM] * len(outs),
+        [pltpu.VMEM((n_class * step, width), BF16)],
     )(pick, rest, projection, *lists)
-    far = mix(pick_far, rest_far, BF16)
-    near = mix(after(pick_near, *far), rest_near, F32)
-    partial = [*near, *far]
-    arrived = [swap(partial[m], "seq", m) for m in range(n - 1, 0, -1)]
-    states = partial[0]
-    for part in arrived:
-        states = states + part.astype(F32)
-    return states.astype(BF16), terms.astype(BF16).T
+    part = tok // 2
+    joined = n // 2
+    far = mix(
+        pick_far,
+        rest_far,
+        [shape((part, cols), F32 if m % 2 and h else BF16) for m in range(joined) for h in range(2)],
+    )
+    helped = [swap(far[2 * m + 1], "seq", 1) for m in range(0, joined, 2)]
+    direct = [swap(far[2 * m], "seq", joined + m) for m in range(joined - 1, -1, -1)]
+    sums = [
+        call(join_kernel, shape((part, cols), BF16), [VMEM] * 2, VMEM)(far[2 * m + 3], got)
+        for m, got in zip(range(0, joined, 2), helped, strict=True)
+    ]
+    passed = [swap(x, "seq", joined + m + 1) for m, x in zip(range(0, joined, 2), sums, strict=True)]
+    near = mix(
+        after(pick_near, *far), rest_near, [shape((tok, cols), F32)] + [shape((tok, cols), BF16)] * (joined - 1)
+    )
+    whole = [swap(near[m], "seq", m) for m in range(1, joined)]
+    states = call(
+        functools.partial(final_kernel, len(whole), len(direct)),
+        shape((tok, cols), BF16),
+        [VMEM] * (1 + len(whole) + len(direct) + len(passed)),
+        VMEM,
+    )(near[0], *whole, *direct, *passed)
+    return states, terms.astype(BF16).T
 
 
 def refine(input_rows, projection, norm_gain):

time: 54.3 us -> 52.3 us (0.963)
  waiting for transfers between devices: 29.4 us -> 25.9 us
  starting transfers between devices: 17.2 us -> 18.7 us
  Pallas kernels: 5.56 us -> 6.31 us
  other arithmetic: 1.25 us -> 0.51 us
    ppermute x17 -> x19, waiting for transfers between devices: 29.4 us -> 25.9 us  [swap(): return lax.ppermute(x, axis, [(i, i ^ k) for i in range(n)])]
    ppermute x17 -> x19, starting transfers between devices: 17.2 us -> 18.7 us  [swap(): return lax.ppermute(x, axis, [(i, i ^ k) for i in range(n)])]
    pallas_call x3 -> x5, Pallas kernels: 3.04 us -> 3.79 us  [the longest x2 2.39 us: shards_in_place(): call(functools.partial(mix_kernel, n_class), outs, [VMEM] * (n_class + 3)...]
    convert_element_type x1 -> x0, other arithmetic: 0.74 us -> none  [shards_in_place(): return (states.astype(BF16), terms.astype(BF16).T)]
  transfers between devices with their start and end apart: 17 -> 19, of which waited for: 12 -> 14; matrix products, arithmetic and copies ran while one was open for 1% -> 1% of each run, Pallas kernels for 7% -> 7%
where the time goes in v5:
time: 52.3 us; the launch traced here: 52.1 us
  waiting for transfers between devices  25.9 us (50%)
  starting transfers between devices  18.7 us (36%)
  Pallas kernels  6.31 us (12%)
  between operations  0.75 us (1%)
    ppermute x19, waiting for transfers between devices, swap(): return lax.ppermute(x, axis, [(i, i ^ k) for i in range(n)])  25.9 us
    ppermute x19, starting transfers between devices, swap(): return lax.ppermute(x, axis, [(i, i ^ k) for i in range(n)])  18.7 us
    pallas_call x2, Pallas kernels, shards_in_place(): call(functools.partial(mix_kernel, n_class), outs, [VMEM] * (n_class + 3)...  2.39 us
    pallas_call x1, Pallas kernels, shards_in_place(): call(functools.partial(early_kernel, n, n_tp), [shape((rows // n_tp, rows...  1.32 us
  transfers between devices with their start and end apart: 19, of which 14 were waited for; matrix products, arithmetic and copies ran while one was open for 1% of the time, Pallas kernels for 7%

profile of v5, /device:TPU:0, one launch (start us, length us, event | category | flops | bytes accessed | tf_op | source)
XLA Modules:
  0.0 52.1 jit_solution(8538248213559051065)
XLA Ops:
  0.7 0.5 collective-permute-start
  1.2 1.3 %shard_map.95 = (bf16[128,256]{1,0:T(8,128)(2,1)S(1)}, bf16[128,640]{1,0:T(8,128)(2,1)S(1)}, bf16[16,128]{1,0:T(8,128)(2,1)S(1)}, f32[1,5120]{1,0:T(1,128)S(1)}) custom-call(bf16[256,640]{1,0:T(8,128)(2,1)} %refs_4_.1, s32[4]{0:T(128)} %lengths.1, s32[4]{0:T(128)} %group_of.1, s32[4]{0:T(128)} %rewards.1, f32[2,128]{1,0:T(2,128)} %bitcast.6, ...), custom_call_target="tpu_custom_call" | custom-call | tf_op jit(solution)/shard_map/pallas_call | solution.py:362
  2.5 0.1 collective-permute-done.sibling
  2.6 0.2 shard_map.96
  2.9 2.9 %collective-permute-start.1 = (bf16[32,1280]{1,0:T(8,128)(2,1)S(1)}, bf16[32,1280]{1,0:T(8,128)(2,1)S(1)}, u32[]{:S(2)}, u32[]{:S(2)}) collective-permute-start(bf16[32,1280]{1,0:T(8,128)(2,1)S(1)} %get-tuple-element.34), channel_id=1, source_target_pairs={{0,8},{8,0},{16,24},{24,16},{1,9},{9,1},{17,25},{25,17},{2,10},{10... | collective-permute-start | bytes 245768 | tf_op jit(solution)/shard_map/ppermute | solution.py:47
  5.8 1.5 %collective-permute-start.2 = (bf16[32,1280]{1,0:T(8,128)(2,1)S(1)}, bf16[32,1280]{1,0:T(8,128)(2,1)S(1)}, u32[]{:S(2)}, u32[]{:S(2)}) collective-permute-start(bf16[32,1280]{1,0:T(8,128)(2,1)S(1)} %get-tuple-element.35), channel_id=1, source_target_pairs={{0,16},{8,24},{16,0},{24,8},{1,17},{9,25},{17,1},{25,9},{2,18},{10... | collective-permute-start | bytes 245768 | tf_op jit(solution)/shard_map/ppermute | solution.py:47
  7.3 0.0 collective-permute-start.3
  7.3 1.2 %collective-permute-done.1.refs_1_ = bf16[32,1280]{1,0:T(8,128)(2,1)S(1)} collective-permute-done((bf16[32,1280]{1,0:T(8,128)(2,1)S(1)}, bf16[32,1280]{1,0:T(8,128)(2,1)S(1)}, u32[]{:S(2)}, u32[]{:S(2)}) %collective-permute-start.1) | collective-permute-done | bytes 81952 | tf_op jit(solution)/shard_map/ppermute | solution.py:47
  8.5 2.5 %collective-permute-done.2.refs_2_ = bf16[32,1280]{1,0:T(8,128)(2,1)S(1)} collective-permute-done((bf16[32,1280]{1,0:T(8,128)(2,1)S(1)}, bf16[32,1280]{1,0:T(8,128)(2,1)S(1)}, u32[]{:S(2)}, u32[]{:S(2)}) %collective-permute-start.2) | collective-permute-done | bytes 81952 | tf_op jit(solution)/shard_map/ppermute | solution.py:47
  11.1 1.6 %collective-permute-done.3.refs_3_ = bf16[32,1280]{1,0:T(8,128)(2,1)S(1)} collective-permute-done((bf16[32,1280]{1,0:T(8,128)(2,1)S(1)}, bf16[32,1280]{1,0:T(8,128)(2,1)S(1)}, u32[]{:S(2)}, u32[]{:S(2)}) %collective-permute-start.3) | collective-permute-done | bytes 81952 | tf_op jit(solution)/shard_map/ppermute | solution.py:47
  12.6 0.2 shard_map.97
  12.9 3.7 %collective-permute-start.4 = (bf16[32,1408]{1,0:T(8,128)(2,1)S(1)}, bf16[32,1408]{1,0:T(8,128)(2,1)S(1)}, u32[]{:S(2)}, u32[]{:S(2)}) collective-permute-start(bf16[32,1408]{1,0:T(8,128)(2,1)S(1)} %get-tuple-element.37), channel_id=1, source_target_pairs={{0,6},{2,4},{4,2},{6,0},{1,7},{3,5},{5,3},{7,1},{8,14},{10,12},{12... | collective-permute-start | bytes 270344 | tf_op jit(solution)/shard_map/ppermute | solution.py:47
  16.5 0.0 collective-permute-start.5
  16.5 0.8 %collective-permute-start.6 = (bf16[32,1408]{1,0:T(8,128)(2,1)S(1)}, bf16[32,1408]{1,0:T(8,128)(2,1)S(1)}, u32[]{:S(2)}, u32[]{:S(2)}) collective-permute-start(bf16[32,1408]{1,0:T(8,128)(2,1)S(1)} %get-tuple-element.39), channel_id=1, source_target_pairs={{0,2},{2,0},{4,6},{6,4},{1,3},{3,1},{5,7},{7,5},{8,10},{10,8},{12,... | collective-permute-start | bytes 270344 | tf_op jit(solution)/shard_map/ppermute | solution.py:47
  17.3 1.9 %collective-permute-done.4.refs_0_ = bf16[32,1408]{1,0:T(8,128)(2,1)S(1)} collective-permute-done((bf16[32,1408]{1,0:T(8,128)(2,1)S(1)}, bf16[32,1408]{1,0:T(8,128)(2,1)S(1)}, u32[]{:S(2)}, u32[]{:S(2)}) %collective-permute-start.4) | collective-permute-done | bytes 90144 | tf_op jit(solution)/shard_map/ppermute | solution.py:47
  19.3 3.7 %collective-permute-done.5.refs_1_ = bf16[32,1408]{1,0:T(8,128)(2,1)S(1)} collective-permute-done((bf16[32,1408]{1,0:T(8,128)(2,1)S(1)}, bf16[32,1408]{1,0:T(8,128)(2,1)S(1)}, u32[]{:S(2)}, u32[]{:S(2)}) %collective-permute-start.5) | collective-permute-done | bytes 90144 | tf_op jit(solution)/shard_map/ppermute | solution.py:47
  23.0 0.0 collective-permute-done.6.refs_2_
  23.0 0.4 shard_map.99.refs_0_
  23.3 0.9 %collective-permute-start.9 = (bf16[72,1280]{1,0:T(8,128)(2,1)S(1)}, bf16[72,1280]{1,0:T(8,128)(2,1)S(1)}, u32[]{:S(2)}, u32[]{:S(2)}) collective-permute-start(bf16[72,1280]{1,0:T(8,128)(2,1)S(1)} %shard_map.99.refs_0_), channel_id=1, source_target_pairs={{0,24},{8,16},{16,8},{24,0},{1,25},{9,17},{17,9},{25,1},{2,26},{10... | collective-permute-start | bytes 552968 | tf_op jit(solution)/shard_map/ppermute | solution.py:47
  24.3 1.4 %collective-permute-start.8 = (bf16[72,1280]{1,0:T(8,128)(2,1)S(1)}, bf16[72,1280]{1,0:T(8,128)(2,1)S(1)}, u32[]{:S(2)}, u32[]{:S(2)}) collective-permute-start(bf16[72,1280]{1,0:T(8,128)(2,1)S(1)} %shard_map.99.refs_0_), channel_id=1, source_target_pairs={{0,16},{8,24},{16,0},{24,8},{1,17},{9,25},{17,1},{25,9},{2,18},{10... | collective-permute-start | bytes 552968 | tf_op jit(solution)/shard_map/ppermute | solution.py:47
  25.7 1.2 %collective-permute-start.7 = (bf16[72,1280]{1,0:T(8,128)(2,1)S(1)}, bf16[72,1280]{1,0:T(8,128)(2,1)S(1)}, u32[]{:S(2)}, u32[]{:S(2)}) collective-permute-start(bf16[72,1280]{1,0:T(8,128)(2,1)S(1)} %shard_map.99.refs_0_), channel_id=1, source_target_pairs={{0,8},{8,0},{16,24},{24,16},{1,9},{9,1},{17,25},{25,17},{2,10},{10... | collective-permute-start | bytes 552968 | tf_op jit(solution)/shard_map/ppermute | solution.py:47
  26.9 0.4 shard_map.100
  27.3 0.6 %shard_map.98 = (bf16[256,640]{1,0:T(8,128)(2,1)S(1)}, bf16[256,640]{1,0:T(8,128)(2,1)S(1)}, f32[256,640]{1,0:T(8,128)S(1)}, f32[256,640]{1,0:T(8,128)S(1)}) custom-call(bf16[32,1408]{1,0:T(8,128)(2,1)S(1)} %collective-permute-done.4.refs_0_, bf16[32,1408]{1,0:T(8,128)(2,1)S(1)} %collective-permute-done.5.refs_1_, ...), custom_call_target="tpu_custom_call" | custom-call | tf_op jit(solution)/shard_map/pallas_call | solution.py:415
  27.9 0.1 collective-permute-start.10
  28.0 3.9 %collective-permute-done.9.refs_3_ = bf16[72,1280]{1,0:T(8,128)(2,1)S(1)} collective-permute-done((bf16[72,1280]{1,0:T(8,128)(2,1)S(1)}, bf16[72,1280]{1,0:T(8,128)(2,1)S(1)}, u32[]{:S(2)}, u32[]{:S(2)}) %collective-permute-start.9) | collective-permute-done | bytes 184352 | tf_op jit(solution)/shard_map/ppermute | solution.py:47
  31.9 1.8 %collective-permute-done.8.refs_2_ = bf16[72,1280]{1,0:T(8,128)(2,1)S(1)} collective-permute-done((bf16[72,1280]{1,0:T(8,128)(2,1)S(1)}, bf16[72,1280]{1,0:T(8,128)(2,1)S(1)}, u32[]{:S(2)}, u32[]{:S(2)}) %collective-permute-start.8) | collective-permute-done | bytes 184352 | tf_op jit(solution)/shard_map/ppermute | solution.py:47
  33.7 0.0 collective-permute-done.7.refs_1_
  33.7 0.0 collective-permute-start.11
  33.7 0.5 collective-permute-start.12
  34.2 0.0 collective-permute-start.13
  34.2 0.0 collective-permute-done.10.refs_4_
  34.2 0.9 %collective-permute-done.11.refs_5_ = bf16[72,1280]{1,0:T(8,128)(2,1)S(1)} collective-permute-done((bf16[72,1280]{1,0:T(8,128)(2,1)S(1)}, bf16[72,1280]{1,0:T(8,128)(2,1)S(1)}, u32[]{:S(2)}, u32[]{:S(2)}) %collective-permute-start.11) | collective-permute-done | bytes 184352 | tf_op jit(solution)/shard_map/ppermute | solution.py:47
  35.1 0.3 collective-permute-done.12.refs_6_
  35.4 0.3 collective-permute-done.13.refs_7_
  35.7 1.2 %shard_map.101 = (bf16[64,640]{1,0:T(8,128)(2,1)S(1)}, bf16[64,640]{1,0:T(8,128)(2,1)S(1)}, bf16[64,640]{1,0:T(8,128)(2,1)S(1)}, f32[64,640]{1,0:T(8,128)S(1)}) custom-call(bf16[256,640]{1,0:T(8,128)(2,1)S(1)} %get-tuple-element.42.pick, f32[256,640]{1,0:T(8,128)S(1)} %get-tuple-element.43.rest, bf16[1280,640]{1,0:T(8,128)(2,1)S(1)} %copy-done, ...), custom_call_target="tpu_custom_call" | custom-call | tf_op jit(solution)/shard_map/pallas_call | solution.py:437
  36.9 0.1 collective-permute-start.17
  37.0 1.0 %collective-permute-start.16 = (bf16[64,640]{1,0:T(8,128)(2,1)S(1)}, bf16[64,640]{1,0:T(8,128)(2,1)S(1)}, u32[]{:S(2)}, u32[]{:S(2)}) collective-permute-start(bf16[64,640]{1,0:T(8,128)(2,1)S(1)} %get-tuple-element.48), channel_id=1, source_target_pairs={{0,4},{2,6},{4,0},{6,2},{1,5},{3,7},{5,1},{7,3},{8,12},{10,14},{12... | collective-permute-start | bytes 245768 | tf_op jit(solution)/shard_map/ppermute | solution.py:47
  38.0 3.4 %collective-permute-start.15 = (bf16[64,640]{1,0:T(8,128)(2,1)S(1)}, bf16[64,640]{1,0:T(8,128)(2,1)S(1)}, u32[]{:S(2)}, u32[]{:S(2)}) collective-permute-start(bf16[64,640]{1,0:T(8,128)(2,1)S(1)} %get-tuple-element.50), channel_id=1, source_target_pairs={{0,6},{2,4},{4,2},{6,0},{1,7},{3,5},{5,3},{7,1},{8,14},{10,12},{12... | collective-permute-start | bytes 245768 | tf_op jit(solution)/shard_map/ppermute | solution.py:47
  41.3 1.2 %shard_map.102 = (f32[128,640]{1,0:T(8,128)S(1)}, bf16[128,640]{1,0:T(8,128)(2,1)S(1)}) custom-call(bf16[256,640]{1,0:T(8,128)(2,1)S(1)} %get-tuple-element.52.pick, f32[256,640]{1,0:T(8,128)S(1)} %get-tuple-element.53.rest, bf16[1280,640]{1,0:T(8,128)(2,1)S(1)} %copy-done, bf16[72,1280]{1,0:T(8,128)(2,1)S(1)} %shard_map.99.refs_0_, ...), custom_call_target="tpu_custom_call" | custom-call | tf_op jit(solution)/shard_map/pallas_call | solution.py:437
  42.5 0.1 collective-permute-start.14
  42.6 0.1 collective-permute-done.17.other
  42.7 0.6 %collective-permute-start.18 = (bf16[64,640]{1,0:T(8,128)(2,1)S(1)}, bf16[64,640]{1,0:T(8,128)(2,1)S(1)}, u32[]{:S(2)}, u32[]{:S(2)}) collective-permute-start(bf16[64,640]{1,0:T(8,128)(2,1)S(1)} %shard_map.103), channel_id=1, source_target_pairs={{0,6},{2,4},{4,2},{6,0},{1,7},{3,5},{5,3},{7,1},{8,14},{10,12},{12... | collective-permute-start | bytes 245768 | tf_op jit(solution)/shard_map/ppermute | solution.py:47
  43.3 0.5 convert_bitcast_fusion
  43.8 3.0 %collective-permute-done.16.refs_3_ = bf16[64,640]{1,0:T(8,128)(2,1)S(1)} collective-permute-done((bf16[64,640]{1,0:T(8,128)(2,1)S(1)}, bf16[64,640]{1,0:T(8,128)(2,1)S(1)}, u32[]{:S(2)}, u32[]{:S(2)}) %collective-permute-start.16) | collective-permute-done | bytes 81952 | tf_op jit(solution)/shard_map/ppermute | solution.py:47
  46.8 0.0 collective-permute-done.15.refs_2_
  46.8 4.6 %collective-permute-done.14.refs_1_ = bf16[128,640]{1,0:T(8,128)(2,1)S(1)} collective-permute-done((bf16[128,640]{1,0:T(8,128)(2,1)S(1)}, bf16[128,640]{1,0:T(8,128)(2,1)S(1)}, u32[]{:S(2)}, u32[]{:S(2)}) %collective-permute-start.14) | collective-permute-done | bytes 163872 | tf_op jit(solution)/shard_map/ppermute | solution.py:47
  51.4 0.0 collective-permute-done.18.refs_4_
  51.4 0.7 %shard_map.104 = bf16[128,640]{1,0:T(8,128)(2,1)} custom-call(f32[128,640]{1,0:T(8,128)S(1)} %get-tuple-element.54.refs_0_, bf16[128,640]{1,0:T(8,128)(2,1)S(1)} %collective-permute-done.14.refs_1_, bf16[64,640]{1,0:T(8,128)(2,1)S(1)} %collective-permute-done.15.refs_2_, bf16[64,640]{1,0:T(8,128)(2,1)S(1)} %collective-permute-done.16.refs_3_, ...), custom_call_target="tpu_custom_call" | custom-call | tf_op jit(solution)/shard_map/pallas_call | solution.py:462
  (5 shorter events, 0.0 us)
Async XLA Ops:
  0.6 26.7 %copy-start.1 = (bf16[256,640]{1,0:T(8,128)(2,1)S(1)}, bf16[256,640]{1,0:T(8,128)(2,1)}, u32[]{:S(2)}) copy-start(bf16[256,640]{1,0:T(8,128)(2,1)} %refs_4_.1) | copy-start | bytes 983044
  0.6 35.0 %copy-start = (bf16[1280,640]{1,0:T(8,128)(2,1)S(1)}, bf16[1280,640]{1,0:T(8,128)(2,1)}, u32[]{:S(2)}) copy-start(bf16[1280,640]{1,0:T(8,128)(2,1)} %projection.3) | copy-start | bytes 4915204
  0.7 2.0 %collective-permute-start = (bf16[256,640]{1,0:T(8,128)(2,1)}, bf16[256,640]{1,0:T(8,128)(2,1)S(1)}, u32[]{:S(2)}, u32[]{:S(2)}) collective-permute-start(bf16[256,640]{1,0:T(8,128)(2,1)} %refs_4_.1), channel_id=1, source_target_pairs={{0,1},{1,0},{2,3},{3,2},{4,5},{5,4},{6,7},{7,6},{8,9},{9,8},{10,11... | collective-permute-start | bytes 983048 | tf_op jit(solution)/shard_map/ppermute | solution.py:47
  2.9 5.7 %collective-permute-start.1 = (bf16[32,1280]{1,0:T(8,128)(2,1)S(1)}, bf16[32,1280]{1,0:T(8,128)(2,1)S(1)}, u32[]{:S(2)}, u32[]{:S(2)}) collective-permute-start(bf16[32,1280]{1,0:T(8,128)(2,1)S(1)} %get-tuple-element.34), channel_id=1, source_target_pairs={{0,8},{8,0},{16,24},{24,16},{1,9},{9,1},{17,25},{25,17},{2,10},{10... | collective-permute-start | bytes 245768 | tf_op jit(solution)/shard_map/ppermute | solution.py:47
  5.8 5.3 %collective-permute-start.2 = (bf16[32,1280]{1,0:T(8,128)(2,1)S(1)}, bf16[32,1280]{1,0:T(8,128)(2,1)S(1)}, u32[]{:S(2)}, u32[]{:S(2)}) collective-permute-start(bf16[32,1280]{1,0:T(8,128)(2,1)S(1)} %get-tuple-element.35), channel_id=1, source_target_pairs={{0,16},{8,24},{16,0},{24,8},{1,17},{9,25},{17,1},{25,9},{2,18},{10... | collective-permute-start | bytes 245768 | tf_op jit(solution)/shard_map/ppermute | solution.py:47
  7.3 5.3 %collective-permute-start.3 = (bf16[32,1280]{1,0:T(8,128)(2,1)S(1)}, bf16[32,1280]{1,0:T(8,128)(2,1)S(1)}, u32[]{:S(2)}, u32[]{:S(2)}) collective-permute-start(bf16[32,1280]{1,0:T(8,128)(2,1)S(1)} %get-tuple-element.36), channel_id=1, source_target_pairs={{0,24},{8,16},{16,8},{24,0},{1,25},{9,17},{17,9},{25,1},{2,26},{10... | collective-permute-start | bytes 245768 | tf_op jit(solution)/shard_map/ppermute | solution.py:47
  12.9 6.4 %collective-permute-start.4 = (bf16[32,1408]{1,0:T(8,128)(2,1)S(1)}, bf16[32,1408]{1,0:T(8,128)(2,1)S(1)}, u32[]{:S(2)}, u32[]{:S(2)}) collective-permute-start(bf16[32,1408]{1,0:T(8,128)(2,1)S(1)} %get-tuple-element.37), channel_id=1, source_target_pairs={{0,6},{2,4},{4,2},{6,0},{1,7},{3,5},{5,3},{7,1},{8,14},{10,12},{12... | collective-permute-start | bytes 270344 | tf_op jit(solution)/shard_map/ppermute | solution.py:47
  16.5 6.4 %collective-permute-start.5 = (bf16[32,1408]{1,0:T(8,128)(2,1)S(1)}, bf16[32,1408]{1,0:T(8,128)(2,1)S(1)}, u32[]{:S(2)}, u32[]{:S(2)}) collective-permute-start(bf16[32,1408]{1,0:T(8,128)(2,1)S(1)} %get-tuple-element.38), channel_id=1, source_target_pairs={{0,4},{2,6},{4,0},{6,2},{1,5},{3,7},{5,1},{7,3},{8,12},{10,14},{12... | collective-permute-start | bytes 270344 | tf_op jit(solution)/shard_map/ppermute | solution.py:47
  16.5 6.4 %collective-permute-start.6 = (bf16[32,1408]{1,0:T(8,128)(2,1)S(1)}, bf16[32,1408]{1,0:T(8,128)(2,1)S(1)}, u32[]{:S(2)}, u32[]{:S(2)}) collective-permute-start(bf16[32,1408]{1,0:T(8,128)(2,1)S(1)} %get-tuple-element.39), channel_id=1, source_target_pairs={{0,2},{2,0},{4,6},{6,4},{1,3},{3,1},{5,7},{7,5},{8,10},{10,8},{12,... | collective-permute-start | bytes 270344 | tf_op jit(solution)/shard_map/ppermute | solution.py:47
  23.3 8.5 %collective-permute-start.9 = (bf16[72,1280]{1,0:T(8,128)(2,1)S(1)}, bf16[72,1280]{1,0:T(8,128)(2,1)S(1)}, u32[]{:S(2)}, u32[]{:S(2)}) collective-permute-start(bf16[72,1280]{1,0:T(8,128)(2,1)S(1)} %shard_map.99.refs_0_), channel_id=1, source_target_pairs={{0,24},{8,16},{16,8},{24,0},{1,25},{9,17},{17,9},{25,1},{2,26},{10... | collective-permute-start | bytes 552968 | tf_op jit(solution)/shard_map/ppermute | solution.py:47
  24.3 9.4 %collective-permute-start.8 = (bf16[72,1280]{1,0:T(8,128)(2,1)S(1)}, bf16[72,1280]{1,0:T(8,128)(2,1)S(1)}, u32[]{:S(2)}, u32[]{:S(2)}) collective-permute-start(bf16[72,1280]{1,0:T(8,128)(2,1)S(1)} %shard_map.99.refs_0_), channel_id=1, source_target_pairs={{0,16},{8,24},{16,0},{24,8},{1,17},{9,25},{17,1},{25,9},{2,18},{10... | collective-permute-start | bytes 552968 | tf_op jit(solution)/shard_map/ppermute | solution.py:47
  25.7 8.0 %collective-permute-start.7 = (bf16[72,1280]{1,0:T(8,128)(2,1)S(1)}, bf16[72,1280]{1,0:T(8,128)(2,1)S(1)}, u32[]{:S(2)}, u32[]{:S(2)}) collective-permute-start(bf16[72,1280]{1,0:T(8,128)(2,1)S(1)} %shard_map.99.refs_0_), channel_id=1, source_target_pairs={{0,8},{8,0},{16,24},{24,16},{1,9},{9,1},{17,25},{25,17},{2,10},{10... | collective-permute-start | bytes 552968 | tf_op jit(solution)/shard_map/ppermute | solution.py:47
  27.9 6.3 %collective-permute-start.10 = (bf16[72,1280]{1,0:T(8,128)(2,1)S(1)}, bf16[72,1280]{1,0:T(8,128)(2,1)S(1)}, u32[]{:S(2)}, u32[]{:S(2)}) collective-permute-start(bf16[72,1280]{1,0:T(8,128)(2,1)S(1)} %shard_map.99.refs_0_), channel_id=1, source_target_pairs={{0,1},{1,0},{2,3},{3,2},{4,5},{5,4},{6,7},{7,6},{8,9},{9,8},{10,11... | collective-permute-start | bytes 552968 | tf_op jit(solution)/shard_map/ppermute | solution.py:47
  33.7 1.4 %collective-permute-start.11 = (bf16[72,1280]{1,0:T(8,128)(2,1)S(1)}, bf16[72,1280]{1,0:T(8,128)(2,1)S(1)}, u32[]{:S(2)}, u32[]{:S(2)}) collective-permute-start(bf16[72,1280]{1,0:T(8,128)(2,1)S(1)} %collective-permute-done.7.refs_1_), channel_id=1, source_target_pairs={{0,1},{1,0},{2,3},{3,2},{4,5},{5,4},{6,7},{7,6},{8,9},{9,8},{10,11... | collective-permute-start | bytes 552968 | tf_op jit(solution)/shard_map/ppermute | solution.py:47
  33.7 1.7 %collective-permute-start.12 = (bf16[72,1280]{1,0:T(8,128)(2,1)S(1)}, bf16[72,1280]{1,0:T(8,128)(2,1)S(1)}, u32[]{:S(2)}, u32[]{:S(2)}) collective-permute-start(bf16[72,1280]{1,0:T(8,128)(2,1)S(1)} %collective-permute-done.8.refs_2_), channel_id=1, source_target_pairs={{0,1},{1,0},{2,3},{3,2},{4,5},{5,4},{6,7},{7,6},{8,9},{9,8},{10,11... | collective-permute-start | bytes 552968 | tf_op jit(solution)/shard_map/ppermute | solution.py:47
  34.2 1.4 %collective-permute-start.13 = (bf16[72,1280]{1,0:T(8,128)(2,1)S(1)}, bf16[72,1280]{1,0:T(8,128)(2,1)S(1)}, u32[]{:S(2)}, u32[]{:S(2)}) collective-permute-start(bf16[72,1280]{1,0:T(8,128)(2,1)S(1)} %collective-permute-done.9.refs_3_), channel_id=1, source_target_pairs={{0,1},{1,0},{2,3},{3,2},{4,5},{5,4},{6,7},{7,6},{8,9},{9,8},{10,11... | collective-permute-start | bytes 552968 | tf_op jit(solution)/shard_map/ppermute | solution.py:47
  36.9 5.8 %collective-permute-start.17 = (bf16[64,640]{1,0:T(8,128)(2,1)S(1)}, bf16[64,640]{1,0:T(8,128)(2,1)S(1)}, u32[]{:S(2)}, u32[]{:S(2)}) collective-permute-start(bf16[64,640]{1,0:T(8,128)(2,1)S(1)} %get-tuple-element.49), channel_id=1, source_target_pairs={{0,2},{2,0},{4,6},{6,4},{1,3},{3,1},{5,7},{7,5},{8,10},{10,8},{12,... | collective-permute-start | bytes 245768 | tf_op jit(solution)/shard_map/ppermute | solution.py:47
  37.0 9.8 %collective-permute-start.16 = (bf16[64,640]{1,0:T(8,128)(2,1)S(1)}, bf16[64,640]{1,0:T(8,128)(2,1)S(1)}, u32[]{:S(2)}, u32[]{:S(2)}) collective-permute-start(bf16[64,640]{1,0:T(8,128)(2,1)S(1)} %get-tuple-element.48), channel_id=1, source_target_pairs={{0,4},{2,6},{4,0},{6,2},{1,5},{3,7},{5,1},{7,3},{8,12},{10,14},{12... | collective-permute-start | bytes 245768 | tf_op jit(solution)/shard_map/ppermute | solution.py:47
  38.0 8.8 %collective-permute-start.15 = (bf16[64,640]{1,0:T(8,128)(2,1)S(1)}, bf16[64,640]{1,0:T(8,128)(2,1)S(1)}, u32[]{:S(2)}, u32[]{:S(2)}) collective-permute-start(bf16[64,640]{1,0:T(8,128)(2,1)S(1)} %get-tuple-element.50), channel_id=1, source_target_pairs={{0,6},{2,4},{4,2},{6,0},{1,7},{3,5},{5,3},{7,1},{8,14},{10,12},{12... | collective-permute-start | bytes 245768 | tf_op jit(solution)/shard_map/ppermute | solution.py:47
  42.5 8.8 %collective-permute-start.14 = (bf16[128,640]{1,0:T(8,128)(2,1)S(1)}, bf16[128,640]{1,0:T(8,128)(2,1)S(1)}, u32[]{:S(2)}, u32[]{:S(2)}) collective-permute-start(bf16[128,640]{1,0:T(8,128)(2,1)S(1)} %get-tuple-element.55), channel_id=1, source_target_pairs={{0,2},{2,0},{4,6},{6,4},{1,3},{3,1},{5,7},{7,5},{8,10},{10,8},{12,... | collective-permute-start | bytes 491528 | tf_op jit(solution)/shard_map/ppermute | solution.py:47
  42.7 8.7 %collective-permute-start.18 = (bf16[64,640]{1,0:T(8,128)(2,1)S(1)}, bf16[64,640]{1,0:T(8,128)(2,1)S(1)}, u32[]{:S(2)}, u32[]{:S(2)}) collective-permute-start(bf16[64,640]{1,0:T(8,128)(2,1)S(1)} %shard_map.103), channel_id=1, source_target_pairs={{0,6},{2,4},{4,2},{6,0},{1,7},{3,5},{5,3},{7,1},{8,14},{10,12},{12... | collective-permute-start | bytes 245768 | tf_op jit(solution)/shard_map/ppermute | solution.py:47

commit v6 on v5

--- a/solution.py
+++ b/solution.py
@@ -20,6 +20,7 @@
 I32 = jnp.int32
 LANES = 128
 INFO = 16
+ARRIVALS = (2, 1, 3, 0)
 
 VMEM = pl.BlockSpec(memory_space=pltpu.VMEM)
 SMEM = pl.BlockSpec(memory_space=pltpu.SMEM)
@@ -108,6 +109,10 @@
         out[:, width : 2 * width] = second[k * slots : (k + 1) * slots]
 
 
+def in_order(order, refs):
+    return [refs[order.index(k)] for k in range(len(order))]
+
+
 def norm_kernel(n, gain, info, *refs):
     inputs, outs, held = refs[:n], refs[2 * n - 1 : n - 1 : -1], refs[2 * n]
     a = lax.axis_index("sec")
@@ -121,14 +126,14 @@
     for k, ref in enumerate(inputs):
         start = pl.multiple_of((a ^ k) * width, LANES)
         held[k] = (ref[...].astype(F32) * scale * gain[:, pl.ds(start, width)]).astype(BF16)
-    beside = jnp.concatenate([info[...]] * (slots // info.shape[0]), axis=0)
     for m, out in enumerate(outs):
-        out[:, 0:width] = held[a ^ s ^ m]
-        out[:, width : width + LANES] = beside
-
-
-def info_of(ref, width):
-    return ref[0:INFO, width : width + LANES].astype(F32)
+        for h in range(slots // INFO):
+            out[:, h * width : (h + 1) * width] = held[a ^ s ^ m, h * INFO : (h + 1) * INFO, :]
+        out[:, out.shape[1] - LANES :] = info[...]
+
+
+def info_of(ref):
+    return ref[:, ref.shape[1] - LANES :].astype(F32)
 
 
 def word_sum(block, row, first, last):
@@ -137,10 +142,10 @@
     return jnp.sum(jnp.where(inside, block, 0.0)).astype(I32)
 
 
-def put_counts(moved, width, row, n_resp, counts):
+def put_counts(moved, row, n_resp, counts):
     s = lax.axis_index("seq")
     for m, ref in enumerate(moved):
-        counts[s ^ m] = word_sum(info_of(ref, width), row, 0, n_resp)
+        counts[s ^ m] = word_sum(info_of(ref), row, 0, n_resp)
 
 
 def class_rows(x, c, n_class):
@@ -177,11 +182,12 @@
 
 
 def pack_kernel(n, n_class, n_resp, tok, row, *refs):
-    moved, (out, held, counts) = refs[n - 1 :: -1], refs[n:]
+    moved, (out, held, counts) = in_order(ARRIVALS, refs[:n]), refs[n:]
     s = lax.axis_index("seq")
     c = lax.axis_index("sec") * lax.axis_size("tp") + lax.axis_index("tp")
-    slots, width = moved[0].shape[0], out.shape[1]
-    put_counts(moved, width, row, n_resp, counts)
+    width = out.shape[1]
+    slots = (moved[0].shape[1] - LANES) // width * INFO
+    put_counts(moved, row, n_resp, counts)
     lane = iota((1, n * slots), 1)
     seq_of = div(lane, slots) ^ s
     q = mod(lane, slots)
@@ -196,7 +202,9 @@
     place = list_place(counts, n, n_class, tok, s, c, seq_of, q, packed)
     place = jnp.where(live, place, -1)
     for m, ref in enumerate(moved):
-        held[m * slots : (m + 1) * slots, :] = ref[:, 0:width]
+        for h in range(slots // INFO):
+            first = m * slots + h * INFO
+            held[first : first + INFO, :] = ref[:, h * width : (h + 1) * width]
     pick = (iota((out.shape[0], n * slots), 0) == place).astype(BF16)
     out[...] = jnp.dot(pick, held[...], preferred_element_type=F32).astype(BF16)
 
@@ -210,16 +218,15 @@
         out[:, j * LANES : (j + 1) * LANES] = (iota(column.shape, 1) + j * LANES == column).astype(BF16)
 
 
-def index_kernel(n, n_class, n_resp, tok, row, step, *refs):
-    moved, hidden = refs[n - 1 :: -1], refs[n]
+def index_kernel(n, n_class, n_resp, tok, row, *refs):
+    moved, hidden = in_order(ARRIVALS, refs[:n]), refs[n]
     pick_far, pick_near, rest_far, rest_near, counts, lens, own = refs[n + 1 :]
     a = lax.axis_index("sec")
     s = lax.axis_index("seq")
     t = lax.axis_index("tp")
     n_tp = lax.axis_size("tp")
-    width = moved[0].shape[1] - LANES
-    put_counts(moved, width, row, n_resp, counts)
-    block = info_of(moved[0], width)
+    put_counts(moved, row, n_resp, counts)
+    block = info_of(moved[0])
     for r in range(n_resp):
         lens[r] = word_sum(block, row, r, r + 1)
     half = n // 2 * tok
@@ -239,7 +246,7 @@
         index = packed - start
         c = mod(index, n_class)
         place = list_place(counts, n, n_class, tok, s, c, seq_of, div(index, n_class), packed)
-        column = ((mod(c, n_tp) ^ t) * n + (div(c, n_tp) ^ a)) * step + place
+        column = ((mod(c, n_tp) ^ t) * n + (div(c, n_tp) ^ a)) * (pick.shape[1] // n_class) + place
         one_hot(upright(column), pick)
         source, ends = index, 0
         for r in range(n_resp):
@@ -253,7 +260,7 @@
     pieces, outs, held = refs[:n_lists], refs[n_lists:-1], refs[-1]
     listed, step = pieces[0].shape[0], held.shape[0] // n_lists
     for k, piece in enumerate(pieces):
-        rows = piece[...].astype(F32)
+        rows = piece[0 : min(step, listed), :].astype(F32)
         if step > listed:
             rows = jnp.concatenate([rows, jnp.zeros((step - listed, rows.shape[1]), F32)], axis=0)
         held[k * step : (k + 1) * step, :] = rows.astype(BF16)
@@ -285,13 +292,12 @@
 
 
 def terms_kernel(n, n_resp, row, *refs):
-    moved, out, words, table = refs[n - 1 :: -1], refs[n], refs[n + 1], refs[n + 2]
+    moved, out, words, table = in_order(ARRIVALS, refs[:n]), refs[n], refs[n + 1], refs[n + 2]
     s = lax.axis_index("seq")
-    width = moved[0].shape[1] - LANES
     tok = out.shape[1]
     group_count = n * n_resp // GROUP
     for m, ref in enumerate(moved):
-        block = info_of(ref, width)
+        block = info_of(ref)
         table[pl.ds((s ^ m) * INFO, INFO), :] = block
         for r in range(3 * n_resp):
             words[s ^ m, r] = word_sum(block, row, r, r + 1)
@@ -354,9 +360,9 @@
     tokens = tok * n
     up = lambda x, m: -(-x // m) * m
     listed = up((tokens + (n_class - 1) * n) // n_class, 8)
-    step = up(listed, 16)
+    far_rows = up((tokens // 2 + (n_class - 1) * (n + 1)) // n_class, 16)
     shape = jax.ShapeDtypeStruct
-    info_like = shape((slots, width + LANES), BF16)
+    info_like = shape((INFO, slots // INFO * width + LANES), BF16)
 
     sibling = swap(hidden, "tp", 1)
     pick, mine, info, gain = call(
@@ -410,27 +416,27 @@
         [VMEM] * n,
         VMEM,
         [pltpu.VMEM((n * slots, width), BF16), pltpu.SMEM((n,), I32)],
-    )(*moved[::-1])
+    )(*(moved[m] for m in ARRIVALS))
     half = n // 2 * tok
     pick_far, pick_near, rest_far, rest_near = call(
-        functools.partial(index_kernel, n, n_class, n_resp, tok, row, step),
+        functools.partial(index_kernel, n, n_class, n_resp, tok, row),
         [
-            shape((half, n_class * step), BF16),
-            shape((half, n_class * step), BF16),
+            shape((half, n_class * far_rows), BF16),
+            shape((half, n_class * up(listed, 16)), BF16),
             shape((half, cols), F32),
             shape((half, cols), F32),
         ],
         [VMEM] * (n + 1),
         [VMEM] * 4,
         [pltpu.SMEM((n,), I32), pltpu.SMEM((n_resp,), I32), pltpu.VMEM((half, rows), BF16)],
-    )(*moved[::-1], hidden)
+    )(*(moved[m] for m in ARRIVALS), hidden)
     terms = call(
         functools.partial(terms_kernel, n, n_resp, row),
         shape((2, tok), F32),
         [VMEM] * n,
         VMEM,
         [pltpu.SMEM((n, 3 * n_resp), I32), pltpu.VMEM((n * INFO, LANES), F32)],
-    )(*moved[::-1])
+    )(*(moved[m] for m in ARRIVALS))
     after = lambda x, *ys: lax.optimization_barrier((x, *ys))[0]
     same = [mine] + [swap(mine, "sec", k) for k in range(1, n)]
     lists = same + [swap(after(x, pick_far, terms), "tp", 1) for x in same]
@@ -439,7 +445,7 @@
         outs,
         [VMEM] * (n_class + 3),
         [VMEM] * len(outs),
-        [pltpu.VMEM((n_class * step, width), BF16)],
+        [pltpu.VMEM((pick.shape[1], width), BF16)],
     )(pick, rest, projection, *lists)
     part = tok // 2
     joined = n // 2
@@ -449,7 +455,6 @@
         [shape((part, cols), F32 if m % 2 and h else BF16) for m in range(joined) for h in range(2)],
     )
     helped = [swap(far[2 * m + 1], "seq", 1) for m in range(0, joined, 2)]
-    direct = [swap(far[2 * m], "seq", joined + m) for m in range(joined - 1, -1, -1)]
     sums = [
         call(join_kernel, shape((part, cols), BF16), [VMEM] * 2, VMEM)(far[2 * m + 3], got)
         for m, got in zip(range(0, joined, 2), helped, strict=True)
@@ -458,6 +463,9 @@
     near = mix(
         after(pick_near, *far), rest_near, [shape((tok, cols), F32)] + [shape((tok, cols), BF16)] * (joined - 1)
     )
+    direct = [swap(far[0], "seq", joined)] + [
+        swap(after(far[2 * m], *near), "seq", joined + m) for m in range(1, joined)
+    ]
     whole = [swap(near[m], "seq", m) for m in range(1, joined)]
     states = call(
         functools.partial(final_kernel, len(whole), len(direct)),

time: 52.3 us -> 50.6 us (0.967)
  waiting for transfers between devices: 25.9 us -> 22.5 us
  starting transfers between devices: 18.7 us -> 20.6 us
    ppermute x19, waiting for transfers between devices: 25.9 us -> 22.5 us  [swap(): return lax.ppermute(x, axis, [(i, i ^ k) for i in range(n)])]
    ppermute x19, starting transfers between devices: 18.7 us -> 20.6 us  [swap(): return lax.ppermute(x, axis, [(i, i ^ k) for i in range(n)])]
  transfers between devices with their start and end apart: 19 -> 19, of which waited for: 14 -> 15; matrix products, arithmetic and copies ran while one was open for 1% -> 1% of each run, Pallas kernels for 7% -> 7%
where the time goes in v6:
time: 50.6 us; the launch traced here: 50.5 us
  waiting for transfers between devices  22.5 us (44%)
  starting transfers between devices  20.6 us (41%)
  Pallas kernels  6.13 us (12%)
  between operations  0.74 us (1%)
  other arithmetic  0.51 us (1%)
    ppermute x19, waiting for transfers between devices, swap(): return lax.ppermute(x, axis, [(i, i ^ k) for i in range(n)])  22.5 us
    ppermute x19, starting transfers between devices, swap(): return lax.ppermute(x, axis, [(i, i ^ k) for i in range(n)])  20.6 us
    pallas_call x2, Pallas kernels, shards_in_place(): call(functools.partial(mix_kernel, n_class), outs, [VMEM] * (n_class + 3)...  2.22 us
    pallas_call x1, Pallas kernels, shards_in_place(): call(functools.partial(early_kernel, n, n_tp), [shape((rows // n_tp, rows...  1.32 us
  transfers between devices with their start and end apart: 19, of which 15 were waited for; matrix products, arithmetic and copies ran while one was open for 1% of the time, Pallas kernels for 7%

profile of v6, /device:TPU:0, one launch (start us, length us, event | category | flops | bytes accessed | tf_op | source)
XLA Modules:
  0.0 50.5 jit_solution(3920853699666102116)
XLA Ops:
  0.7 0.5 %collective-permute-start = (bf16[256,640]{1,0:T(8,128)(2,1)}, bf16[256,640]{1,0:T(8,128)(2,1)S(1)}, u32[]{:S(2)}, u32[]{:S(2)}) collective-permute-start(bf16[256,640]{1,0:T(8,128)(2,1)} %refs_4_.1), channel_id=1, source_target_pairs={{0,1},{1,0},{2,3},{3,2},{4,5},{5,4},{6,7},{7,6},{8,9},{9,8},{10,11... | collective-permute-start | bytes 983048 | tf_op jit(solution)/shard_map/ppermute | solution.py:48
  1.2 1.3 %shard_map.95 = (bf16[128,256]{1,0:T(8,128)(2,1)S(1)}, bf16[128,640]{1,0:T(8,128)(2,1)S(1)}, bf16[16,128]{1,0:T(8,128)(2,1)S(1)}, f32[1,5120]{1,0:T(1,128)S(1)}) custom-call(bf16[256,640]{1,0:T(8,128)(2,1)} %refs_4_.1, s32[4]{0:T(128)} %lengths.1, s32[4]{0:T(128)} %group_of.1, s32[4]{0:T(128)} %rewards.1, f32[2,128]{1,0:T(2,128)} %bitcast.6, ...), custom_call_target="tpu_custom_call" | custom-call | tf_op jit(solution)/shard_map/pallas_call | solution.py:368
  2.5 0.1 collective-permute-done.sibling
  2.6 0.2 shard_map.96
  2.9 2.9 %collective-permute-start.1 = (bf16[32,1280]{1,0:T(8,128)(2,1)S(1)}, bf16[32,1280]{1,0:T(8,128)(2,1)S(1)}, u32[]{:S(2)}, u32[]{:S(2)}) collective-permute-start(bf16[32,1280]{1,0:T(8,128)(2,1)S(1)} %get-tuple-element.35), channel_id=1, source_target_pairs={{0,8},{8,0},{16,24},{24,16},{1,9},{9,1},{17,25},{25,17},{2,10},{10... | collective-permute-start | bytes 245768 | tf_op jit(solution)/shard_map/ppermute | solution.py:48
  5.8 1.5 %collective-permute-start.2 = (bf16[32,1280]{1,0:T(8,128)(2,1)S(1)}, bf16[32,1280]{1,0:T(8,128)(2,1)S(1)}, u32[]{:S(2)}, u32[]{:S(2)}) collective-permute-start(bf16[32,1280]{1,0:T(8,128)(2,1)S(1)} %get-tuple-element.36), channel_id=1, source_target_pairs={{0,16},{8,24},{16,0},{24,8},{1,17},{9,25},{17,1},{25,9},{2,18},{10... | collective-permute-start | bytes 245768 | tf_op jit(solution)/shard_map/ppermute | solution.py:48
  7.3 0.0 collective-permute-start.3
  7.3 1.2 %collective-permute-done.1.refs_1_ = bf16[32,1280]{1,0:T(8,128)(2,1)S(1)} collective-permute-done((bf16[32,1280]{1,0:T(8,128)(2,1)S(1)}, bf16[32,1280]{1,0:T(8,128)(2,1)S(1)}, u32[]{:S(2)}, u32[]{:S(2)}) %collective-permute-start.1) | collective-permute-done | bytes 81952 | tf_op jit(solution)/shard_map/ppermute | solution.py:48
  8.5 2.5 %collective-permute-done.2.refs_2_ = bf16[32,1280]{1,0:T(8,128)(2,1)S(1)} collective-permute-done((bf16[32,1280]{1,0:T(8,128)(2,1)S(1)}, bf16[32,1280]{1,0:T(8,128)(2,1)S(1)}, u32[]{:S(2)}, u32[]{:S(2)}) %collective-permute-start.2) | collective-permute-done | bytes 81952 | tf_op jit(solution)/shard_map/ppermute | solution.py:48
  11.1 1.6 %collective-permute-done.3.refs_3_ = bf16[32,1280]{1,0:T(8,128)(2,1)S(1)} collective-permute-done((bf16[32,1280]{1,0:T(8,128)(2,1)S(1)}, bf16[32,1280]{1,0:T(8,128)(2,1)S(1)}, u32[]{:S(2)}, u32[]{:S(2)}) %collective-permute-start.3) | collective-permute-done | bytes 81952 | tf_op jit(solution)/shard_map/ppermute | solution.py:48
  12.6 0.2 shard_map.97
  12.9 2.7 %collective-permute-start.4 = (bf16[16,2688]{1,0:T(8,128)(2,1)S(1)}, bf16[16,2688]{1,0:T(8,128)(2,1)S(1)}, u32[]{:S(2)}, u32[]{:S(2)}) collective-permute-start(bf16[16,2688]{1,0:T(8,128)(2,1)S(1)} %get-tuple-element.38), channel_id=1, source_target_pairs={{0,4},{2,6},{4,0},{6,2},{1,5},{3,7},{5,1},{7,3},{8,12},{10,14},{12... | collective-permute-start | bytes 258056 | tf_op jit(solution)/shard_map/ppermute | solution.py:48
  15.5 1.6 %collective-permute-start.5 = (bf16[16,2688]{1,0:T(8,128)(2,1)S(1)}, bf16[16,2688]{1,0:T(8,128)(2,1)S(1)}, u32[]{:S(2)}, u32[]{:S(2)}) collective-permute-start(bf16[16,2688]{1,0:T(8,128)(2,1)S(1)} %get-tuple-element.39), channel_id=1, source_target_pairs={{0,2},{2,0},{4,6},{6,4},{1,3},{3,1},{5,7},{7,5},{8,10},{10,8},{12,... | collective-permute-start | bytes 258056 | tf_op jit(solution)/shard_map/ppermute | solution.py:48
  17.1 0.2 collective-permute-start.6
  17.3 3.6 %collective-permute-done.4.refs_0_ = bf16[16,2688]{1,0:T(8,128)(2,1)S(1)} collective-permute-done((bf16[16,2688]{1,0:T(8,128)(2,1)S(1)}, bf16[16,2688]{1,0:T(8,128)(2,1)S(1)}, u32[]{:S(2)}, u32[]{:S(2)}) %collective-permute-start.4) | collective-permute-done | bytes 86048 | tf_op jit(solution)/shard_map/ppermute | solution.py:48
  20.9 0.4 collective-permute-done.5.refs_1_
  21.3 2.1 %collective-permute-done.6.refs_2_ = bf16[16,2688]{1,0:T(8,128)(2,1)S(1)} collective-permute-done((bf16[16,2688]{1,0:T(8,128)(2,1)S(1)}, bf16[16,2688]{1,0:T(8,128)(2,1)S(1)}, u32[]{:S(2)}, u32[]{:S(2)}) %collective-permute-start.6) | collective-permute-done | bytes 86048 | tf_op jit(solution)/shard_map/ppermute | solution.py:48
  23.4 0.4 shard_map.99.refs_0_
  23.8 0.9 %collective-permute-start.9 = (bf16[72,1280]{1,0:T(8,128)(2,1)S(1)}, bf16[72,1280]{1,0:T(8,128)(2,1)S(1)}, u32[]{:S(2)}, u32[]{:S(2)}) collective-permute-start(bf16[72,1280]{1,0:T(8,128)(2,1)S(1)} %shard_map.99.refs_0_), channel_id=1, source_target_pairs={{0,24},{8,16},{16,8},{24,0},{1,25},{9,17},{17,9},{25,1},{2,26},{10... | collective-permute-start | bytes 552968 | tf_op jit(solution)/shard_map/ppermute | solution.py:48
  24.7 1.2 %collective-permute-start.8 = (bf16[72,1280]{1,0:T(8,128)(2,1)S(1)}, bf16[72,1280]{1,0:T(8,128)(2,1)S(1)}, u32[]{:S(2)}, u32[]{:S(2)}) collective-permute-start(bf16[72,1280]{1,0:T(8,128)(2,1)S(1)} %shard_map.99.refs_0_), channel_id=1, source_target_pairs={{0,16},{8,24},{16,0},{24,8},{1,17},{9,25},{17,1},{25,9},{2,18},{10... | collective-permute-start | bytes 552968 | tf_op jit(solution)/shard_map/ppermute | solution.py:48
  25.8 1.5 %collective-permute-start.7 = (bf16[72,1280]{1,0:T(8,128)(2,1)S(1)}, bf16[72,1280]{1,0:T(8,128)(2,1)S(1)}, u32[]{:S(2)}, u32[]{:S(2)}) collective-permute-start(bf16[72,1280]{1,0:T(8,128)(2,1)S(1)} %shard_map.99.refs_0_), channel_id=1, source_target_pairs={{0,8},{8,0},{16,24},{24,16},{1,9},{9,1},{17,25},{25,17},{2,10},{10... | collective-permute-start | bytes 552968 | tf_op jit(solution)/shard_map/ppermute | solution.py:48
  27.3 0.4 shard_map.100
  27.7 0.6 %shard_map.98 = (bf16[256,384]{1,0:T(8,128)(2,1)S(1)}, bf16[256,640]{1,0:T(8,128)(2,1)S(1)}, f32[256,640]{1,0:T(8,128)S(1)}, f32[256,640]{1,0:T(8,128)S(1)}) custom-call(bf16[16,2688]{1,0:T(8,128)(2,1)S(1)} %collective-permute-done.4.refs_0_, bf16[16,2688]{1,0:T(8,128)(2,1)S(1)} %collective-permute-done.5.refs_1_, ...), custom_call_target="tpu_custom_call" | custom-call | tf_op jit(solution)/shard_map/pallas_call | solution.py:421
  28.4 0.1 collective-permute-start.10
  28.4 2.6 %collective-permute-done.9.refs_3_ = bf16[72,1280]{1,0:T(8,128)(2,1)S(1)} collective-permute-done((bf16[72,1280]{1,0:T(8,128)(2,1)S(1)}, bf16[72,1280]{1,0:T(8,128)(2,1)S(1)}, u32[]{:S(2)}, u32[]{:S(2)}) %collective-permute-start.9) | collective-permute-done | bytes 184352 | tf_op jit(solution)/shard_map/ppermute | solution.py:48
  31.0 1.5 %collective-permute-done.8.refs_2_ = bf16[72,1280]{1,0:T(8,128)(2,1)S(1)} collective-permute-done((bf16[72,1280]{1,0:T(8,128)(2,1)S(1)}, bf16[72,1280]{1,0:T(8,128)(2,1)S(1)}, u32[]{:S(2)}, u32[]{:S(2)}) %collective-permute-start.8) | collective-permute-done | bytes 184352 | tf_op jit(solution)/shard_map/ppermute | solution.py:48
  32.5 0.0 collective-permute-done.7.refs_1_
  32.5 0.0 collective-permute-start.11
  32.5 0.5 %collective-permute-start.12 = (bf16[72,1280]{1,0:T(8,128)(2,1)S(1)}, bf16[72,1280]{1,0:T(8,128)(2,1)S(1)}, u32[]{:S(2)}, u32[]{:S(2)}) collective-permute-start(bf16[72,1280]{1,0:T(8,128)(2,1)S(1)} %collective-permute-done.8.refs_2_), channel_id=1, source_target_pairs={{0,1},{1,0},{2,3},{3,2},{4,5},{5,4},{6,7},{7,6},{8,9},{9,8},{10,11... | collective-permute-start | bytes 552968 | tf_op jit(solution)/shard_map/ppermute | solution.py:48
  33.0 0.0 collective-permute-start.13
  33.0 0.0 collective-permute-done.10.refs_4_
  33.0 0.9 %collective-permute-done.11.refs_5_ = bf16[72,1280]{1,0:T(8,128)(2,1)S(1)} collective-permute-done((bf16[72,1280]{1,0:T(8,128)(2,1)S(1)}, bf16[72,1280]{1,0:T(8,128)(2,1)S(1)}, u32[]{:S(2)}, u32[]{:S(2)}) %collective-permute-start.11) | collective-permute-done | bytes 184352 | tf_op jit(solution)/shard_map/ppermute | solution.py:48
  33.9 0.3 collective-permute-done.12.refs_6_
  34.2 0.3 collective-permute-done.13.refs_7_
  34.5 1.0 %shard_map.101 = (bf16[64,640]{1,0:T(8,128)(2,1)S(1)}, bf16[64,640]{1,0:T(8,128)(2,1)S(1)}, bf16[64,640]{1,0:T(8,128)(2,1)S(1)}, f32[64,640]{1,0:T(8,128)S(1)}) custom-call(bf16[256,384]{1,0:T(8,128)(2,1)S(1)} %get-tuple-element.43.pick, f32[256,640]{1,0:T(8,128)S(1)} %get-tuple-element.44.rest, bf16[1280,640]{1,0:T(8,128)(2,1)S(1)} %copy-done, ...), custom_call_target="tpu_custom_call" | custom-call | tf_op jit(solution)/shard_map/pallas_call | solution.py:443
  35.5 0.4 collective-permute-start.17
  35.9 1.3 %collective-permute-start.15 = (bf16[64,640]{1,0:T(8,128)(2,1)S(1)}, bf16[64,640]{1,0:T(8,128)(2,1)S(1)}, u32[]{:S(2)}, u32[]{:S(2)}) collective-permute-start(bf16[64,640]{1,0:T(8,128)(2,1)S(1)} %get-tuple-element.49), channel_id=1, source_target_pairs={{0,4},{2,6},{4,0},{6,2},{1,5},{3,7},{5,1},{7,3},{8,12},{10,14},{12... | collective-permute-start | bytes 245768 | tf_op jit(solution)/shard_map/ppermute | solution.py:48
  37.2 1.2 %shard_map.102 = (f32[128,640]{1,0:T(8,128)S(1)}, bf16[128,640]{1,0:T(8,128)(2,1)S(1)}) custom-call(bf16[256,640]{1,0:T(8,128)(2,1)S(1)} %get-tuple-element.53.pick, f32[256,640]{1,0:T(8,128)S(1)} %get-tuple-element.54.rest, bf16[1280,640]{1,0:T(8,128)(2,1)S(1)} %copy-done, bf16[72,1280]{1,0:T(8,128)(2,1)S(1)} %shard_map.99.refs_0_, ...), custom_call_target="tpu_custom_call" | custom-call | tf_op jit(solution)/shard_map/pallas_call | solution.py:443
  38.4 1.7 %collective-permute-start.14 = (bf16[128,640]{1,0:T(8,128)(2,1)S(1)}, bf16[128,640]{1,0:T(8,128)(2,1)S(1)}, u32[]{:S(2)}, u32[]{:S(2)}) collective-permute-start(bf16[128,640]{1,0:T(8,128)(2,1)S(1)} %get-tuple-element.56), channel_id=1, source_target_pairs={{0,2},{2,0},{4,6},{6,4},{1,3},{3,1},{5,7},{7,5},{8,10},{10,8},{12,... | collective-permute-start | bytes 491528 | tf_op jit(solution)/shard_map/ppermute | solution.py:48
  40.1 1.5 %collective-permute-start.16 = (bf16[64,640]{1,0:T(8,128)(2,1)S(1)}, bf16[64,640]{1,0:T(8,128)(2,1)S(1)}, u32[]{:S(2)}, u32[]{:S(2)}) collective-permute-start(bf16[64,640]{1,0:T(8,128)(2,1)S(1)} %get-tuple-element.57), channel_id=1, source_target_pairs={{0,6},{2,4},{4,2},{6,0},{1,7},{3,5},{5,3},{7,1},{8,14},{10,12},{12... | collective-permute-start | bytes 245768 | tf_op jit(solution)/shard_map/ppermute | solution.py:48
  41.6 0.3 collective-permute-done.17.other
  41.9 2.1 %collective-permute-start.18 = (bf16[64,640]{1,0:T(8,128)(2,1)S(1)}, bf16[64,640]{1,0:T(8,128)(2,1)S(1)}, u32[]{:S(2)}, u32[]{:S(2)}) collective-permute-start(bf16[64,640]{1,0:T(8,128)(2,1)S(1)} %shard_map.103), channel_id=1, source_target_pairs={{0,6},{2,4},{4,2},{6,0},{1,7},{3,5},{5,3},{7,1},{8,14},{10,12},{12... | collective-permute-start | bytes 245768 | tf_op jit(solution)/shard_map/ppermute | solution.py:48
  44.0 0.5 %convert_bitcast_fusion = bf16[128,2]{0,1:T(2,128)(2,1)} fusion(f32[2,128]{1,0:T(2,128)S(1)} %shard_map.100), kind=kLoop, calls=%fused_computation | loop fusion | flops 256 | bytes 1536 | tf_op jit(solution)/shard_map/transpose | solution.py:476
  44.6 4.0 %collective-permute-done.16.refs_3_ = bf16[64,640]{1,0:T(8,128)(2,1)S(1)} collective-permute-done((bf16[64,640]{1,0:T(8,128)(2,1)S(1)}, bf16[64,640]{1,0:T(8,128)(2,1)S(1)}, u32[]{:S(2)}, u32[]{:S(2)}) %collective-permute-start.16) | collective-permute-done | bytes 81952 | tf_op jit(solution)/shard_map/ppermute | solution.py:48
  48.6 0.0 collective-permute-done.15.refs_2_
  48.6 0.0 collective-permute-done.14.refs_1_
  48.6 1.1 %collective-permute-done.18.refs_4_ = bf16[64,640]{1,0:T(8,128)(2,1)S(1)} collective-permute-done((bf16[64,640]{1,0:T(8,128)(2,1)S(1)}, bf16[64,640]{1,0:T(8,128)(2,1)S(1)}, u32[]{:S(2)}, u32[]{:S(2)}) %collective-permute-start.18) | collective-permute-done | bytes 81952 | tf_op jit(solution)/shard_map/ppermute | solution.py:48
  49.8 0.7 %shard_map.104 = bf16[128,640]{1,0:T(8,128)(2,1)} custom-call(f32[128,640]{1,0:T(8,128)S(1)} %get-tuple-element.55.refs_0_, bf16[128,640]{1,0:T(8,128)(2,1)S(1)} %collective-permute-done.14.refs_1_, bf16[64,640]{1,0:T(8,128)(2,1)S(1)} %collective-permute-done.15.refs_2_, bf16[64,640]{1,0:T(8,128)(2,1)S(1)} %collective-permute-done.16.refs_3_, ...), custom_call_target="tpu_custom_call" | custom-call | tf_op jit(solution)/shard_map/pallas_call | solution.py:470
  (5 shorter events, 0.0 us)
Async XLA Ops:
  0.6 27.1 %copy-start.1 = (bf16[256,640]{1,0:T(8,128)(2,1)S(1)}, bf16[256,640]{1,0:T(8,128)(2,1)}, u32[]{:S(2)}) copy-start(bf16[256,640]{1,0:T(8,128)(2,1)} %refs_4_.1) | copy-start | bytes 983044
  0.6 33.8 %copy-start = (bf16[1280,640]{1,0:T(8,128)(2,1)S(1)}, bf16[1280,640]{1,0:T(8,128)(2,1)}, u32[]{:S(2)}) copy-start(bf16[1280,640]{1,0:T(8,128)(2,1)} %projection.3) | copy-start | bytes 4915204
  0.7 2.0 %collective-permute-start = (bf16[256,640]{1,0:T(8,128)(2,1)}, bf16[256,640]{1,0:T(8,128)(2,1)S(1)}, u32[]{:S(2)}, u32[]{:S(2)}) collective-permute-start(bf16[256,640]{1,0:T(8,128)(2,1)} %refs_4_.1), channel_id=1, source_target_pairs={{0,1},{1,0},{2,3},{3,2},{4,5},{5,4},{6,7},{7,6},{8,9},{9,8},{10,11... | collective-permute-start | bytes 983048 | tf_op jit(solution)/shard_map/ppermute | solution.py:48
  2.9 5.7 %collective-permute-start.1 = (bf16[32,1280]{1,0:T(8,128)(2,1)S(1)}, bf16[32,1280]{1,0:T(8,128)(2,1)S(1)}, u32[]{:S(2)}, u32[]{:S(2)}) collective-permute-start(bf16[32,1280]{1,0:T(8,128)(2,1)S(1)} %get-tuple-element.35), channel_id=1, source_target_pairs={{0,8},{8,0},{16,24},{24,16},{1,9},{9,1},{17,25},{25,17},{2,10},{10... | collective-permute-start | bytes 245768 | tf_op jit(solution)/shard_map/ppermute | solution.py:48
  5.8 5.3 %collective-permute-start.2 = (bf16[32,1280]{1,0:T(8,128)(2,1)S(1)}, bf16[32,1280]{1,0:T(8,128)(2,1)S(1)}, u32[]{:S(2)}, u32[]{:S(2)}) collective-permute-start(bf16[32,1280]{1,0:T(8,128)(2,1)S(1)} %get-tuple-element.36), channel_id=1, source_target_pairs={{0,16},{8,24},{16,0},{24,8},{1,17},{9,25},{17,1},{25,9},{2,18},{10... | collective-permute-start | bytes 245768 | tf_op jit(solution)/shard_map/ppermute | solution.py:48
  7.3 5.3 %collective-permute-start.3 = (bf16[32,1280]{1,0:T(8,128)(2,1)S(1)}, bf16[32,1280]{1,0:T(8,128)(2,1)S(1)}, u32[]{:S(2)}, u32[]{:S(2)}) collective-permute-start(bf16[32,1280]{1,0:T(8,128)(2,1)S(1)} %get-tuple-element.37), channel_id=1, source_target_pairs={{0,24},{8,16},{16,8},{24,0},{1,25},{9,17},{17,9},{25,1},{2,26},{10... | collective-permute-start | bytes 245768 | tf_op jit(solution)/shard_map/ppermute | solution.py:48
  12.9 8.0 %collective-permute-start.4 = (bf16[16,2688]{1,0:T(8,128)(2,1)S(1)}, bf16[16,2688]{1,0:T(8,128)(2,1)S(1)}, u32[]{:S(2)}, u32[]{:S(2)}) collective-permute-start(bf16[16,2688]{1,0:T(8,128)(2,1)S(1)} %get-tuple-element.38), channel_id=1, source_target_pairs={{0,4},{2,6},{4,0},{6,2},{1,5},{3,7},{5,1},{7,3},{8,12},{10,14},{12... | collective-permute-start | bytes 258056 | tf_op jit(solution)/shard_map/ppermute | solution.py:48
  15.5 5.7 %collective-permute-start.5 = (bf16[16,2688]{1,0:T(8,128)(2,1)S(1)}, bf16[16,2688]{1,0:T(8,128)(2,1)S(1)}, u32[]{:S(2)}, u32[]{:S(2)}) collective-permute-start(bf16[16,2688]{1,0:T(8,128)(2,1)S(1)} %get-tuple-element.39), channel_id=1, source_target_pairs={{0,2},{2,0},{4,6},{6,4},{1,3},{3,1},{5,7},{7,5},{8,10},{10,8},{12,... | collective-permute-start | bytes 258056 | tf_op jit(solution)/shard_map/ppermute | solution.py:48
  17.1 6.3 %collective-permute-start.6 = (bf16[16,2688]{1,0:T(8,128)(2,1)S(1)}, bf16[16,2688]{1,0:T(8,128)(2,1)S(1)}, u32[]{:S(2)}, u32[]{:S(2)}) collective-permute-start(bf16[16,2688]{1,0:T(8,128)(2,1)S(1)} %get-tuple-element.40), channel_id=1, source_target_pairs={{0,6},{2,4},{4,2},{6,0},{1,7},{3,5},{5,3},{7,1},{8,14},{10,12},{12... | collective-permute-start | bytes 258056 | tf_op jit(solution)/shard_map/ppermute | solution.py:48
  23.8 7.3 %collective-permute-start.9 = (bf16[72,1280]{1,0:T(8,128)(2,1)S(1)}, bf16[72,1280]{1,0:T(8,128)(2,1)S(1)}, u32[]{:S(2)}, u32[]{:S(2)}) collective-permute-start(bf16[72,1280]{1,0:T(8,128)(2,1)S(1)} %shard_map.99.refs_0_), channel_id=1, source_target_pairs={{0,24},{8,16},{16,8},{24,0},{1,25},{9,17},{17,9},{25,1},{2,26},{10... | collective-permute-start | bytes 552968 | tf_op jit(solution)/shard_map/ppermute | solution.py:48
  24.7 7.8 %collective-permute-start.8 = (bf16[72,1280]{1,0:T(8,128)(2,1)S(1)}, bf16[72,1280]{1,0:T(8,128)(2,1)S(1)}, u32[]{:S(2)}, u32[]{:S(2)}) collective-permute-start(bf16[72,1280]{1,0:T(8,128)(2,1)S(1)} %shard_map.99.refs_0_), channel_id=1, source_target_pairs={{0,16},{8,24},{16,0},{24,8},{1,17},{9,25},{17,1},{25,9},{2,18},{10... | collective-permute-start | bytes 552968 | tf_op jit(solution)/shard_map/ppermute | solution.py:48
  25.8 6.7 %collective-permute-start.7 = (bf16[72,1280]{1,0:T(8,128)(2,1)S(1)}, bf16[72,1280]{1,0:T(8,128)(2,1)S(1)}, u32[]{:S(2)}, u32[]{:S(2)}) collective-permute-start(bf16[72,1280]{1,0:T(8,128)(2,1)S(1)} %shard_map.99.refs_0_), channel_id=1, source_target_pairs={{0,8},{8,0},{16,24},{24,16},{1,9},{9,1},{17,25},{25,17},{2,10},{10... | collective-permute-start | bytes 552968 | tf_op jit(solution)/shard_map/ppermute | solution.py:48
  28.4 4.7 %collective-permute-start.10 = (bf16[72,1280]{1,0:T(8,128)(2,1)S(1)}, bf16[72,1280]{1,0:T(8,128)(2,1)S(1)}, u32[]{:S(2)}, u32[]{:S(2)}) collective-permute-start(bf16[72,1280]{1,0:T(8,128)(2,1)S(1)} %shard_map.99.refs_0_), channel_id=1, source_target_pairs={{0,1},{1,0},{2,3},{3,2},{4,5},{5,4},{6,7},{7,6},{8,9},{9,8},{10,11... | collective-permute-start | bytes 552968 | tf_op jit(solution)/shard_map/ppermute | solution.py:48
  32.5 1.4 %collective-permute-start.11 = (bf16[72,1280]{1,0:T(8,128)(2,1)S(1)}, bf16[72,1280]{1,0:T(8,128)(2,1)S(1)}, u32[]{:S(2)}, u32[]{:S(2)}) collective-permute-start(bf16[72,1280]{1,0:T(8,128)(2,1)S(1)} %collective-permute-done.7.refs_1_), channel_id=1, source_target_pairs={{0,1},{1,0},{2,3},{3,2},{4,5},{5,4},{6,7},{7,6},{8,9},{9,8},{10,11... | collective-permute-start | bytes 552968 | tf_op jit(solution)/shard_map/ppermute | solution.py:48
  32.5 1.7 %collective-permute-start.12 = (bf16[72,1280]{1,0:T(8,128)(2,1)S(1)}, bf16[72,1280]{1,0:T(8,128)(2,1)S(1)}, u32[]{:S(2)}, u32[]{:S(2)}) collective-permute-start(bf16[72,1280]{1,0:T(8,128)(2,1)S(1)} %collective-permute-done.8.refs_2_), channel_id=1, source_target_pairs={{0,1},{1,0},{2,3},{3,2},{4,5},{5,4},{6,7},{7,6},{8,9},{9,8},{10,11... | collective-permute-start | bytes 552968 | tf_op jit(solution)/shard_map/ppermute | solution.py:48
  33.0 1.4 %collective-permute-start.13 = (bf16[72,1280]{1,0:T(8,128)(2,1)S(1)}, bf16[72,1280]{1,0:T(8,128)(2,1)S(1)}, u32[]{:S(2)}, u32[]{:S(2)}) collective-permute-start(bf16[72,1280]{1,0:T(8,128)(2,1)S(1)} %collective-permute-done.9.refs_3_), channel_id=1, source_target_pairs={{0,1},{1,0},{2,3},{3,2},{4,5},{5,4},{6,7},{7,6},{8,9},{9,8},{10,11... | collective-permute-start | bytes 552968 | tf_op jit(solution)/shard_map/ppermute | solution.py:48
  35.5 6.4 %collective-permute-start.17 = (bf16[64,640]{1,0:T(8,128)(2,1)S(1)}, bf16[64,640]{1,0:T(8,128)(2,1)S(1)}, u32[]{:S(2)}, u32[]{:S(2)}) collective-permute-start(bf16[64,640]{1,0:T(8,128)(2,1)S(1)} %get-tuple-element.50), channel_id=1, source_target_pairs={{0,2},{2,0},{4,6},{6,4},{1,3},{3,1},{5,7},{7,5},{8,10},{10,8},{12,... | collective-permute-start | bytes 245768 | tf_op jit(solution)/shard_map/ppermute | solution.py:48
  35.9 12.7 %collective-permute-start.15 = (bf16[64,640]{1,0:T(8,128)(2,1)S(1)}, bf16[64,640]{1,0:T(8,128)(2,1)S(1)}, u32[]{:S(2)}, u32[]{:S(2)}) collective-permute-start(bf16[64,640]{1,0:T(8,128)(2,1)S(1)} %get-tuple-element.49), channel_id=1, source_target_pairs={{0,4},{2,6},{4,0},{6,2},{1,5},{3,7},{5,1},{7,3},{8,12},{10,14},{12... | collective-permute-start | bytes 245768 | tf_op jit(solution)/shard_map/ppermute | solution.py:48
  38.4 10.2 %collective-permute-start.14 = (bf16[128,640]{1,0:T(8,128)(2,1)S(1)}, bf16[128,640]{1,0:T(8,128)(2,1)S(1)}, u32[]{:S(2)}, u32[]{:S(2)}) collective-permute-start(bf16[128,640]{1,0:T(8,128)(2,1)S(1)} %get-tuple-element.56), channel_id=1, source_target_pairs={{0,2},{2,0},{4,6},{6,4},{1,3},{3,1},{5,7},{7,5},{8,10},{10,8},{12,... | collective-permute-start | bytes 491528 | tf_op jit(solution)/shard_map/ppermute | solution.py:48
  40.1 8.5 %collective-permute-start.16 = (bf16[64,640]{1,0:T(8,128)(2,1)S(1)}, bf16[64,640]{1,0:T(8,128)(2,1)S(1)}, u32[]{:S(2)}, u32[]{:S(2)}) collective-permute-start(bf16[64,640]{1,0:T(8,128)(2,1)S(1)} %get-tuple-element.57), channel_id=1, source_target_pairs={{0,6},{2,4},{4,2},{6,0},{1,7},{3,5},{5,3},{7,1},{8,14},{10,12},{12... | collective-permute-start | bytes 245768 | tf_op jit(solution)/shard_map/ppermute | solution.py:48
  41.9 7.8 %collective-permute-start.18 = (bf16[64,640]{1,0:T(8,128)(2,1)S(1)}, bf16[64,640]{1,0:T(8,128)(2,1)S(1)}, u32[]{:S(2)}, u32[]{:S(2)}) collective-permute-start(bf16[64,640]{1,0:T(8,128)(2,1)S(1)} %shard_map.103), channel_id=1, source_target_pairs={{0,6},{2,4},{4,2},{6,0},{1,7},{3,5},{5,3},{7,1},{8,14},{10,12},{12... | collective-permute-start | bytes 245768 | tf_op jit(solution)/shard_map/ppermute | solution.py:48

commit v7 on v6

--- a/solution.py
+++ b/solution.py
@@ -359,7 +359,7 @@
     tok = TOK_DEV
     tokens = tok * n
     up = lambda x, m: -(-x // m) * m
-    listed = up((tokens + (n_class - 1) * n) // n_class, 8)
+    listed = up((tokens + (n_class - 1) * n) // n_class, 16)
     far_rows = up((tokens // 2 + (n_class - 1) * (n + 1)) // n_class, 16)
     shape = jax.ShapeDtypeStruct
     info_like = shape((INFO, slots // INFO * width + LANES), BF16)

time: 50.6 us -> 51.6 us (1.020)
  waiting for transfers between devices: 22.5 us -> 23.3 us
    ppermute x19, waiting for transfers between devices: 22.5 us -> 23.3 us  [swap(): return lax.ppermute(x, axis, [(i, i ^ k) for i in range(n)])]
where the time goes in v7:
time: 51.6 us; the launch traced here: 51.4 us
  waiting for transfers between devices  23.3 us (45%)
  starting transfers between devices  20.7 us (40%)
  Pallas kernels  6.14 us (12%)
  between operations  0.74 us (1%)
    ppermute x19, waiting for transfers between devices, swap(): return lax.ppermute(x, axis, [(i, i ^ k) for i in range(n)])  23.3 us
    ppermute x19, starting transfers between devices, swap(): return lax.ppermute(x, axis, [(i, i ^ k) for i in range(n)])  20.7 us
    pallas_call x2, Pallas kernels, shards_in_place(): call(functools.partial(mix_kernel, n_class), outs, [VMEM] * (n_class + 3)...  2.23 us
    pallas_call x1, Pallas kernels, shards_in_place(): call(functools.partial(early_kernel, n, n_tp), [shape((rows // n_tp, rows...  1.32 us
  transfers between devices with their start and end apart: 19, of which 15 were waited for; matrix products, arithmetic and copies ran while one was open for 1% of the time, Pallas kernels for 7%

profile of v7, /device:TPU:0, one launch (start us, length us, event | category | flops | bytes accessed | tf_op | source)
XLA Modules:
  0.0 51.4 jit_solution(16489036560285035642)
XLA Ops:
  0.7 0.5 %collective-permute-start = (bf16[256,640]{1,0:T(8,128)(2,1)}, bf16[256,640]{1,0:T(8,128)(2,1)S(1)}, u32[]{:S(2)}, u32[]{:S(2)}) collective-permute-start(bf16[256,640]{1,0:T(8,128)(2,1)} %refs_4_.1), channel_id=1, source_target_pairs={{0,1},{1,0},{2,3},{3,2},{4,5},{5,4},{6,7},{7,6},{8,9},{9,8},{10,11... | collective-permute-start | bytes 983048 | tf_op jit(solution)/shard_map/ppermute | solution.py:48
  1.2 1.3 %shard_map.95 = (bf16[128,256]{1,0:T(8,128)(2,1)S(1)}, bf16[128,640]{1,0:T(8,128)(2,1)S(1)}, bf16[16,128]{1,0:T(8,128)(2,1)S(1)}, f32[1,5120]{1,0:T(1,128)S(1)}) custom-call(bf16[256,640]{1,0:T(8,128)(2,1)} %refs_4_.1, s32[4]{0:T(128)} %lengths.1, s32[4]{0:T(128)} %group_of.1, s32[4]{0:T(128)} %rewards.1, f32[2,128]{1,0:T(2,128)} %bitcast.6, ...), custom_call_target="tpu_custom_call" | custom-call | tf_op jit(solution)/shard_map/pallas_call | solution.py:368
  2.5 0.1 collective-permute-done.sibling
  2.6 0.2 shard_map.96
  2.9 2.9 %collective-permute-start.1 = (bf16[32,1280]{1,0:T(8,128)(2,1)S(1)}, bf16[32,1280]{1,0:T(8,128)(2,1)S(1)}, u32[]{:S(2)}, u32[]{:S(2)}) collective-permute-start(bf16[32,1280]{1,0:T(8,128)(2,1)S(1)} %get-tuple-element.35), channel_id=1, source_target_pairs={{0,8},{8,0},{16,24},{24,16},{1,9},{9,1},{17,25},{25,17},{2,10},{10... | collective-permute-start | bytes 245768 | tf_op jit(solution)/shard_map/ppermute | solution.py:48
  5.8 1.5 %collective-permute-start.2 = (bf16[32,1280]{1,0:T(8,128)(2,1)S(1)}, bf16[32,1280]{1,0:T(8,128)(2,1)S(1)}, u32[]{:S(2)}, u32[]{:S(2)}) collective-permute-start(bf16[32,1280]{1,0:T(8,128)(2,1)S(1)} %get-tuple-element.36), channel_id=1, source_target_pairs={{0,16},{8,24},{16,0},{24,8},{1,17},{9,25},{17,1},{25,9},{2,18},{10... | collective-permute-start | bytes 245768 | tf_op jit(solution)/shard_map/ppermute | solution.py:48
  7.3 0.0 collective-permute-start.3
  7.3 1.2 %collective-permute-done.1.refs_1_ = bf16[32,1280]{1,0:T(8,128)(2,1)S(1)} collective-permute-done((bf16[32,1280]{1,0:T(8,128)(2,1)S(1)}, bf16[32,1280]{1,0:T(8,128)(2,1)S(1)}, u32[]{:S(2)}, u32[]{:S(2)}) %collective-permute-start.1) | collective-permute-done | bytes 81952 | tf_op jit(solution)/shard_map/ppermute | solution.py:48
  8.5 2.5 %collective-permute-done.2.refs_2_ = bf16[32,1280]{1,0:T(8,128)(2,1)S(1)} collective-permute-done((bf16[32,1280]{1,0:T(8,128)(2,1)S(1)}, bf16[32,1280]{1,0:T(8,128)(2,1)S(1)}, u32[]{:S(2)}, u32[]{:S(2)}) %collective-permute-start.2) | collective-permute-done | bytes 81952 | tf_op jit(solution)/shard_map/ppermute | solution.py:48
  11.1 1.6 %collective-permute-done.3.refs_3_ = bf16[32,1280]{1,0:T(8,128)(2,1)S(1)} collective-permute-done((bf16[32,1280]{1,0:T(8,128)(2,1)S(1)}, bf16[32,1280]{1,0:T(8,128)(2,1)S(1)}, u32[]{:S(2)}, u32[]{:S(2)}) %collective-permute-start.3) | collective-permute-done | bytes 81952 | tf_op jit(solution)/shard_map/ppermute | solution.py:48
  12.6 0.2 shard_map.97
  12.9 2.7 %collective-permute-start.4 = (bf16[16,2688]{1,0:T(8,128)(2,1)S(1)}, bf16[16,2688]{1,0:T(8,128)(2,1)S(1)}, u32[]{:S(2)}, u32[]{:S(2)}) collective-permute-start(bf16[16,2688]{1,0:T(8,128)(2,1)S(1)} %get-tuple-element.38), channel_id=1, source_target_pairs={{0,4},{2,6},{4,0},{6,2},{1,5},{3,7},{5,1},{7,3},{8,12},{10,14},{12... | collective-permute-start | bytes 258056 | tf_op jit(solution)/shard_map/ppermute | solution.py:48
  15.5 1.6 %collective-permute-start.5 = (bf16[16,2688]{1,0:T(8,128)(2,1)S(1)}, bf16[16,2688]{1,0:T(8,128)(2,1)S(1)}, u32[]{:S(2)}, u32[]{:S(2)}) collective-permute-start(bf16[16,2688]{1,0:T(8,128)(2,1)S(1)} %get-tuple-element.39), channel_id=1, source_target_pairs={{0,2},{2,0},{4,6},{6,4},{1,3},{3,1},{5,7},{7,5},{8,10},{10,8},{12,... | collective-permute-start | bytes 258056 | tf_op jit(solution)/shard_map/ppermute | solution.py:48
  17.1 0.2 collective-permute-start.6
  17.3 3.6 %collective-permute-done.4.refs_0_ = bf16[16,2688]{1,0:T(8,128)(2,1)S(1)} collective-permute-done((bf16[16,2688]{1,0:T(8,128)(2,1)S(1)}, bf16[16,2688]{1,0:T(8,128)(2,1)S(1)}, u32[]{:S(2)}, u32[]{:S(2)}) %collective-permute-start.4) | collective-permute-done | bytes 86048 | tf_op jit(solution)/shard_map/ppermute | solution.py:48
  20.9 0.4 collective-permute-done.5.refs_1_
  21.3 2.1 %collective-permute-done.6.refs_2_ = bf16[16,2688]{1,0:T(8,128)(2,1)S(1)} collective-permute-done((bf16[16,2688]{1,0:T(8,128)(2,1)S(1)}, bf16[16,2688]{1,0:T(8,128)(2,1)S(1)}, u32[]{:S(2)}, u32[]{:S(2)}) %collective-permute-start.6) | collective-permute-done | bytes 86048 | tf_op jit(solution)/shard_map/ppermute | solution.py:48
  23.4 0.4 shard_map.99.refs_0_
  23.8 0.9 %collective-permute-start.9 = (bf16[80,1280]{1,0:T(8,128)(2,1)S(1)}, bf16[80,1280]{1,0:T(8,128)(2,1)S(1)}, u32[]{:S(2)}, u32[]{:S(2)}) collective-permute-start(bf16[80,1280]{1,0:T(8,128)(2,1)S(1)} %shard_map.99.refs_0_), channel_id=1, source_target_pairs={{0,24},{8,16},{16,8},{24,0},{1,25},{9,17},{17,9},{25,1},{2,26},{10... | collective-permute-start | bytes 614408 | tf_op jit(solution)/shard_map/ppermute | solution.py:48
  24.7 1.2 %collective-permute-start.8 = (bf16[80,1280]{1,0:T(8,128)(2,1)S(1)}, bf16[80,1280]{1,0:T(8,128)(2,1)S(1)}, u32[]{:S(2)}, u32[]{:S(2)}) collective-permute-start(bf16[80,1280]{1,0:T(8,128)(2,1)S(1)} %shard_map.99.refs_0_), channel_id=1, source_target_pairs={{0,16},{8,24},{16,0},{24,8},{1,17},{9,25},{17,1},{25,9},{2,18},{10... | collective-permute-start | bytes 614408 | tf_op jit(solution)/shard_map/ppermute | solution.py:48
  25.8 1.5 %collective-permute-start.7 = (bf16[80,1280]{1,0:T(8,128)(2,1)S(1)}, bf16[80,1280]{1,0:T(8,128)(2,1)S(1)}, u32[]{:S(2)}, u32[]{:S(2)}) collective-permute-start(bf16[80,1280]{1,0:T(8,128)(2,1)S(1)} %shard_map.99.refs_0_), channel_id=1, source_target_pairs={{0,8},{8,0},{16,24},{24,16},{1,9},{9,1},{17,25},{25,17},{2,10},{10... | collective-permute-start | bytes 614408 | tf_op jit(solution)/shard_map/ppermute | solution.py:48
  27.3 0.4 shard_map.100
  27.7 0.6 %shard_map.98 = (bf16[256,384]{1,0:T(8,128)(2,1)S(1)}, bf16[256,640]{1,0:T(8,128)(2,1)S(1)}, f32[256,640]{1,0:T(8,128)S(1)}, f32[256,640]{1,0:T(8,128)S(1)}) custom-call(bf16[16,2688]{1,0:T(8,128)(2,1)S(1)} %collective-permute-done.4.refs_0_, bf16[16,2688]{1,0:T(8,128)(2,1)S(1)} %collective-permute-done.5.refs_1_, ...), custom_call_target="tpu_custom_call" | custom-call | tf_op jit(solution)/shard_map/pallas_call | solution.py:421
  28.4 0.1 collective-permute-start.10
  28.4 3.2 %collective-permute-done.9.refs_3_ = bf16[80,1280]{1,0:T(8,128)(2,1)S(1)} collective-permute-done((bf16[80,1280]{1,0:T(8,128)(2,1)S(1)}, bf16[80,1280]{1,0:T(8,128)(2,1)S(1)}, u32[]{:S(2)}, u32[]{:S(2)}) %collective-permute-start.9) | collective-permute-done | bytes 204832 | tf_op jit(solution)/shard_map/ppermute | solution.py:48
  31.7 1.7 %collective-permute-done.8.refs_2_ = bf16[80,1280]{1,0:T(8,128)(2,1)S(1)} collective-permute-done((bf16[80,1280]{1,0:T(8,128)(2,1)S(1)}, bf16[80,1280]{1,0:T(8,128)(2,1)S(1)}, u32[]{:S(2)}, u32[]{:S(2)}) %collective-permute-start.8) | collective-permute-done | bytes 204832 | tf_op jit(solution)/shard_map/ppermute | solution.py:48
  33.4 0.0 collective-permute-done.7.refs_1_
  33.4 0.0 collective-permute-start.11
  33.4 0.5 collective-permute-start.12
  33.9 0.0 collective-permute-start.13
  33.9 0.0 collective-permute-done.10.refs_4_
  33.9 0.9 %collective-permute-done.11.refs_5_ = bf16[80,1280]{1,0:T(8,128)(2,1)S(1)} collective-permute-done((bf16[80,1280]{1,0:T(8,128)(2,1)S(1)}, bf16[80,1280]{1,0:T(8,128)(2,1)S(1)}, u32[]{:S(2)}, u32[]{:S(2)}) %collective-permute-start.11) | collective-permute-done | bytes 204832 | tf_op jit(solution)/shard_map/ppermute | solution.py:48
  34.8 0.3 collective-permute-done.12.refs_6_
  35.1 0.3 collective-permute-done.13.refs_7_
  35.4 1.0 %shard_map.101 = (bf16[64,640]{1,0:T(8,128)(2,1)S(1)}, bf16[64,640]{1,0:T(8,128)(2,1)S(1)}, bf16[64,640]{1,0:T(8,128)(2,1)S(1)}, f32[64,640]{1,0:T(8,128)S(1)}) custom-call(bf16[256,384]{1,0:T(8,128)(2,1)S(1)} %get-tuple-element.43.pick, f32[256,640]{1,0:T(8,128)S(1)} %get-tuple-element.44.rest, bf16[1280,640]{1,0:T(8,128)(2,1)S(1)} %copy-done, ...), custom_call_target="tpu_custom_call" | custom-call | tf_op jit(solution)/shard_map/pallas_call | solution.py:443
  36.5 0.4 collective-permute-start.17
  36.9 1.3 %collective-permute-start.15 = (bf16[64,640]{1,0:T(8,128)(2,1)S(1)}, bf16[64,640]{1,0:T(8,128)(2,1)S(1)}, u32[]{:S(2)}, u32[]{:S(2)}) collective-permute-start(bf16[64,640]{1,0:T(8,128)(2,1)S(1)} %get-tuple-element.49), channel_id=1, source_target_pairs={{0,4},{2,6},{4,0},{6,2},{1,5},{3,7},{5,1},{7,3},{8,12},{10,14},{12... | collective-permute-start | bytes 245768 | tf_op jit(solution)/shard_map/ppermute | solution.py:48
  38.2 1.2 %shard_map.102 = (f32[128,640]{1,0:T(8,128)S(1)}, bf16[128,640]{1,0:T(8,128)(2,1)S(1)}) custom-call(bf16[256,640]{1,0:T(8,128)(2,1)S(1)} %get-tuple-element.53.pick, f32[256,640]{1,0:T(8,128)S(1)} %get-tuple-element.54.rest, bf16[1280,640]{1,0:T(8,128)(2,1)S(1)} %copy-done, bf16[80,1280]{1,0:T(8,128)(2,1)S(1)} %shard_map.99.refs_0_, ...), custom_call_target="tpu_custom_call" | custom-call | tf_op jit(solution)/shard_map/pallas_call | solution.py:443
  39.4 1.7 %collective-permute-start.14 = (bf16[128,640]{1,0:T(8,128)(2,1)S(1)}, bf16[128,640]{1,0:T(8,128)(2,1)S(1)}, u32[]{:S(2)}, u32[]{:S(2)}) collective-permute-start(bf16[128,640]{1,0:T(8,128)(2,1)S(1)} %get-tuple-element.56), channel_id=1, source_target_pairs={{0,2},{2,0},{4,6},{6,4},{1,3},{3,1},{5,7},{7,5},{8,10},{10,8},{12,... | collective-permute-start | bytes 491528 | tf_op jit(solution)/shard_map/ppermute | solution.py:48
  41.1 1.5 %collective-permute-start.16 = (bf16[64,640]{1,0:T(8,128)(2,1)S(1)}, bf16[64,640]{1,0:T(8,128)(2,1)S(1)}, u32[]{:S(2)}, u32[]{:S(2)}) collective-permute-start(bf16[64,640]{1,0:T(8,128)(2,1)S(1)} %get-tuple-element.57), channel_id=1, source_target_pairs={{0,6},{2,4},{4,2},{6,0},{1,7},{3,5},{5,3},{7,1},{8,14},{10,12},{12... | collective-permute-start | bytes 245768 | tf_op jit(solution)/shard_map/ppermute | solution.py:48
  42.6 0.2 collective-permute-done.17.other
  42.8 2.2 %collective-permute-start.18 = (bf16[64,640]{1,0:T(8,128)(2,1)S(1)}, bf16[64,640]{1,0:T(8,128)(2,1)S(1)}, u32[]{:S(2)}, u32[]{:S(2)}) collective-permute-start(bf16[64,640]{1,0:T(8,128)(2,1)S(1)} %shard_map.103), channel_id=1, source_target_pairs={{0,6},{2,4},{4,2},{6,0},{1,7},{3,5},{5,3},{7,1},{8,14},{10,12},{12... | collective-permute-start | bytes 245768 | tf_op jit(solution)/shard_map/ppermute | solution.py:48
  45.0 0.5 convert_bitcast_fusion
  45.5 4.0 %collective-permute-done.16.refs_3_ = bf16[64,640]{1,0:T(8,128)(2,1)S(1)} collective-permute-done((bf16[64,640]{1,0:T(8,128)(2,1)S(1)}, bf16[64,640]{1,0:T(8,128)(2,1)S(1)}, u32[]{:S(2)}, u32[]{:S(2)}) %collective-permute-start.16) | collective-permute-done | bytes 81952 | tf_op jit(solution)/shard_map/ppermute | solution.py:48
  49.6 0.0 collective-permute-done.15.refs_2_
  49.6 0.0 collective-permute-done.14.refs_1_
  49.6 1.1 %collective-permute-done.18.refs_4_ = bf16[64,640]{1,0:T(8,128)(2,1)S(1)} collective-permute-done((bf16[64,640]{1,0:T(8,128)(2,1)S(1)}, bf16[64,640]{1,0:T(8,128)(2,1)S(1)}, u32[]{:S(2)}, u32[]{:S(2)}) %collective-permute-start.18) | collective-permute-done | bytes 81952 | tf_op jit(solution)/shard_map/ppermute | solution.py:48
  50.7 0.7 %shard_map.104 = bf16[128,640]{1,0:T(8,128)(2,1)} custom-call(f32[128,640]{1,0:T(8,128)S(1)} %get-tuple-element.55.refs_0_, bf16[128,640]{1,0:T(8,128)(2,1)S(1)} %collective-permute-done.14.refs_1_, bf16[64,640]{1,0:T(8,128)(2,1)S(1)} %collective-permute-done.15.refs_2_, bf16[64,640]{1,0:T(8,128)(2,1)S(1)} %collective-permute-done.16.refs_3_, ...), custom_call_target="tpu_custom_call" | custom-call | tf_op jit(solution)/shard_map/pallas_call | solution.py:470
  (5 shorter events, 0.0 us)
Async XLA Ops:
  0.6 27.1 %copy-start.1 = (bf16[256,640]{1,0:T(8,128)(2,1)S(1)}, bf16[256,640]{1,0:T(8,128)(2,1)}, u32[]{:S(2)}) copy-start(bf16[256,640]{1,0:T(8,128)(2,1)} %refs_4_.1) | copy-start | bytes 983044
  0.6 34.8 %copy-start = (bf16[1280,640]{1,0:T(8,128)(2,1)S(1)}, bf16[1280,640]{1,0:T(8,128)(2,1)}, u32[]{:S(2)}) copy-start(bf16[1280,640]{1,0:T(8,128)(2,1)} %projection.3) | copy-start | bytes 4915204
  0.7 2.0 %collective-permute-start = (bf16[256,640]{1,0:T(8,128)(2,1)}, bf16[256,640]{1,0:T(8,128)(2,1)S(1)}, u32[]{:S(2)}, u32[]{:S(2)}) collective-permute-start(bf16[256,640]{1,0:T(8,128)(2,1)} %refs_4_.1), channel_id=1, source_target_pairs={{0,1},{1,0},{2,3},{3,2},{4,5},{5,4},{6,7},{7,6},{8,9},{9,8},{10,11... | collective-permute-start | bytes 983048 | tf_op jit(solution)/shard_map/ppermute | solution.py:48
  2.9 5.7 %collective-permute-start.1 = (bf16[32,1280]{1,0:T(8,128)(2,1)S(1)}, bf16[32,1280]{1,0:T(8,128)(2,1)S(1)}, u32[]{:S(2)}, u32[]{:S(2)}) collective-permute-start(bf16[32,1280]{1,0:T(8,128)(2,1)S(1)} %get-tuple-element.35), channel_id=1, source_target_pairs={{0,8},{8,0},{16,24},{24,16},{1,9},{9,1},{17,25},{25,17},{2,10},{10... | collective-permute-start | bytes 245768 | tf_op jit(solution)/shard_map/ppermute | solution.py:48
  5.8 5.3 %collective-permute-start.2 = (bf16[32,1280]{1,0:T(8,128)(2,1)S(1)}, bf16[32,1280]{1,0:T(8,128)(2,1)S(1)}, u32[]{:S(2)}, u32[]{:S(2)}) collective-permute-start(bf16[32,1280]{1,0:T(8,128)(2,1)S(1)} %get-tuple-element.36), channel_id=1, source_target_pairs={{0,16},{8,24},{16,0},{24,8},{1,17},{9,25},{17,1},{25,9},{2,18},{10... | collective-permute-start | bytes 245768 | tf_op jit(solution)/shard_map/ppermute | solution.py:48
  7.3 5.3 %collective-permute-start.3 = (bf16[32,1280]{1,0:T(8,128)(2,1)S(1)}, bf16[32,1280]{1,0:T(8,128)(2,1)S(1)}, u32[]{:S(2)}, u32[]{:S(2)}) collective-permute-start(bf16[32,1280]{1,0:T(8,128)(2,1)S(1)} %get-tuple-element.37), channel_id=1, source_target_pairs={{0,24},{8,16},{16,8},{24,0},{1,25},{9,17},{17,9},{25,1},{2,26},{10... | collective-permute-start | bytes 245768 | tf_op jit(solution)/shard_map/ppermute | solution.py:48
  12.9 8.0 %collective-permute-start.4 = (bf16[16,2688]{1,0:T(8,128)(2,1)S(1)}, bf16[16,2688]{1,0:T(8,128)(2,1)S(1)}, u32[]{:S(2)}, u32[]{:S(2)}) collective-permute-start(bf16[16,2688]{1,0:T(8,128)(2,1)S(1)} %get-tuple-element.38), channel_id=1, source_target_pairs={{0,4},{2,6},{4,0},{6,2},{1,5},{3,7},{5,1},{7,3},{8,12},{10,14},{12... | collective-permute-start | bytes 258056 | tf_op jit(solution)/shard_map/ppermute | solution.py:48
  15.5 5.7 %collective-permute-start.5 = (bf16[16,2688]{1,0:T(8,128)(2,1)S(1)}, bf16[16,2688]{1,0:T(8,128)(2,1)S(1)}, u32[]{:S(2)}, u32[]{:S(2)}) collective-permute-start(bf16[16,2688]{1,0:T(8,128)(2,1)S(1)} %get-tuple-element.39), channel_id=1, source_target_pairs={{0,2},{2,0},{4,6},{6,4},{1,3},{3,1},{5,7},{7,5},{8,10},{10,8},{12,... | collective-permute-start | bytes 258056 | tf_op jit(solution)/shard_map/ppermute | solution.py:48
  17.1 6.3 %collective-permute-start.6 = (bf16[16,2688]{1,0:T(8,128)(2,1)S(1)}, bf16[16,2688]{1,0:T(8,128)(2,1)S(1)}, u32[]{:S(2)}, u32[]{:S(2)}) collective-permute-start(bf16[16,2688]{1,0:T(8,128)(2,1)S(1)} %get-tuple-element.40), channel_id=1, source_target_pairs={{0,6},{2,4},{4,2},{6,0},{1,7},{3,5},{5,3},{7,1},{8,14},{10,12},{12... | collective-permute-start | bytes 258056 | tf_op jit(solution)/shard_map/ppermute | solution.py:48
  23.8 7.9 %collective-permute-start.9 = (bf16[80,1280]{1,0:T(8,128)(2,1)S(1)}, bf16[80,1280]{1,0:T(8,128)(2,1)S(1)}, u32[]{:S(2)}, u32[]{:S(2)}) collective-permute-start(bf16[80,1280]{1,0:T(8,128)(2,1)S(1)} %shard_map.99.refs_0_), channel_id=1, source_target_pairs={{0,24},{8,16},{16,8},{24,0},{1,25},{9,17},{17,9},{25,1},{2,26},{10... | collective-permute-start | bytes 614408 | tf_op jit(solution)/shard_map/ppermute | solution.py:48
  24.7 8.7 %collective-permute-start.8 = (bf16[80,1280]{1,0:T(8,128)(2,1)S(1)}, bf16[80,1280]{1,0:T(8,128)(2,1)S(1)}, u32[]{:S(2)}, u32[]{:S(2)}) collective-permute-start(bf16[80,1280]{1,0:T(8,128)(2,1)S(1)} %shard_map.99.refs_0_), channel_id=1, source_target_pairs={{0,16},{8,24},{16,0},{24,8},{1,17},{9,25},{17,1},{25,9},{2,18},{10... | collective-permute-start | bytes 614408 | tf_op jit(solution)/shard_map/ppermute | solution.py:48
  25.8 7.5 %collective-permute-start.7 = (bf16[80,1280]{1,0:T(8,128)(2,1)S(1)}, bf16[80,1280]{1,0:T(8,128)(2,1)S(1)}, u32[]{:S(2)}, u32[]{:S(2)}) collective-permute-start(bf16[80,1280]{1,0:T(8,128)(2,1)S(1)} %shard_map.99.refs_0_), channel_id=1, source_target_pairs={{0,8},{8,0},{16,24},{24,16},{1,9},{9,1},{17,25},{25,17},{2,10},{10... | collective-permute-start | bytes 614408 | tf_op jit(solution)/shard_map/ppermute | solution.py:48
  28.4 5.5 %collective-permute-start.10 = (bf16[80,1280]{1,0:T(8,128)(2,1)S(1)}, bf16[80,1280]{1,0:T(8,128)(2,1)S(1)}, u32[]{:S(2)}, u32[]{:S(2)}) collective-permute-start(bf16[80,1280]{1,0:T(8,128)(2,1)S(1)} %shard_map.99.refs_0_), channel_id=1, source_target_pairs={{0,1},{1,0},{2,3},{3,2},{4,5},{5,4},{6,7},{7,6},{8,9},{9,8},{10,11... | collective-permute-start | bytes 614408 | tf_op jit(solution)/shard_map/ppermute | solution.py:48
  33.4 1.5 %collective-permute-start.11 = (bf16[80,1280]{1,0:T(8,128)(2,1)S(1)}, bf16[80,1280]{1,0:T(8,128)(2,1)S(1)}, u32[]{:S(2)}, u32[]{:S(2)}) collective-permute-start(bf16[80,1280]{1,0:T(8,128)(2,1)S(1)} %collective-permute-done.7.refs_1_), channel_id=1, source_target_pairs={{0,1},{1,0},{2,3},{3,2},{4,5},{5,4},{6,7},{7,6},{8,9},{9,8},{10,11... | collective-permute-start | bytes 614408 | tf_op jit(solution)/shard_map/ppermute | solution.py:48
  33.4 1.7 %collective-permute-start.12 = (bf16[80,1280]{1,0:T(8,128)(2,1)S(1)}, bf16[80,1280]{1,0:T(8,128)(2,1)S(1)}, u32[]{:S(2)}, u32[]{:S(2)}) collective-permute-start(bf16[80,1280]{1,0:T(8,128)(2,1)S(1)} %collective-permute-done.8.refs_2_), channel_id=1, source_target_pairs={{0,1},{1,0},{2,3},{3,2},{4,5},{5,4},{6,7},{7,6},{8,9},{9,8},{10,11... | collective-permute-start | bytes 614408 | tf_op jit(solution)/shard_map/ppermute | solution.py:48
  33.9 1.5 %collective-permute-start.13 = (bf16[80,1280]{1,0:T(8,128)(2,1)S(1)}, bf16[80,1280]{1,0:T(8,128)(2,1)S(1)}, u32[]{:S(2)}, u32[]{:S(2)}) collective-permute-start(bf16[80,1280]{1,0:T(8,128)(2,1)S(1)} %collective-permute-done.9.refs_3_), channel_id=1, source_target_pairs={{0,1},{1,0},{2,3},{3,2},{4,5},{5,4},{6,7},{7,6},{8,9},{9,8},{10,11... | collective-permute-start | bytes 614408 | tf_op jit(solution)/shard_map/ppermute | solution.py:48
  36.5 6.3 %collective-permute-start.17 = (bf16[64,640]{1,0:T(8,128)(2,1)S(1)}, bf16[64,640]{1,0:T(8,128)(2,1)S(1)}, u32[]{:S(2)}, u32[]{:S(2)}) collective-permute-start(bf16[64,640]{1,0:T(8,128)(2,1)S(1)} %get-tuple-element.50), channel_id=1, source_target_pairs={{0,2},{2,0},{4,6},{6,4},{1,3},{3,1},{5,7},{7,5},{8,10},{10,8},{12,... | collective-permute-start | bytes 245768 | tf_op jit(solution)/shard_map/ppermute | solution.py:48
  36.9 12.7 %collective-permute-start.15 = (bf16[64,640]{1,0:T(8,128)(2,1)S(1)}, bf16[64,640]{1,0:T(8,128)(2,1)S(1)}, u32[]{:S(2)}, u32[]{:S(2)}) collective-permute-start(bf16[64,640]{1,0:T(8,128)(2,1)S(1)} %get-tuple-element.49), channel_id=1, source_target_pairs={{0,4},{2,6},{4,0},{6,2},{1,5},{3,7},{5,1},{7,3},{8,12},{10,14},{12... | collective-permute-start | bytes 245768 | tf_op jit(solution)/shard_map/ppermute | solution.py:48
  39.4 10.2 %collective-permute-start.14 = (bf16[128,640]{1,0:T(8,128)(2,1)S(1)}, bf16[128,640]{1,0:T(8,128)(2,1)S(1)}, u32[]{:S(2)}, u32[]{:S(2)}) collective-permute-start(bf16[128,640]{1,0:T(8,128)(2,1)S(1)} %get-tuple-element.56), channel_id=1, source_target_pairs={{0,2},{2,0},{4,6},{6,4},{1,3},{3,1},{5,7},{7,5},{8,10},{10,8},{12,... | collective-permute-start | bytes 491528 | tf_op jit(solution)/shard_map/ppermute | solution.py:48
  41.1 8.5 %collective-permute-start.16 = (bf16[64,640]{1,0:T(8,128)(2,1)S(1)}, bf16[64,640]{1,0:T(8,128)(2,1)S(1)}, u32[]{:S(2)}, u32[]{:S(2)}) collective-permute-start(bf16[64,640]{1,0:T(8,128)(2,1)S(1)} %get-tuple-element.57), channel_id=1, source_target_pairs={{0,6},{2,4},{4,2},{6,0},{1,7},{3,5},{5,3},{7,1},{8,14},{10,12},{12... | collective-permute-start | bytes 245768 | tf_op jit(solution)/shard_map/ppermute | solution.py:48
  42.8 7.9 %collective-permute-start.18 = (bf16[64,640]{1,0:T(8,128)(2,1)S(1)}, bf16[64,640]{1,0:T(8,128)(2,1)S(1)}, u32[]{:S(2)}, u32[]{:S(2)}) collective-permute-start(bf16[64,640]{1,0:T(8,128)(2,1)S(1)} %shard_map.103), channel_id=1, source_target_pairs={{0,6},{2,4},{4,2},{6,0},{1,7},{3,5},{5,3},{7,1},{8,14},{10,12},{12... | collective-permute-start | bytes 245768 | tf_op jit(solution)/shard_map/ppermute | solution.py:48

commit v8 on v6

--- a/solution.py
+++ b/solution.py
@@ -256,15 +256,26 @@
         rest[...] = jnp.dot(own[...], hidden[...], preferred_element_type=F32)
 
 
-def mix_kernel(n_lists, pick, rest, projection, *refs):
-    pieces, outs, held = refs[:n_lists], refs[n_lists:-1], refs[-1]
-    listed, step = pieces[0].shape[0], held.shape[0] // n_lists
+def hold(held, pieces):
+    listed, step = pieces[0].shape[0], held.shape[0] // len(pieces)
     for k, piece in enumerate(pieces):
         rows = piece[0 : min(step, listed), :].astype(F32)
         if step > listed:
             rows = jnp.concatenate([rows, jnp.zeros((step - listed, rows.shape[1]), F32)], axis=0)
         held[k * step : (k + 1) * step, :] = rows.astype(BF16)
-    tokens = jnp.dot(pick[...], held[...], preferred_element_type=F32).astype(BF16)
+
+
+def own_kernel(pick, *refs):
+    pieces, out, held = refs[:-2], refs[-2], refs[-1]
+    hold(held, pieces)
+    out[...] = jnp.dot(pick[:, 0 : held.shape[0]], held[...], preferred_element_type=F32).astype(BF16)
+
+
+def mix_kernel(n_lists, pick, found, rest, projection, *refs):
+    pieces, outs, held = refs[:n_lists], refs[n_lists:-1], refs[-1]
+    hold(held, pieces)
+    other = jnp.dot(pick[:, held.shape[0] :], held[...], preferred_element_type=F32)
+    tokens = (other + found[...].astype(F32)).astype(BF16)
     total = jnp.dot(tokens, projection[...], preferred_element_type=F32) + rest[...]
     first = 0
     for out in outs:
@@ -439,18 +450,26 @@
     )(*(moved[m] for m in ARRIVALS))
     after = lambda x, *ys: lax.optimization_barrier((x, *ys))[0]
     same = [mine] + [swap(mine, "sec", k) for k in range(1, n)]
-    lists = same + [swap(after(x, pick_far, terms), "tp", 1) for x in same]
-    mix = lambda pick, rest, outs: call(
-        functools.partial(mix_kernel, n_class),
-        outs,
-        [VMEM] * (n_class + 3),
-        [VMEM] * len(outs),
-        [pltpu.VMEM((pick.shape[1], width), BF16)],
-    )(pick, rest, projection, *lists)
+    other = [swap(after(x, pick_far, terms), "tp", 1) for x in same]
+
+    def held_lists(pick):
+        return [pltpu.VMEM((pick.shape[1] // n_tp, width), BF16)]
+
+    def own_part(pick):
+        shapes = shape((half, width), BF16), [VMEM] * (n + 1), VMEM, held_lists(pick)
+        return call(own_kernel, *shapes)(pick, *same)
+
+    def mix(pick, found, rest, outs):
+        return call(
+            functools.partial(mix_kernel, n), outs, [VMEM] * (n + 4), [VMEM] * len(outs), held_lists(pick)
+        )(pick, found, rest, projection, *other)
+
+    found_far, found_near = own_part(pick_far), own_part(pick_near)
     part = tok // 2
     joined = n // 2
     far = mix(
-        pick_far,
+        after(pick_far, found_near),
+        found_far,
         rest_far,
         [shape((part, cols), F32 if m % 2 and h else BF16) for m in range(joined) for h in range(2)],
     )
@@ -461,7 +480,7 @@
     ]
     passed = [swap(x, "seq", joined + m + 1) for m, x in zip(range(0, joined, 2), sums, strict=True)]
     near = mix(
-        after(pick_near, *far), rest_near, [shape((tok, cols), F32)] + [shape((tok, cols), BF16)] * (joined - 1)
+        after(pick_near, *far), found_near, rest_near, [shape((tok, cols), F32)] + [shape((tok, cols), BF16)] * (joined - 1)
     )
     direct = [swap(far[0], "seq", joined)] + [
         swap(after(far[2 * m], *near), "seq", joined + m) for m in range(1, joined)

time: 50.6 us -> 50.3 us (level)
  waiting for transfers between devices: 22.5 us -> 20.8 us
  starting transfers between devices: 20.6 us -> 21.2 us
  Pallas kernels: 6.13 us -> 6.64 us
    ppermute x19, waiting for transfers between devices: 22.5 us -> 20.8 us  [swap(): return lax.ppermute(x, axis, [(i, i ^ k) for i in range(n)])]
    ppermute x19, starting transfers between devices: 20.6 us -> 21.2 us  [swap(): return lax.ppermute(x, axis, [(i, i ^ k) for i in range(n)])]
    pallas_call x2 -> x4, Pallas kernels: 2.22 us -> 2.76 us  [the longest x2 1.94 us: mix(): call(functools.partial(mix_kernel, n), outs, [VMEM] * (n + 4), [VMEM] * l...]
  transfers between devices with their start and end apart: 19 -> 19, of which waited for: 15 -> 12; matrix products, arithmetic and copies ran while one was open for 1% -> 1% of each run, Pallas kernels for 7% -> 8%
where the time goes in v8:
time: 50.3 us; the launch traced here: 50.2 us
  starting transfers between devices  21.2 us (42%)
  waiting for transfers between devices  20.8 us (41%)
  Pallas kernels  6.64 us (13%)
  between operations  0.75 us (1%)
  other arithmetic  0.51 us (1%)
    ppermute x19, starting transfers between devices, swap(): return lax.ppermute(x, axis, [(i, i ^ k) for i in range(n)])  21.2 us
    ppermute x19, waiting for transfers between devices, swap(): return lax.ppermute(x, axis, [(i, i ^ k) for i in range(n)])  20.8 us
    pallas_call x2, Pallas kernels, mix(): call(functools.partial(mix_kernel, n), outs, [VMEM] * (n + 4), [VMEM] * l...  1.94 us
    pallas_call x1, Pallas kernels, shards_in_place(): call(functools.partial(early_kernel, n, n_tp), [shape((rows // n_tp, rows...  1.27 us
  transfers between devices with their start and end apart: 19, of which 12 were waited for; matrix products, arithmetic and copies ran while one was open for 1% of the time, Pallas kernels for 8%

profile of v8, /device:TPU:0, one launch (start us, length us, event | category | flops | bytes accessed | tf_op | source)
XLA Modules:
  0.0 50.2 jit_solution(2559604914317181350)
XLA Ops:
  0.6 0.5 %collective-permute-start = (bf16[256,640]{1,0:T(8,128)(2,1)}, bf16[256,640]{1,0:T(8,128)(2,1)S(1)}, u32[]{:S(2)}, u32[]{:S(2)}) collective-permute-start(bf16[256,640]{1,0:T(8,128)(2,1)} %refs_4_.1), channel_id=1, source_target_pairs={{0,1},{1,0},{2,3},{3,2},{4,5},{5,4},{6,7},{7,6},{8,9},{9,8},{10,11... | collective-permute-start | bytes 983048 | tf_op jit(solution)/shard_map/ppermute | solution.py:48
  1.2 1.3 %shard_map.95 = (bf16[128,256]{1,0:T(8,128)(2,1)S(1)}, bf16[128,640]{1,0:T(8,128)(2,1)S(1)}, bf16[16,128]{1,0:T(8,128)(2,1)S(1)}, f32[1,5120]{1,0:T(1,128)S(1)}) custom-call(bf16[256,640]{1,0:T(8,128)(2,1)} %refs_4_.1, s32[4]{0:T(128)} %lengths.1, s32[4]{0:T(128)} %group_of.1, s32[4]{0:T(128)} %rewards.1, f32[2,128]{1,0:T(2,128)} %bitcast.6, ...), custom_call_target="tpu_custom_call" | custom-call | tf_op jit(solution)/shard_map/pallas_call | solution.py:379
  2.4 0.2 collective-permute-done.sibling
  2.6 0.2 shard_map.96
  2.8 2.9 %collective-permute-start.1 = (bf16[32,1280]{1,0:T(8,128)(2,1)S(1)}, bf16[32,1280]{1,0:T(8,128)(2,1)S(1)}, u32[]{:S(2)}, u32[]{:S(2)}) collective-permute-start(bf16[32,1280]{1,0:T(8,128)(2,1)S(1)} %get-tuple-element.36), channel_id=1, source_target_pairs={{0,8},{8,0},{16,24},{24,16},{1,9},{9,1},{17,25},{25,17},{2,10},{10... | collective-permute-start | bytes 245768 | tf_op jit(solution)/shard_map/ppermute | solution.py:48
  5.8 1.5 %collective-permute-start.2 = (bf16[32,1280]{1,0:T(8,128)(2,1)S(1)}, bf16[32,1280]{1,0:T(8,128)(2,1)S(1)}, u32[]{:S(2)}, u32[]{:S(2)}) collective-permute-start(bf16[32,1280]{1,0:T(8,128)(2,1)S(1)} %get-tuple-element.37), channel_id=1, source_target_pairs={{0,16},{8,24},{16,0},{24,8},{1,17},{9,25},{17,1},{25,9},{2,18},{10... | collective-permute-start | bytes 245768 | tf_op jit(solution)/shard_map/ppermute | solution.py:48
  7.3 0.0 collective-permute-start.3
  7.3 1.2 %collective-permute-done.1.refs_1_ = bf16[32,1280]{1,0:T(8,128)(2,1)S(1)} collective-permute-done((bf16[32,1280]{1,0:T(8,128)(2,1)S(1)}, bf16[32,1280]{1,0:T(8,128)(2,1)S(1)}, u32[]{:S(2)}, u32[]{:S(2)}) %collective-permute-start.1) | collective-permute-done | bytes 81952 | tf_op jit(solution)/shard_map/ppermute | solution.py:48
  8.5 2.5 %collective-permute-done.2.refs_2_ = bf16[32,1280]{1,0:T(8,128)(2,1)S(1)} collective-permute-done((bf16[32,1280]{1,0:T(8,128)(2,1)S(1)}, bf16[32,1280]{1,0:T(8,128)(2,1)S(1)}, u32[]{:S(2)}, u32[]{:S(2)}) %collective-permute-start.2) | collective-permute-done | bytes 81952 | tf_op jit(solution)/shard_map/ppermute | solution.py:48
  11.0 1.6 %collective-permute-done.3.refs_3_ = bf16[32,1280]{1,0:T(8,128)(2,1)S(1)} collective-permute-done((bf16[32,1280]{1,0:T(8,128)(2,1)S(1)}, bf16[32,1280]{1,0:T(8,128)(2,1)S(1)}, u32[]{:S(2)}, u32[]{:S(2)}) %collective-permute-start.3) | collective-permute-done | bytes 81952 | tf_op jit(solution)/shard_map/ppermute | solution.py:48
  12.6 0.2 shard_map.97
  12.9 2.7 %collective-permute-start.4 = (bf16[16,2688]{1,0:T(8,128)(2,1)S(1)}, bf16[16,2688]{1,0:T(8,128)(2,1)S(1)}, u32[]{:S(2)}, u32[]{:S(2)}) collective-permute-start(bf16[16,2688]{1,0:T(8,128)(2,1)S(1)} %get-tuple-element.39), channel_id=1, source_target_pairs={{0,4},{2,6},{4,0},{6,2},{1,5},{3,7},{5,1},{7,3},{8,12},{10,14},{12... | collective-permute-start | bytes 258056 | tf_op jit(solution)/shard_map/ppermute | solution.py:48
  15.5 1.6 %collective-permute-start.5 = (bf16[16,2688]{1,0:T(8,128)(2,1)S(1)}, bf16[16,2688]{1,0:T(8,128)(2,1)S(1)}, u32[]{:S(2)}, u32[]{:S(2)}) collective-permute-start(bf16[16,2688]{1,0:T(8,128)(2,1)S(1)} %get-tuple-element.40), channel_id=1, source_target_pairs={{0,2},{2,0},{4,6},{6,4},{1,3},{3,1},{5,7},{7,5},{8,10},{10,8},{12,... | collective-permute-start | bytes 258056 | tf_op jit(solution)/shard_map/ppermute | solution.py:48
  17.1 0.2 collective-permute-start.6
  17.3 3.5 %collective-permute-done.4.refs_0_ = bf16[16,2688]{1,0:T(8,128)(2,1)S(1)} collective-permute-done((bf16[16,2688]{1,0:T(8,128)(2,1)S(1)}, bf16[16,2688]{1,0:T(8,128)(2,1)S(1)}, u32[]{:S(2)}, u32[]{:S(2)}) %collective-permute-start.4) | collective-permute-done | bytes 86048 | tf_op jit(solution)/shard_map/ppermute | solution.py:48
  20.9 0.4 collective-permute-done.5.refs_1_
  21.3 2.1 %collective-permute-done.6.refs_2_ = bf16[16,2688]{1,0:T(8,128)(2,1)S(1)} collective-permute-done((bf16[16,2688]{1,0:T(8,128)(2,1)S(1)}, bf16[16,2688]{1,0:T(8,128)(2,1)S(1)}, u32[]{:S(2)}, u32[]{:S(2)}) %collective-permute-start.6) | collective-permute-done | bytes 86048 | tf_op jit(solution)/shard_map/ppermute | solution.py:48
  23.4 0.4 shard_map.99.refs_0_
  23.8 0.6 %collective-permute-start.7 = (bf16[72,1280]{1,0:T(8,128)(2,1)S(1)}, bf16[72,1280]{1,0:T(8,128)(2,1)S(1)}, u32[]{:S(2)}, u32[]{:S(2)}) collective-permute-start(bf16[72,1280]{1,0:T(8,128)(2,1)S(1)} %shard_map.99.refs_0_), channel_id=1, source_target_pairs={{0,8},{8,0},{16,24},{24,16},{1,9},{9,1},{17,25},{25,17},{2,10},{10... | collective-permute-start | bytes 552968 | tf_op jit(solution)/shard_map/ppermute | solution.py:48
  24.4 0.9 %collective-permute-start.8 = (bf16[72,1280]{1,0:T(8,128)(2,1)S(1)}, bf16[72,1280]{1,0:T(8,128)(2,1)S(1)}, u32[]{:S(2)}, u32[]{:S(2)}) collective-permute-start(bf16[72,1280]{1,0:T(8,128)(2,1)S(1)} %shard_map.99.refs_0_), channel_id=1, source_target_pairs={{0,16},{8,24},{16,0},{24,8},{1,17},{9,25},{17,1},{25,9},{2,18},{10... | collective-permute-start | bytes 552968 | tf_op jit(solution)/shard_map/ppermute | solution.py:48
  25.2 2.1 %collective-permute-start.9 = (bf16[72,1280]{1,0:T(8,128)(2,1)S(1)}, bf16[72,1280]{1,0:T(8,128)(2,1)S(1)}, u32[]{:S(2)}, u32[]{:S(2)}) collective-permute-start(bf16[72,1280]{1,0:T(8,128)(2,1)S(1)} %shard_map.99.refs_0_), channel_id=1, source_target_pairs={{0,24},{8,16},{16,8},{24,0},{1,25},{9,17},{17,9},{25,1},{2,26},{10... | collective-permute-start | bytes 552968 | tf_op jit(solution)/shard_map/ppermute | solution.py:48
  27.3 0.6 %shard_map.98 = (bf16[256,384]{1,0:T(8,128)(2,1)S(1)}, bf16[256,640]{1,0:T(8,128)(2,1)S(1)}, f32[256,640]{1,0:T(8,128)S(1)}, f32[256,640]{1,0:T(8,128)S(1)}) custom-call(bf16[16,2688]{1,0:T(8,128)(2,1)S(1)} %collective-permute-done.4.refs_0_, bf16[16,2688]{1,0:T(8,128)(2,1)S(1)} %collective-permute-done.5.refs_1_, ...), custom_call_target="tpu_custom_call" | custom-call | tf_op jit(solution)/shard_map/pallas_call | solution.py:432
  28.0 0.4 shard_map.102
  28.4 0.1 collective-permute-start.10
  28.4 1.5 %collective-permute-done.7.refs_1_ = bf16[72,1280]{1,0:T(8,128)(2,1)S(1)} collective-permute-done((bf16[72,1280]{1,0:T(8,128)(2,1)S(1)}, bf16[72,1280]{1,0:T(8,128)(2,1)S(1)}, u32[]{:S(2)}, u32[]{:S(2)}) %collective-permute-start.7) | collective-permute-done | bytes 184352 | tf_op jit(solution)/shard_map/ppermute | solution.py:48
  30.0 0.0 collective-permute-start.11
  30.0 2.3 %collective-permute-done.8.refs_2_ = bf16[72,1280]{1,0:T(8,128)(2,1)S(1)} collective-permute-done((bf16[72,1280]{1,0:T(8,128)(2,1)S(1)}, bf16[72,1280]{1,0:T(8,128)(2,1)S(1)}, u32[]{:S(2)}, u32[]{:S(2)}) %collective-permute-start.8) | collective-permute-done | bytes 184352 | tf_op jit(solution)/shard_map/ppermute | solution.py:48
  32.2 0.0 collective-permute-start.12
  32.2 0.0 collective-permute-done.9.refs_3_
  32.2 0.5 %collective-permute-start.13 = (bf16[72,1280]{1,0:T(8,128)(2,1)S(1)}, bf16[72,1280]{1,0:T(8,128)(2,1)S(1)}, u32[]{:S(2)}, u32[]{:S(2)}) collective-permute-start(bf16[72,1280]{1,0:T(8,128)(2,1)S(1)} %collective-permute-done.9.refs_3_), channel_id=1, source_target_pairs={{0,1},{1,0},{2,3},{3,2},{4,5},{5,4},{6,7},{7,6},{8,9},{9,8},{10,11... | collective-permute-start | bytes 552968 | tf_op jit(solution)/shard_map/ppermute | solution.py:48
  32.7 0.5 shard_map.100.found
  33.2 0.3 shard_map.101.found
  33.6 0.0 collective-permute-done.11.refs_1_
  33.6 0.0 collective-permute-done.12.refs_2_
  33.7 0.3 collective-permute-done.13.refs_3_
  33.9 0.3 copy-done
  34.2 0.9 %shard_map.103 = (bf16[64,640]{1,0:T(8,128)(2,1)S(1)}, bf16[64,640]{1,0:T(8,128)(2,1)S(1)}, bf16[64,640]{1,0:T(8,128)(2,1)S(1)}, f32[64,640]{1,0:T(8,128)S(1)}) custom-call(bf16[256,384]{1,0:T(8,128)(2,1)S(1)} %get-tuple-element.45.pick, bf16[256,1280]{1,0:T(8,128)(2,1)S(1)} %shard_map.101.found, f32[256,640]{1,0:T(8,128)S(1)} %get-tuple-element.46.rest, ...), custom_call_target="tpu_custom_call" | custom-call | tf_op jit(solution)/shard_map/pallas_call | solution.py:463
  35.1 0.6 %collective-permute-start.17 = (bf16[64,640]{1,0:T(8,128)(2,1)S(1)}, bf16[64,640]{1,0:T(8,128)(2,1)S(1)}, u32[]{:S(2)}, u32[]{:S(2)}) collective-permute-start(bf16[64,640]{1,0:T(8,128)(2,1)S(1)} %get-tuple-element.52), channel_id=1, source_target_pairs={{0,2},{2,0},{4,6},{6,4},{1,3},{3,1},{5,7},{7,5},{8,10},{10,8},{12,... | collective-permute-start | bytes 245768 | tf_op jit(solution)/shard_map/ppermute | solution.py:48
  35.7 1.6 %collective-permute-start.15 = (bf16[64,640]{1,0:T(8,128)(2,1)S(1)}, bf16[64,640]{1,0:T(8,128)(2,1)S(1)}, u32[]{:S(2)}, u32[]{:S(2)}) collective-permute-start(bf16[64,640]{1,0:T(8,128)(2,1)S(1)} %get-tuple-element.51), channel_id=1, source_target_pairs={{0,4},{2,6},{4,0},{6,2},{1,5},{3,7},{5,1},{7,3},{8,12},{10,14},{12... | collective-permute-start | bytes 245768 | tf_op jit(solution)/shard_map/ppermute | solution.py:48
  37.3 1.1 %shard_map.104 = (f32[128,640]{1,0:T(8,128)S(1)}, bf16[128,640]{1,0:T(8,128)(2,1)S(1)}) custom-call(bf16[256,640]{1,0:T(8,128)(2,1)S(1)} %get-tuple-element.55.pick, bf16[256,1280]{1,0:T(8,128)(2,1)S(1)} %shard_map.100.found, f32[256,640]{1,0:T(8,128)S(1)} %get-tuple-element.56.rest, bf16[1280,640]{1,0:T(8,128)(2,1)S(1)} %copy-done, ...), custom_call_target="tpu_custom_call" | custom-call | tf_op jit(solution)/shard_map/pallas_call | solution.py:463
  38.4 1.5 %collective-permute-start.14 = (bf16[128,640]{1,0:T(8,128)(2,1)S(1)}, bf16[128,640]{1,0:T(8,128)(2,1)S(1)}, u32[]{:S(2)}, u32[]{:S(2)}) collective-permute-start(bf16[128,640]{1,0:T(8,128)(2,1)S(1)} %get-tuple-element.58), channel_id=1, source_target_pairs={{0,2},{2,0},{4,6},{6,4},{1,3},{3,1},{5,7},{7,5},{8,10},{10,8},{12,... | collective-permute-start | bytes 491528 | tf_op jit(solution)/shard_map/ppermute | solution.py:48
  39.8 1.3 %collective-permute-start.16 = (bf16[64,640]{1,0:T(8,128)(2,1)S(1)}, bf16[64,640]{1,0:T(8,128)(2,1)S(1)}, u32[]{:S(2)}, u32[]{:S(2)}) collective-permute-start(bf16[64,640]{1,0:T(8,128)(2,1)S(1)} %get-tuple-element.59), channel_id=1, source_target_pairs={{0,6},{2,4},{4,2},{6,0},{1,7},{3,5},{5,3},{7,1},{8,14},{10,12},{12... | collective-permute-start | bytes 245768 | tf_op jit(solution)/shard_map/ppermute | solution.py:48
  41.2 2.5 %collective-permute-start.18 = (bf16[64,640]{1,0:T(8,128)(2,1)S(1)}, bf16[64,640]{1,0:T(8,128)(2,1)S(1)}, u32[]{:S(2)}, u32[]{:S(2)}) collective-permute-start(bf16[64,640]{1,0:T(8,128)(2,1)S(1)} %shard_map.105), channel_id=1, source_target_pairs={{0,6},{2,4},{4,2},{6,0},{1,7},{3,5},{5,3},{7,1},{8,14},{10,12},{12... | collective-permute-start | bytes 245768 | tf_op jit(solution)/shard_map/ppermute | solution.py:48
  43.7 0.5 %convert_bitcast_fusion = bf16[128,2]{0,1:T(2,128)(2,1)} fusion(f32[2,128]{1,0:T(2,128)S(1)} %shard_map.102), kind=kLoop, calls=%fused_computation | loop fusion | flops 256 | bytes 1536 | tf_op jit(solution)/shard_map/transpose | solution.py:495
  44.3 4.2 %collective-permute-done.16.refs_3_ = bf16[64,640]{1,0:T(8,128)(2,1)S(1)} collective-permute-done((bf16[64,640]{1,0:T(8,128)(2,1)S(1)}, bf16[64,640]{1,0:T(8,128)(2,1)S(1)}, u32[]{:S(2)}, u32[]{:S(2)}) %collective-permute-start.16) | collective-permute-done | bytes 81952 | tf_op jit(solution)/shard_map/ppermute | solution.py:48
  48.4 0.0 collective-permute-done.14.refs_1_
  48.4 1.0 %collective-permute-done.18.refs_4_ = bf16[64,640]{1,0:T(8,128)(2,1)S(1)} collective-permute-done((bf16[64,640]{1,0:T(8,128)(2,1)S(1)}, bf16[64,640]{1,0:T(8,128)(2,1)S(1)}, u32[]{:S(2)}, u32[]{:S(2)}) %collective-permute-start.18) | collective-permute-done | bytes 81952 | tf_op jit(solution)/shard_map/ppermute | solution.py:48
  49.4 0.7 %shard_map.106 = bf16[128,640]{1,0:T(8,128)(2,1)} custom-call(f32[128,640]{1,0:T(8,128)S(1)} %get-tuple-element.57.refs_0_, bf16[128,640]{1,0:T(8,128)(2,1)S(1)} %collective-permute-done.14.refs_1_, bf16[64,640]{1,0:T(8,128)(2,1)S(1)} %collective-permute-done.15.refs_2_, bf16[64,640]{1,0:T(8,128)(2,1)S(1)} %collective-permute-done.16.refs_3_, ...), custom_call_target="tpu_custom_call" | custom-call | tf_op jit(solution)/shard_map/pallas_call | solution.py:489
  (7 shorter events, 0.0 us)
Async XLA Ops:
  0.6 26.7 %copy-start.1 = (bf16[256,640]{1,0:T(8,128)(2,1)S(1)}, bf16[256,640]{1,0:T(8,128)(2,1)}, u32[]{:S(2)}) copy-start(bf16[256,640]{1,0:T(8,128)(2,1)} %refs_4_.1) | copy-start | bytes 983044
  0.6 2.0 %collective-permute-start = (bf16[256,640]{1,0:T(8,128)(2,1)}, bf16[256,640]{1,0:T(8,128)(2,1)S(1)}, u32[]{:S(2)}, u32[]{:S(2)}) collective-permute-start(bf16[256,640]{1,0:T(8,128)(2,1)} %refs_4_.1), channel_id=1, source_target_pairs={{0,1},{1,0},{2,3},{3,2},{4,5},{5,4},{6,7},{7,6},{8,9},{9,8},{10,11... | collective-permute-start | bytes 983048 | tf_op jit(solution)/shard_map/ppermute | solution.py:48
  2.8 5.7 %collective-permute-start.1 = (bf16[32,1280]{1,0:T(8,128)(2,1)S(1)}, bf16[32,1280]{1,0:T(8,128)(2,1)S(1)}, u32[]{:S(2)}, u32[]{:S(2)}) collective-permute-start(bf16[32,1280]{1,0:T(8,128)(2,1)S(1)} %get-tuple-element.36), channel_id=1, source_target_pairs={{0,8},{8,0},{16,24},{24,16},{1,9},{9,1},{17,25},{25,17},{2,10},{10... | collective-permute-start | bytes 245768 | tf_op jit(solution)/shard_map/ppermute | solution.py:48
  5.8 5.3 %collective-permute-start.2 = (bf16[32,1280]{1,0:T(8,128)(2,1)S(1)}, bf16[32,1280]{1,0:T(8,128)(2,1)S(1)}, u32[]{:S(2)}, u32[]{:S(2)}) collective-permute-start(bf16[32,1280]{1,0:T(8,128)(2,1)S(1)} %get-tuple-element.37), channel_id=1, source_target_pairs={{0,16},{8,24},{16,0},{24,8},{1,17},{9,25},{17,1},{25,9},{2,18},{10... | collective-permute-start | bytes 245768 | tf_op jit(solution)/shard_map/ppermute | solution.py:48
  7.3 5.3 %collective-permute-start.3 = (bf16[32,1280]{1,0:T(8,128)(2,1)S(1)}, bf16[32,1280]{1,0:T(8,128)(2,1)S(1)}, u32[]{:S(2)}, u32[]{:S(2)}) collective-permute-start(bf16[32,1280]{1,0:T(8,128)(2,1)S(1)} %get-tuple-element.38), channel_id=1, source_target_pairs={{0,24},{8,16},{16,8},{24,0},{1,25},{9,17},{17,9},{25,1},{2,26},{10... | collective-permute-start | bytes 245768 | tf_op jit(solution)/shard_map/ppermute | solution.py:48
  12.9 8.0 %collective-permute-start.4 = (bf16[16,2688]{1,0:T(8,128)(2,1)S(1)}, bf16[16,2688]{1,0:T(8,128)(2,1)S(1)}, u32[]{:S(2)}, u32[]{:S(2)}) collective-permute-start(bf16[16,2688]{1,0:T(8,128)(2,1)S(1)} %get-tuple-element.39), channel_id=1, source_target_pairs={{0,4},{2,6},{4,0},{6,2},{1,5},{3,7},{5,1},{7,3},{8,12},{10,14},{12... | collective-permute-start | bytes 258056 | tf_op jit(solution)/shard_map/ppermute | solution.py:48
  15.5 5.7 %collective-permute-start.5 = (bf16[16,2688]{1,0:T(8,128)(2,1)S(1)}, bf16[16,2688]{1,0:T(8,128)(2,1)S(1)}, u32[]{:S(2)}, u32[]{:S(2)}) collective-permute-start(bf16[16,2688]{1,0:T(8,128)(2,1)S(1)} %get-tuple-element.40), channel_id=1, source_target_pairs={{0,2},{2,0},{4,6},{6,4},{1,3},{3,1},{5,7},{7,5},{8,10},{10,8},{12,... | collective-permute-start | bytes 258056 | tf_op jit(solution)/shard_map/ppermute | solution.py:48
  17.1 6.3 %collective-permute-start.6 = (bf16[16,2688]{1,0:T(8,128)(2,1)S(1)}, bf16[16,2688]{1,0:T(8,128)(2,1)S(1)}, u32[]{:S(2)}, u32[]{:S(2)}) collective-permute-start(bf16[16,2688]{1,0:T(8,128)(2,1)S(1)} %get-tuple-element.41), channel_id=1, source_target_pairs={{0,6},{2,4},{4,2},{6,0},{1,7},{3,5},{5,3},{7,1},{8,14},{10,12},{12... | collective-permute-start | bytes 258056 | tf_op jit(solution)/shard_map/ppermute | solution.py:48
  23.8 6.2 %collective-permute-start.7 = (bf16[72,1280]{1,0:T(8,128)(2,1)S(1)}, bf16[72,1280]{1,0:T(8,128)(2,1)S(1)}, u32[]{:S(2)}, u32[]{:S(2)}) collective-permute-start(bf16[72,1280]{1,0:T(8,128)(2,1)S(1)} %shard_map.99.refs_0_), channel_id=1, source_target_pairs={{0,8},{8,0},{16,24},{24,16},{1,9},{9,1},{17,25},{25,17},{2,10},{10... | collective-permute-start | bytes 552968 | tf_op jit(solution)/shard_map/ppermute | solution.py:48
  24.4 7.9 %collective-permute-start.8 = (bf16[72,1280]{1,0:T(8,128)(2,1)S(1)}, bf16[72,1280]{1,0:T(8,128)(2,1)S(1)}, u32[]{:S(2)}, u32[]{:S(2)}) collective-permute-start(bf16[72,1280]{1,0:T(8,128)(2,1)S(1)} %shard_map.99.refs_0_), channel_id=1, source_target_pairs={{0,16},{8,24},{16,0},{24,8},{1,17},{9,25},{17,1},{25,9},{2,18},{10... | collective-permute-start | bytes 552968 | tf_op jit(solution)/shard_map/ppermute | solution.py:48
  25.2 7.0 %collective-permute-start.9 = (bf16[72,1280]{1,0:T(8,128)(2,1)S(1)}, bf16[72,1280]{1,0:T(8,128)(2,1)S(1)}, u32[]{:S(2)}, u32[]{:S(2)}) collective-permute-start(bf16[72,1280]{1,0:T(8,128)(2,1)S(1)} %shard_map.99.refs_0_), channel_id=1, source_target_pairs={{0,24},{8,16},{16,8},{24,0},{1,25},{9,17},{17,9},{25,1},{2,26},{10... | collective-permute-start | bytes 552968 | tf_op jit(solution)/shard_map/ppermute | solution.py:48
  28.4 5.2 %collective-permute-start.10 = (bf16[72,1280]{1,0:T(8,128)(2,1)S(1)}, bf16[72,1280]{1,0:T(8,128)(2,1)S(1)}, u32[]{:S(2)}, u32[]{:S(2)}) collective-permute-start(bf16[72,1280]{1,0:T(8,128)(2,1)S(1)} %shard_map.99.refs_0_), channel_id=1, source_target_pairs={{0,1},{1,0},{2,3},{3,2},{4,5},{5,4},{6,7},{7,6},{8,9},{9,8},{10,11... | collective-permute-start | bytes 552968 | tf_op jit(solution)/shard_map/ppermute | solution.py:48
  30.0 3.6 %collective-permute-start.11 = (bf16[72,1280]{1,0:T(8,128)(2,1)S(1)}, bf16[72,1280]{1,0:T(8,128)(2,1)S(1)}, u32[]{:S(2)}, u32[]{:S(2)}) collective-permute-start(bf16[72,1280]{1,0:T(8,128)(2,1)S(1)} %collective-permute-done.7.refs_1_), channel_id=1, source_target_pairs={{0,1},{1,0},{2,3},{3,2},{4,5},{5,4},{6,7},{7,6},{8,9},{9,8},{10,11... | collective-permute-start | bytes 552968 | tf_op jit(solution)/shard_map/ppermute | solution.py:48
  32.2 1.4 %collective-permute-start.12 = (bf16[72,1280]{1,0:T(8,128)(2,1)S(1)}, bf16[72,1280]{1,0:T(8,128)(2,1)S(1)}, u32[]{:S(2)}, u32[]{:S(2)}) collective-permute-start(bf16[72,1280]{1,0:T(8,128)(2,1)S(1)} %collective-permute-done.8.refs_2_), channel_id=1, source_target_pairs={{0,1},{1,0},{2,3},{3,2},{4,5},{5,4},{6,7},{7,6},{8,9},{9,8},{10,11... | collective-permute-start | bytes 552968 | tf_op jit(solution)/shard_map/ppermute | solution.py:48
  32.2 1.7 %collective-permute-start.13 = (bf16[72,1280]{1,0:T(8,128)(2,1)S(1)}, bf16[72,1280]{1,0:T(8,128)(2,1)S(1)}, u32[]{:S(2)}, u32[]{:S(2)}) collective-permute-start(bf16[72,1280]{1,0:T(8,128)(2,1)S(1)} %collective-permute-done.9.refs_3_), channel_id=1, source_target_pairs={{0,1},{1,0},{2,3},{3,2},{4,5},{5,4},{6,7},{7,6},{8,9},{9,8},{10,11... | collective-permute-start | bytes 552968 | tf_op jit(solution)/shard_map/ppermute | solution.py:48
  32.7 1.4 %copy-start = (bf16[1280,640]{1,0:T(8,128)(2,1)S(1)}, bf16[1280,640]{1,0:T(8,128)(2,1)}, u32[]{:S(2)}) copy-start(bf16[1280,640]{1,0:T(8,128)(2,1)} %projection.3) | copy-start | bytes 4915204
  35.1 6.1 %collective-permute-start.17 = (bf16[64,640]{1,0:T(8,128)(2,1)S(1)}, bf16[64,640]{1,0:T(8,128)(2,1)S(1)}, u32[]{:S(2)}, u32[]{:S(2)}) collective-permute-start(bf16[64,640]{1,0:T(8,128)(2,1)S(1)} %get-tuple-element.52), channel_id=1, source_target_pairs={{0,2},{2,0},{4,6},{6,4},{1,3},{3,1},{5,7},{7,5},{8,10},{10,8},{12,... | collective-permute-start | bytes 245768 | tf_op jit(solution)/shard_map/ppermute | solution.py:48
  35.7 8.6 %collective-permute-start.15 = (bf16[64,640]{1,0:T(8,128)(2,1)S(1)}, bf16[64,640]{1,0:T(8,128)(2,1)S(1)}, u32[]{:S(2)}, u32[]{:S(2)}) collective-permute-start(bf16[64,640]{1,0:T(8,128)(2,1)S(1)} %get-tuple-element.51), channel_id=1, source_target_pairs={{0,4},{2,6},{4,0},{6,2},{1,5},{3,7},{5,1},{7,3},{8,12},{10,14},{12... | collective-permute-start | bytes 245768 | tf_op jit(solution)/shard_map/ppermute | solution.py:48
  38.4 10.0 %collective-permute-start.14 = (bf16[128,640]{1,0:T(8,128)(2,1)S(1)}, bf16[128,640]{1,0:T(8,128)(2,1)S(1)}, u32[]{:S(2)}, u32[]{:S(2)}) collective-permute-start(bf16[128,640]{1,0:T(8,128)(2,1)S(1)} %get-tuple-element.58), channel_id=1, source_target_pairs={{0,2},{2,0},{4,6},{6,4},{1,3},{3,1},{5,7},{7,5},{8,10},{10,8},{12,... | collective-permute-start | bytes 491528 | tf_op jit(solution)/shard_map/ppermute | solution.py:48
  39.8 8.6 %collective-permute-start.16 = (bf16[64,640]{1,0:T(8,128)(2,1)S(1)}, bf16[64,640]{1,0:T(8,128)(2,1)S(1)}, u32[]{:S(2)}, u32[]{:S(2)}) collective-permute-start(bf16[64,640]{1,0:T(8,128)(2,1)S(1)} %get-tuple-element.59), channel_id=1, source_target_pairs={{0,6},{2,4},{4,2},{6,0},{1,7},{3,5},{5,3},{7,1},{8,14},{10,12},{12... | collective-permute-start | bytes 245768 | tf_op jit(solution)/shard_map/ppermute | solution.py:48
  41.2 8.2 %collective-permute-start.18 = (bf16[64,640]{1,0:T(8,128)(2,1)S(1)}, bf16[64,640]{1,0:T(8,128)(2,1)S(1)}, u32[]{:S(2)}, u32[]{:S(2)}) collective-permute-start(bf16[64,640]{1,0:T(8,128)(2,1)S(1)} %shard_map.105), channel_id=1, source_target_pairs={{0,6},{2,4},{4,2},{6,0},{1,7},{3,5},{5,3},{7,1},{8,14},{10,12},{12... | collective-permute-start | bytes 245768 | tf_op jit(solution)/shard_map/ppermute | solution.py:48

commit v9 on v8

--- a/solution.py
+++ b/solution.py
@@ -220,6 +220,7 @@
 
 def index_kernel(n, n_class, n_resp, tok, row, *refs):
     moved, hidden = in_order(ARRIVALS, refs[:n]), refs[n]
+    refs = refs[: n + 1] + refs[n + 2 :]
     pick_far, pick_near, rest_far, rest_near, counts, lens, own = refs[n + 1 :]
     a = lax.axis_index("sec")
     s = lax.axis_index("seq")
@@ -437,10 +438,10 @@
             shape((half, cols), F32),
             shape((half, cols), F32),
         ],
-        [VMEM] * (n + 1),
+        [VMEM] * (n + 2),
         [VMEM] * 4,
         [pltpu.SMEM((n,), I32), pltpu.SMEM((n_resp,), I32), pltpu.VMEM((half, rows), BF16)],
-    )(*(moved[m] for m in ARRIVALS), hidden)
+    )(*(moved[m] for m in ARRIVALS), hidden, projection)
     terms = call(
         functools.partial(terms_kernel, n, n_resp, row),
         shape((2, tok), F32),

time: 50.3 us -> 50.2 us (level)
  transfers between devices with their start and end apart: 19 -> 19, of which waited for: 12 -> 13; matrix products, arithmetic and copies ran while one was open for 1% -> 1% of each run, Pallas kernels for 8% -> 8%
where the time goes in v9:
time: 50.2 us; the launch traced here: 50.1 us
  waiting for transfers between devices  21.1 us (42%)
  starting transfers between devices  21 us (42%)
  Pallas kernels  6.69 us (13%)
  between operations  0.77 us (2%)
  other arithmetic  0.51 us (1%)
    ppermute x19, waiting for transfers between devices, swap(): return lax.ppermute(x, axis, [(i, i ^ k) for i in range(n)])  21.1 us
    ppermute x19, starting transfers between devices, swap(): return lax.ppermute(x, axis, [(i, i ^ k) for i in range(n)])  21 us
    pallas_call x2, Pallas kernels, mix(): call(functools.partial(mix_kernel, n), outs, [VMEM] * (n + 4), [VMEM] * l...  1.94 us
    pallas_call x1, Pallas kernels, shards_in_place(): call(functools.partial(early_kernel, n, n_tp), [shape((rows // n_tp, rows...  1.32 us
  transfers between devices with their start and end apart: 19, of which 13 were waited for; matrix products, arithmetic and copies ran while one was open for 1% of the time, Pallas kernels for 8%

profile of v9, /device:TPU:0, one launch (start us, length us, event | category | flops | bytes accessed | tf_op | source)
XLA Modules:
  0.0 50.1 jit_solution(4780278520503395025)
XLA Ops:
  0.7 0.5 %collective-permute-start = (bf16[256,640]{1,0:T(8,128)(2,1)}, bf16[256,640]{1,0:T(8,128)(2,1)S(1)}, u32[]{:S(2)}, u32[]{:S(2)}) collective-permute-start(bf16[256,640]{1,0:T(8,128)(2,1)} %refs_4_.1), channel_id=1, source_target_pairs={{0,1},{1,0},{2,3},{3,2},{4,5},{5,4},{6,7},{7,6},{8,9},{9,8},{10,11... | collective-permute-start | bytes 983048 | tf_op jit(solution)/shard_map/ppermute | solution.py:48
  1.2 1.3 %shard_map.95 = (bf16[128,256]{1,0:T(8,128)(2,1)S(1)}, bf16[128,640]{1,0:T(8,128)(2,1)S(1)}, bf16[16,128]{1,0:T(8,128)(2,1)S(1)}, f32[1,5120]{1,0:T(1,128)S(1)}) custom-call(bf16[256,640]{1,0:T(8,128)(2,1)} %refs_4_.1, s32[4]{0:T(128)} %lengths.1, s32[4]{0:T(128)} %group_of.1, s32[4]{0:T(128)} %rewards.1, f32[2,128]{1,0:T(2,128)} %bitcast.6, ...), custom_call_target="tpu_custom_call" | custom-call | tf_op jit(solution)/shard_map/pallas_call | solution.py:380
  2.5 0.1 collective-permute-done.sibling
  2.6 0.2 shard_map.96
  2.9 2.9 %collective-permute-start.1 = (bf16[32,1280]{1,0:T(8,128)(2,1)S(1)}, bf16[32,1280]{1,0:T(8,128)(2,1)S(1)}, u32[]{:S(2)}, u32[]{:S(2)}) collective-permute-start(bf16[32,1280]{1,0:T(8,128)(2,1)S(1)} %get-tuple-element.36), channel_id=1, source_target_pairs={{0,8},{8,0},{16,24},{24,16},{1,9},{9,1},{17,25},{25,17},{2,10},{10... | collective-permute-start | bytes 245768 | tf_op jit(solution)/shard_map/ppermute | solution.py:48
  5.8 1.5 %collective-permute-start.2 = (bf16[32,1280]{1,0:T(8,128)(2,1)S(1)}, bf16[32,1280]{1,0:T(8,128)(2,1)S(1)}, u32[]{:S(2)}, u32[]{:S(2)}) collective-permute-start(bf16[32,1280]{1,0:T(8,128)(2,1)S(1)} %get-tuple-element.37), channel_id=1, source_target_pairs={{0,16},{8,24},{16,0},{24,8},{1,17},{9,25},{17,1},{25,9},{2,18},{10... | collective-permute-start | bytes 245768 | tf_op jit(solution)/shard_map/ppermute | solution.py:48
  7.3 0.0 collective-permute-start.3
  7.3 1.2 %collective-permute-done.1.refs_1_ = bf16[32,1280]{1,0:T(8,128)(2,1)S(1)} collective-permute-done((bf16[32,1280]{1,0:T(8,128)(2,1)S(1)}, bf16[32,1280]{1,0:T(8,128)(2,1)S(1)}, u32[]{:S(2)}, u32[]{:S(2)}) %collective-permute-start.1) | collective-permute-done | bytes 81952 | tf_op jit(solution)/shard_map/ppermute | solution.py:48
  8.5 2.5 %collective-permute-done.2.refs_2_ = bf16[32,1280]{1,0:T(8,128)(2,1)S(1)} collective-permute-done((bf16[32,1280]{1,0:T(8,128)(2,1)S(1)}, bf16[32,1280]{1,0:T(8,128)(2,1)S(1)}, u32[]{:S(2)}, u32[]{:S(2)}) %collective-permute-start.2) | collective-permute-done | bytes 81952 | tf_op jit(solution)/shard_map/ppermute | solution.py:48
  11.1 1.6 %collective-permute-done.3.refs_3_ = bf16[32,1280]{1,0:T(8,128)(2,1)S(1)} collective-permute-done((bf16[32,1280]{1,0:T(8,128)(2,1)S(1)}, bf16[32,1280]{1,0:T(8,128)(2,1)S(1)}, u32[]{:S(2)}, u32[]{:S(2)}) %collective-permute-start.3) | collective-permute-done | bytes 81952 | tf_op jit(solution)/shard_map/ppermute | solution.py:48
  12.6 0.2 shard_map.97
  12.9 2.7 %collective-permute-start.4 = (bf16[16,2688]{1,0:T(8,128)(2,1)S(1)}, bf16[16,2688]{1,0:T(8,128)(2,1)S(1)}, u32[]{:S(2)}, u32[]{:S(2)}) collective-permute-start(bf16[16,2688]{1,0:T(8,128)(2,1)S(1)} %get-tuple-element.39), channel_id=1, source_target_pairs={{0,4},{2,6},{4,0},{6,2},{1,5},{3,7},{5,1},{7,3},{8,12},{10,14},{12... | collective-permute-start | bytes 258056 | tf_op jit(solution)/shard_map/ppermute | solution.py:48
  15.5 1.6 %collective-permute-start.5 = (bf16[16,2688]{1,0:T(8,128)(2,1)S(1)}, bf16[16,2688]{1,0:T(8,128)(2,1)S(1)}, u32[]{:S(2)}, u32[]{:S(2)}) collective-permute-start(bf16[16,2688]{1,0:T(8,128)(2,1)S(1)} %get-tuple-element.40), channel_id=1, source_target_pairs={{0,2},{2,0},{4,6},{6,4},{1,3},{3,1},{5,7},{7,5},{8,10},{10,8},{12,... | collective-permute-start | bytes 258056 | tf_op jit(solution)/shard_map/ppermute | solution.py:48
  17.1 0.2 collective-permute-start.6
  17.3 3.6 %collective-permute-done.4.refs_0_ = bf16[16,2688]{1,0:T(8,128)(2,1)S(1)} collective-permute-done((bf16[16,2688]{1,0:T(8,128)(2,1)S(1)}, bf16[16,2688]{1,0:T(8,128)(2,1)S(1)}, u32[]{:S(2)}, u32[]{:S(2)}) %collective-permute-start.4) | collective-permute-done | bytes 86048 | tf_op jit(solution)/shard_map/ppermute | solution.py:48
  20.9 0.4 collective-permute-done.5.refs_1_
  21.3 2.1 %collective-permute-done.6.refs_2_ = bf16[16,2688]{1,0:T(8,128)(2,1)S(1)} collective-permute-done((bf16[16,2688]{1,0:T(8,128)(2,1)S(1)}, bf16[16,2688]{1,0:T(8,128)(2,1)S(1)}, u32[]{:S(2)}, u32[]{:S(2)}) %collective-permute-start.6) | collective-permute-done | bytes 86048 | tf_op jit(solution)/shard_map/ppermute | solution.py:48
  23.4 0.4 shard_map.99.refs_0_
  23.8 0.6 %collective-permute-start.7 = (bf16[72,1280]{1,0:T(8,128)(2,1)S(1)}, bf16[72,1280]{1,0:T(8,128)(2,1)S(1)}, u32[]{:S(2)}, u32[]{:S(2)}) collective-permute-start(bf16[72,1280]{1,0:T(8,128)(2,1)S(1)} %shard_map.99.refs_0_), channel_id=1, source_target_pairs={{0,8},{8,0},{16,24},{24,16},{1,9},{9,1},{17,25},{25,17},{2,10},{10... | collective-permute-start | bytes 552968 | tf_op jit(solution)/shard_map/ppermute | solution.py:48
  24.4 0.9 %collective-permute-start.8 = (bf16[72,1280]{1,0:T(8,128)(2,1)S(1)}, bf16[72,1280]{1,0:T(8,128)(2,1)S(1)}, u32[]{:S(2)}, u32[]{:S(2)}) collective-permute-start(bf16[72,1280]{1,0:T(8,128)(2,1)S(1)} %shard_map.99.refs_0_), channel_id=1, source_target_pairs={{0,16},{8,24},{16,0},{24,8},{1,17},{9,25},{17,1},{25,9},{2,18},{10... | collective-permute-start | bytes 552968 | tf_op jit(solution)/shard_map/ppermute | solution.py:48
  25.2 2.1 %collective-permute-start.9 = (bf16[72,1280]{1,0:T(8,128)(2,1)S(1)}, bf16[72,1280]{1,0:T(8,128)(2,1)S(1)}, u32[]{:S(2)}, u32[]{:S(2)}) collective-permute-start(bf16[72,1280]{1,0:T(8,128)(2,1)S(1)} %shard_map.99.refs_0_), channel_id=1, source_target_pairs={{0,24},{8,16},{16,8},{24,0},{1,25},{9,17},{17,9},{25,1},{2,26},{10... | collective-permute-start | bytes 552968 | tf_op jit(solution)/shard_map/ppermute | solution.py:48
  27.3 0.4 shard_map.102
  27.7 0.6 %shard_map.98 = (bf16[256,384]{1,0:T(8,128)(2,1)S(1)}, bf16[256,640]{1,0:T(8,128)(2,1)S(1)}, f32[256,640]{1,0:T(8,128)S(1)}, f32[256,640]{1,0:T(8,128)S(1)}) custom-call(bf16[16,2688]{1,0:T(8,128)(2,1)S(1)} %collective-permute-done.4.refs_0_, bf16[16,2688]{1,0:T(8,128)(2,1)S(1)} %collective-permute-done.5.refs_1_, ...), custom_call_target="tpu_custom_call" | custom-call | tf_op jit(solution)/shard_map/pallas_call | solution.py:433
  28.4 0.1 collective-permute-start.10
  28.5 1.5 %collective-permute-done.7.refs_1_ = bf16[72,1280]{1,0:T(8,128)(2,1)S(1)} collective-permute-done((bf16[72,1280]{1,0:T(8,128)(2,1)S(1)}, bf16[72,1280]{1,0:T(8,128)(2,1)S(1)}, u32[]{:S(2)}, u32[]{:S(2)}) %collective-permute-start.7) | collective-permute-done | bytes 184352 | tf_op jit(solution)/shard_map/ppermute | solution.py:48
  30.0 0.0 collective-permute-start.11
  30.0 2.3 %collective-permute-done.8.refs_2_ = bf16[72,1280]{1,0:T(8,128)(2,1)S(1)} collective-permute-done((bf16[72,1280]{1,0:T(8,128)(2,1)S(1)}, bf16[72,1280]{1,0:T(8,128)(2,1)S(1)}, u32[]{:S(2)}, u32[]{:S(2)}) %collective-permute-start.8) | collective-permute-done | bytes 184352 | tf_op jit(solution)/shard_map/ppermute | solution.py:48
  32.2 0.0 collective-permute-start.12
  32.2 0.0 collective-permute-done.9.refs_3_
  32.2 0.5 %collective-permute-start.13 = (bf16[72,1280]{1,0:T(8,128)(2,1)S(1)}, bf16[72,1280]{1,0:T(8,128)(2,1)S(1)}, u32[]{:S(2)}, u32[]{:S(2)}) collective-permute-start(bf16[72,1280]{1,0:T(8,128)(2,1)S(1)} %collective-permute-done.9.refs_3_), channel_id=1, source_target_pairs={{0,1},{1,0},{2,3},{3,2},{4,5},{5,4},{6,7},{7,6},{8,9},{9,8},{10,11... | collective-permute-start | bytes 552968 | tf_op jit(solution)/shard_map/ppermute | solution.py:48
  32.8 0.5 %shard_map.100.found = bf16[256,1280]{1,0:T(8,128)(2,1)S(1)} custom-call(bf16[256,640]{1,0:T(8,128)(2,1)S(1)} %get-tuple-element.55.pick, bf16[72,1280]{1,0:T(8,128)(2,1)S(1)} %shard_map.99.refs_0_, bf16[72,1280]{1,0:T(8,128)(2,1)S(1)} %collective-permute-done.7.refs_1_, bf16[72,1280]{1,0:T(8,128)(2,1)S(1)} %collective-permute-done.8.refs_2_, ...), custom_call_target="tpu_custom_call" | custom-call | tf_op jit(solution)/shard_map/pallas_call | solution.py:461
  33.3 0.3 shard_map.101.found
  33.6 0.0 collective-permute-done.10.refs_0_
  33.6 0.0 collective-permute-done.12.refs_2_
  33.7 0.3 collective-permute-done.13.refs_3_
  33.9 0.9 %shard_map.103 = (bf16[64,640]{1,0:T(8,128)(2,1)S(1)}, bf16[64,640]{1,0:T(8,128)(2,1)S(1)}, bf16[64,640]{1,0:T(8,128)(2,1)S(1)}, f32[64,640]{1,0:T(8,128)S(1)}) custom-call(bf16[256,384]{1,0:T(8,128)(2,1)S(1)} %get-tuple-element.45.pick, bf16[256,1280]{1,0:T(8,128)(2,1)S(1)} %shard_map.101.found, f32[256,640]{1,0:T(8,128)S(1)} %get-tuple-element.46.rest, ...), custom_call_target="tpu_custom_call" | custom-call | tf_op jit(solution)/shard_map/pallas_call | solution.py:464
  34.8 0.6 %collective-permute-start.17 = (bf16[64,640]{1,0:T(8,128)(2,1)S(1)}, bf16[64,640]{1,0:T(8,128)(2,1)S(1)}, u32[]{:S(2)}, u32[]{:S(2)}) collective-permute-start(bf16[64,640]{1,0:T(8,128)(2,1)S(1)} %get-tuple-element.52), channel_id=1, source_target_pairs={{0,2},{2,0},{4,6},{6,4},{1,3},{3,1},{5,7},{7,5},{8,10},{10,8},{12,... | collective-permute-start | bytes 245768 | tf_op jit(solution)/shard_map/ppermute | solution.py:48
  35.4 1.6 %collective-permute-start.15 = (bf16[64,640]{1,0:T(8,128)(2,1)S(1)}, bf16[64,640]{1,0:T(8,128)(2,1)S(1)}, u32[]{:S(2)}, u32[]{:S(2)}) collective-permute-start(bf16[64,640]{1,0:T(8,128)(2,1)S(1)} %get-tuple-element.51), channel_id=1, source_target_pairs={{0,4},{2,6},{4,0},{6,2},{1,5},{3,7},{5,1},{7,3},{8,12},{10,14},{12... | collective-permute-start | bytes 245768 | tf_op jit(solution)/shard_map/ppermute | solution.py:48
  37.0 1.1 %shard_map.104 = (f32[128,640]{1,0:T(8,128)S(1)}, bf16[128,640]{1,0:T(8,128)(2,1)S(1)}) custom-call(bf16[256,640]{1,0:T(8,128)(2,1)S(1)} %get-tuple-element.55.pick, bf16[256,1280]{1,0:T(8,128)(2,1)S(1)} %shard_map.100.found, f32[256,640]{1,0:T(8,128)S(1)} %get-tuple-element.56.rest, bf16[1280,640]{1,0:T(8,128)(2,1)S(1)} %copy-done, ...), custom_call_target="tpu_custom_call" | custom-call | tf_op jit(solution)/shard_map/pallas_call | solution.py:464
  38.1 1.5 %collective-permute-start.14 = (bf16[128,640]{1,0:T(8,128)(2,1)S(1)}, bf16[128,640]{1,0:T(8,128)(2,1)S(1)}, u32[]{:S(2)}, u32[]{:S(2)}) collective-permute-start(bf16[128,640]{1,0:T(8,128)(2,1)S(1)} %get-tuple-element.58), channel_id=1, source_target_pairs={{0,2},{2,0},{4,6},{6,4},{1,3},{3,1},{5,7},{7,5},{8,10},{10,8},{12,... | collective-permute-start | bytes 491528 | tf_op jit(solution)/shard_map/ppermute | solution.py:48
  39.6 1.4 %collective-permute-start.16 = (bf16[64,640]{1,0:T(8,128)(2,1)S(1)}, bf16[64,640]{1,0:T(8,128)(2,1)S(1)}, u32[]{:S(2)}, u32[]{:S(2)}) collective-permute-start(bf16[64,640]{1,0:T(8,128)(2,1)S(1)} %get-tuple-element.59), channel_id=1, source_target_pairs={{0,6},{2,4},{4,2},{6,0},{1,7},{3,5},{5,3},{7,1},{8,14},{10,12},{12... | collective-permute-start | bytes 245768 | tf_op jit(solution)/shard_map/ppermute | solution.py:48
  40.9 0.1 collective-permute-done.17.other
  41.1 2.4 %collective-permute-start.18 = (bf16[64,640]{1,0:T(8,128)(2,1)S(1)}, bf16[64,640]{1,0:T(8,128)(2,1)S(1)}, u32[]{:S(2)}, u32[]{:S(2)}) collective-permute-start(bf16[64,640]{1,0:T(8,128)(2,1)S(1)} %shard_map.105), channel_id=1, source_target_pairs={{0,6},{2,4},{4,2},{6,0},{1,7},{3,5},{5,3},{7,1},{8,14},{10,12},{12... | collective-permute-start | bytes 245768 | tf_op jit(solution)/shard_map/ppermute | solution.py:48
  43.5 0.5 %convert_bitcast_fusion = bf16[128,2]{0,1:T(2,128)(2,1)} fusion(f32[2,128]{1,0:T(2,128)S(1)} %shard_map.102), kind=kLoop, calls=%fused_computation | loop fusion | flops 256 | bytes 1536 | tf_op jit(solution)/shard_map/transpose | solution.py:496
  44.0 0.0 collective-permute-done.15.refs_2_
  44.0 4.2 %collective-permute-done.16.refs_3_ = bf16[64,640]{1,0:T(8,128)(2,1)S(1)} collective-permute-done((bf16[64,640]{1,0:T(8,128)(2,1)S(1)}, bf16[64,640]{1,0:T(8,128)(2,1)S(1)}, u32[]{:S(2)}, u32[]{:S(2)}) %collective-permute-start.16) | collective-permute-done | bytes 81952 | tf_op jit(solution)/shard_map/ppermute | solution.py:48
  48.2 1.1 %collective-permute-done.18.refs_4_ = bf16[64,640]{1,0:T(8,128)(2,1)S(1)} collective-permute-done((bf16[64,640]{1,0:T(8,128)(2,1)S(1)}, bf16[64,640]{1,0:T(8,128)(2,1)S(1)}, u32[]{:S(2)}, u32[]{:S(2)}) %collective-permute-start.18) | collective-permute-done | bytes 81952 | tf_op jit(solution)/shard_map/ppermute | solution.py:48
  49.3 0.7 %shard_map.106 = bf16[128,640]{1,0:T(8,128)(2,1)} custom-call(f32[128,640]{1,0:T(8,128)S(1)} %get-tuple-element.57.refs_0_, bf16[128,640]{1,0:T(8,128)(2,1)S(1)} %collective-permute-done.14.refs_1_, bf16[64,640]{1,0:T(8,128)(2,1)S(1)} %collective-permute-done.15.refs_2_, bf16[64,640]{1,0:T(8,128)(2,1)S(1)} %collective-permute-done.16.refs_3_, ...), custom_call_target="tpu_custom_call" | custom-call | tf_op jit(solution)/shard_map/pallas_call | solution.py:490
  (7 shorter events, 0.0 us)
Async XLA Ops:
  0.6 27.1 %copy-start.1 = (bf16[256,640]{1,0:T(8,128)(2,1)S(1)}, bf16[256,640]{1,0:T(8,128)(2,1)}, u32[]{:S(2)}) copy-start(bf16[256,640]{1,0:T(8,128)(2,1)} %refs_4_.1) | copy-start | bytes 983044
  0.6 27.1 %copy-start = (bf16[1280,640]{1,0:T(8,128)(2,1)S(1)}, bf16[1280,640]{1,0:T(8,128)(2,1)}, u32[]{:S(2)}) copy-start(bf16[1280,640]{1,0:T(8,128)(2,1)} %projection.3) | copy-start | bytes 4915204
  0.7 2.0 %collective-permute-start = (bf16[256,640]{1,0:T(8,128)(2,1)}, bf16[256,640]{1,0:T(8,128)(2,1)S(1)}, u32[]{:S(2)}, u32[]{:S(2)}) collective-permute-start(bf16[256,640]{1,0:T(8,128)(2,1)} %refs_4_.1), channel_id=1, source_target_pairs={{0,1},{1,0},{2,3},{3,2},{4,5},{5,4},{6,7},{7,6},{8,9},{9,8},{10,11... | collective-permute-start | bytes 983048 | tf_op jit(solution)/shard_map/ppermute | solution.py:48
  2.9 5.7 %collective-permute-start.1 = (bf16[32,1280]{1,0:T(8,128)(2,1)S(1)}, bf16[32,1280]{1,0:T(8,128)(2,1)S(1)}, u32[]{:S(2)}, u32[]{:S(2)}) collective-permute-start(bf16[32,1280]{1,0:T(8,128)(2,1)S(1)} %get-tuple-element.36), channel_id=1, source_target_pairs={{0,8},{8,0},{16,24},{24,16},{1,9},{9,1},{17,25},{25,17},{2,10},{10... | collective-permute-start | bytes 245768 | tf_op jit(solution)/shard_map/ppermute | solution.py:48
  5.8 5.3 %collective-permute-start.2 = (bf16[32,1280]{1,0:T(8,128)(2,1)S(1)}, bf16[32,1280]{1,0:T(8,128)(2,1)S(1)}, u32[]{:S(2)}, u32[]{:S(2)}) collective-permute-start(bf16[32,1280]{1,0:T(8,128)(2,1)S(1)} %get-tuple-element.37), channel_id=1, source_target_pairs={{0,16},{8,24},{16,0},{24,8},{1,17},{9,25},{17,1},{25,9},{2,18},{10... | collective-permute-start | bytes 245768 | tf_op jit(solution)/shard_map/ppermute | solution.py:48
  7.3 5.3 %collective-permute-start.3 = (bf16[32,1280]{1,0:T(8,128)(2,1)S(1)}, bf16[32,1280]{1,0:T(8,128)(2,1)S(1)}, u32[]{:S(2)}, u32[]{:S(2)}) collective-permute-start(bf16[32,1280]{1,0:T(8,128)(2,1)S(1)} %get-tuple-element.38), channel_id=1, source_target_pairs={{0,24},{8,16},{16,8},{24,0},{1,25},{9,17},{17,9},{25,1},{2,26},{10... | collective-permute-start | bytes 245768 | tf_op jit(solution)/shard_map/ppermute | solution.py:48
  12.9 8.0 %collective-permute-start.4 = (bf16[16,2688]{1,0:T(8,128)(2,1)S(1)}, bf16[16,2688]{1,0:T(8,128)(2,1)S(1)}, u32[]{:S(2)}, u32[]{:S(2)}) collective-permute-start(bf16[16,2688]{1,0:T(8,128)(2,1)S(1)} %get-tuple-element.39), channel_id=1, source_target_pairs={{0,4},{2,6},{4,0},{6,2},{1,5},{3,7},{5,1},{7,3},{8,12},{10,14},{12... | collective-permute-start | bytes 258056 | tf_op jit(solution)/shard_map/ppermute | solution.py:48
  15.5 5.7 %collective-permute-start.5 = (bf16[16,2688]{1,0:T(8,128)(2,1)S(1)}, bf16[16,2688]{1,0:T(8,128)(2,1)S(1)}, u32[]{:S(2)}, u32[]{:S(2)}) collective-permute-start(bf16[16,2688]{1,0:T(8,128)(2,1)S(1)} %get-tuple-element.40), channel_id=1, source_target_pairs={{0,2},{2,0},{4,6},{6,4},{1,3},{3,1},{5,7},{7,5},{8,10},{10,8},{12,... | collective-permute-start | bytes 258056 | tf_op jit(solution)/shard_map/ppermute | solution.py:48
  17.1 6.3 %collective-permute-start.6 = (bf16[16,2688]{1,0:T(8,128)(2,1)S(1)}, bf16[16,2688]{1,0:T(8,128)(2,1)S(1)}, u32[]{:S(2)}, u32[]{:S(2)}) collective-permute-start(bf16[16,2688]{1,0:T(8,128)(2,1)S(1)} %get-tuple-element.41), channel_id=1, source_target_pairs={{0,6},{2,4},{4,2},{6,0},{1,7},{3,5},{5,3},{7,1},{8,14},{10,12},{12... | collective-permute-start | bytes 258056 | tf_op jit(solution)/shard_map/ppermute | solution.py:48
  23.8 6.2 %collective-permute-start.7 = (bf16[72,1280]{1,0:T(8,128)(2,1)S(1)}, bf16[72,1280]{1,0:T(8,128)(2,1)S(1)}, u32[]{:S(2)}, u32[]{:S(2)}) collective-permute-start(bf16[72,1280]{1,0:T(8,128)(2,1)S(1)} %shard_map.99.refs_0_), channel_id=1, source_target_pairs={{0,8},{8,0},{16,24},{24,16},{1,9},{9,1},{17,25},{25,17},{2,10},{10... | collective-permute-start | bytes 552968 | tf_op jit(solution)/shard_map/ppermute | solution.py:48
  24.4 7.9 %collective-permute-start.8 = (bf16[72,1280]{1,0:T(8,128)(2,1)S(1)}, bf16[72,1280]{1,0:T(8,128)(2,1)S(1)}, u32[]{:S(2)}, u32[]{:S(2)}) collective-permute-start(bf16[72,1280]{1,0:T(8,128)(2,1)S(1)} %shard_map.99.refs_0_), channel_id=1, source_target_pairs={{0,16},{8,24},{16,0},{24,8},{1,17},{9,25},{17,1},{25,9},{2,18},{10... | collective-permute-start | bytes 552968 | tf_op jit(solution)/shard_map/ppermute | solution.py:48
  25.2 7.0 %collective-permute-start.9 = (bf16[72,1280]{1,0:T(8,128)(2,1)S(1)}, bf16[72,1280]{1,0:T(8,128)(2,1)S(1)}, u32[]{:S(2)}, u32[]{:S(2)}) collective-permute-start(bf16[72,1280]{1,0:T(8,128)(2,1)S(1)} %shard_map.99.refs_0_), channel_id=1, source_target_pairs={{0,24},{8,16},{16,8},{24,0},{1,25},{9,17},{17,9},{25,1},{2,26},{10... | collective-permute-start | bytes 552968 | tf_op jit(solution)/shard_map/ppermute | solution.py:48
  28.4 5.2 %collective-permute-start.10 = (bf16[72,1280]{1,0:T(8,128)(2,1)S(1)}, bf16[72,1280]{1,0:T(8,128)(2,1)S(1)}, u32[]{:S(2)}, u32[]{:S(2)}) collective-permute-start(bf16[72,1280]{1,0:T(8,128)(2,1)S(1)} %shard_map.99.refs_0_), channel_id=1, source_target_pairs={{0,1},{1,0},{2,3},{3,2},{4,5},{5,4},{6,7},{7,6},{8,9},{9,8},{10,11... | collective-permute-start | bytes 552968 | tf_op jit(solution)/shard_map/ppermute | solution.py:48
  30.0 3.6 %collective-permute-start.11 = (bf16[72,1280]{1,0:T(8,128)(2,1)S(1)}, bf16[72,1280]{1,0:T(8,128)(2,1)S(1)}, u32[]{:S(2)}, u32[]{:S(2)}) collective-permute-start(bf16[72,1280]{1,0:T(8,128)(2,1)S(1)} %collective-permute-done.7.refs_1_), channel_id=1, source_target_pairs={{0,1},{1,0},{2,3},{3,2},{4,5},{5,4},{6,7},{7,6},{8,9},{9,8},{10,11... | collective-permute-start | bytes 552968 | tf_op jit(solution)/shard_map/ppermute | solution.py:48
  32.2 1.4 %collective-permute-start.12 = (bf16[72,1280]{1,0:T(8,128)(2,1)S(1)}, bf16[72,1280]{1,0:T(8,128)(2,1)S(1)}, u32[]{:S(2)}, u32[]{:S(2)}) collective-permute-start(bf16[72,1280]{1,0:T(8,128)(2,1)S(1)} %collective-permute-done.8.refs_2_), channel_id=1, source_target_pairs={{0,1},{1,0},{2,3},{3,2},{4,5},{5,4},{6,7},{7,6},{8,9},{9,8},{10,11... | collective-permute-start | bytes 552968 | tf_op jit(solution)/shard_map/ppermute | solution.py:48
  32.2 1.7 %collective-permute-start.13 = (bf16[72,1280]{1,0:T(8,128)(2,1)S(1)}, bf16[72,1280]{1,0:T(8,128)(2,1)S(1)}, u32[]{:S(2)}, u32[]{:S(2)}) collective-permute-start(bf16[72,1280]{1,0:T(8,128)(2,1)S(1)} %collective-permute-done.9.refs_3_), channel_id=1, source_target_pairs={{0,1},{1,0},{2,3},{3,2},{4,5},{5,4},{6,7},{7,6},{8,9},{9,8},{10,11... | collective-permute-start | bytes 552968 | tf_op jit(solution)/shard_map/ppermute | solution.py:48
  34.8 6.2 %collective-permute-start.17 = (bf16[64,640]{1,0:T(8,128)(2,1)S(1)}, bf16[64,640]{1,0:T(8,128)(2,1)S(1)}, u32[]{:S(2)}, u32[]{:S(2)}) collective-permute-start(bf16[64,640]{1,0:T(8,128)(2,1)S(1)} %get-tuple-element.52), channel_id=1, source_target_pairs={{0,2},{2,0},{4,6},{6,4},{1,3},{3,1},{5,7},{7,5},{8,10},{10,8},{12,... | collective-permute-start | bytes 245768 | tf_op jit(solution)/shard_map/ppermute | solution.py:48
  35.4 8.6 %collective-permute-start.15 = (bf16[64,640]{1,0:T(8,128)(2,1)S(1)}, bf16[64,640]{1,0:T(8,128)(2,1)S(1)}, u32[]{:S(2)}, u32[]{:S(2)}) collective-permute-start(bf16[64,640]{1,0:T(8,128)(2,1)S(1)} %get-tuple-element.51), channel_id=1, source_target_pairs={{0,4},{2,6},{4,0},{6,2},{1,5},{3,7},{5,1},{7,3},{8,12},{10,14},{12... | collective-permute-start | bytes 245768 | tf_op jit(solution)/shard_map/ppermute | solution.py:48
  38.1 10.1 %collective-permute-start.14 = (bf16[128,640]{1,0:T(8,128)(2,1)S(1)}, bf16[128,640]{1,0:T(8,128)(2,1)S(1)}, u32[]{:S(2)}, u32[]{:S(2)}) collective-permute-start(bf16[128,640]{1,0:T(8,128)(2,1)S(1)} %get-tuple-element.58), channel_id=1, source_target_pairs={{0,2},{2,0},{4,6},{6,4},{1,3},{3,1},{5,7},{7,5},{8,10},{10,8},{12,... | collective-permute-start | bytes 491528 | tf_op jit(solution)/shard_map/ppermute | solution.py:48
  39.6 8.6 %collective-permute-start.16 = (bf16[64,640]{1,0:T(8,128)(2,1)S(1)}, bf16[64,640]{1,0:T(8,128)(2,1)S(1)}, u32[]{:S(2)}, u32[]{:S(2)}) collective-permute-start(bf16[64,640]{1,0:T(8,128)(2,1)S(1)} %get-tuple-element.59), channel_id=1, source_target_pairs={{0,6},{2,4},{4,2},{6,0},{1,7},{3,5},{5,3},{7,1},{8,14},{10,12},{12... | collective-permute-start | bytes 245768 | tf_op jit(solution)/shard_map/ppermute | solution.py:48
  41.1 8.2 %collective-permute-start.18 = (bf16[64,640]{1,0:T(8,128)(2,1)S(1)}, bf16[64,640]{1,0:T(8,128)(2,1)S(1)}, u32[]{:S(2)}, u32[]{:S(2)}) collective-permute-start(bf16[64,640]{1,0:T(8,128)(2,1)S(1)} %shard_map.105), channel_id=1, source_target_pairs={{0,6},{2,4},{4,2},{6,0},{1,7},{3,5},{5,3},{7,1},{8,14},{10,12},{12... | collective-permute-start | bytes 245768 | tf_op jit(solution)/shard_map/ppermute | solution.py:48

commit v10 on v9

--- a/solution.py
+++ b/solution.py
@@ -290,7 +290,7 @@
 
 def final_kernel(n_whole, n_first, *refs):
     own, parts, out = refs[0], refs[1:-1], refs[-1]
-    half = out.shape[0] // 2
+    half = parts[n_whole].shape[0]
     total = own[...]
     for part in parts[:n_whole]:
         total = total + part[...].astype(F32)
@@ -466,17 +466,17 @@
         )(pick, found, rest, projection, *other)
 
     found_far, found_near = own_part(pick_far), own_part(pick_near)
-    part = tok // 2
+    parts = (tok * 5 // 8, tok * 3 // 8)
     joined = n // 2
     far = mix(
         after(pick_far, found_near),
         found_far,
         rest_far,
-        [shape((part, cols), F32 if m % 2 and h else BF16) for m in range(joined) for h in range(2)],
+        [shape((parts[h], cols), F32 if m % 2 and h else BF16) for m in range(joined) for h in range(2)],
     )
     helped = [swap(far[2 * m + 1], "seq", 1) for m in range(0, joined, 2)]
     sums = [
-        call(join_kernel, shape((part, cols), BF16), [VMEM] * 2, VMEM)(far[2 * m + 3], got)
+        call(join_kernel, shape((parts[1], cols), BF16), [VMEM] * 2, VMEM)(far[2 * m + 3], got)
         for m, got in zip(range(0, joined, 2), helped, strict=True)
     ]
     passed = [swap(x, "seq", joined + m + 1) for m, x in zip(range(0, joined, 2), sums, strict=True)]

time: 50.2 us -> 50.3 us (level)
  no operation moved by 1% of the time
where the time goes in v10:
time: 50.3 us; the launch traced here: 50.1 us
  starting transfers between devices  21.2 us (42%)
  waiting for transfers between devices  21 us (42%)
  Pallas kernels  6.69 us (13%)
  between operations  0.77 us (2%)
  other arithmetic  0.51 us (1%)
    ppermute x19, starting transfers between devices, swap(): return lax.ppermute(x, axis, [(i, i ^ k) for i in range(n)])  21.2 us
    ppermute x19, waiting for transfers between devices, swap(): return lax.ppermute(x, axis, [(i, i ^ k) for i in range(n)])  21 us
    pallas_call x2, Pallas kernels, mix(): call(functools.partial(mix_kernel, n), outs, [VMEM] * (n + 4), [VMEM] * l...  1.94 us
    pallas_call x1, Pallas kernels, shards_in_place(): call(functools.partial(early_kernel, n, n_tp), [shape((rows // n_tp, rows...  1.32 us
  transfers between devices with their start and end apart: 19, of which 13 were waited for; matrix products, arithmetic and copies ran while one was open for 1% of the time, Pallas kernels for 8%

profile of v10, /device:TPU:0, one launch (start us, length us, event | category | flops | bytes accessed | tf_op | source)
XLA Modules:
  0.0 50.1 jit_solution(5896045545828445492)
XLA Ops:
  0.7 0.5 %collective-permute-start = (bf16[256,640]{1,0:T(8,128)(2,1)}, bf16[256,640]{1,0:T(8,128)(2,1)S(1)}, u32[]{:S(2)}, u32[]{:S(2)}) collective-permute-start(bf16[256,640]{1,0:T(8,128)(2,1)} %refs_4_.1), channel_id=1, source_target_pairs={{0,1},{1,0},{2,3},{3,2},{4,5},{5,4},{6,7},{7,6},{8,9},{9,8},{10,11... | collective-permute-start | bytes 983048 | tf_op jit(solution)/shard_map/ppermute | solution.py:48
  1.2 1.3 %shard_map.95 = (bf16[128,256]{1,0:T(8,128)(2,1)S(1)}, bf16[128,640]{1,0:T(8,128)(2,1)S(1)}, bf16[16,128]{1,0:T(8,128)(2,1)S(1)}, f32[1,5120]{1,0:T(1,128)S(1)}) custom-call(bf16[256,640]{1,0:T(8,128)(2,1)} %refs_4_.1, s32[4]{0:T(128)} %lengths.1, s32[4]{0:T(128)} %group_of.1, s32[4]{0:T(128)} %rewards.1, f32[2,128]{1,0:T(2,128)} %bitcast.6, ...), custom_call_target="tpu_custom_call" | custom-call | tf_op jit(solution)/shard_map/pallas_call | solution.py:380
  2.5 0.1 collective-permute-done.sibling
  2.6 0.2 shard_map.96
  2.9 2.9 %collective-permute-start.1 = (bf16[32,1280]{1,0:T(8,128)(2,1)S(1)}, bf16[32,1280]{1,0:T(8,128)(2,1)S(1)}, u32[]{:S(2)}, u32[]{:S(2)}) collective-permute-start(bf16[32,1280]{1,0:T(8,128)(2,1)S(1)} %get-tuple-element.36), channel_id=1, source_target_pairs={{0,8},{8,0},{16,24},{24,16},{1,9},{9,1},{17,25},{25,17},{2,10},{10... | collective-permute-start | bytes 245768 | tf_op jit(solution)/shard_map/ppermute | solution.py:48
  5.8 1.5 %collective-permute-start.2 = (bf16[32,1280]{1,0:T(8,128)(2,1)S(1)}, bf16[32,1280]{1,0:T(8,128)(2,1)S(1)}, u32[]{:S(2)}, u32[]{:S(2)}) collective-permute-start(bf16[32,1280]{1,0:T(8,128)(2,1)S(1)} %get-tuple-element.37), channel_id=1, source_target_pairs={{0,16},{8,24},{16,0},{24,8},{1,17},{9,25},{17,1},{25,9},{2,18},{10... | collective-permute-start | bytes 245768 | tf_op jit(solution)/shard_map/ppermute | solution.py:48
  7.3 0.0 collective-permute-start.3
  7.3 1.2 %collective-permute-done.1.refs_1_ = bf16[32,1280]{1,0:T(8,128)(2,1)S(1)} collective-permute-done((bf16[32,1280]{1,0:T(8,128)(2,1)S(1)}, bf16[32,1280]{1,0:T(8,128)(2,1)S(1)}, u32[]{:S(2)}, u32[]{:S(2)}) %collective-permute-start.1) | collective-permute-done | bytes 81952 | tf_op jit(solution)/shard_map/ppermute | solution.py:48
  8.5 2.5 %collective-permute-done.2.refs_2_ = bf16[32,1280]{1,0:T(8,128)(2,1)S(1)} collective-permute-done((bf16[32,1280]{1,0:T(8,128)(2,1)S(1)}, bf16[32,1280]{1,0:T(8,128)(2,1)S(1)}, u32[]{:S(2)}, u32[]{:S(2)}) %collective-permute-start.2) | collective-permute-done | bytes 81952 | tf_op jit(solution)/shard_map/ppermute | solution.py:48
  11.1 1.6 %collective-permute-done.3.refs_3_ = bf16[32,1280]{1,0:T(8,128)(2,1)S(1)} collective-permute-done((bf16[32,1280]{1,0:T(8,128)(2,1)S(1)}, bf16[32,1280]{1,0:T(8,128)(2,1)S(1)}, u32[]{:S(2)}, u32[]{:S(2)}) %collective-permute-start.3) | collective-permute-done | bytes 81952 | tf_op jit(solution)/shard_map/ppermute | solution.py:48
  12.6 0.2 shard_map.97
  12.9 2.7 %collective-permute-start.4 = (bf16[16,2688]{1,0:T(8,128)(2,1)S(1)}, bf16[16,2688]{1,0:T(8,128)(2,1)S(1)}, u32[]{:S(2)}, u32[]{:S(2)}) collective-permute-start(bf16[16,2688]{1,0:T(8,128)(2,1)S(1)} %get-tuple-element.39), channel_id=1, source_target_pairs={{0,4},{2,6},{4,0},{6,2},{1,5},{3,7},{5,1},{7,3},{8,12},{10,14},{12... | collective-permute-start | bytes 258056 | tf_op jit(solution)/shard_map/ppermute | solution.py:48
  15.5 1.6 %collective-permute-start.5 = (bf16[16,2688]{1,0:T(8,128)(2,1)S(1)}, bf16[16,2688]{1,0:T(8,128)(2,1)S(1)}, u32[]{:S(2)}, u32[]{:S(2)}) collective-permute-start(bf16[16,2688]{1,0:T(8,128)(2,1)S(1)} %get-tuple-element.40), channel_id=1, source_target_pairs={{0,2},{2,0},{4,6},{6,4},{1,3},{3,1},{5,7},{7,5},{8,10},{10,8},{12,... | collective-permute-start | bytes 258056 | tf_op jit(solution)/shard_map/ppermute | solution.py:48
  17.1 0.2 collective-permute-start.6
  17.3 3.6 %collective-permute-done.4.refs_0_ = bf16[16,2688]{1,0:T(8,128)(2,1)S(1)} collective-permute-done((bf16[16,2688]{1,0:T(8,128)(2,1)S(1)}, bf16[16,2688]{1,0:T(8,128)(2,1)S(1)}, u32[]{:S(2)}, u32[]{:S(2)}) %collective-permute-start.4) | collective-permute-done | bytes 86048 | tf_op jit(solution)/shard_map/ppermute | solution.py:48
  20.9 0.4 collective-permute-done.5.refs_1_
  21.3 2.1 %collective-permute-done.6.refs_2_ = bf16[16,2688]{1,0:T(8,128)(2,1)S(1)} collective-permute-done((bf16[16,2688]{1,0:T(8,128)(2,1)S(1)}, bf16[16,2688]{1,0:T(8,128)(2,1)S(1)}, u32[]{:S(2)}, u32[]{:S(2)}) %collective-permute-start.6) | collective-permute-done | bytes 86048 | tf_op jit(solution)/shard_map/ppermute | solution.py:48
  23.4 0.4 shard_map.99.refs_0_
  23.8 0.6 %collective-permute-start.7 = (bf16[72,1280]{1,0:T(8,128)(2,1)S(1)}, bf16[72,1280]{1,0:T(8,128)(2,1)S(1)}, u32[]{:S(2)}, u32[]{:S(2)}) collective-permute-start(bf16[72,1280]{1,0:T(8,128)(2,1)S(1)} %shard_map.99.refs_0_), channel_id=1, source_target_pairs={{0,8},{8,0},{16,24},{24,16},{1,9},{9,1},{17,25},{25,17},{2,10},{10... | collective-permute-start | bytes 552968 | tf_op jit(solution)/shard_map/ppermute | solution.py:48
  24.4 0.9 %collective-permute-start.8 = (bf16[72,1280]{1,0:T(8,128)(2,1)S(1)}, bf16[72,1280]{1,0:T(8,128)(2,1)S(1)}, u32[]{:S(2)}, u32[]{:S(2)}) collective-permute-start(bf16[72,1280]{1,0:T(8,128)(2,1)S(1)} %shard_map.99.refs_0_), channel_id=1, source_target_pairs={{0,16},{8,24},{16,0},{24,8},{1,17},{9,25},{17,1},{25,9},{2,18},{10... | collective-permute-start | bytes 552968 | tf_op jit(solution)/shard_map/ppermute | solution.py:48
  25.2 2.1 %collective-permute-start.9 = (bf16[72,1280]{1,0:T(8,128)(2,1)S(1)}, bf16[72,1280]{1,0:T(8,128)(2,1)S(1)}, u32[]{:S(2)}, u32[]{:S(2)}) collective-permute-start(bf16[72,1280]{1,0:T(8,128)(2,1)S(1)} %shard_map.99.refs_0_), channel_id=1, source_target_pairs={{0,24},{8,16},{16,8},{24,0},{1,25},{9,17},{17,9},{25,1},{2,26},{10... | collective-permute-start | bytes 552968 | tf_op jit(solution)/shard_map/ppermute | solution.py:48
  27.3 0.4 shard_map.102
  27.7 0.6 %shard_map.98 = (bf16[256,384]{1,0:T(8,128)(2,1)S(1)}, bf16[256,640]{1,0:T(8,128)(2,1)S(1)}, f32[256,640]{1,0:T(8,128)S(1)}, f32[256,640]{1,0:T(8,128)S(1)}) custom-call(bf16[16,2688]{1,0:T(8,128)(2,1)S(1)} %collective-permute-done.4.refs_0_, bf16[16,2688]{1,0:T(8,128)(2,1)S(1)} %collective-permute-done.5.refs_1_, ...), custom_call_target="tpu_custom_call" | custom-call | tf_op jit(solution)/shard_map/pallas_call | solution.py:433
  28.4 0.1 collective-permute-start.10
  28.5 1.5 %collective-permute-done.7.refs_1_ = bf16[72,1280]{1,0:T(8,128)(2,1)S(1)} collective-permute-done((bf16[72,1280]{1,0:T(8,128)(2,1)S(1)}, bf16[72,1280]{1,0:T(8,128)(2,1)S(1)}, u32[]{:S(2)}, u32[]{:S(2)}) %collective-permute-start.7) | collective-permute-done | bytes 184352 | tf_op jit(solution)/shard_map/ppermute | solution.py:48
  30.0 2.3 %collective-permute-done.8.refs_2_ = bf16[72,1280]{1,0:T(8,128)(2,1)S(1)} collective-permute-done((bf16[72,1280]{1,0:T(8,128)(2,1)S(1)}, bf16[72,1280]{1,0:T(8,128)(2,1)S(1)}, u32[]{:S(2)}, u32[]{:S(2)}) %collective-permute-start.8) | collective-permute-done | bytes 184352 | tf_op jit(solution)/shard_map/ppermute | solution.py:48
  32.2 0.0 collective-permute-start.12
  32.2 0.0 collective-permute-done.9.refs_3_
  32.2 0.5 %collective-permute-start.13 = (bf16[72,1280]{1,0:T(8,128)(2,1)S(1)}, bf16[72,1280]{1,0:T(8,128)(2,1)S(1)}, u32[]{:S(2)}, u32[]{:S(2)}) collective-permute-start(bf16[72,1280]{1,0:T(8,128)(2,1)S(1)} %collective-permute-done.9.refs_3_), channel_id=1, source_target_pairs={{0,1},{1,0},{2,3},{3,2},{4,5},{5,4},{6,7},{7,6},{8,9},{9,8},{10,11... | collective-permute-start | bytes 552968 | tf_op jit(solution)/shard_map/ppermute | solution.py:48
  32.8 0.5 %shard_map.100.found = bf16[256,1280]{1,0:T(8,128)(2,1)S(1)} custom-call(bf16[256,640]{1,0:T(8,128)(2,1)S(1)} %get-tuple-element.55.pick, bf16[72,1280]{1,0:T(8,128)(2,1)S(1)} %shard_map.99.refs_0_, bf16[72,1280]{1,0:T(8,128)(2,1)S(1)} %collective-permute-done.7.refs_1_, bf16[72,1280]{1,0:T(8,128)(2,1)S(1)} %collective-permute-done.8.refs_2_, ...), custom_call_target="tpu_custom_call" | custom-call | tf_op jit(solution)/shard_map/pallas_call | solution.py:461
  33.3 0.3 shard_map.101.found
  33.6 0.0 collective-permute-done.10.refs_0_
  33.6 0.0 collective-permute-done.11.refs_1_
  33.6 0.0 collective-permute-done.12.refs_2_
  33.7 0.3 collective-permute-done.13.refs_3_
  33.9 0.9 %shard_map.103 = (bf16[80,640]{1,0:T(8,128)(2,1)S(1)}, bf16[48,640]{1,0:T(8,128)(2,1)S(1)}, bf16[80,640]{1,0:T(8,128)(2,1)S(1)}, f32[48,640]{1,0:T(8,128)S(1)}) custom-call(bf16[256,384]{1,0:T(8,128)(2,1)S(1)} %get-tuple-element.45.pick, bf16[256,1280]{1,0:T(8,128)(2,1)S(1)} %shard_map.101.found, f32[256,640]{1,0:T(8,128)S(1)} %get-tuple-element.46.rest, ...), custom_call_target="tpu_custom_call" | custom-call | tf_op jit(solution)/shard_map/pallas_call | solution.py:464
  34.8 0.6 %collective-permute-start.17 = (bf16[48,640]{1,0:T(8,128)(2,1)S(1)}, bf16[48,640]{1,0:T(8,128)(2,1)S(1)}, u32[]{:S(2)}, u32[]{:S(2)}) collective-permute-start(bf16[48,640]{1,0:T(8,128)(2,1)S(1)} %get-tuple-element.52), channel_id=1, source_target_pairs={{0,2},{2,0},{4,6},{6,4},{1,3},{3,1},{5,7},{7,5},{8,10},{10,8},{12,... | collective-permute-start | bytes 184328 | tf_op jit(solution)/shard_map/ppermute | solution.py:48
  35.4 1.6 %collective-permute-start.15 = (bf16[80,640]{1,0:T(8,128)(2,1)S(1)}, bf16[80,640]{1,0:T(8,128)(2,1)S(1)}, u32[]{:S(2)}, u32[]{:S(2)}) collective-permute-start(bf16[80,640]{1,0:T(8,128)(2,1)S(1)} %get-tuple-element.51), channel_id=1, source_target_pairs={{0,4},{2,6},{4,0},{6,2},{1,5},{3,7},{5,1},{7,3},{8,12},{10,14},{12... | collective-permute-start | bytes 307208 | tf_op jit(solution)/shard_map/ppermute | solution.py:48
  37.0 1.1 %shard_map.104 = (f32[128,640]{1,0:T(8,128)S(1)}, bf16[128,640]{1,0:T(8,128)(2,1)S(1)}) custom-call(bf16[256,640]{1,0:T(8,128)(2,1)S(1)} %get-tuple-element.55.pick, bf16[256,1280]{1,0:T(8,128)(2,1)S(1)} %shard_map.100.found, f32[256,640]{1,0:T(8,128)S(1)} %get-tuple-element.56.rest, bf16[1280,640]{1,0:T(8,128)(2,1)S(1)} %copy-done, ...), custom_call_target="tpu_custom_call" | custom-call | tf_op jit(solution)/shard_map/pallas_call | solution.py:464
  38.1 1.5 %collective-permute-start.14 = (bf16[128,640]{1,0:T(8,128)(2,1)S(1)}, bf16[128,640]{1,0:T(8,128)(2,1)S(1)}, u32[]{:S(2)}, u32[]{:S(2)}) collective-permute-start(bf16[128,640]{1,0:T(8,128)(2,1)S(1)} %get-tuple-element.58), channel_id=1, source_target_pairs={{0,2},{2,0},{4,6},{6,4},{1,3},{3,1},{5,7},{7,5},{8,10},{10,8},{12,... | collective-permute-start | bytes 491528 | tf_op jit(solution)/shard_map/ppermute | solution.py:48
  39.6 1.4 %collective-permute-start.16 = (bf16[80,640]{1,0:T(8,128)(2,1)S(1)}, bf16[80,640]{1,0:T(8,128)(2,1)S(1)}, u32[]{:S(2)}, u32[]{:S(2)}) collective-permute-start(bf16[80,640]{1,0:T(8,128)(2,1)S(1)} %get-tuple-element.59), channel_id=1, source_target_pairs={{0,6},{2,4},{4,2},{6,0},{1,7},{3,5},{5,3},{7,1},{8,14},{10,12},{12... | collective-permute-start | bytes 307208 | tf_op jit(solution)/shard_map/ppermute | solution.py:48
  41.0 2.5 %collective-permute-start.18 = (bf16[48,640]{1,0:T(8,128)(2,1)S(1)}, bf16[48,640]{1,0:T(8,128)(2,1)S(1)}, u32[]{:S(2)}, u32[]{:S(2)}) collective-permute-start(bf16[48,640]{1,0:T(8,128)(2,1)S(1)} %shard_map.105), channel_id=1, source_target_pairs={{0,6},{2,4},{4,2},{6,0},{1,7},{3,5},{5,3},{7,1},{8,14},{10,12},{12... | collective-permute-start | bytes 184328 | tf_op jit(solution)/shard_map/ppermute | solution.py:48
  43.5 0.5 %convert_bitcast_fusion = bf16[128,2]{0,1:T(2,128)(2,1)} fusion(f32[2,128]{1,0:T(2,128)S(1)} %shard_map.102), kind=kLoop, calls=%fused_computation | loop fusion | flops 256 | bytes 1536 | tf_op jit(solution)/shard_map/transpose | solution.py:496
  44.0 0.2 collective-permute-done.15.refs_2_
  44.2 4.5 %collective-permute-done.16.refs_3_ = bf16[80,640]{1,0:T(8,128)(2,1)S(1)} collective-permute-done((bf16[80,640]{1,0:T(8,128)(2,1)S(1)}, bf16[80,640]{1,0:T(8,128)(2,1)S(1)}, u32[]{:S(2)}, u32[]{:S(2)}) %collective-permute-start.16) | collective-permute-done | bytes 102432 | tf_op jit(solution)/shard_map/ppermute | solution.py:48
  48.7 0.7 %collective-permute-done.18.refs_4_ = bf16[48,640]{1,0:T(8,128)(2,1)S(1)} collective-permute-done((bf16[48,640]{1,0:T(8,128)(2,1)S(1)}, bf16[48,640]{1,0:T(8,128)(2,1)S(1)}, u32[]{:S(2)}, u32[]{:S(2)}) %collective-permute-start.18) | collective-permute-done | bytes 61472 | tf_op jit(solution)/shard_map/ppermute | solution.py:48
  49.4 0.0 collective-permute-done.14.refs_1_
  49.4 0.7 %shard_map.106 = bf16[128,640]{1,0:T(8,128)(2,1)} custom-call(f32[128,640]{1,0:T(8,128)S(1)} %get-tuple-element.57.refs_0_, bf16[128,640]{1,0:T(8,128)(2,1)S(1)} %collective-permute-done.14.refs_1_, bf16[80,640]{1,0:T(8,128)(2,1)S(1)} %collective-permute-done.15.refs_2_, bf16[80,640]{1,0:T(8,128)(2,1)S(1)} %collective-permute-done.16.refs_3_, ...), custom_call_target="tpu_custom_call" | custom-call | tf_op jit(solution)/shard_map/pallas_call | solution.py:490
  (7 shorter events, 0.0 us)
Async XLA Ops:
  0.6 27.1 %copy-start.1 = (bf16[256,640]{1,0:T(8,128)(2,1)S(1)}, bf16[256,640]{1,0:T(8,128)(2,1)}, u32[]{:S(2)}) copy-start(bf16[256,640]{1,0:T(8,128)(2,1)} %refs_4_.1) | copy-start | bytes 983044
  0.6 27.1 %copy-start = (bf16[1280,640]{1,0:T(8,128)(2,1)S(1)}, bf16[1280,640]{1,0:T(8,128)(2,1)}, u32[]{:S(2)}) copy-start(bf16[1280,640]{1,0:T(8,128)(2,1)} %projection.3) | copy-start | bytes 4915204
  0.7 2.0 %collective-permute-start = (bf16[256,640]{1,0:T(8,128)(2,1)}, bf16[256,640]{1,0:T(8,128)(2,1)S(1)}, u32[]{:S(2)}, u32[]{:S(2)}) collective-permute-start(bf16[256,640]{1,0:T(8,128)(2,1)} %refs_4_.1), channel_id=1, source_target_pairs={{0,1},{1,0},{2,3},{3,2},{4,5},{5,4},{6,7},{7,6},{8,9},{9,8},{10,11... | collective-permute-start | bytes 983048 | tf_op jit(solution)/shard_map/ppermute | solution.py:48
  2.9 5.7 %collective-permute-start.1 = (bf16[32,1280]{1,0:T(8,128)(2,1)S(1)}, bf16[32,1280]{1,0:T(8,128)(2,1)S(1)}, u32[]{:S(2)}, u32[]{:S(2)}) collective-permute-start(bf16[32,1280]{1,0:T(8,128)(2,1)S(1)} %get-tuple-element.36), channel_id=1, source_target_pairs={{0,8},{8,0},{16,24},{24,16},{1,9},{9,1},{17,25},{25,17},{2,10},{10... | collective-permute-start | bytes 245768 | tf_op jit(solution)/shard_map/ppermute | solution.py:48
  5.8 5.3 %collective-permute-start.2 = (bf16[32,1280]{1,0:T(8,128)(2,1)S(1)}, bf16[32,1280]{1,0:T(8,128)(2,1)S(1)}, u32[]{:S(2)}, u32[]{:S(2)}) collective-permute-start(bf16[32,1280]{1,0:T(8,128)(2,1)S(1)} %get-tuple-element.37), channel_id=1, source_target_pairs={{0,16},{8,24},{16,0},{24,8},{1,17},{9,25},{17,1},{25,9},{2,18},{10... | collective-permute-start | bytes 245768 | tf_op jit(solution)/shard_map/ppermute | solution.py:48
  7.3 5.3 %collective-permute-start.3 = (bf16[32,1280]{1,0:T(8,128)(2,1)S(1)}, bf16[32,1280]{1,0:T(8,128)(2,1)S(1)}, u32[]{:S(2)}, u32[]{:S(2)}) collective-permute-start(bf16[32,1280]{1,0:T(8,128)(2,1)S(1)} %get-tuple-element.38), channel_id=1, source_target_pairs={{0,24},{8,16},{16,8},{24,0},{1,25},{9,17},{17,9},{25,1},{2,26},{10... | collective-permute-start | bytes 245768 | tf_op jit(solution)/shard_map/ppermute | solution.py:48
  12.9 8.0 %collective-permute-start.4 = (bf16[16,2688]{1,0:T(8,128)(2,1)S(1)}, bf16[16,2688]{1,0:T(8,128)(2,1)S(1)}, u32[]{:S(2)}, u32[]{:S(2)}) collective-permute-start(bf16[16,2688]{1,0:T(8,128)(2,1)S(1)} %get-tuple-element.39), channel_id=1, source_target_pairs={{0,4},{2,6},{4,0},{6,2},{1,5},{3,7},{5,1},{7,3},{8,12},{10,14},{12... | collective-permute-start | bytes 258056 | tf_op jit(solution)/shard_map/ppermute | solution.py:48
  15.5 5.7 %collective-permute-start.5 = (bf16[16,2688]{1,0:T(8,128)(2,1)S(1)}, bf16[16,2688]{1,0:T(8,128)(2,1)S(1)}, u32[]{:S(2)}, u32[]{:S(2)}) collective-permute-start(bf16[16,2688]{1,0:T(8,128)(2,1)S(1)} %get-tuple-element.40), channel_id=1, source_target_pairs={{0,2},{2,0},{4,6},{6,4},{1,3},{3,1},{5,7},{7,5},{8,10},{10,8},{12,... | collective-permute-start | bytes 258056 | tf_op jit(solution)/shard_map/ppermute | solution.py:48
  17.1 6.3 %collective-permute-start.6 = (bf16[16,2688]{1,0:T(8,128)(2,1)S(1)}, bf16[16,2688]{1,0:T(8,128)(2,1)S(1)}, u32[]{:S(2)}, u32[]{:S(2)}) collective-permute-start(bf16[16,2688]{1,0:T(8,128)(2,1)S(1)} %get-tuple-element.41), channel_id=1, source_target_pairs={{0,6},{2,4},{4,2},{6,0},{1,7},{3,5},{5,3},{7,1},{8,14},{10,12},{12... | collective-permute-start | bytes 258056 | tf_op jit(solution)/shard_map/ppermute | solution.py:48
  23.8 6.2 %collective-permute-start.7 = (bf16[72,1280]{1,0:T(8,128)(2,1)S(1)}, bf16[72,1280]{1,0:T(8,128)(2,1)S(1)}, u32[]{:S(2)}, u32[]{:S(2)}) collective-permute-start(bf16[72,1280]{1,0:T(8,128)(2,1)S(1)} %shard_map.99.refs_0_), channel_id=1, source_target_pairs={{0,8},{8,0},{16,24},{24,16},{1,9},{9,1},{17,25},{25,17},{2,10},{10... | collective-permute-start | bytes 552968 | tf_op jit(solution)/shard_map/ppermute | solution.py:48
  24.4 7.9 %collective-permute-start.8 = (bf16[72,1280]{1,0:T(8,128)(2,1)S(1)}, bf16[72,1280]{1,0:T(8,128)(2,1)S(1)}, u32[]{:S(2)}, u32[]{:S(2)}) collective-permute-start(bf16[72,1280]{1,0:T(8,128)(2,1)S(1)} %shard_map.99.refs_0_), channel_id=1, source_target_pairs={{0,16},{8,24},{16,0},{24,8},{1,17},{9,25},{17,1},{25,9},{2,18},{10... | collective-permute-start | bytes 552968 | tf_op jit(solution)/shard_map/ppermute | solution.py:48
  25.2 7.0 %collective-permute-start.9 = (bf16[72,1280]{1,0:T(8,128)(2,1)S(1)}, bf16[72,1280]{1,0:T(8,128)(2,1)S(1)}, u32[]{:S(2)}, u32[]{:S(2)}) collective-permute-start(bf16[72,1280]{1,0:T(8,128)(2,1)S(1)} %shard_map.99.refs_0_), channel_id=1, source_target_pairs={{0,24},{8,16},{16,8},{24,0},{1,25},{9,17},{17,9},{25,1},{2,26},{10... | collective-permute-start | bytes 552968 | tf_op jit(solution)/shard_map/ppermute | solution.py:48
  28.4 5.2 %collective-permute-start.10 = (bf16[72,1280]{1,0:T(8,128)(2,1)S(1)}, bf16[72,1280]{1,0:T(8,128)(2,1)S(1)}, u32[]{:S(2)}, u32[]{:S(2)}) collective-permute-start(bf16[72,1280]{1,0:T(8,128)(2,1)S(1)} %shard_map.99.refs_0_), channel_id=1, source_target_pairs={{0,1},{1,0},{2,3},{3,2},{4,5},{5,4},{6,7},{7,6},{8,9},{9,8},{10,11... | collective-permute-start | bytes 552968 | tf_op jit(solution)/shard_map/ppermute | solution.py:48
  30.0 3.6 %collective-permute-start.11 = (bf16[72,1280]{1,0:T(8,128)(2,1)S(1)}, bf16[72,1280]{1,0:T(8,128)(2,1)S(1)}, u32[]{:S(2)}, u32[]{:S(2)}) collective-permute-start(bf16[72,1280]{1,0:T(8,128)(2,1)S(1)} %collective-permute-done.7.refs_1_), channel_id=1, source_target_pairs={{0,1},{1,0},{2,3},{3,2},{4,5},{5,4},{6,7},{7,6},{8,9},{9,8},{10,11... | collective-permute-start | bytes 552968 | tf_op jit(solution)/shard_map/ppermute | solution.py:48
  32.2 1.4 %collective-permute-start.12 = (bf16[72,1280]{1,0:T(8,128)(2,1)S(1)}, bf16[72,1280]{1,0:T(8,128)(2,1)S(1)}, u32[]{:S(2)}, u32[]{:S(2)}) collective-permute-start(bf16[72,1280]{1,0:T(8,128)(2,1)S(1)} %collective-permute-done.8.refs_2_), channel_id=1, source_target_pairs={{0,1},{1,0},{2,3},{3,2},{4,5},{5,4},{6,7},{7,6},{8,9},{9,8},{10,11... | collective-permute-start | bytes 552968 | tf_op jit(solution)/shard_map/ppermute | solution.py:48
  32.2 1.7 %collective-permute-start.13 = (bf16[72,1280]{1,0:T(8,128)(2,1)S(1)}, bf16[72,1280]{1,0:T(8,128)(2,1)S(1)}, u32[]{:S(2)}, u32[]{:S(2)}) collective-permute-start(bf16[72,1280]{1,0:T(8,128)(2,1)S(1)} %collective-permute-done.9.refs_3_), channel_id=1, source_target_pairs={{0,1},{1,0},{2,3},{3,2},{4,5},{5,4},{6,7},{7,6},{8,9},{9,8},{10,11... | collective-permute-start | bytes 552968 | tf_op jit(solution)/shard_map/ppermute | solution.py:48
  34.8 6.1 %collective-permute-start.17 = (bf16[48,640]{1,0:T(8,128)(2,1)S(1)}, bf16[48,640]{1,0:T(8,128)(2,1)S(1)}, u32[]{:S(2)}, u32[]{:S(2)}) collective-permute-start(bf16[48,640]{1,0:T(8,128)(2,1)S(1)} %get-tuple-element.52), channel_id=1, source_target_pairs={{0,2},{2,0},{4,6},{6,4},{1,3},{3,1},{5,7},{7,5},{8,10},{10,8},{12,... | collective-permute-start | bytes 184328 | tf_op jit(solution)/shard_map/ppermute | solution.py:48
  35.4 8.8 %collective-permute-start.15 = (bf16[80,640]{1,0:T(8,128)(2,1)S(1)}, bf16[80,640]{1,0:T(8,128)(2,1)S(1)}, u32[]{:S(2)}, u32[]{:S(2)}) collective-permute-start(bf16[80,640]{1,0:T(8,128)(2,1)S(1)} %get-tuple-element.51), channel_id=1, source_target_pairs={{0,4},{2,6},{4,0},{6,2},{1,5},{3,7},{5,1},{7,3},{8,12},{10,14},{12... | collective-permute-start | bytes 307208 | tf_op jit(solution)/shard_map/ppermute | solution.py:48
  38.1 11.3 %collective-permute-start.14 = (bf16[128,640]{1,0:T(8,128)(2,1)S(1)}, bf16[128,640]{1,0:T(8,128)(2,1)S(1)}, u32[]{:S(2)}, u32[]{:S(2)}) collective-permute-start(bf16[128,640]{1,0:T(8,128)(2,1)S(1)} %get-tuple-element.58), channel_id=1, source_target_pairs={{0,2},{2,0},{4,6},{6,4},{1,3},{3,1},{5,7},{7,5},{8,10},{10,8},{12,... | collective-permute-start | bytes 491528 | tf_op jit(solution)/shard_map/ppermute | solution.py:48
  39.6 9.2 %collective-permute-start.16 = (bf16[80,640]{1,0:T(8,128)(2,1)S(1)}, bf16[80,640]{1,0:T(8,128)(2,1)S(1)}, u32[]{:S(2)}, u32[]{:S(2)}) collective-permute-start(bf16[80,640]{1,0:T(8,128)(2,1)S(1)} %get-tuple-element.59), channel_id=1, source_target_pairs={{0,6},{2,4},{4,2},{6,0},{1,7},{3,5},{5,3},{7,1},{8,14},{10,12},{12... | collective-permute-start | bytes 307208 | tf_op jit(solution)/shard_map/ppermute | solution.py:48
  41.0 8.4 %collective-permute-start.18 = (bf16[48,640]{1,0:T(8,128)(2,1)S(1)}, bf16[48,640]{1,0:T(8,128)(2,1)S(1)}, u32[]{:S(2)}, u32[]{:S(2)}) collective-permute-start(bf16[48,640]{1,0:T(8,128)(2,1)S(1)} %shard_map.105), channel_id=1, source_target_pairs={{0,6},{2,4},{4,2},{6,0},{1,7},{3,5},{5,3},{7,1},{8,14},{10,12},{12... | collective-permute-start | bytes 184328 | tf_op jit(solution)/shard_map/ppermute | solution.py:48

commit v11 on v9

--- a/solution.py
+++ b/solution.py
@@ -484,7 +484,7 @@
         after(pick_near, *far), found_near, rest_near, [shape((tok, cols), F32)] + [shape((tok, cols), BF16)] * (joined - 1)
     )
     direct = [swap(far[0], "seq", joined)] + [
-        swap(after(far[2 * m], *near), "seq", joined + m) for m in range(1, joined)
+        swap(after(far[2 * m], *near, *sums), "seq", joined + m) for m in range(1, joined)
     ]
     whole = [swap(near[m], "seq", m) for m in range(1, joined)]
     states = call(

time: 50.2 us -> 50.2 us (level)
  transfers between devices with their start and end apart: 19 -> 19, of which waited for: 13 -> 12; matrix products, arithmetic and copies ran while one was open for 1% -> 1% of each run, Pallas kernels for 8% -> 8%
where the time goes in v11:
time: 50.2 us; the launch traced here: 50.1 us
  starting transfers between devices  21.2 us (42%)
  waiting for transfers between devices  20.9 us (42%)
  Pallas kernels  6.69 us (13%)
  between operations  0.78 us (2%)
  other arithmetic  0.51 us (1%)
    ppermute x19, starting transfers between devices, swap(): return lax.ppermute(x, axis, [(i, i ^ k) for i in range(n)])  21.2 us
    ppermute x19, waiting for transfers between devices, swap(): return lax.ppermute(x, axis, [(i, i ^ k) for i in range(n)])  20.9 us
    pallas_call x2, Pallas kernels, mix(): call(functools.partial(mix_kernel, n), outs, [VMEM] * (n + 4), [VMEM] * l...  1.94 us
    pallas_call x1, Pallas kernels, shards_in_place(): call(functools.partial(early_kernel, n, n_tp), [shape((rows // n_tp, rows...  1.32 us
  transfers between devices with their start and end apart: 19, of which 12 were waited for; matrix products, arithmetic and copies ran while one was open for 1% of the time, Pallas kernels for 8%

profile of v11, /device:TPU:0, one launch (start us, length us, event | category | flops | bytes accessed | tf_op | source)
XLA Modules:
  0.0 50.1 jit_solution(13919168369190512494)
XLA Ops:
  0.7 0.5 %collective-permute-start = (bf16[256,640]{1,0:T(8,128)(2,1)}, bf16[256,640]{1,0:T(8,128)(2,1)S(1)}, u32[]{:S(2)}, u32[]{:S(2)}) collective-permute-start(bf16[256,640]{1,0:T(8,128)(2,1)} %refs_4_.1), channel_id=1, source_target_pairs={{0,1},{1,0},{2,3},{3,2},{4,5},{5,4},{6,7},{7,6},{8,9},{9,8},{10,11... | collective-permute-start | bytes 983048 | tf_op jit(solution)/shard_map/ppermute | solution.py:48
  1.2 1.3 %shard_map.95 = (bf16[128,256]{1,0:T(8,128)(2,1)S(1)}, bf16[128,640]{1,0:T(8,128)(2,1)S(1)}, bf16[16,128]{1,0:T(8,128)(2,1)S(1)}, f32[1,5120]{1,0:T(1,128)S(1)}) custom-call(bf16[256,640]{1,0:T(8,128)(2,1)} %refs_4_.1, s32[4]{0:T(128)} %lengths.1, s32[4]{0:T(128)} %group_of.1, s32[4]{0:T(128)} %rewards.1, f32[2,128]{1,0:T(2,128)} %bitcast.6, ...), custom_call_target="tpu_custom_call" | custom-call | tf_op jit(solution)/shard_map/pallas_call | solution.py:380
  2.5 0.1 collective-permute-done.sibling
  2.6 0.2 shard_map.96
  2.9 2.9 %collective-permute-start.1 = (bf16[32,1280]{1,0:T(8,128)(2,1)S(1)}, bf16[32,1280]{1,0:T(8,128)(2,1)S(1)}, u32[]{:S(2)}, u32[]{:S(2)}) collective-permute-start(bf16[32,1280]{1,0:T(8,128)(2,1)S(1)} %get-tuple-element.36), channel_id=1, source_target_pairs={{0,8},{8,0},{16,24},{24,16},{1,9},{9,1},{17,25},{25,17},{2,10},{10... | collective-permute-start | bytes 245768 | tf_op jit(solution)/shard_map/ppermute | solution.py:48
  5.8 1.5 %collective-permute-start.2 = (bf16[32,1280]{1,0:T(8,128)(2,1)S(1)}, bf16[32,1280]{1,0:T(8,128)(2,1)S(1)}, u32[]{:S(2)}, u32[]{:S(2)}) collective-permute-start(bf16[32,1280]{1,0:T(8,128)(2,1)S(1)} %get-tuple-element.37), channel_id=1, source_target_pairs={{0,16},{8,24},{16,0},{24,8},{1,17},{9,25},{17,1},{25,9},{2,18},{10... | collective-permute-start | bytes 245768 | tf_op jit(solution)/shard_map/ppermute | solution.py:48
  7.3 0.0 collective-permute-start.3
  7.3 1.2 %collective-permute-done.1.refs_1_ = bf16[32,1280]{1,0:T(8,128)(2,1)S(1)} collective-permute-done((bf16[32,1280]{1,0:T(8,128)(2,1)S(1)}, bf16[32,1280]{1,0:T(8,128)(2,1)S(1)}, u32[]{:S(2)}, u32[]{:S(2)}) %collective-permute-start.1) | collective-permute-done | bytes 81952 | tf_op jit(solution)/shard_map/ppermute | solution.py:48
  8.5 2.5 %collective-permute-done.2.refs_2_ = bf16[32,1280]{1,0:T(8,128)(2,1)S(1)} collective-permute-done((bf16[32,1280]{1,0:T(8,128)(2,1)S(1)}, bf16[32,1280]{1,0:T(8,128)(2,1)S(1)}, u32[]{:S(2)}, u32[]{:S(2)}) %collective-permute-start.2) | collective-permute-done | bytes 81952 | tf_op jit(solution)/shard_map/ppermute | solution.py:48
  11.1 1.6 %collective-permute-done.3.refs_3_ = bf16[32,1280]{1,0:T(8,128)(2,1)S(1)} collective-permute-done((bf16[32,1280]{1,0:T(8,128)(2,1)S(1)}, bf16[32,1280]{1,0:T(8,128)(2,1)S(1)}, u32[]{:S(2)}, u32[]{:S(2)}) %collective-permute-start.3) | collective-permute-done | bytes 81952 | tf_op jit(solution)/shard_map/ppermute | solution.py:48
  12.6 0.2 shard_map.97
  12.9 2.7 %collective-permute-start.4 = (bf16[16,2688]{1,0:T(8,128)(2,1)S(1)}, bf16[16,2688]{1,0:T(8,128)(2,1)S(1)}, u32[]{:S(2)}, u32[]{:S(2)}) collective-permute-start(bf16[16,2688]{1,0:T(8,128)(2,1)S(1)} %get-tuple-element.39), channel_id=1, source_target_pairs={{0,4},{2,6},{4,0},{6,2},{1,5},{3,7},{5,1},{7,3},{8,12},{10,14},{12... | collective-permute-start | bytes 258056 | tf_op jit(solution)/shard_map/ppermute | solution.py:48
  15.5 1.6 %collective-permute-start.5 = (bf16[16,2688]{1,0:T(8,128)(2,1)S(1)}, bf16[16,2688]{1,0:T(8,128)(2,1)S(1)}, u32[]{:S(2)}, u32[]{:S(2)}) collective-permute-start(bf16[16,2688]{1,0:T(8,128)(2,1)S(1)} %get-tuple-element.40), channel_id=1, source_target_pairs={{0,2},{2,0},{4,6},{6,4},{1,3},{3,1},{5,7},{7,5},{8,10},{10,8},{12,... | collective-permute-start | bytes 258056 | tf_op jit(solution)/shard_map/ppermute | solution.py:48
  17.1 0.2 collective-permute-start.6
  17.3 3.6 %collective-permute-done.4.refs_0_ = bf16[16,2688]{1,0:T(8,128)(2,1)S(1)} collective-permute-done((bf16[16,2688]{1,0:T(8,128)(2,1)S(1)}, bf16[16,2688]{1,0:T(8,128)(2,1)S(1)}, u32[]{:S(2)}, u32[]{:S(2)}) %collective-permute-start.4) | collective-permute-done | bytes 86048 | tf_op jit(solution)/shard_map/ppermute | solution.py:48
  20.9 0.4 collective-permute-done.5.refs_1_
  21.3 2.1 %collective-permute-done.6.refs_2_ = bf16[16,2688]{1,0:T(8,128)(2,1)S(1)} collective-permute-done((bf16[16,2688]{1,0:T(8,128)(2,1)S(1)}, bf16[16,2688]{1,0:T(8,128)(2,1)S(1)}, u32[]{:S(2)}, u32[]{:S(2)}) %collective-permute-start.6) | collective-permute-done | bytes 86048 | tf_op jit(solution)/shard_map/ppermute | solution.py:48
  23.4 0.4 shard_map.99.refs_0_
  23.8 0.6 %collective-permute-start.7 = (bf16[72,1280]{1,0:T(8,128)(2,1)S(1)}, bf16[72,1280]{1,0:T(8,128)(2,1)S(1)}, u32[]{:S(2)}, u32[]{:S(2)}) collective-permute-start(bf16[72,1280]{1,0:T(8,128)(2,1)S(1)} %shard_map.99.refs_0_), channel_id=1, source_target_pairs={{0,8},{8,0},{16,24},{24,16},{1,9},{9,1},{17,25},{25,17},{2,10},{10... | collective-permute-start | bytes 552968 | tf_op jit(solution)/shard_map/ppermute | solution.py:48
  24.4 0.9 %collective-permute-start.8 = (bf16[72,1280]{1,0:T(8,128)(2,1)S(1)}, bf16[72,1280]{1,0:T(8,128)(2,1)S(1)}, u32[]{:S(2)}, u32[]{:S(2)}) collective-permute-start(bf16[72,1280]{1,0:T(8,128)(2,1)S(1)} %shard_map.99.refs_0_), channel_id=1, source_target_pairs={{0,16},{8,24},{16,0},{24,8},{1,17},{9,25},{17,1},{25,9},{2,18},{10... | collective-permute-start | bytes 552968 | tf_op jit(solution)/shard_map/ppermute | solution.py:48
  25.2 2.1 %collective-permute-start.9 = (bf16[72,1280]{1,0:T(8,128)(2,1)S(1)}, bf16[72,1280]{1,0:T(8,128)(2,1)S(1)}, u32[]{:S(2)}, u32[]{:S(2)}) collective-permute-start(bf16[72,1280]{1,0:T(8,128)(2,1)S(1)} %shard_map.99.refs_0_), channel_id=1, source_target_pairs={{0,24},{8,16},{16,8},{24,0},{1,25},{9,17},{17,9},{25,1},{2,26},{10... | collective-permute-start | bytes 552968 | tf_op jit(solution)/shard_map/ppermute | solution.py:48
  27.3 0.4 shard_map.102
  27.7 0.6 %shard_map.98 = (bf16[256,384]{1,0:T(8,128)(2,1)S(1)}, bf16[256,640]{1,0:T(8,128)(2,1)S(1)}, f32[256,640]{1,0:T(8,128)S(1)}, f32[256,640]{1,0:T(8,128)S(1)}) custom-call(bf16[16,2688]{1,0:T(8,128)(2,1)S(1)} %collective-permute-done.4.refs_0_, bf16[16,2688]{1,0:T(8,128)(2,1)S(1)} %collective-permute-done.5.refs_1_, ...), custom_call_target="tpu_custom_call" | custom-call | tf_op jit(solution)/shard_map/pallas_call | solution.py:433
  28.4 0.1 collective-permute-start.10
  28.5 1.5 %collective-permute-done.7.refs_1_ = bf16[72,1280]{1,0:T(8,128)(2,1)S(1)} collective-permute-done((bf16[72,1280]{1,0:T(8,128)(2,1)S(1)}, bf16[72,1280]{1,0:T(8,128)(2,1)S(1)}, u32[]{:S(2)}, u32[]{:S(2)}) %collective-permute-start.7) | collective-permute-done | bytes 184352 | tf_op jit(solution)/shard_map/ppermute | solution.py:48
  30.0 0.0 collective-permute-start.11
  30.0 2.3 %collective-permute-done.8.refs_2_ = bf16[72,1280]{1,0:T(8,128)(2,1)S(1)} collective-permute-done((bf16[72,1280]{1,0:T(8,128)(2,1)S(1)}, bf16[72,1280]{1,0:T(8,128)(2,1)S(1)}, u32[]{:S(2)}, u32[]{:S(2)}) %collective-permute-start.8) | collective-permute-done | bytes 184352 | tf_op jit(solution)/shard_map/ppermute | solution.py:48
  32.2 0.0 collective-permute-start.12
  32.2 0.0 collective-permute-done.9.refs_3_
  32.2 0.5 %collective-permute-start.13 = (bf16[72,1280]{1,0:T(8,128)(2,1)S(1)}, bf16[72,1280]{1,0:T(8,128)(2,1)S(1)}, u32[]{:S(2)}, u32[]{:S(2)}) collective-permute-start(bf16[72,1280]{1,0:T(8,128)(2,1)S(1)} %collective-permute-done.9.refs_3_), channel_id=1, source_target_pairs={{0,1},{1,0},{2,3},{3,2},{4,5},{5,4},{6,7},{7,6},{8,9},{9,8},{10,11... | collective-permute-start | bytes 552968 | tf_op jit(solution)/shard_map/ppermute | solution.py:48
  32.8 0.5 %shard_map.100.found = bf16[256,1280]{1,0:T(8,128)(2,1)S(1)} custom-call(bf16[256,640]{1,0:T(8,128)(2,1)S(1)} %get-tuple-element.55.pick, bf16[72,1280]{1,0:T(8,128)(2,1)S(1)} %shard_map.99.refs_0_, bf16[72,1280]{1,0:T(8,128)(2,1)S(1)} %collective-permute-done.7.refs_1_, bf16[72,1280]{1,0:T(8,128)(2,1)S(1)} %collective-permute-done.8.refs_2_, ...), custom_call_target="tpu_custom_call" | custom-call | tf_op jit(solution)/shard_map/pallas_call | solution.py:461
  33.3 0.3 shard_map.101.found
  33.6 0.0 collective-permute-done.10.refs_0_
  33.6 0.0 collective-permute-done.11.refs_1_
  33.6 0.0 collective-permute-done.12.refs_2_
  33.7 0.3 collective-permute-done.13.refs_3_
  33.9 0.9 %shard_map.103 = (bf16[64,640]{1,0:T(8,128)(2,1)S(1)}, bf16[64,640]{1,0:T(8,128)(2,1)S(1)}, bf16[64,640]{1,0:T(8,128)(2,1)S(1)}, f32[64,640]{1,0:T(8,128)S(1)}) custom-call(bf16[256,384]{1,0:T(8,128)(2,1)S(1)} %get-tuple-element.45.pick, bf16[256,1280]{1,0:T(8,128)(2,1)S(1)} %shard_map.101.found, f32[256,640]{1,0:T(8,128)S(1)} %get-tuple-element.46.rest, ...), custom_call_target="tpu_custom_call" | custom-call | tf_op jit(solution)/shard_map/pallas_call | solution.py:464
  34.8 0.6 %collective-permute-start.16 = (bf16[64,640]{1,0:T(8,128)(2,1)S(1)}, bf16[64,640]{1,0:T(8,128)(2,1)S(1)}, u32[]{:S(2)}, u32[]{:S(2)}) collective-permute-start(bf16[64,640]{1,0:T(8,128)(2,1)S(1)} %get-tuple-element.52), channel_id=1, source_target_pairs={{0,2},{2,0},{4,6},{6,4},{1,3},{3,1},{5,7},{7,5},{8,10},{10,8},{12,... | collective-permute-start | bytes 245768 | tf_op jit(solution)/shard_map/ppermute | solution.py:48
  35.4 1.6 %collective-permute-start.15 = (bf16[64,640]{1,0:T(8,128)(2,1)S(1)}, bf16[64,640]{1,0:T(8,128)(2,1)S(1)}, u32[]{:S(2)}, u32[]{:S(2)}) collective-permute-start(bf16[64,640]{1,0:T(8,128)(2,1)S(1)} %get-tuple-element.51), channel_id=1, source_target_pairs={{0,4},{2,6},{4,0},{6,2},{1,5},{3,7},{5,1},{7,3},{8,12},{10,14},{12... | collective-permute-start | bytes 245768 | tf_op jit(solution)/shard_map/ppermute | solution.py:48
  37.0 1.1 %shard_map.104 = (f32[128,640]{1,0:T(8,128)S(1)}, bf16[128,640]{1,0:T(8,128)(2,1)S(1)}) custom-call(bf16[256,640]{1,0:T(8,128)(2,1)S(1)} %get-tuple-element.55.pick, bf16[256,1280]{1,0:T(8,128)(2,1)S(1)} %shard_map.100.found, f32[256,640]{1,0:T(8,128)S(1)} %get-tuple-element.56.rest, bf16[1280,640]{1,0:T(8,128)(2,1)S(1)} %copy-done, ...), custom_call_target="tpu_custom_call" | custom-call | tf_op jit(solution)/shard_map/pallas_call | solution.py:464
  38.1 1.5 %collective-permute-start.14 = (bf16[128,640]{1,0:T(8,128)(2,1)S(1)}, bf16[128,640]{1,0:T(8,128)(2,1)S(1)}, u32[]{:S(2)}, u32[]{:S(2)}) collective-permute-start(bf16[128,640]{1,0:T(8,128)(2,1)S(1)} %get-tuple-element.58), channel_id=1, source_target_pairs={{0,2},{2,0},{4,6},{6,4},{1,3},{3,1},{5,7},{7,5},{8,10},{10,8},{12,... | collective-permute-start | bytes 491528 | tf_op jit(solution)/shard_map/ppermute | solution.py:48
  39.6 1.5 %collective-permute-done.16.other = bf16[64,640]{1,0:T(8,128)(2,1)S(1)} collective-permute-done((bf16[64,640]{1,0:T(8,128)(2,1)S(1)}, bf16[64,640]{1,0:T(8,128)(2,1)S(1)}, u32[]{:S(2)}, u32[]{:S(2)}) %collective-permute-start.16) | collective-permute-done | bytes 81952 | tf_op jit(solution)/shard_map/ppermute | solution.py:48
  41.1 0.1 collective-permute-start.18
  41.2 3.8 %collective-permute-start.17 = (bf16[64,640]{1,0:T(8,128)(2,1)S(1)}, bf16[64,640]{1,0:T(8,128)(2,1)S(1)}, u32[]{:S(2)}, u32[]{:S(2)}) collective-permute-start(bf16[64,640]{1,0:T(8,128)(2,1)S(1)} %get-tuple-element.59), channel_id=1, source_target_pairs={{0,6},{2,4},{4,2},{6,0},{1,7},{3,5},{5,3},{7,1},{8,14},{10,12},{12... | collective-permute-start | bytes 245768 | tf_op jit(solution)/shard_map/ppermute | solution.py:48
  45.0 0.5 %convert_bitcast_fusion = bf16[128,2]{0,1:T(2,128)(2,1)} fusion(f32[2,128]{1,0:T(2,128)S(1)} %shard_map.102), kind=kLoop, calls=%fused_computation | loop fusion | flops 256 | bytes 1536 | tf_op jit(solution)/shard_map/transpose | solution.py:496
  45.5 3.8 %collective-permute-done.17.refs_3_ = bf16[64,640]{1,0:T(8,128)(2,1)S(1)} collective-permute-done((bf16[64,640]{1,0:T(8,128)(2,1)S(1)}, bf16[64,640]{1,0:T(8,128)(2,1)S(1)}, u32[]{:S(2)}, u32[]{:S(2)}) %collective-permute-start.17) | collective-permute-done | bytes 81952 | tf_op jit(solution)/shard_map/ppermute | solution.py:48
  49.3 0.0 collective-permute-done.18.refs_4_
  49.3 0.7 %shard_map.106 = bf16[128,640]{1,0:T(8,128)(2,1)} custom-call(f32[128,640]{1,0:T(8,128)S(1)} %get-tuple-element.57.refs_0_, bf16[128,640]{1,0:T(8,128)(2,1)S(1)} %collective-permute-done.14.refs_1_, bf16[64,640]{1,0:T(8,128)(2,1)S(1)} %collective-permute-done.15.refs_2_, bf16[64,640]{1,0:T(8,128)(2,1)S(1)} %collective-permute-done.17.refs_3_, ...), custom_call_target="tpu_custom_call" | custom-call | tf_op jit(solution)/shard_map/pallas_call | solution.py:490
  (7 shorter events, 0.0 us)
Async XLA Ops:
  0.6 27.1 %copy-start.1 = (bf16[256,640]{1,0:T(8,128)(2,1)S(1)}, bf16[256,640]{1,0:T(8,128)(2,1)}, u32[]{:S(2)}) copy-start(bf16[256,640]{1,0:T(8,128)(2,1)} %refs_4_.1) | copy-start | bytes 983044
  0.6 27.1 %copy-start = (bf16[1280,640]{1,0:T(8,128)(2,1)S(1)}, bf16[1280,640]{1,0:T(8,128)(2,1)}, u32[]{:S(2)}) copy-start(bf16[1280,640]{1,0:T(8,128)(2,1)} %projection.3) | copy-start | bytes 4915204
  0.7 2.0 %collective-permute-start = (bf16[256,640]{1,0:T(8,128)(2,1)}, bf16[256,640]{1,0:T(8,128)(2,1)S(1)}, u32[]{:S(2)}, u32[]{:S(2)}) collective-permute-start(bf16[256,640]{1,0:T(8,128)(2,1)} %refs_4_.1), channel_id=1, source_target_pairs={{0,1},{1,0},{2,3},{3,2},{4,5},{5,4},{6,7},{7,6},{8,9},{9,8},{10,11... | collective-permute-start | bytes 983048 | tf_op jit(solution)/shard_map/ppermute | solution.py:48
  2.9 5.7 %collective-permute-start.1 = (bf16[32,1280]{1,0:T(8,128)(2,1)S(1)}, bf16[32,1280]{1,0:T(8,128)(2,1)S(1)}, u32[]{:S(2)}, u32[]{:S(2)}) collective-permute-start(bf16[32,1280]{1,0:T(8,128)(2,1)S(1)} %get-tuple-element.36), channel_id=1, source_target_pairs={{0,8},{8,0},{16,24},{24,16},{1,9},{9,1},{17,25},{25,17},{2,10},{10... | collective-permute-start | bytes 245768 | tf_op jit(solution)/shard_map/ppermute | solution.py:48
  5.8 5.3 %collective-permute-start.2 = (bf16[32,1280]{1,0:T(8,128)(2,1)S(1)}, bf16[32,1280]{1,0:T(8,128)(2,1)S(1)}, u32[]{:S(2)}, u32[]{:S(2)}) collective-permute-start(bf16[32,1280]{1,0:T(8,128)(2,1)S(1)} %get-tuple-element.37), channel_id=1, source_target_pairs={{0,16},{8,24},{16,0},{24,8},{1,17},{9,25},{17,1},{25,9},{2,18},{10... | collective-permute-start | bytes 245768 | tf_op jit(solution)/shard_map/ppermute | solution.py:48
  7.3 5.3 %collective-permute-start.3 = (bf16[32,1280]{1,0:T(8,128)(2,1)S(1)}, bf16[32,1280]{1,0:T(8,128)(2,1)S(1)}, u32[]{:S(2)}, u32[]{:S(2)}) collective-permute-start(bf16[32,1280]{1,0:T(8,128)(2,1)S(1)} %get-tuple-element.38), channel_id=1, source_target_pairs={{0,24},{8,16},{16,8},{24,0},{1,25},{9,17},{17,9},{25,1},{2,26},{10... | collective-permute-start | bytes 245768 | tf_op jit(solution)/shard_map/ppermute | solution.py:48
  12.9 8.0 %collective-permute-start.4 = (bf16[16,2688]{1,0:T(8,128)(2,1)S(1)}, bf16[16,2688]{1,0:T(8,128)(2,1)S(1)}, u32[]{:S(2)}, u32[]{:S(2)}) collective-permute-start(bf16[16,2688]{1,0:T(8,128)(2,1)S(1)} %get-tuple-element.39), channel_id=1, source_target_pairs={{0,4},{2,6},{4,0},{6,2},{1,5},{3,7},{5,1},{7,3},{8,12},{10,14},{12... | collective-permute-start | bytes 258056 | tf_op jit(solution)/shard_map/ppermute | solution.py:48
  15.5 5.7 %collective-permute-start.5 = (bf16[16,2688]{1,0:T(8,128)(2,1)S(1)}, bf16[16,2688]{1,0:T(8,128)(2,1)S(1)}, u32[]{:S(2)}, u32[]{:S(2)}) collective-permute-start(bf16[16,2688]{1,0:T(8,128)(2,1)S(1)} %get-tuple-element.40), channel_id=1, source_target_pairs={{0,2},{2,0},{4,6},{6,4},{1,3},{3,1},{5,7},{7,5},{8,10},{10,8},{12,... | collective-permute-start | bytes 258056 | tf_op jit(solution)/shard_map/ppermute | solution.py:48
  17.1 6.3 %collective-permute-start.6 = (bf16[16,2688]{1,0:T(8,128)(2,1)S(1)}, bf16[16,2688]{1,0:T(8,128)(2,1)S(1)}, u32[]{:S(2)}, u32[]{:S(2)}) collective-permute-start(bf16[16,2688]{1,0:T(8,128)(2,1)S(1)} %get-tuple-element.41), channel_id=1, source_target_pairs={{0,6},{2,4},{4,2},{6,0},{1,7},{3,5},{5,3},{7,1},{8,14},{10,12},{12... | collective-permute-start | bytes 258056 | tf_op jit(solution)/shard_map/ppermute | solution.py:48
  23.8 6.2 %collective-permute-start.7 = (bf16[72,1280]{1,0:T(8,128)(2,1)S(1)}, bf16[72,1280]{1,0:T(8,128)(2,1)S(1)}, u32[]{:S(2)}, u32[]{:S(2)}) collective-permute-start(bf16[72,1280]{1,0:T(8,128)(2,1)S(1)} %shard_map.99.refs_0_), channel_id=1, source_target_pairs={{0,8},{8,0},{16,24},{24,16},{1,9},{9,1},{17,25},{25,17},{2,10},{10... | collective-permute-start | bytes 552968 | tf_op jit(solution)/shard_map/ppermute | solution.py:48
  24.4 7.9 %collective-permute-start.8 = (bf16[72,1280]{1,0:T(8,128)(2,1)S(1)}, bf16[72,1280]{1,0:T(8,128)(2,1)S(1)}, u32[]{:S(2)}, u32[]{:S(2)}) collective-permute-start(bf16[72,1280]{1,0:T(8,128)(2,1)S(1)} %shard_map.99.refs_0_), channel_id=1, source_target_pairs={{0,16},{8,24},{16,0},{24,8},{1,17},{9,25},{17,1},{25,9},{2,18},{10... | collective-permute-start | bytes 552968 | tf_op jit(solution)/shard_map/ppermute | solution.py:48
  25.2 7.0 %collective-permute-start.9 = (bf16[72,1280]{1,0:T(8,128)(2,1)S(1)}, bf16[72,1280]{1,0:T(8,128)(2,1)S(1)}, u32[]{:S(2)}, u32[]{:S(2)}) collective-permute-start(bf16[72,1280]{1,0:T(8,128)(2,1)S(1)} %shard_map.99.refs_0_), channel_id=1, source_target_pairs={{0,24},{8,16},{16,8},{24,0},{1,25},{9,17},{17,9},{25,1},{2,26},{10... | collective-permute-start | bytes 552968 | tf_op jit(solution)/shard_map/ppermute | solution.py:48
  28.4 5.2 %collective-permute-start.10 = (bf16[72,1280]{1,0:T(8,128)(2,1)S(1)}, bf16[72,1280]{1,0:T(8,128)(2,1)S(1)}, u32[]{:S(2)}, u32[]{:S(2)}) collective-permute-start(bf16[72,1280]{1,0:T(8,128)(2,1)S(1)} %shard_map.99.refs_0_), channel_id=1, source_target_pairs={{0,1},{1,0},{2,3},{3,2},{4,5},{5,4},{6,7},{7,6},{8,9},{9,8},{10,11... | collective-permute-start | bytes 552968 | tf_op jit(solution)/shard_map/ppermute | solution.py:48
  30.0 3.6 %collective-permute-start.11 = (bf16[72,1280]{1,0:T(8,128)(2,1)S(1)}, bf16[72,1280]{1,0:T(8,128)(2,1)S(1)}, u32[]{:S(2)}, u32[]{:S(2)}) collective-permute-start(bf16[72,1280]{1,0:T(8,128)(2,1)S(1)} %collective-permute-done.7.refs_1_), channel_id=1, source_target_pairs={{0,1},{1,0},{2,3},{3,2},{4,5},{5,4},{6,7},{7,6},{8,9},{9,8},{10,11... | collective-permute-start | bytes 552968 | tf_op jit(solution)/shard_map/ppermute | solution.py:48
  32.2 1.4 %collective-permute-start.12 = (bf16[72,1280]{1,0:T(8,128)(2,1)S(1)}, bf16[72,1280]{1,0:T(8,128)(2,1)S(1)}, u32[]{:S(2)}, u32[]{:S(2)}) collective-permute-start(bf16[72,1280]{1,0:T(8,128)(2,1)S(1)} %collective-permute-done.8.refs_2_), channel_id=1, source_target_pairs={{0,1},{1,0},{2,3},{3,2},{4,5},{5,4},{6,7},{7,6},{8,9},{9,8},{10,11... | collective-permute-start | bytes 552968 | tf_op jit(solution)/shard_map/ppermute | solution.py:48
  32.2 1.7 %collective-permute-start.13 = (bf16[72,1280]{1,0:T(8,128)(2,1)S(1)}, bf16[72,1280]{1,0:T(8,128)(2,1)S(1)}, u32[]{:S(2)}, u32[]{:S(2)}) collective-permute-start(bf16[72,1280]{1,0:T(8,128)(2,1)S(1)} %collective-permute-done.9.refs_3_), channel_id=1, source_target_pairs={{0,1},{1,0},{2,3},{3,2},{4,5},{5,4},{6,7},{7,6},{8,9},{9,8},{10,11... | collective-permute-start | bytes 552968 | tf_op jit(solution)/shard_map/ppermute | solution.py:48
  34.8 6.2 %collective-permute-start.16 = (bf16[64,640]{1,0:T(8,128)(2,1)S(1)}, bf16[64,640]{1,0:T(8,128)(2,1)S(1)}, u32[]{:S(2)}, u32[]{:S(2)}) collective-permute-start(bf16[64,640]{1,0:T(8,128)(2,1)S(1)} %get-tuple-element.52), channel_id=1, source_target_pairs={{0,2},{2,0},{4,6},{6,4},{1,3},{3,1},{5,7},{7,5},{8,10},{10,8},{12,... | collective-permute-start | bytes 245768 | tf_op jit(solution)/shard_map/ppermute | solution.py:48
  35.4 10.1 %collective-permute-start.15 = (bf16[64,640]{1,0:T(8,128)(2,1)S(1)}, bf16[64,640]{1,0:T(8,128)(2,1)S(1)}, u32[]{:S(2)}, u32[]{:S(2)}) collective-permute-start(bf16[64,640]{1,0:T(8,128)(2,1)S(1)} %get-tuple-element.51), channel_id=1, source_target_pairs={{0,4},{2,6},{4,0},{6,2},{1,5},{3,7},{5,1},{7,3},{8,12},{10,14},{12... | collective-permute-start | bytes 245768 | tf_op jit(solution)/shard_map/ppermute | solution.py:48
  38.1 7.4 %collective-permute-start.14 = (bf16[128,640]{1,0:T(8,128)(2,1)S(1)}, bf16[128,640]{1,0:T(8,128)(2,1)S(1)}, u32[]{:S(2)}, u32[]{:S(2)}) collective-permute-start(bf16[128,640]{1,0:T(8,128)(2,1)S(1)} %get-tuple-element.58), channel_id=1, source_target_pairs={{0,2},{2,0},{4,6},{6,4},{1,3},{3,1},{5,7},{7,5},{8,10},{10,8},{12,... | collective-permute-start | bytes 491528 | tf_op jit(solution)/shard_map/ppermute | solution.py:48
  41.1 8.3 %collective-permute-start.18 = (bf16[64,640]{1,0:T(8,128)(2,1)S(1)}, bf16[64,640]{1,0:T(8,128)(2,1)S(1)}, u32[]{:S(2)}, u32[]{:S(2)}) collective-permute-start(bf16[64,640]{1,0:T(8,128)(2,1)S(1)} %shard_map.105), channel_id=1, source_target_pairs={{0,6},{2,4},{4,2},{6,0},{1,7},{3,5},{5,3},{7,1},{8,14},{10,12},{12... | collective-permute-start | bytes 245768 | tf_op jit(solution)/shard_map/ppermute | solution.py:48
  41.2 8.2 %collective-permute-start.17 = (bf16[64,640]{1,0:T(8,128)(2,1)S(1)}, bf16[64,640]{1,0:T(8,128)(2,1)S(1)}, u32[]{:S(2)}, u32[]{:S(2)}) collective-permute-start(bf16[64,640]{1,0:T(8,128)(2,1)S(1)} %get-tuple-element.59), channel_id=1, source_target_pairs={{0,6},{2,4},{4,2},{6,0},{1,7},{3,5},{5,3},{7,1},{8,14},{10,12},{12... | collective-permute-start | bytes 245768 | tf_op jit(solution)/shard_map/ppermute | solution.py:48
